TPU v7x, 256 devices: a whole 4x4x8 slice. The times are simulated.
256 devices in a mesh: dp: 64 (over z, x_lo, y), tensor: 4 (over x_hi, core).
Axes of the slice: x: 4 (x_hi: 2, x_lo: 2; x = x_hi * 2 + x_lo), y: 4, z: 8, core: 2. Of those that a mesh axis runs over, the one named last changes fastest.
Arguments:
- head_outputs: bfloat16 [32768, 4096], P('dp', 'tensor'), may hold values from -6 to 6
- output_gradient: bfloat16 [32768, 4608], P(('dp', 'tensor')), may hold values from -6 to 6
- frozen_weight: bfloat16 [4608, 4096], P('dp', 'tensor'), may hold values from -0.09375 to 0.09375
- adapter_down_factors: bfloat16 [4096, 8192], P('tensor', 'dp'), may hold values from -0.09375 to 0.09375
- adapter_up_factors: bfloat16 [8192, 4608], P('dp'), may hold values from -0.09375 to 0.09375
- tenant_index: int32 [32768], P('dp'), may hold values from 0 to 511, as said below
- tenant_group_counts: int32 [64], P('dp'), may hold values from 32 to 512, as said below
Outputs:
- head_feature_gradient: bfloat16 [32768, 4096], P('dp', 'tensor')
- down_factor_gradient: float32 [4096, 8192], P('tensor', 'dp')
- up_factor_gradient: float32 [8192, 4608], P('dp')
Inputs may be any that keep to these rules, and one draw needn't show every extreme that they name: `tenant_index`: the tenants of group g (rows g * 512 to (g + 1) * 512 - 1) are g * 8 to (g + 1) * 8 - 1. `tenant_group_counts`: some group holds exactly 512 live rows.
All inputs are finite; a program needn't handle non-finite values.
Results may differ from a plain program's by a relative error of at most 0.0034.
Values may be sent and summed in bfloat16 or wider, within the bound.
No kernel may reach another device: no remote copies, remote signals or barrier semaphores. Data moves between devices by JAX's collectives and lax.ppermute only.
A program may use at most 128 MiB of HBM per device.

v0:
```python
import jax
import jax.numpy as jnp
from jax import lax
from jax.experimental import pallas as pl
from jax.experimental.pallas import tpu as pltpu
from jax.sharding import PartitionSpec as P

ADAPTER_RANK = 16
TEN_DEV = 8
ADAPTER_SCALE = 2.0
NZ, NX, NY = 8, 2, 4


def contract(left, right, left_dim, right_dim):
    return lax.dot_general(
        left, right, (((left_dim,), (right_dim,)), ((), ())), preferred_element_type=jnp.float32
    )


def fetch(x, dz=0, dx=0, dy=0):
    pairs = []
    for z in range(NZ):
        for a in range(NX):
            for y in range(NY):
                source = (((z + dz) % NZ) * NX + (a + dx) % NX) * NY + (y + dy) % NY
                pairs.append((source, (z * NX + a) * NY + y))
    return lax.ppermute(x, "dp", pairs)


def swap_tensor(x, mask):
    return lax.ppermute(x, "tensor", [(t, t ^ mask) for t in range(4)])


def together(*values):
    return lax.optimization_barrier(values)


def split_kernel(start_ref, g_ref, out_ref):
    width = out_ref.shape[2]
    for block in range(NZ):
        slot = lax.rem(block - start_ref[0] + NZ, NZ)
        out_ref[slot] = g_ref[:, block * width : (block + 1) * width]


def split_columns(gradients, start):
    rows, depth = gradients.shape
    step = rows // 4
    width = depth // NZ
    return pl.pallas_call(
        split_kernel,
        grid_spec=pltpu.PrefetchScalarGridSpec(
            num_scalar_prefetch=1,
            grid=(4,),
            in_specs=[pl.BlockSpec((step, depth), lambda i, s: (i, 0))],
            out_specs=pl.BlockSpec((NZ, step, width), lambda i, s: (0, i, 0)),
        ),
        out_shape=jax.ShapeDtypeStruct((NZ, rows, width), gradients.dtype),
        compiler_params=pltpu.CompilerParams(vmem_limit_bytes=32 * 1024 * 1024),
    )(start, gradients)


def put(buffer, chunk, index):
    axis = buffer.ndim - 3
    return lax.dynamic_update_slice_in_dim(buffer, jnp.expand_dims(chunk, axis), index % NY, axis)


def in_y_order(chunks, y):
    own = chunks[0]
    buffer = jnp.broadcast_to(
        jnp.expand_dims(own, own.ndim - 2), own.shape[:-2] + (NY,) + own.shape[-2:]
    )
    for offset, chunk in chunks.items():
        if offset:
            buffer = put(buffer, chunk, y + offset)
    return buffer


def body(
    head_outputs,
    output_gradient,
    frozen_weight,
    adapter_down_factors,
    adapter_up_factors,
    tenant_index,
    tenant_group_counts,
):
    row_count = head_outputs.shape[0]
    shard_rows, feature_width = frozen_weight.shape
    a_width = feature_width * 5 // 8
    group = lax.axis_index("dp").astype(jnp.int32)
    z, xl, y = group // (NX * NY), (group // NY) % NX, group % NY

    other = fetch(frozen_weight, dx=1)
    gradients = lax.all_gather(output_gradient, "tensor", axis=0, tiled=True)
    partial = jnp.dot(head_outputs, adapter_down_factors, preferred_element_type=jnp.float32)
    core_partial = swap_tensor(partial, 1)

    def pair(columns):
        mine, far = frozen_weight[:, columns], other[:, columns]
        return jnp.where(xl == 0, jnp.stack([mine, far]), jnp.stack([far, mine]))

    pair_a, pair_b = pair(slice(0, a_width)), pair(slice(a_width, None))

    a_p1, a_m1 = fetch(pair_a, dz=1), fetch(pair_a, dz=-1)
    b_p, b_m, b_o = fetch(pair_b, dy=1), fetch(pair_b, dy=-1), fetch(pair_b, dy=2)

    a_p1, a_m1 = together(a_p1, a_m1)
    a_p2, a_m2 = fetch(a_p1, dz=1), fetch(a_m1, dz=-1)
    b_p, b_m, b_o, pair_b, a_p1, a_m1 = together(b_p, b_m, b_o, pair_b, a_p1, a_m1)
    b_own = in_y_order({0: pair_b, 1: b_p, 3: b_m, 2: b_o}, y)
    b_own = b_own.reshape(NX * NY * shard_rows, -1)
    b_p1, b_m1 = fetch(b_own, dz=1), fetch(b_own, dz=-1)

    a_p2, a_m2, b_own = together(a_p2, a_m2, b_own)
    a_p3, a_m3 = fetch(a_p2, dz=1), fetch(a_m2, dz=-1)
    first = jnp.stack([a_m1, pair_a, a_p1, a_p2])
    f_p, f_m = fetch(first, dy=1), fetch(first, dy=-1)
    partial, core_partial, first = together(partial, core_partial, first)
    chip_sum = partial + core_partial
    far_sum = swap_tensor(chip_sum, 2)

    a_p3, a_m3 = together(a_p3, a_m3)
    a_o = fetch(a_p3, dz=1)

    a_o, b_p1, b_m1 = together(a_o, b_p1, b_m1)
    b_p2, b_m2 = fetch(b_p1, dz=1), fetch(b_m1, dz=-1)
    second = jnp.stack([a_p3, a_o, a_m3, a_m2])

    f_p, f_m, second = together(f_p, f_m, second)
    f_o = fetch(f_m, dy=-1)
    s_p, s_m = fetch(second, dy=1), fetch(second, dy=-1)

    b_p2, b_m2, f_p, f_m = together(b_p2, b_m2, f_p, f_m)
    b_p3, b_m3 = fetch(b_p2, dz=1), fetch(b_m2, dz=-1)

    f_o, s_p, s_m, b_p2, gradients = together(f_o, s_p, s_m, b_p2, gradients)
    s_o = fetch(s_p, dy=1)
    by_z = split_columns(gradients, ((z + NZ - 1) % NZ).reshape(1))

    b_p3, b_m3, s_p, f_o, by_z = together(b_p3, b_m3, s_p, f_o, by_z)
    cut = b_own.shape[0] // 3 // 16 * 16
    b_o4 = [fetch(b_p3[:cut], dz=1), fetch(b_m3[cut:], dz=-1)]

    position = jnp.arange(row_count, dtype=jnp.int32)
    active_rows = position < tenant_group_counts[0]
    slot_lookup = jnp.arange(adapter_down_factors.shape[1], dtype=jnp.int32) // ADAPTER_RANK
    select_rows = (
        active_rows[:, None] & (slot_lookup[None, :] == (tenant_index % TEN_DEV)[:, None])
    ).astype(jnp.float32)
    adapter_input = ((chip_sum + far_sum) * select_rows).astype(jnp.bfloat16)
    (adapter_input,) = together(adapter_input)
    adapter_backward = (contract(gradients, adapter_up_factors, 1, 1) * select_rows).astype(
        jnp.bfloat16
    )
    down_factor_gradient = ADAPTER_SCALE * contract(head_outputs, adapter_backward, 0, 0)
    up_factor_gradient = ADAPTER_SCALE * contract(adapter_input, gradients, 0, 0)

    def product(total, terms):
        for slot, chunk in terms:
            total = total + contract(by_z[slot], chunk.reshape(by_z.shape[2], -1), 1, 0)
        return total

    first_all = in_y_order({0: first, 1: f_p, 3: f_m, 2: f_o}, y)
    second_all = in_y_order({0: second, 1: s_p, 3: s_m}, y)
    a_total = product(
        ADAPTER_SCALE * contract(adapter_backward, adapter_down_factors[:a_width], 1, 1),
        [(i, first_all[i]) for i in range(4)],
    )
    b_total = product(
        ADAPTER_SCALE * contract(adapter_backward, adapter_down_factors[a_width:], 1, 1),
        [(1, b_own), (0, b_m1), (2, b_p1), (7, b_m2), (3, b_p2), (6, b_m3), (4, b_p3)],
    )
    (
        s_o, b_p4, b_m4, second_all, a_total, b_total, down_factor_gradient, up_factor_gradient
    ) = together(
        s_o, *b_o4, second_all, a_total, b_total, down_factor_gradient, up_factor_gradient
    )
    second_all = put(second_all, s_o, y + 2)
    b_total = product(b_total, [(5, jnp.concatenate([b_p4, b_m4], 0))])
    a_total = product(a_total, [(4 + i, second_all[i]) for i in range(4)])
    head_feature_gradient = jnp.where(
        active_rows[:, None], jnp.concatenate([a_total, b_total], 1), 0.0
    ).astype(jnp.bfloat16)
    return (head_feature_gradient, down_factor_gradient, up_factor_gradient)


def solution(mesh):
    in_specs = (
        P("dp", "tensor"),
        P(("dp", "tensor"), None),
        P("dp", "tensor"),
        P("tensor", "dp"),
        P("dp", None),
        P("dp"),
        P("dp"),
    )
    out_specs = (P("dp", "tensor"), P("tensor", "dp"), P("dp", None))
    return jax.shard_map(body, mesh=mesh, in_specs=in_specs, out_specs=out_specs, check_vma=False)
```

profile of v0, /device:TPU:6, one launch (start us, length us, event | category | flops | bytes accessed | tf_op | source)
XLA Modules:
  0.0 149.3 jit_solution(2275928376406872911)
XLA Ops:
  10.6 3.2 %collective-permute-done = bf16[72,1024]{1,0:T(8,128)(2,1)S(1)} collective-permute-done((bf16[72,1024]{1,0:T(8,128)(2,1)}, bf16[72,1024]{1,0:T(8,128)(2,1)S(1)}, u32[]{:S(2)}, u32[]{:S(2)}) %collective-permute-start) | collective-permute-done | bytes 147488 | tf_op jit(solution)/shard_map/ppermute | solution.py:27
  13.9 5.9 %collective-permute-start.4 = (bf16[2,72,640]{2,1,0:T(8,128)(2,1)S(1)}, bf16[2,72,640]{2,1,0:T(8,128)(2,1)S(1)}, u32[]{:S(2)}, u32[]{:S(2)}) collective-permute-start(bf16[2,72,640]{2,1,0:T(8,128)(2,1)S(1)} %maximum_select_fusion.1), channel_id=1, source_target_pairs={{32,0},{36,4},{40,8},{44,12},{48,16},{52,20},{56,24},{60,28},{64,3... | collective-permute-start | bytes 552968 | tf_op jit(solution)/shard_map/ppermute | solution.py:27
  19.9 3.1 %collective-permute-start.1 = (bf16[2,72,384]{2,1,0:T(8,128)(2,1)S(1)}, bf16[2,72,384]{2,1,0:T(8,128)(2,1)S(1)}, u32[]{:S(2)}, u32[]{:S(2)}) collective-permute-start(bf16[2,72,384]{2,1,0:T(8,128)(2,1)S(1)} %maximum_select_fusion.3), channel_id=1, source_target_pairs={{4,0},{8,4},{12,8},{0,12},{20,16},{24,20},{28,24},{16,28},{36,32},... | collective-permute-start | bytes 331784 | tf_op jit(solution)/shard_map/ppermute | solution.py:27
  23.0 2.2 %collective-permute-start.3 = (bf16[2,72,384]{2,1,0:T(8,128)(2,1)S(1)}, bf16[2,72,384]{2,1,0:T(8,128)(2,1)S(1)}, u32[]{:S(2)}, u32[]{:S(2)}) collective-permute-start(bf16[2,72,384]{2,1,0:T(8,128)(2,1)S(1)} %maximum_select_fusion.3), channel_id=1, source_target_pairs={{8,0},{12,4},{0,8},{4,12},{24,16},{28,20},{16,24},{20,28},{40,32},... | collective-permute-start | bytes 331784 | tf_op jit(solution)/shard_map/ppermute | solution.py:27
  25.2 1.9 %fusion.60 = f32[512,128]{1,0:T(8,128)S(1)} fusion(bf16[512,1024]{1,0:T(8,128)(2,1)} %param.7, bf16[1024,128]{1,0:T(8,128)(2,1)} %param.10), kind=kOutput, calls=%fused_computation.102 | convolution fusion | flops 134217728 | bytes 1572864 | tf_op jit(solution)/shard_map/dot_general | solution.py:95
  27.2 3.3 %collective-permute-start.6 = (bf16[2,72,640]{2,1,0:T(8,128)(2,1)S(1)}, bf16[2,72,640]{2,1,0:T(8,128)(2,1)S(1)}, u32[]{:S(2)}, u32[]{:S(2)}) collective-permute-start(bf16[2,72,640]{2,1,0:T(8,128)(2,1)S(1)} %collective-permute-done.4), channel_id=1, source_target_pairs={{32,0},{36,4},{40,8},{44,12},{48,16},{52,20},{56,24},{60,28},{64,3... | collective-permute-start | bytes 552968 | tf_op jit(solution)/shard_map/ppermute | solution.py:27
  30.7 4.3 %collective-permute-done.6 = bf16[2,72,640]{2,1,0:T(8,128)(2,1)S(1)} collective-permute-done((bf16[2,72,640]{2,1,0:T(8,128)(2,1)S(1)}, bf16[2,72,640]{2,1,0:T(8,128)(2,1)S(1)}, u32[]{:S(2)}, u32[]{:S(2)}) %collective-permute-start.6) | collective-permute-done | bytes 184352 | tf_op jit(solution)/shard_map/ppermute | solution.py:27
  35.0 3.4 %collective-permute-done.7 = bf16[2,72,640]{2,1,0:T(8,128)(2,1)S(1)} collective-permute-done((bf16[2,72,640]{2,1,0:T(8,128)(2,1)S(1)}, bf16[2,72,640]{2,1,0:T(8,128)(2,1)S(1)}, u32[]{:S(2)}, u32[]{:S(2)}) %collective-permute-start.7) | collective-permute-done | bytes 184352 | tf_op jit(solution)/shard_map/ppermute | solution.py:27
  38.7 1.7 %collective-permute-start.11 = (bf16[2,72,640]{2,1,0:T(8,128)(2,1)S(1)}, bf16[2,72,640]{2,1,0:T(8,128)(2,1)S(1)}, u32[]{:S(2)}, u32[]{:S(2)}) collective-permute-start(bf16[2,72,640]{2,1,0:T(8,128)(2,1)S(1)} %collective-permute-done.7), channel_id=1, source_target_pairs={{224,0},{228,4},{232,8},{236,12},{240,16},{244,20},{248,24},{252,2... | collective-permute-start | bytes 552968 | tf_op jit(solution)/shard_map/ppermute | solution.py:27
  43.3 2.8 %collective-permute-done.10 = bf16[2,72,640]{2,1,0:T(8,128)(2,1)} collective-permute-done((bf16[2,72,640]{2,1,0:T(8,128)(2,1)S(1)}, bf16[2,72,640]{2,1,0:T(8,128)(2,1)}, u32[]{:S(2)}, u32[]{:S(2)}) %collective-permute-start.10) | collective-permute-done | bytes 184352 | tf_op jit(solution)/shard_map/ppermute | solution.py:27
  46.1 1.8 %collective-permute-start.9 = (bf16[4,2,72,640]{3,2,1,0:T(8,128)(2,1)S(1)}, bf16[4,2,72,640]{3,2,1,0:T(8,128)(2,1)}, u32[]{:S(2)}, u32[]{:S(2)}) collective-permute-start(bf16[4,2,72,640]{3,2,1,0:T(8,128)(2,1)S(1)} %pad_maximum_fusion), channel_id=1, source_target_pairs={{12,0},{0,4},{4,8},{8,12},{28,16},{16,20},{20,24},{24,28},{44,32},... | collective-permute-start | bytes 2211848 | tf_op jit(solution)/shard_map/ppermute | solution.py:27
  48.0 3.2 %collective-permute-start.12 = (bf16[2,72,640]{2,1,0:T(8,128)(2,1)}, bf16[2,72,640]{2,1,0:T(8,128)(2,1)S(1)}, u32[]{:S(2)}, u32[]{:S(2)}) collective-permute-start(bf16[2,72,640]{2,1,0:T(8,128)(2,1)} %collective-permute-done.10), channel_id=1, source_target_pairs={{32,0},{36,4},{40,8},{44,12},{48,16},{52,20},{56,24},{60,28},{64,3... | collective-permute-start | bytes 552968 | tf_op jit(solution)/shard_map/ppermute | solution.py:27
  51.2 4.4 %collective-permute-done.13 = bf16[576,384]{1,0:T(8,128)(2,1)} collective-permute-done((bf16[576,384]{1,0:T(8,128)(2,1)S(1)}, bf16[576,384]{1,0:T(8,128)(2,1)}, u32[]{:S(2)}, u32[]{:S(2)}) %collective-permute-start.13) | collective-permute-done | bytes 442400 | tf_op jit(solution)/shard_map/ppermute | solution.py:27
  62.7 2.0 %collective-permute-start.17 = (bf16[4,2,72,640]{3,2,1,0:T(8,128)(2,1)S(1)}, bf16[4,2,72,640]{3,2,1,0:T(8,128)(2,1)}, u32[]{:S(2)}, u32[]{:S(2)}) collective-permute-start(bf16[4,2,72,640]{3,2,1,0:T(8,128)(2,1)S(1)} %pad_maximum_fusion.1), channel_id=1, source_target_pairs={{12,0},{0,4},{4,8},{8,12},{28,16},{16,20},{20,24},{24,28},{44,32},... | collective-permute-start | bytes 2211848 | tf_op jit(solution)/shard_map/ppermute | solution.py:27
  65.6 3.3 %collective-permute-done.18 = bf16[576,384]{1,0:T(8,128)(2,1)} collective-permute-done((bf16[576,384]{1,0:T(8,128)(2,1)}, bf16[576,384]{1,0:T(8,128)(2,1)}, u32[]{:S(2)}, u32[]{:S(2)}) %collective-permute-start.18) | collective-permute-done | bytes 442400 | tf_op jit(solution)/shard_map/ppermute | solution.py:27
  68.8 3.3 %collective-permute-done.19 = bf16[576,384]{1,0:T(8,128)(2,1)} collective-permute-done((bf16[576,384]{1,0:T(8,128)(2,1)}, bf16[576,384]{1,0:T(8,128)(2,1)}, u32[]{:S(2)}, u32[]{:S(2)}) %collective-permute-start.19) | collective-permute-done | bytes 442400 | tf_op jit(solution)/shard_map/ppermute | solution.py:27
  72.4 1.7 %collective-permute-start.22 = (bf16[576,384]{1,0:T(8,128)(2,1)}, bf16[576,384]{1,0:T(8,128)(2,1)S(1)}, u32[]{:S(2)}, u32[]{:S(2)}) collective-permute-start(bf16[576,384]{1,0:T(8,128)(2,1)} %collective-permute-done.19), channel_id=1, source_target_pairs={{224,0},{228,4},{232,8},{236,12},{240,16},{244,20},{248,24},{252,2... | collective-permute-start | bytes 1327112 | tf_op jit(solution)/shard_map/ppermute | solution.py:27
  74.1 1.9 %broadcast_in_dim.69 = bf16[4,2,4,72,640]{4,3,2,1,0:T(8,128)(2,1)} broadcast(bf16[4,2,72,640]{3,2,1,0:T(8,128)(2,1)S(1)} %pad_maximum_fusion), dimensions={0,1,3,4} | broadcast | bytes 3686400 | tf_op jit(solution)/shard_map/broadcast_in_dim | solution.py:69
  76.0 2.1 %bitcast_dynamic-update-slice_fusion.3 = bf16[4,2,4,72,640]{4,3,2,1,0:T(8,128)(2,1)} fusion(bf16[4,2,4,72,640]{4,3,2,1,0:T(8,128)(2,1)} %broadcast_in_dim.69, s32[]{:T(128)S(6)} %select_n.117, bf16[4,2,72,640]{3,2,1,0:T(8,128)(2,1)} %collective-permute-done.8), kind=kLoop, calls=%fused_computation.26 | loop fusion | bytes 1474564 | tf_op jit(solution)/shard_map/dynamic_update_slice | solution.py:64
  78.1 2.1 %bitcast_dynamic-update-slice_fusion.2 = bf16[4,2,4,72,640]{4,3,2,1,0:T(8,128)(2,1)} fusion(bf16[4,2,4,72,640]{4,3,2,1,0:T(8,128)(2,1)} %bitcast_dynamic-update-slice_fusion.3, s32[]{:T(128)S(6)} %select_n.119, bf16[4,2,72,640]{3,2,1,0:T(8,128)(2,1)} %collective-permute-done.9), kind=kLoop, calls=%fused_computation.25 | loop fusion | bytes 1474564 | tf_op jit(solution)/shard_map/dynamic_update_slice | solution.py:64
  80.2 15.7 %collective-permute-done.15 = bf16[4,2,72,640]{3,2,1,0:T(8,128)(2,1)S(1)} collective-permute-done((bf16[4,2,72,640]{3,2,1,0:T(8,128)(2,1)}, bf16[4,2,72,640]{3,2,1,0:T(8,128)(2,1)S(1)}, u32[]{:S(2)}, u32[]{:S(2)}) %collective-permute-start.15) | collective-permute-done | bytes 737312 | tf_op jit(solution)/shard_map/ppermute | solution.py:27
  97.6 2.3 %copy-done.2 = bf16[512,4608]{1,0:T(8,128)(2,1)S(1)} copy-done((bf16[512,4608]{1,0:T(8,128)(2,1)S(1)}, bf16[512,4608]{1,0:T(8,128)(2,1)}, u32[]{:S(2)}) %copy-start.2) | copy-done | bytes 4718616
  101.6 1.9 %fusion.22 = f32[512,384]{1,0:T(8,128)S(1)} fusion(bf16[576,384]{1,0:T(8,128)(2,1)} %collective-permute-done.19, bf16[8,512,576]{2,1,0:T(8,128)(2,1)S(1)} %shard_map.94), kind=kOutput, calls=%fused_computation.42 | convolution fusion | flops 226492416 | bytes 1884160 | tf_op jit(solution)/shard_map/dot_general | solution.py:15
  112.9 2.0 %fusion.59 = (bf16[1,2,4,72,640]{4,3,2,1,0:T(8,128)(2,1)S(1)}, bf16[1,2,4,72,640]{4,3,2,1,0:T(8,128)(2,1)S(1)}, bf16[1,2,4,72,640]{4,3,2,1,0:T(8,128)(2,1)S(1)}, bf16[1,2,4,72,640]{4,3,2,1,0:T(8,128)(2,1)S(1)}) fusion(bf16[4,2,4,72,640]{4,3,2,1,0:T(8,128)(2,1)} %bitcast_dynamic-update-slice_fusion.1), kind=kLoop, calls=%fused_computation.101 | loop fusion | bytes 5898240 | tf_op jit(solution)/shard_map/slice | solution.py:167
  115.0 2.2 %convolution_multiply_fusion = f32[128,4608]{1,0:T(8,128)} fusion(bf16[512,128]{1,0:T(8,128)(2,1)S(1)} %select_convert_fusion, bf16[512,4608]{1,0:T(8,128)(2,1)S(1)} %copy-done.2), kind=kOutput, calls=%fused_computation | convolution fusion | flops 604569600 | bytes 7208960 | tf_op jit(solution)/shard_map/dot_general | solution.py:15
  117.2 3.2 %collective-permute-start.23 = (bf16[192,384]{1,0:T(8,128)(2,1)S(1)}, bf16[192,384]{1,0:T(8,128)(2,1)S(1)}, u32[]{:S(2)}, u32[]{:S(2)}) collective-permute-start(bf16[192,384]{1,0:T(8,128)(2,1)S(1)} %slice.84), channel_id=1, source_target_pairs={{32,0},{36,4},{40,8},{44,12},{48,16},{52,20},{56,24},{60,28},{64,3... | collective-permute-start | bytes 442376 | tf_op jit(solution)/shard_map/ppermute | solution.py:27
  129.0 1.9 %fusion.13 = f32[512,640]{1,0:T(8,128)} fusion(bf16[576,640]{1,0:T(8,128)(2,1)S(1)} %bitcast.135, bf16[8,512,576]{2,1,0:T(8,128)(2,1)S(1)} %shard_map.94), kind=kOutput, calls=%fused_computation.33 | convolution fusion | flops 377487360 | bytes 2703360 | tf_op jit(solution)/shard_map/dot_general | solution.py:15
  130.9 1.9 %fusion.11 = f32[512,640]{1,0:T(8,128)} fusion(bf16[576,640]{1,0:T(8,128)(2,1)S(1)} %bitcast.134, bf16[8,512,576]{2,1,0:T(8,128)(2,1)S(1)} %shard_map.94), kind=kOutput, calls=%fused_computation.31 | convolution fusion | flops 377487360 | bytes 2703360 | tf_op jit(solution)/shard_map/dot_general | solution.py:15
  132.7 1.9 %fusion.17 = f32[512,640]{1,0:T(8,128)} fusion(bf16[576,640]{1,0:T(8,128)(2,1)S(1)} %bitcast.133, bf16[8,512,576]{2,1,0:T(8,128)(2,1)S(1)} %shard_map.94), kind=kOutput, calls=%fused_computation.37 | convolution fusion | flops 377487360 | bytes 2703360 | tf_op jit(solution)/shard_map/dot_general | solution.py:15
  134.6 2.0 %copy.21 = f32[1024,128]{1,0:T(8,128)} copy(f32[1024,128]{0,1:T(8,128)} %fusion.7) | data formatting | bytes 1048576
  136.6 1.8 %fusion.9 = f32[512,384]{1,0:T(8,128)S(1)} fusion(bf16[8,512,576]{2,1,0:T(8,128)(2,1)} %copy-done.1, bf16[384,384]{1,0:T(8,128)(2,1)} %copy-done.18, bf16[192,384]{1,0:T(8,128)(2,1)S(1)} %collective-permute-done.23), kind=kOutput, calls=%fused_computation.29 | convolution fusion | flops 227377152 | bytes 1884160 | tf_op jit(solution)/shard_map/dot_general | solution.py:15
  139.0 2.2 %convolution_add_fusion = bf16[512,640]{1,0:T(8,128)(2,1)S(1)} fusion(bf16[576,640]{1,0:T(8,128)(2,1)} %bitcast.132, f32[512,640]{1,0:T(8,128)S(1)} %copy-done.5, f32[512,640]{1,0:T(8,128)S(1)} %copy-done.4, f32[512,640]{1,0:T(8,128)S(1)} %convolution_add_fusion.1, f32[512,640]{1,0:T(8,128)S(1)} %copy-done.3, bf16[8,512,576]{2,1,0:T(8,128)(2,1)} %copy-done.1), kind=kOutput, calls=%fused_computation.3 | convolution fusion | flops 379125760 | bytes 7290880 | tf_op jit(solution)/shard_map/dot_general | solution.py:15
  (119 shorter events, 37.3 us)
Async XLA Ops:
  7.2 99.3 %copy-start = (bf16[128,4608]{1,0:T(8,128)(2,1)S(1)}, bf16[128,4608]{1,0:T(8,128)(2,1)}, u32[]{:S(2)}) copy-start(bf16[128,4608]{1,0:T(8,128)(2,1)} %param.11) | copy-start | bytes 3538948
  7.2 90.4 %all-gather.2.cloned.1.call-start = ((), (), s32[]{:S(2)}) async-start(), calls=%async_computation | async-start | bytes 5898240 | tf_op jit(solution)/shard_map/all_gather | solution.py:94
  7.9 5.9 %collective-permute-start = (bf16[72,1024]{1,0:T(8,128)(2,1)}, bf16[72,1024]{1,0:T(8,128)(2,1)S(1)}, u32[]{:S(2)}, u32[]{:S(2)}) collective-permute-start(bf16[72,1024]{1,0:T(8,128)(2,1)} %param.9), channel_id=1, source_target_pairs={{16,0},{20,4},{24,8},{28,12},{0,16},{4,20},{8,24},{12,28},{48,32},... | collective-permute-start | bytes 442376 | tf_op jit(solution)/shard_map/ppermute | solution.py:27
  9.8 41.4 %copy-start.17 = (s32[512]{0:T(512)S(1)}, s32[512]{0:T(512)}, u32[]{:S(2)}) copy-start(s32[512]{0:T(512)} %param.12) | copy-start | bytes 6148
  13.9 13.2 %collective-permute-start.4 = (bf16[2,72,640]{2,1,0:T(8,128)(2,1)S(1)}, bf16[2,72,640]{2,1,0:T(8,128)(2,1)S(1)}, u32[]{:S(2)}, u32[]{:S(2)}) collective-permute-start(bf16[2,72,640]{2,1,0:T(8,128)(2,1)S(1)} %maximum_select_fusion.1), channel_id=1, source_target_pairs={{32,0},{36,4},{40,8},{44,12},{48,16},{52,20},{56,24},{60,28},{64,3... | collective-permute-start | bytes 552968 | tf_op jit(solution)/shard_map/ppermute | solution.py:27
  19.8 7.4 %collective-permute-start.5 = (bf16[2,72,640]{2,1,0:T(8,128)(2,1)S(1)}, bf16[2,72,640]{2,1,0:T(8,128)(2,1)S(1)}, u32[]{:S(2)}, u32[]{:S(2)}) collective-permute-start(bf16[2,72,640]{2,1,0:T(8,128)(2,1)S(1)} %maximum_select_fusion.1), channel_id=1, source_target_pairs={{224,0},{228,4},{232,8},{236,12},{240,16},{244,20},{248,24},{252,2... | collective-permute-start | bytes 552968 | tf_op jit(solution)/shard_map/ppermute | solution.py:27
  19.9 10.7 %collective-permute-start.1 = (bf16[2,72,384]{2,1,0:T(8,128)(2,1)S(1)}, bf16[2,72,384]{2,1,0:T(8,128)(2,1)S(1)}, u32[]{:S(2)}, u32[]{:S(2)}) collective-permute-start(bf16[2,72,384]{2,1,0:T(8,128)(2,1)S(1)} %maximum_select_fusion.3), channel_id=1, source_target_pairs={{4,0},{8,4},{12,8},{0,12},{20,16},{24,20},{28,24},{16,28},{36,32},... | collective-permute-start | bytes 331784 | tf_op jit(solution)/shard_map/ppermute | solution.py:27
  23.0 7.6 %collective-permute-start.2 = (bf16[2,72,384]{2,1,0:T(8,128)(2,1)S(1)}, bf16[2,72,384]{2,1,0:T(8,128)(2,1)S(1)}, u32[]{:S(2)}, u32[]{:S(2)}) collective-permute-start(bf16[2,72,384]{2,1,0:T(8,128)(2,1)S(1)} %maximum_select_fusion.3), channel_id=1, source_target_pairs={{12,0},{0,4},{4,8},{8,12},{28,16},{16,20},{20,24},{24,28},{44,32},... | collective-permute-start | bytes 331784 | tf_op jit(solution)/shard_map/ppermute | solution.py:27
  23.0 7.6 %collective-permute-start.3 = (bf16[2,72,384]{2,1,0:T(8,128)(2,1)S(1)}, bf16[2,72,384]{2,1,0:T(8,128)(2,1)S(1)}, u32[]{:S(2)}, u32[]{:S(2)}) collective-permute-start(bf16[2,72,384]{2,1,0:T(8,128)(2,1)S(1)} %maximum_select_fusion.3), channel_id=1, source_target_pairs={{8,0},{12,4},{0,8},{4,12},{24,16},{28,20},{16,24},{20,28},{40,32},... | collective-permute-start | bytes 331784 | tf_op jit(solution)/shard_map/ppermute | solution.py:27
  27.1 20.8 %collective-permute-start.25 = (f32[512,128]{1,0:T(8,128)S(1)}, f32[512,128]{1,0:T(8,128)S(1)}, u32[]{:S(2)}, u32[]{:S(2)}) collective-permute-start(f32[512,128]{1,0:T(8,128)S(1)} %fusion.60), channel_id=1, source_target_pairs={{0,1},{1,0},{2,3},{3,2},{4,5},{5,4},{6,7},{7,6},{8,9},{9,8},{10,11... | collective-permute-start | bytes 786440 | tf_op jit(solution)/shard_map/ppermute | solution.py:31
  27.2 7.8 %collective-permute-start.6 = (bf16[2,72,640]{2,1,0:T(8,128)(2,1)S(1)}, bf16[2,72,640]{2,1,0:T(8,128)(2,1)S(1)}, u32[]{:S(2)}, u32[]{:S(2)}) collective-permute-start(bf16[2,72,640]{2,1,0:T(8,128)(2,1)S(1)} %collective-permute-done.4), channel_id=1, source_target_pairs={{32,0},{36,4},{40,8},{44,12},{48,16},{52,20},{56,24},{60,28},{64,3... | collective-permute-start | bytes 552968 | tf_op jit(solution)/shard_map/ppermute | solution.py:27
  30.5 7.9 %collective-permute-start.7 = (bf16[2,72,640]{2,1,0:T(8,128)(2,1)S(1)}, bf16[2,72,640]{2,1,0:T(8,128)(2,1)S(1)}, u32[]{:S(2)}, u32[]{:S(2)}) collective-permute-start(bf16[2,72,640]{2,1,0:T(8,128)(2,1)S(1)} %collective-permute-done.5), channel_id=1, source_target_pairs={{224,0},{228,4},{232,8},{236,12},{240,16},{244,20},{248,24},{252,2... | collective-permute-start | bytes 552968 | tf_op jit(solution)/shard_map/ppermute | solution.py:27
  30.7 45.3 %copy-start.9 = (bf16[2,4,72,384]{3,2,1,0:T(8,128)(2,1)}, bf16[2,4,72,384]{3,2,1,0:T(8,128)(2,1)S(1)}, u32[]{:S(2)}) copy-start(bf16[2,4,72,384]{3,2,1,0:T(8,128)(2,1)S(1)} %bitcast_dynamic-update-slice_fusion.8) | copy-start | bytes 1327108
  38.4 7.7 %collective-permute-start.10 = (bf16[2,72,640]{2,1,0:T(8,128)(2,1)S(1)}, bf16[2,72,640]{2,1,0:T(8,128)(2,1)}, u32[]{:S(2)}, u32[]{:S(2)}) collective-permute-start(bf16[2,72,640]{2,1,0:T(8,128)(2,1)S(1)} %collective-permute-done.6), channel_id=1, source_target_pairs={{32,0},{36,4},{40,8},{44,12},{48,16},{52,20},{56,24},{60,28},{64,3... | collective-permute-start | bytes 552968 | tf_op jit(solution)/shard_map/ppermute | solution.py:27
  38.7 9.2 %collective-permute-start.11 = (bf16[2,72,640]{2,1,0:T(8,128)(2,1)S(1)}, bf16[2,72,640]{2,1,0:T(8,128)(2,1)S(1)}, u32[]{:S(2)}, u32[]{:S(2)}) collective-permute-start(bf16[2,72,640]{2,1,0:T(8,128)(2,1)S(1)} %collective-permute-done.7), channel_id=1, source_target_pairs={{224,0},{228,4},{232,8},{236,12},{240,16},{244,20},{248,24},{252,2... | collective-permute-start | bytes 552968 | tf_op jit(solution)/shard_map/ppermute | solution.py:27
  40.5 15.1 %collective-permute-start.13 = (bf16[576,384]{1,0:T(8,128)(2,1)S(1)}, bf16[576,384]{1,0:T(8,128)(2,1)}, u32[]{:S(2)}, u32[]{:S(2)}) collective-permute-start(bf16[576,384]{1,0:T(8,128)(2,1)S(1)} %bitcast.140), channel_id=1, source_target_pairs={{32,0},{36,4},{40,8},{44,12},{48,16},{52,20},{56,24},{60,28},{64,3... | collective-permute-start | bytes 1327112 | tf_op jit(solution)/shard_map/ppermute | solution.py:27
  42.2 18.9 %collective-permute-start.8 = (bf16[4,2,72,640]{3,2,1,0:T(8,128)(2,1)S(1)}, bf16[4,2,72,640]{3,2,1,0:T(8,128)(2,1)}, u32[]{:S(2)}, u32[]{:S(2)}) collective-permute-start(bf16[4,2,72,640]{3,2,1,0:T(8,128)(2,1)S(1)} %pad_maximum_fusion), channel_id=1, source_target_pairs={{4,0},{8,4},{12,8},{0,12},{20,16},{24,20},{28,24},{16,28},{36,32},... | collective-permute-start | bytes 2211848 | tf_op jit(solution)/shard_map/ppermute | solution.py:27
  46.1 16.6 %collective-permute-start.9 = (bf16[4,2,72,640]{3,2,1,0:T(8,128)(2,1)S(1)}, bf16[4,2,72,640]{3,2,1,0:T(8,128)(2,1)}, u32[]{:S(2)}, u32[]{:S(2)}) collective-permute-start(bf16[4,2,72,640]{3,2,1,0:T(8,128)(2,1)S(1)} %pad_maximum_fusion), channel_id=1, source_target_pairs={{12,0},{0,4},{4,8},{8,12},{28,16},{16,20},{20,24},{24,28},{44,32},... | collective-permute-start | bytes 2211848 | tf_op jit(solution)/shard_map/ppermute | solution.py:27
  47.9 10.0 %collective-permute-start.14 = (bf16[576,384]{1,0:T(8,128)(2,1)S(1)}, bf16[576,384]{1,0:T(8,128)(2,1)}, u32[]{:S(2)}, u32[]{:S(2)}) collective-permute-start(bf16[576,384]{1,0:T(8,128)(2,1)S(1)} %bitcast.141), channel_id=1, source_target_pairs={{224,0},{228,4},{232,8},{236,12},{240,16},{244,20},{248,24},{252,2... | collective-permute-start | bytes 1327112 | tf_op jit(solution)/shard_map/ppermute | solution.py:27
  48.0 10.0 %collective-permute-start.12 = (bf16[2,72,640]{2,1,0:T(8,128)(2,1)}, bf16[2,72,640]{2,1,0:T(8,128)(2,1)S(1)}, u32[]{:S(2)}, u32[]{:S(2)}) collective-permute-start(bf16[2,72,640]{2,1,0:T(8,128)(2,1)} %collective-permute-done.10), channel_id=1, source_target_pairs={{32,0},{36,4},{40,8},{44,12},{48,16},{52,20},{56,24},{60,28},{64,3... | collective-permute-start | bytes 552968 | tf_op jit(solution)/shard_map/ppermute | solution.py:27
  55.6 9.2 %collective-permute-start.26 = (f32[512,128]{1,0:T(8,128)S(1)}, f32[512,128]{1,0:T(8,128)S(1)}, u32[]{:S(2)}, u32[]{:S(2)}) collective-permute-start(f32[512,128]{1,0:T(8,128)S(1)} %add.150), channel_id=1, source_target_pairs={{0,2},{1,3},{2,0},{3,1},{4,6},{5,7},{6,4},{7,5},{8,10},{9,11},{10,... | collective-permute-start | bytes 786440 | tf_op jit(solution)/shard_map/ppermute | solution.py:31
  58.0 10.9 %collective-permute-start.18 = (bf16[576,384]{1,0:T(8,128)(2,1)}, bf16[576,384]{1,0:T(8,128)(2,1)}, u32[]{:S(2)}, u32[]{:S(2)}) collective-permute-start(bf16[576,384]{1,0:T(8,128)(2,1)} %collective-permute-done.13), channel_id=1, source_target_pairs={{32,0},{36,4},{40,8},{44,12},{48,16},{52,20},{56,24},{60,28},{64,3... | collective-permute-start | bytes 1327112 | tf_op jit(solution)/shard_map/ppermute | solution.py:27
  59.6 12.5 %collective-permute-start.19 = (bf16[576,384]{1,0:T(8,128)(2,1)}, bf16[576,384]{1,0:T(8,128)(2,1)}, u32[]{:S(2)}, u32[]{:S(2)}) collective-permute-start(bf16[576,384]{1,0:T(8,128)(2,1)} %collective-permute-done.14), channel_id=1, source_target_pairs={{224,0},{228,4},{232,8},{236,12},{240,16},{244,20},{248,24},{252,2... | collective-permute-start | bytes 1327112 | tf_op jit(solution)/shard_map/ppermute | solution.py:27
  62.7 33.2 %collective-permute-start.16 = (bf16[4,2,72,640]{3,2,1,0:T(8,128)(2,1)S(1)}, bf16[4,2,72,640]{3,2,1,0:T(8,128)(2,1)S(1)}, u32[]{:S(2)}, u32[]{:S(2)}) collective-permute-start(bf16[4,2,72,640]{3,2,1,0:T(8,128)(2,1)S(1)} %pad_maximum_fusion.1), channel_id=1, source_target_pairs={{4,0},{8,4},{12,8},{0,12},{20,16},{24,20},{28,24},{16,28},{36,32},... | collective-permute-start | bytes 2211848 | tf_op jit(solution)/shard_map/ppermute | solution.py:27
  62.7 34.9 %collective-permute-start.17 = (bf16[4,2,72,640]{3,2,1,0:T(8,128)(2,1)S(1)}, bf16[4,2,72,640]{3,2,1,0:T(8,128)(2,1)}, u32[]{:S(2)}, u32[]{:S(2)}) collective-permute-start(bf16[4,2,72,640]{3,2,1,0:T(8,128)(2,1)S(1)} %pad_maximum_fusion.1), channel_id=1, source_target_pairs={{12,0},{0,4},{4,8},{8,12},{28,16},{16,20},{20,24},{24,28},{44,32},... | collective-permute-start | bytes 2211848 | tf_op jit(solution)/shard_map/ppermute | solution.py:27
  64.8 31.1 %collective-permute-start.15 = (bf16[4,2,72,640]{3,2,1,0:T(8,128)(2,1)}, bf16[4,2,72,640]{3,2,1,0:T(8,128)(2,1)S(1)}, u32[]{:S(2)}, u32[]{:S(2)}) collective-permute-start(bf16[4,2,72,640]{3,2,1,0:T(8,128)(2,1)} %collective-permute-done.9), channel_id=1, source_target_pairs={{12,0},{0,4},{4,8},{8,12},{28,16},{16,20},{20,24},{24,28},{44,32},... | collective-permute-start | bytes 2211848 | tf_op jit(solution)/shard_map/ppermute | solution.py:27
  72.1 29.4 %collective-permute-start.21 = (bf16[576,384]{1,0:T(8,128)(2,1)}, bf16[576,384]{1,0:T(8,128)(2,1)S(1)}, u32[]{:S(2)}, u32[]{:S(2)}) collective-permute-start(bf16[576,384]{1,0:T(8,128)(2,1)} %collective-permute-done.18), channel_id=1, source_target_pairs={{32,0},{36,4},{40,8},{44,12},{48,16},{52,20},{56,24},{60,28},{64,3... | collective-permute-start | bytes 1327112 | tf_op jit(solution)/shard_map/ppermute | solution.py:27
  72.4 29.2 %collective-permute-start.22 = (bf16[576,384]{1,0:T(8,128)(2,1)}, bf16[576,384]{1,0:T(8,128)(2,1)S(1)}, u32[]{:S(2)}, u32[]{:S(2)}) collective-permute-start(bf16[576,384]{1,0:T(8,128)(2,1)} %collective-permute-done.19), channel_id=1, source_target_pairs={{224,0},{228,4},{232,8},{236,12},{240,16},{244,20},{248,24},{252,2... | collective-permute-start | bytes 1327112 | tf_op jit(solution)/shard_map/ppermute | solution.py:27
  101.5 31.2 %copy-start.1 = (bf16[8,512,576]{2,1,0:T(8,128)(2,1)}, bf16[8,512,576]{2,1,0:T(8,128)(2,1)S(1)}, u32[]{:S(2)}) copy-start(bf16[8,512,576]{2,1,0:T(8,128)(2,1)S(1)} %shard_map.94) | copy-start | bytes 14155780
  109.7 18.0 %collective-permute-start.20 = (bf16[4,2,72,640]{3,2,1,0:T(8,128)(2,1)S(1)}, bf16[4,2,72,640]{3,2,1,0:T(8,128)(2,1)S(1)}, u32[]{:S(2)}, u32[]{:S(2)}) collective-permute-start(bf16[4,2,72,640]{3,2,1,0:T(8,128)(2,1)S(1)} %copy-done.13), channel_id=1, source_target_pairs={{4,0},{8,4},{12,8},{0,12},{20,16},{24,20},{28,24},{16,28},{36,32},... | collective-permute-start | bytes 2211848 | tf_op jit(solution)/shard_map/ppermute | solution.py:27
  117.2 10.5 %collective-permute-start.24 = (bf16[384,384]{1,0:T(8,128)(2,1)S(1)}, bf16[384,384]{1,0:T(8,128)(2,1)S(1)}, u32[]{:S(2)}, u32[]{:S(2)}) collective-permute-start(bf16[384,384]{1,0:T(8,128)(2,1)S(1)} %slice.85), channel_id=1, source_target_pairs={{224,0},{228,4},{232,8},{236,12},{240,16},{244,20},{248,24},{252,2... | collective-permute-start | bytes 884744 | tf_op jit(solution)/shard_map/ppermute | solution.py:27
  117.2 10.5 %collective-permute-start.23 = (bf16[192,384]{1,0:T(8,128)(2,1)S(1)}, bf16[192,384]{1,0:T(8,128)(2,1)S(1)}, u32[]{:S(2)}, u32[]{:S(2)}) collective-permute-start(bf16[192,384]{1,0:T(8,128)(2,1)S(1)} %slice.84), channel_id=1, source_target_pairs={{32,0},{36,4},{40,8},{44,12},{48,16},{52,20},{56,24},{60,28},{64,3... | collective-permute-start | bytes 442376 | tf_op jit(solution)/shard_map/ppermute | solution.py:27
  (15 other events, 49.2 us)
Sparse Core Ops, SparseCore 0:
  9.8 45.4 all-gather.1
where the time goes:
time: 150 us; the launch traced here: 149 us
  waiting for transfers between devices  43 us (29%)
  starting transfers between devices  37.3 us (25%)
  matrix products  28 us (19%)
  local copies, waits for them, and re-layouts  21.2 us (14%)
  between operations  15.3 us (10%)
  other arithmetic  2.93 us (2%)
  Pallas kernels  1.58 us (1%)
    ppermute x25, waiting for transfers between devices, fetch(): return lax.ppermute(x, 'dp', pairs)  42.3 us
    ppermute x25, starting transfers between devices, fetch(): return lax.ppermute(x, 'dp', pairs)  35.8 us
    dot_general x21, matrix products, contract(): lax.dot_general(left, right, (((left_dim,), (right_dim,)), ((), ())), pre...  26.2 us
    unnamed x39, local copies, waits for them, and re-layouts  7.36 us
    dynamic_update_slice x9, local copies, waits for them, and re-layouts, put(): lax.dynamic_update_slice_in_dim(buffer, jnp.expand_dims(chunk, axis), ind...  6.67 us
  transfers between devices with their start and end apart: 28, of which 10 were waited for; matrix products, arithmetic and copies ran while one was open for 16% of the time, Pallas kernels for 1%

commit v1 on v0

v1 whole, which is shorter than its diff:
```python
import jax
import jax.numpy as jnp
from jax import lax
from jax.experimental import pallas as pl
from jax.experimental.pallas import tpu as pltpu
from jax.sharding import PartitionSpec as P

ADAPTER_RANK = 16
TEN_DEV = 8
ADAPTER_SCALE = 2.0
NZ, NX, NY = 8, 2, 4


def contract(left, right, left_dim, right_dim):
    return lax.dot_general(
        left, right, (((left_dim,), (right_dim,)), ((), ())), preferred_element_type=jnp.float32
    )


def fetch(x, dz=0, dx=0, dy=0):
    pairs = []
    for z in range(NZ):
        for a in range(NX):
            for y in range(NY):
                source = (((z + dz) % NZ) * NX + (a + dx) % NX) * NY + (y + dy) % NY
                pairs.append((source, (z * NX + a) * NY + y))
    return lax.ppermute(x, "dp", pairs)


def swap_tensor(x, mask):
    return lax.ppermute(x, "tensor", [(t, t ^ mask) for t in range(4)])


def together(*values):
    return lax.optimization_barrier(values)


def split_kernel(start_ref, g_ref, z_ref, x_ref):
    width = z_ref.shape[2]
    half = width // NX
    for block in range(NZ):
        slot = lax.rem(block - start_ref[0] + NZ, NZ)
        z_ref[slot] = g_ref[:, block * width : (block + 1) * width]
        for x in range(NX):
            to, at = (x * NZ + block) * half, (block * NX + x) * half
            x_ref[:, to : to + half] = g_ref[:, at : at + half]


def split_columns(gradients, start):
    rows, depth = gradients.shape
    step = rows // 4
    width = depth // NZ
    return pl.pallas_call(
        split_kernel,
        grid_spec=pltpu.PrefetchScalarGridSpec(
            num_scalar_prefetch=1,
            grid=(4,),
            in_specs=[pl.BlockSpec((step, depth), lambda i, s: (i, 0))],
            out_specs=[
                pl.BlockSpec((NZ, step, width), lambda i, s: (0, i, 0)),
                pl.BlockSpec((step, depth), lambda i, s: (i, 0)),
            ],
        ),
        out_shape=[
            jax.ShapeDtypeStruct((NZ, rows, width), gradients.dtype),
            jax.ShapeDtypeStruct((rows, depth), gradients.dtype),
        ],
        compiler_params=pltpu.CompilerParams(vmem_limit_bytes=32 * 1024 * 1024),
    )(start, gradients)


def put(buffer, chunk, index):
    axis = buffer.ndim - 3
    return lax.dynamic_update_slice_in_dim(buffer, jnp.expand_dims(chunk, axis), index % NY, axis)


def in_y_order(chunks, y):
    own = chunks[0]
    buffer = jnp.broadcast_to(
        jnp.expand_dims(own, own.ndim - 2), own.shape[:-2] + (NY,) + own.shape[-2:]
    )
    for offset, chunk in chunks.items():
        if offset:
            buffer = put(buffer, chunk, y + offset)
    return buffer


def body(
    head_outputs,
    output_gradient,
    frozen_weight,
    adapter_down_factors,
    adapter_up_factors,
    tenant_index,
    tenant_group_counts,
):
    row_count = head_outputs.shape[0]
    part_rows, depth = output_gradient.shape
    shard_rows, feature_width = frozen_weight.shape
    a_width = feature_width * 3 // 4
    group = lax.axis_index("dp").astype(jnp.int32)
    z, xl, y = group // (NX * NY), (group // NY) % NX, group % NY
    tensor = lax.axis_index("tensor").astype(jnp.int32)

    other = fetch(frozen_weight, dx=1)
    from_core = swap_tensor(output_gradient, 1)
    partial = jnp.dot(head_outputs, adapter_down_factors, preferred_element_type=jnp.float32)
    core_partial = swap_tensor(partial, 1)

    def pair(columns):
        mine, far = frozen_weight[:, columns], other[:, columns]
        return jnp.where(xl == 0, jnp.stack([mine, far]), jnp.stack([far, mine]))

    pair_a, pair_b = together(pair(slice(0, a_width)), pair(slice(a_width, None)))
    rings = [
        [((k * NX + x) * NY) + j for k in range(NZ) for j in range(NY)] for x in range(NX)
    ]
    a_all = lax.all_gather(pair_a, "dp", axis=1, tiled=True, axis_index_groups=rings)
    a_all = a_all.reshape(depth, a_width)

    b_p, b_m, b_o = fetch(pair_b, dy=1), fetch(pair_b, dy=-1), fetch(pair_b, dy=2)
    gradient_later, pair_b = together(output_gradient, pair_b)
    from_chip = swap_tensor(gradient_later, 2)
    b_own = in_y_order({0: pair_b, 1: b_p, 3: b_m, 2: b_o}, y)
    b_own = b_own.reshape(NX * NY * shard_rows, -1)
    b_p1, b_m1 = fetch(b_own, dz=1), fetch(b_own, dz=-1)

    partial, core_partial, b_own = together(partial, core_partial, b_own)
    chip_sum = partial + core_partial
    far_sum = swap_tensor(chip_sum, 2)

    b_p1, b_m1, far_sum = together(b_p1, b_m1, far_sum)
    b_p2, b_m2 = fetch(b_p1, dz=1), fetch(b_m1, dz=-1)
    from_chip, b_p1, b_m1 = together(from_chip, b_p1, b_m1)
    from_both = swap_tensor(from_chip, 1)

    b_p2, b_m2, from_both = together(b_p2, b_m2, from_both)
    b_p3, b_m3 = fetch(b_p2, dz=1), fetch(b_m2, dz=-1)

    b_p3, b_m3 = together(b_p3, b_m3)
    cut = b_own.shape[0] // 2 // 16 * 16
    b_p4, b_m4 = fetch(b_p3[:cut], dz=1), fetch(b_m3[cut:], dz=-1)

    gradients = jnp.zeros((row_count, depth), output_gradient.dtype)
    for block, mask in ((output_gradient, 0), (from_core, 1), (from_chip, 2), (from_both, 3)):
        gradients = lax.dynamic_update_slice_in_dim(
            gradients, block, (tensor ^ mask) * part_rows, 0
        )
    by_z, by_x = split_columns(gradients, z.reshape(1))

    position = jnp.arange(row_count, dtype=jnp.int32)
    active_rows = position < tenant_group_counts[0]
    slot_lookup = jnp.arange(adapter_down_factors.shape[1], dtype=jnp.int32) // ADAPTER_RANK
    select_rows = (
        active_rows[:, None] & (slot_lookup[None, :] == (tenant_index % TEN_DEV)[:, None])
    ).astype(jnp.float32)
    adapter_input = ((chip_sum + far_sum) * select_rows).astype(jnp.bfloat16)
    (adapter_input,) = together(adapter_input)
    adapter_backward = (contract(gradients, adapter_up_factors, 1, 1) * select_rows).astype(
        jnp.bfloat16
    )
    down_factor_gradient = ADAPTER_SCALE * contract(head_outputs, adapter_backward, 0, 0)
    up_factor_gradient = ADAPTER_SCALE * contract(adapter_input, gradients, 0, 0)

    a_total = ADAPTER_SCALE * contract(adapter_backward, adapter_down_factors[:a_width], 1, 1)
    b_total = ADAPTER_SCALE * contract(adapter_backward, adapter_down_factors[a_width:], 1, 1)
    chunks = (b_own, b_p1, b_p2, b_p3, jnp.concatenate([b_p4, b_m4], 0), b_m3, b_m2, b_m1)
    for slot in (0, 1, 7, 2, 6, 3, 5, 4):
        b_total = b_total + contract(by_z[slot], chunks[slot], 1, 0)
    live = active_rows[:, None]
    b_out = jnp.where(live, b_total, 0.0).astype(jnp.bfloat16)

    a_all, a_total, b_out, by_x, down_factor_gradient, up_factor_gradient = together(
        a_all, a_total, b_out, by_x, down_factor_gradient, up_factor_gradient
    )
    a_total = a_total + contract(by_x, a_all, 1, 0)
    a_out = jnp.where(live, a_total, 0.0).astype(jnp.bfloat16)
    return (jnp.concatenate([a_out, b_out], 1), down_factor_gradient, up_factor_gradient)


def solution(mesh):
    in_specs = (
        P("dp", "tensor"),
        P(("dp", "tensor"), None),
        P("dp", "tensor"),
        P("tensor", "dp"),
        P("dp", None),
        P("dp"),
        P("dp"),
    )
    out_specs = (P("dp", "tensor"), P("tensor", "dp"), P("dp", None))
    return jax.shard_map(body, mesh=mesh, in_specs=in_specs, out_specs=out_specs, check_vma=False)
```

time: 150 us -> 137 us (0.913)
  starting transfers between devices: 37.3 us -> 25.8 us
  local copies, waits for them, and re-layouts: 21.2 us -> 12.3 us
  waiting for transfers between devices: 43 us -> 49.8 us
  matrix products: 28 us -> 24.2 us
  Pallas kernels: 1.58 us -> 4.99 us
    ppermute x25 -> x12, starting transfers between devices: 35.8 us -> 22.2 us  [fetch(): return lax.ppermute(x, 'dp', pairs)]
    ppermute x2 -> x5, waiting for transfers between devices: 0.01 us -> 11.5 us  [swap_tensor(): return lax.ppermute(x, 'tensor', [(t, t ^ mask) for t in range(4)])]
    ppermute x25 -> x12, waiting for transfers between devices: 42.3 us -> 34 us  [fetch(): return lax.ppermute(x, 'dp', pairs)]
    dynamic_update_slice x0 -> x4, local copies, waits for them, and re-layouts: none -> 7.01 us  [body(): lax.dynamic_update_slice_in_dim(gradients, block, (tensor ^ mask) * part_...]
    dynamic_update_slice x9 -> x3, local copies, waits for them, and re-layouts: 6.67 us -> 0.03 us  [put(): lax.dynamic_update_slice_in_dim(buffer, jnp.expand_dims(chunk, axis), ind...]
    unnamed x39 -> x17, local copies, waits for them, and re-layouts: 7.36 us -> 1.04 us
    all_gather x1, waiting for transfers between devices: 0.01 us -> 4.36 us  [body(): lax.all_gather(pair_a, 'dp', axis=1, tiled=True, axis_index_groups=rings)]
    dot_general x21 -> x14, matrix products: 26.2 us -> 22.5 us  [contract(): lax.dot_general(left, right, (((left_dim,), (right_dim,)), ((), ())), pre...]
  transfers between devices with their start and end apart: 28 -> 18, of which waited for: 10 -> 10; matrix products, arithmetic and copies ran while one was open for 16% -> 21% of each run, Pallas kernels for 1% -> 4%
where the time goes in v1:
time: 137 us; the launch traced here: 135 us
  waiting for transfers between devices  49.8 us (36%)
  starting transfers between devices  25.8 us (19%)
  matrix products  24.2 us (18%)
  between operations  15 us (11%)
  local copies, waits for them, and re-layouts  12.3 us (9%)
  Pallas kernels  4.99 us (4%)
  other arithmetic  3.03 us (2%)
    ppermute x12, waiting for transfers between devices, fetch(): return lax.ppermute(x, 'dp', pairs)  34 us
    dot_general x14, matrix products, contract(): lax.dot_general(left, right, (((left_dim,), (right_dim,)), ((), ())), pre...  22.5 us
    ppermute x12, starting transfers between devices, fetch(): return lax.ppermute(x, 'dp', pairs)  22.2 us
    ppermute x5, waiting for transfers between devices, swap_tensor(): return lax.ppermute(x, 'tensor', [(t, t ^ mask) for t in range(4)])  11.5 us
    dynamic_update_slice x4, local copies, waits for them, and re-layouts, body(): lax.dynamic_update_slice_in_dim(gradients, block, (tensor ^ mask) * part_...  7.01 us
    pallas_call x1, Pallas kernels, split_columns(): pl.pallas_call(split_kernel, grid_spec=pltpu.PrefetchScalarGridSpec(num_s...  4.99 us
    all_gather x1, waiting for transfers between devices, body(): lax.all_gather(pair_a, 'dp', axis=1, tiled=True, axis_index_groups=rings)  4.36 us
    ppermute x5, starting transfers between devices, swap_tensor(): return lax.ppermute(x, 'tensor', [(t, t ^ mask) for t in range(4)])  3.54 us
  transfers between devices with their start and end apart: 18, of which 10 were waited for; matrix products, arithmetic and copies ran while one was open for 21% of the time, Pallas kernels for 4%

profile of v1, /device:TPU:6, one launch (start us, length us, event | category | flops | bytes accessed | tf_op | source)
XLA Modules:
  0.0 135.1 jit_solution(2479958469623149313)
XLA Ops:
  9.9 3.3 %collective-permute-done = bf16[72,1024]{1,0:T(8,128)(2,1)S(1)} collective-permute-done((bf16[72,1024]{1,0:T(8,128)(2,1)}, bf16[72,1024]{1,0:T(8,128)(2,1)S(1)}, u32[]{:S(2)}, u32[]{:S(2)}) %collective-permute-start) | collective-permute-done | bytes 147488 | tf_op jit(solution)/shard_map/ppermute | solution.py:27
  13.9 1.7 %fusion.41 = f32[512,128]{1,0:T(8,128)S(1)} fusion(bf16[512,1024]{1,0:T(8,128)(2,1)} %param.7, bf16[1024,128]{1,0:T(8,128)(2,1)} %param.10), kind=kOutput, calls=%fused_computation.72 | convolution fusion | flops 134217728 | bytes 1572864 | tf_op jit(solution)/shard_map/dot_general | solution.py:107
  16.9 2.4 %broadcast_in_dim.47 = bf16[512,4608]{1,0:T(8,128)(2,1)} broadcast(bf16[]{:T(256)} %constant.103.clone.1), dimensions={} | broadcast | bytes 4718594 | tf_op jit(solution)/shard_map/broadcast_in_dim | solution.py:144
  19.3 1.1 constant_dynamic-update-slice_fusion.3
  20.4 3.0 %collective-permute-start.3 = (bf16[2,72,256]{2,1,0:T(8,128)(2,1)S(1)}, bf16[2,72,256]{2,1,0:T(8,128)(2,1)S(1)}, u32[]{:S(2)}, u32[]{:S(2)}) collective-permute-start(bf16[2,72,256]{2,1,0:T(8,128)(2,1)S(1)} %maximum_select_fusion.1), channel_id=1, source_target_pairs={{4,0},{8,4},{12,8},{0,12},{20,16},{24,20},{28,24},{16,28},{36,32},... | collective-permute-start | bytes 221192 | tf_op jit(solution)/shard_map/ppermute | solution.py:27
  23.4 2.2 %collective-permute-start.5 = (bf16[2,72,256]{2,1,0:T(8,128)(2,1)S(1)}, bf16[2,72,256]{2,1,0:T(8,128)(2,1)S(1)}, u32[]{:S(2)}, u32[]{:S(2)}) collective-permute-start(bf16[2,72,256]{2,1,0:T(8,128)(2,1)S(1)} %maximum_select_fusion.1), channel_id=1, source_target_pairs={{8,0},{12,4},{0,8},{4,12},{24,16},{28,20},{16,24},{20,28},{40,32},... | collective-permute-start | bytes 221192 | tf_op jit(solution)/shard_map/ppermute | solution.py:27
  25.6 1.4 %collective-permute-start.2 = (bf16[128,4608]{1,0:T(8,128)(2,1)S(1)}, bf16[128,4608]{1,0:T(8,128)(2,1)}, u32[]{:S(2)}, u32[]{:S(2)}) collective-permute-start(bf16[128,4608]{1,0:T(8,128)(2,1)S(1)} %copy-done.5), channel_id=1, source_target_pairs={{0,2},{1,3},{2,0},{3,1},{4,6},{5,7},{6,4},{7,5},{8,10},{9,11},{10,... | collective-permute-start | bytes 3538952 | tf_op jit(solution)/shard_map/ppermute | solution.py:31
  27.1 3.1 %collective-permute-done.4 = bf16[2,72,256]{2,1,0:T(8,128)(2,1)S(1)} collective-permute-done((bf16[2,72,256]{2,1,0:T(8,128)(2,1)S(1)}, bf16[2,72,256]{2,1,0:T(8,128)(2,1)S(1)}, u32[]{:S(2)}, u32[]{:S(2)}) %collective-permute-start.4) | collective-permute-done | bytes 73760 | tf_op jit(solution)/shard_map/ppermute | solution.py:27
  30.2 5.9 %collective-permute-start.6 = (bf16[576,256]{1,0:T(8,128)(2,1)S(1)}, bf16[576,256]{1,0:T(8,128)(2,1)S(1)}, u32[]{:S(2)}, u32[]{:S(2)}) collective-permute-start(bf16[576,256]{1,0:T(8,128)(2,1)S(1)} %bitcast.68), channel_id=1, source_target_pairs={{32,0},{36,4},{40,8},{44,12},{48,16},{52,20},{56,24},{60,28},{64,3... | collective-permute-start | bytes 884744 | tf_op jit(solution)/shard_map/ppermute | solution.py:27
  36.2 1.0 add.106
  37.2 1.5 %collective-permute-start.9 = (f32[512,128]{1,0:T(8,128)S(1)}, f32[512,128]{1,0:T(8,128)S(1)}, u32[]{:S(2)}, u32[]{:S(2)}) collective-permute-start(f32[512,128]{1,0:T(8,128)S(1)} %add.106), channel_id=1, source_target_pairs={{0,2},{1,3},{2,0},{3,1},{4,6},{5,7},{6,4},{7,5},{8,10},{9,11},{10,... | collective-permute-start | bytes 786440 | tf_op jit(solution)/shard_map/ppermute | solution.py:31
  38.7 5.5 %collective-permute-done.6 = bf16[576,256]{1,0:T(8,128)(2,1)S(1)} collective-permute-done((bf16[576,256]{1,0:T(8,128)(2,1)S(1)}, bf16[576,256]{1,0:T(8,128)(2,1)S(1)}, u32[]{:S(2)}, u32[]{:S(2)}) %collective-permute-start.6) | collective-permute-done | bytes 294944 | tf_op jit(solution)/shard_map/ppermute | solution.py:27
  44.2 4.2 %collective-permute-done.7 = bf16[576,256]{1,0:T(8,128)(2,1)} collective-permute-done((bf16[576,256]{1,0:T(8,128)(2,1)S(1)}, bf16[576,256]{1,0:T(8,128)(2,1)}, u32[]{:S(2)}, u32[]{:S(2)}) %collective-permute-start.7) | collective-permute-done | bytes 294944 | tf_op jit(solution)/shard_map/ppermute | solution.py:27
  48.4 11.5 %collective-permute-done.9 = f32[512,128]{1,0:T(8,128)S(1)} collective-permute-done((f32[512,128]{1,0:T(8,128)S(1)}, f32[512,128]{1,0:T(8,128)S(1)}, u32[]{:S(2)}, u32[]{:S(2)}) %collective-permute-start.9) | collective-permute-done | bytes 262176 | tf_op jit(solution)/shard_map/ppermute | solution.py:31
  60.1 5.9 %collective-permute-start.10 = (bf16[576,256]{1,0:T(8,128)(2,1)S(1)}, bf16[576,256]{1,0:T(8,128)(2,1)S(1)}, u32[]{:S(2)}, u32[]{:S(2)}) collective-permute-start(bf16[576,256]{1,0:T(8,128)(2,1)S(1)} %collective-permute-done.6), channel_id=1, source_target_pairs={{32,0},{36,4},{40,8},{44,12},{48,16},{52,20},{56,24},{60,28},{64,3... | collective-permute-start | bytes 884744 | tf_op jit(solution)/shard_map/ppermute | solution.py:27
  66.0 2.4 %constant_dynamic-update-slice_fusion.2 = bf16[512,4608]{1,0:T(8,128)(2,1)} fusion(bf16[512,4608]{1,0:T(8,128)(2,1)} %constant_dynamic-update-slice_fusion.3, bf16[128,4608]{1,0:T(8,128)(2,1)} %collective-permute-done.1, s32[]{:T(128)S(6)} %select_n.99), kind=kLoop, calls=%fused_computation.66 | loop fusion | bytes 2359300 | tf_op jit(solution)/shard_map/dynamic_update_slice | solution.py:146
  68.4 2.4 %constant_dynamic-update-slice_fusion.1 = bf16[512,4608]{1,0:T(8,128)(2,1)} fusion(bf16[512,4608]{1,0:T(8,128)(2,1)} %constant_dynamic-update-slice_fusion.2, bf16[128,4608]{1,0:T(8,128)(2,1)} %collective-permute-done.2, s32[]{:T(128)S(6)} %select_n.107), kind=kLoop, calls=%fused_computation.65 | loop fusion | bytes 2359300 | tf_op jit(solution)/shard_map/dynamic_update_slice | solution.py:146
  70.8 6.1 %collective-permute-done.10 = bf16[576,256]{1,0:T(8,128)(2,1)S(1)} collective-permute-done((bf16[576,256]{1,0:T(8,128)(2,1)S(1)}, bf16[576,256]{1,0:T(8,128)(2,1)S(1)}, u32[]{:S(2)}, u32[]{:S(2)}) %collective-permute-start.10) | collective-permute-done | bytes 294944 | tf_op jit(solution)/shard_map/ppermute | solution.py:27
  77.0 3.7 %collective-permute-done.11 = bf16[576,256]{1,0:T(8,128)(2,1)S(1)} collective-permute-done((bf16[576,256]{1,0:T(8,128)(2,1)}, bf16[576,256]{1,0:T(8,128)(2,1)S(1)}, u32[]{:S(2)}, u32[]{:S(2)}) %collective-permute-start.11) | collective-permute-done | bytes 294944 | tf_op jit(solution)/shard_map/ppermute | solution.py:27
  80.7 2.0 %collective-permute-start.14 = (bf16[576,256]{1,0:T(8,128)(2,1)S(1)}, bf16[576,256]{1,0:T(8,128)(2,1)S(1)}, u32[]{:S(2)}, u32[]{:S(2)}) collective-permute-start(bf16[576,256]{1,0:T(8,128)(2,1)S(1)} %collective-permute-done.11), channel_id=1, source_target_pairs={{224,0},{228,4},{232,8},{236,12},{240,16},{244,20},{248,24},{252,2... | collective-permute-start | bytes 884744 | tf_op jit(solution)/shard_map/ppermute | solution.py:27
  82.7 1.1 constant_dynamic-update-slice_fusion.g_ref
  83.8 5.0 %shard_map.94 = (bf16[8,512,576]{2,1,0:T(8,128)(2,1)S(1)}, bf16[512,4608]{1,0:T(8,128)(2,1)S(1)}) custom-call(s32[1]{0:T(128)} %bitcast.12.start_ref, bf16[512,4608]{1,0:T(8,128)(2,1)} %constant_dynamic-update-slice_fusion.g_ref), custom_call_target="tpu_custom_call" | custom-call | tf_op jit(solution)/shard_map/pallas_call | solution.py:53
  90.0 2.2 %fusion.21 = f32[512,256]{1,0:T(8,128)S(1)} fusion(bf16[576,256]{1,0:T(8,128)(2,1)} %collective-permute-done.7, bf16[8,512,576]{2,1,0:T(8,128)(2,1)S(1)} %get-tuple-element.39), kind=kOutput, calls=%fused_computation.29 | convolution fusion | flops 150994944 | bytes 1474560 | tf_op jit(solution)/shard_map/dot_general | solution.py:15
  92.2 3.8 %fusion.10 = bf16[512,128]{1,0:T(8,128)(2,1)S(1)} fusion(bf16[512,4608]{1,0:T(8,128)(2,1)} %constant_dynamic-update-slice_fusion.g_ref, bf16[128,4608]{1,0:T(8,128)(2,1)S(1)} %copy-done, s32[128]{0:T(128)S(1)} %and_select_fusion, s32[512]{0:T(512)S(1)} %add_select_fusion, pred[512]{0:T(512)(128)(4,1)S(1)} %iota_compare_fusion), kind=kOutput, calls=%fused_computation.17 | convolution fusion | flops 604241920 | bytes 6032384 | tf_op jit(solution)/shard_map/dot_general | solution.py:15
  96.4 4.6 %convolution_multiply_fusion = f32[128,4608]{1,0:T(8,128)} fusion(bf16[512,128]{1,0:T(8,128)(2,1)S(1)} %select_convert_fusion.1, bf16[512,4608]{1,0:T(8,128)(2,1)} %constant_dynamic-update-slice_fusion.g_ref), kind=kOutput, calls=%fused_computation | convolution fusion | flops 604569600 | bytes 7208960 | tf_op jit(solution)/shard_map/dot_general | solution.py:15
  101.6 1.4 %collective-permute-start.15 = (bf16[288,256]{1,0:T(8,128)(2,1)S(1)}, bf16[288,256]{1,0:T(8,128)(2,1)S(1)}, u32[]{:S(2)}, u32[]{:S(2)}) collective-permute-start(bf16[288,256]{1,0:T(8,128)(2,1)S(1)} %slice.62), channel_id=1, source_target_pairs={{32,0},{36,4},{40,8},{44,12},{48,16},{52,20},{56,24},{60,28},{64,3... | collective-permute-start | bytes 442376 | tf_op jit(solution)/shard_map/ppermute | solution.py:27
  104.6 5.3 %collective-permute-done.15 = bf16[288,256]{1,0:T(8,128)(2,1)S(1)} collective-permute-done((bf16[288,256]{1,0:T(8,128)(2,1)S(1)}, bf16[288,256]{1,0:T(8,128)(2,1)S(1)}, u32[]{:S(2)}, u32[]{:S(2)}) %collective-permute-start.15) | collective-permute-done | bytes 147488 | tf_op jit(solution)/shard_map/ppermute | solution.py:27
  109.9 2.7 %collective-permute-done.16 = bf16[288,256]{1,0:T(8,128)(2,1)S(1)} collective-permute-done((bf16[288,256]{1,0:T(8,128)(2,1)S(1)}, bf16[288,256]{1,0:T(8,128)(2,1)S(1)}, u32[]{:S(2)}, u32[]{:S(2)}) %collective-permute-start.16) | collective-permute-done | bytes 147488 | tf_op jit(solution)/shard_map/ppermute | solution.py:27
  113.5 4.4 %all-gather.2.cloned.1.call-done = bf16[2,2304,768]{2,1,0:T(8,128)(2,1)} async-done(((bf16[2,72,768]{2,1,0:T(8,128)(2,1)}), bf16[2,2304,768]{2,1,0:T(8,128)(2,1)}) %all-gather.2.cloned.1.call-update) | async-done | bytes 7077904 | tf_op jit(solution)/shard_map/all_gather | solution.py:118
  117.9 1.0 copy.13
  118.9 8.3 %select_convert_fusion = bf16[512,768]{1,0:T(8,128)(2,1)S(1)} fusion(f32[512,768]{1,0:T(8,128)S(1)} %convolution_multiply_fusion.1, bf16[512,4608]{1,0:T(8,128)(2,1)} %copy-done.1, bf16[4608,768]{1,0:T(8,128)(2,1)} %bitcast.71, pred[512]{0:T(512)(128)(4,1)S(1)} %iota_compare_fusion), kind=kOutput, calls=%fused_computation.1 | convolution fusion | flops 3625058304 | bytes 14156288 | tf_op jit(solution)/shard_map/dot_general | solution.py:15
  127.1 1.1 pad_maximum_fusion
  (61 shorter events, 8.8 us)
Async XLA Ops:
  7.2 85.0 %copy-start = (bf16[128,4608]{1,0:T(8,128)(2,1)S(1)}, bf16[128,4608]{1,0:T(8,128)(2,1)}, u32[]{:S(2)}) copy-start(bf16[128,4608]{1,0:T(8,128)(2,1)} %param.11) | copy-start | bytes 3538948
  7.2 12.1 %copy-start.5 = (bf16[128,4608]{1,0:T(8,128)(2,1)S(1)}, bf16[128,4608]{1,0:T(8,128)(2,1)}, u32[]{:S(2)}) copy-start(bf16[128,4608]{1,0:T(8,128)(2,1)} %param.8) | copy-start | bytes 3538948
  7.2 110.7 %all-gather.2.cloned.1.call-start = ((), (), s32[]{:S(2)}) async-start(), calls=%async_computation | async-start | bytes 7299072 | tf_op jit(solution)/shard_map/all_gather | solution.py:118
  7.2 5.9 %collective-permute-start = (bf16[72,1024]{1,0:T(8,128)(2,1)}, bf16[72,1024]{1,0:T(8,128)(2,1)S(1)}, u32[]{:S(2)}, u32[]{:S(2)}) collective-permute-start(bf16[72,1024]{1,0:T(8,128)(2,1)} %param.9), channel_id=1, source_target_pairs={{16,0},{20,4},{24,8},{28,12},{0,16},{4,20},{8,24},{12,28},{48,32},... | collective-permute-start | bytes 442376 | tf_op jit(solution)/shard_map/ppermute | solution.py:27
  15.6 23.1 %copy-start.7 = (s32[512]{0:T(512)S(1)}, s32[512]{0:T(512)}, u32[]{:S(2)}) copy-start(s32[512]{0:T(512)} %param.12) | copy-start | bytes 6148
  15.6 20.6 %collective-permute-start.8 = (f32[512,128]{1,0:T(8,128)S(1)}, f32[512,128]{1,0:T(8,128)}, u32[]{:S(2)}, u32[]{:S(2)}) collective-permute-start(f32[512,128]{1,0:T(8,128)S(1)} %fusion.41), channel_id=1, source_target_pairs={{0,1},{1,0},{2,3},{3,2},{4,5},{5,4},{6,7},{7,6},{8,9},{9,8},{10,11... | collective-permute-start | bytes 786440 | tf_op jit(solution)/shard_map/ppermute | solution.py:31
  15.7 50.3 %collective-permute-start.1 = (bf16[128,4608]{1,0:T(8,128)(2,1)}, bf16[128,4608]{1,0:T(8,128)(2,1)}, u32[]{:S(2)}, u32[]{:S(2)}) collective-permute-start(bf16[128,4608]{1,0:T(8,128)(2,1)} %param.8), channel_id=1, source_target_pairs={{0,1},{1,0},{2,3},{3,2},{4,5},{5,4},{6,7},{7,6},{8,9},{9,8},{10,11... | collective-permute-start | bytes 3538952 | tf_op jit(solution)/shard_map/ppermute | solution.py:31
  20.4 5.2 %collective-permute-start.3 = (bf16[2,72,256]{2,1,0:T(8,128)(2,1)S(1)}, bf16[2,72,256]{2,1,0:T(8,128)(2,1)S(1)}, u32[]{:S(2)}, u32[]{:S(2)}) collective-permute-start(bf16[2,72,256]{2,1,0:T(8,128)(2,1)S(1)} %maximum_select_fusion.1), channel_id=1, source_target_pairs={{4,0},{8,4},{12,8},{0,12},{20,16},{24,20},{28,24},{16,28},{36,32},... | collective-permute-start | bytes 221192 | tf_op jit(solution)/shard_map/ppermute | solution.py:27
  23.4 6.8 %collective-permute-start.4 = (bf16[2,72,256]{2,1,0:T(8,128)(2,1)S(1)}, bf16[2,72,256]{2,1,0:T(8,128)(2,1)S(1)}, u32[]{:S(2)}, u32[]{:S(2)}) collective-permute-start(bf16[2,72,256]{2,1,0:T(8,128)(2,1)S(1)} %maximum_select_fusion.1), channel_id=1, source_target_pairs={{12,0},{0,4},{4,8},{8,12},{28,16},{16,20},{20,24},{24,28},{44,32},... | collective-permute-start | bytes 221192 | tf_op jit(solution)/shard_map/ppermute | solution.py:27
  23.4 6.8 %collective-permute-start.5 = (bf16[2,72,256]{2,1,0:T(8,128)(2,1)S(1)}, bf16[2,72,256]{2,1,0:T(8,128)(2,1)S(1)}, u32[]{:S(2)}, u32[]{:S(2)}) collective-permute-start(bf16[2,72,256]{2,1,0:T(8,128)(2,1)S(1)} %maximum_select_fusion.1), channel_id=1, source_target_pairs={{8,0},{12,4},{0,8},{4,12},{24,16},{28,20},{16,24},{20,28},{40,32},... | collective-permute-start | bytes 221192 | tf_op jit(solution)/shard_map/ppermute | solution.py:27
  25.6 40.4 %collective-permute-start.2 = (bf16[128,4608]{1,0:T(8,128)(2,1)S(1)}, bf16[128,4608]{1,0:T(8,128)(2,1)}, u32[]{:S(2)}, u32[]{:S(2)}) collective-permute-start(bf16[128,4608]{1,0:T(8,128)(2,1)S(1)} %copy-done.5), channel_id=1, source_target_pairs={{0,2},{1,3},{2,0},{3,1},{4,6},{5,7},{6,4},{7,5},{8,10},{9,11},{10,... | collective-permute-start | bytes 3538952 | tf_op jit(solution)/shard_map/ppermute | solution.py:31
  30.2 58.6 %copy-start.3 = (bf16[2,4,72,256]{3,2,1,0:T(8,128)(2,1)}, bf16[2,4,72,256]{3,2,1,0:T(8,128)(2,1)S(1)}, u32[]{:S(2)}) copy-start(bf16[2,4,72,256]{3,2,1,0:T(8,128)(2,1)S(1)} %bitcast_dynamic-update-slice_fusion.2) | copy-start | bytes 884740
  30.2 14.0 %collective-permute-start.6 = (bf16[576,256]{1,0:T(8,128)(2,1)S(1)}, bf16[576,256]{1,0:T(8,128)(2,1)S(1)}, u32[]{:S(2)}, u32[]{:S(2)}) collective-permute-start(bf16[576,256]{1,0:T(8,128)(2,1)S(1)} %bitcast.68), channel_id=1, source_target_pairs={{32,0},{36,4},{40,8},{44,12},{48,16},{52,20},{56,24},{60,28},{64,3... | collective-permute-start | bytes 884744 | tf_op jit(solution)/shard_map/ppermute | solution.py:27
  36.2 12.2 %collective-permute-start.7 = (bf16[576,256]{1,0:T(8,128)(2,1)S(1)}, bf16[576,256]{1,0:T(8,128)(2,1)}, u32[]{:S(2)}, u32[]{:S(2)}) collective-permute-start(bf16[576,256]{1,0:T(8,128)(2,1)S(1)} %bitcast.69), channel_id=1, source_target_pairs={{224,0},{228,4},{232,8},{236,12},{240,16},{244,20},{248,24},{252,2... | collective-permute-start | bytes 884744 | tf_op jit(solution)/shard_map/ppermute | solution.py:27
  37.2 22.7 %collective-permute-start.9 = (f32[512,128]{1,0:T(8,128)S(1)}, f32[512,128]{1,0:T(8,128)S(1)}, u32[]{:S(2)}, u32[]{:S(2)}) collective-permute-start(f32[512,128]{1,0:T(8,128)S(1)} %add.106), channel_id=1, source_target_pairs={{0,2},{1,3},{2,0},{3,1},{4,6},{5,7},{6,4},{7,5},{8,10},{9,11},{10,... | collective-permute-start | bytes 786440 | tf_op jit(solution)/shard_map/ppermute | solution.py:31
  60.1 16.9 %collective-permute-start.10 = (bf16[576,256]{1,0:T(8,128)(2,1)S(1)}, bf16[576,256]{1,0:T(8,128)(2,1)S(1)}, u32[]{:S(2)}, u32[]{:S(2)}) collective-permute-start(bf16[576,256]{1,0:T(8,128)(2,1)S(1)} %collective-permute-done.6), channel_id=1, source_target_pairs={{32,0},{36,4},{40,8},{44,12},{48,16},{52,20},{56,24},{60,28},{64,3... | collective-permute-start | bytes 884744 | tf_op jit(solution)/shard_map/ppermute | solution.py:27
  66.0 14.7 %collective-permute-start.11 = (bf16[576,256]{1,0:T(8,128)(2,1)}, bf16[576,256]{1,0:T(8,128)(2,1)S(1)}, u32[]{:S(2)}, u32[]{:S(2)}) collective-permute-start(bf16[576,256]{1,0:T(8,128)(2,1)} %collective-permute-done.7), channel_id=1, source_target_pairs={{224,0},{228,4},{232,8},{236,12},{240,16},{244,20},{248,24},{252,2... | collective-permute-start | bytes 884744 | tf_op jit(solution)/shard_map/ppermute | solution.py:27
  66.0 14.7 %collective-permute-start.12 = (bf16[128,4608]{1,0:T(8,128)(2,1)}, bf16[128,4608]{1,0:T(8,128)(2,1)S(1)}, u32[]{:S(2)}, u32[]{:S(2)}) collective-permute-start(bf16[128,4608]{1,0:T(8,128)(2,1)} %collective-permute-done.2), channel_id=1, source_target_pairs={{0,1},{1,0},{2,3},{3,2},{4,5},{5,4},{6,7},{7,6},{8,9},{9,8},{10,11... | collective-permute-start | bytes 3538952 | tf_op jit(solution)/shard_map/ppermute | solution.py:31
  80.7 20.9 %collective-permute-start.13 = (bf16[576,256]{1,0:T(8,128)(2,1)S(1)}, bf16[576,256]{1,0:T(8,128)(2,1)S(1)}, u32[]{:S(2)}, u32[]{:S(2)}) collective-permute-start(bf16[576,256]{1,0:T(8,128)(2,1)S(1)} %collective-permute-done.10), channel_id=1, source_target_pairs={{32,0},{36,4},{40,8},{44,12},{48,16},{52,20},{56,24},{60,28},{64,3... | collective-permute-start | bytes 884744 | tf_op jit(solution)/shard_map/ppermute | solution.py:27
  80.7 20.9 %collective-permute-start.14 = (bf16[576,256]{1,0:T(8,128)(2,1)S(1)}, bf16[576,256]{1,0:T(8,128)(2,1)S(1)}, u32[]{:S(2)}, u32[]{:S(2)}) collective-permute-start(bf16[576,256]{1,0:T(8,128)(2,1)S(1)} %collective-permute-done.11), channel_id=1, source_target_pairs={{224,0},{228,4},{232,8},{236,12},{240,16},{244,20},{248,24},{252,2... | collective-permute-start | bytes 884744 | tf_op jit(solution)/shard_map/ppermute | solution.py:27
  88.8 7.1 %copy-start.1 = (bf16[512,4608]{1,0:T(8,128)(2,1)}, bf16[512,4608]{1,0:T(8,128)(2,1)S(1)}, u32[]{:S(2)}) copy-start(bf16[512,4608]{1,0:T(8,128)(2,1)S(1)} %get-tuple-element.50) | copy-start | bytes 14155780
  89.6 6.4 %copy-start.2 = (bf16[512,1024]{1,0:T(8,128)(2,1)S(1)}, bf16[512,1024]{1,0:T(8,128)(2,1)}, u32[]{:S(2)}) copy-start(bf16[512,1024]{1,0:T(8,128)(2,1)} %param.7) | copy-start | bytes 3145732
  96.0 4.9 %copy-start.6 = (bf16[1024,128]{1,0:T(8,128)(2,1)S(1)}, bf16[1024,128]{1,0:T(8,128)(2,1)}, u32[]{:S(2)}) copy-start(bf16[1024,128]{1,0:T(8,128)(2,1)} %param.10) | copy-start | bytes 786436
  101.0 12.0 %copy-start.4 = (bf16[2,4,72,256]{3,2,1,0:T(8,128)(2,1)S(1)}, bf16[2,4,72,256]{3,2,1,0:T(8,128)(2,1)}, u32[]{:S(2)}) copy-start(bf16[2,4,72,256]{3,2,1,0:T(8,128)(2,1)} %copy-done.3) | copy-start | bytes 884740
  101.6 8.3 %collective-permute-start.15 = (bf16[288,256]{1,0:T(8,128)(2,1)S(1)}, bf16[288,256]{1,0:T(8,128)(2,1)S(1)}, u32[]{:S(2)}, u32[]{:S(2)}) collective-permute-start(bf16[288,256]{1,0:T(8,128)(2,1)S(1)} %slice.62), channel_id=1, source_target_pairs={{32,0},{36,4},{40,8},{44,12},{48,16},{52,20},{56,24},{60,28},{64,3... | collective-permute-start | bytes 442376 | tf_op jit(solution)/shard_map/ppermute | solution.py:27
  103.0 9.6 %collective-permute-start.16 = (bf16[288,256]{1,0:T(8,128)(2,1)S(1)}, bf16[288,256]{1,0:T(8,128)(2,1)S(1)}, u32[]{:S(2)}, u32[]{:S(2)}) collective-permute-start(bf16[288,256]{1,0:T(8,128)(2,1)S(1)} %slice.63), channel_id=1, source_target_pairs={{224,0},{228,4},{232,8},{236,12},{240,16},{244,20},{248,24},{252,2... | collective-permute-start | bytes 442376 | tf_op jit(solution)/shard_map/ppermute | solution.py:27
Sparse Core Ops, SparseCore 0:
  14.0 103.7 all-gather.1

commit v2 on v1

v2 whole, which is shorter than its diff:
```python
import jax
import jax.numpy as jnp
from jax import lax
from jax.experimental import pallas as pl
from jax.experimental.pallas import tpu as pltpu
from jax.sharding import PartitionSpec as P

ADAPTER_RANK = 16
TEN_DEV = 8
ADAPTER_SCALE = 2.0
NZ, NX, NY = 8, 2, 4


def contract(left, right, left_dim, right_dim):
    return lax.dot_general(
        left, right, (((left_dim,), (right_dim,)), ((), ())), preferred_element_type=jnp.float32
    )


def fetch(x, dz=0, dx=0, dy=0):
    pairs = []
    for z in range(NZ):
        for a in range(NX):
            for y in range(NY):
                source = (((z + dz) % NZ) * NX + (a + dx) % NX) * NY + (y + dy) % NY
                pairs.append((source, (z * NX + a) * NY + y))
    return lax.ppermute(x, "dp", pairs)


def swap_tensor(x, mask):
    return lax.ppermute(x, "tensor", [(t, t ^ mask) for t in range(4)])


def together(*values):
    return lax.optimization_barrier(values)


def split_kernel(start_ref, g_ref, z_ref):
    width = z_ref.shape[2]
    for block in range(NZ):
        slot = lax.rem(block - start_ref[0] + NZ, NZ)
        z_ref[slot] = g_ref[:, block * width : (block + 1) * width]


def split_columns(gradients, start):
    rows, depth = gradients.shape
    step = rows // 4
    width = depth // NZ
    return pl.pallas_call(
        split_kernel,
        grid_spec=pltpu.PrefetchScalarGridSpec(
            num_scalar_prefetch=1,
            grid=(4,),
            in_specs=[pl.BlockSpec((step, depth), lambda i, s: (i, 0))],
            out_specs=pl.BlockSpec((NZ, step, width), lambda i, s: (0, i, 0)),
        ),
        out_shape=jax.ShapeDtypeStruct((NZ, rows, width), gradients.dtype),
        compiler_params=pltpu.CompilerParams(vmem_limit_bytes=32 * 1024 * 1024),
    )(start, gradients)


def last_kernel(g_ref, w_ref, back_ref, down_ref, live_ref, b_ref, out_ref, total_ref):
    step = pl.program_id(0)
    width = w_ref.shape[1]

    @pl.when(step == 0)
    def _():
        total_ref[...] = ADAPTER_SCALE * contract(back_ref[...], down_ref[...], 1, 1)

    total_ref[...] += contract(g_ref[...], w_ref[...], 1, 0)

    @pl.when(step == pl.num_programs(0) - 1)
    def _():
        out_ref[:, :width] = jnp.where(live_ref[...] > 0, total_ref[...], 0.0).astype(
            out_ref.dtype
        )
        out_ref[:, width:] = b_ref[...]


def last_product(gradients, weight, back, down, live, b_out, steps=6):
    rows, depth = gradients.shape
    width = weight.shape[1]
    total = width + b_out.shape[1]
    block = depth // steps

    def whole(array):
        return pl.BlockSpec(array.shape, lambda i: (0, 0))

    return pl.pallas_call(
        last_kernel,
        grid=(steps,),
        in_specs=[
            pl.BlockSpec((rows, block), lambda i: (0, i)),
            pl.BlockSpec((block, width), lambda i: (i, 0)),
            whole(back),
            whole(down),
            whole(live),
            whole(b_out),
        ],
        out_specs=pl.BlockSpec((rows, total), lambda i: (0, 0)),
        out_shape=jax.ShapeDtypeStruct((rows, total), b_out.dtype),
        scratch_shapes=[pltpu.VMEM((rows, width), jnp.float32)],
        compiler_params=pltpu.CompilerParams(vmem_limit_bytes=32 * 1024 * 1024),
    )(gradients, weight, back, down, live, b_out)


def put(buffer, chunk, index):
    axis = buffer.ndim - 3
    return lax.dynamic_update_slice_in_dim(buffer, jnp.expand_dims(chunk, axis), index % NY, axis)


def in_y_order(chunks, y):
    own = chunks[0]
    buffer = jnp.broadcast_to(
        jnp.expand_dims(own, own.ndim - 2), own.shape[:-2] + (NY,) + own.shape[-2:]
    )
    for offset, chunk in chunks.items():
        if offset:
            buffer = put(buffer, chunk, y + offset)
    return buffer


def body(
    head_outputs,
    output_gradient,
    frozen_weight,
    adapter_down_factors,
    adapter_up_factors,
    tenant_index,
    tenant_group_counts,
):
    row_count = head_outputs.shape[0]
    part_rows, depth = output_gradient.shape
    shard_rows, feature_width = frozen_weight.shape
    a_width = feature_width // 2
    group = lax.axis_index("dp").astype(jnp.int32)
    z, xl, y = group // (NX * NY), (group // NY) % NX, group % NY
    tensor = lax.axis_index("tensor").astype(jnp.int32)

    other = fetch(frozen_weight, dx=1)

    def pair(columns):
        mine, far = frozen_weight[:, columns], other[:, columns]
        return jnp.where(xl == 0, jnp.stack([mine, far]), jnp.stack([far, mine]))

    pair_a, pair_b = pair(slice(0, a_width)), pair(slice(a_width, None))

    a_p1, a_m1 = fetch(pair_a, dz=1), fetch(pair_a, dz=-1)
    gradient_later, pair_a = together(output_gradient, pair_a)
    from_chip = swap_tensor(gradient_later, 2)
    a_p1, a_m1 = together(a_p1, a_m1)
    a_p2, a_m2 = fetch(a_p1, dz=1), fetch(a_m1, dz=-1)
    a_p2, a_m2, pair_b = together(a_p2, a_m2, pair_b)
    a_p3, a_m3 = fetch(a_p2, dz=1), fetch(a_m2, dz=-1)
    b_p, b_m, b_o = fetch(pair_b, dy=1), fetch(pair_b, dy=-1), fetch(pair_b, dy=2)
    b_p, b_m, b_o, a_p2 = together(b_p, b_m, b_o, a_p2)
    b_own = in_y_order({0: pair_b, 1: b_p, 3: b_m, 2: b_o}, y)
    b_own = b_own.reshape(NX * NY * shard_rows, -1)
    a_p3, a_m3, b_own = together(a_p3, a_m3, b_own)
    a_p4 = fetch(a_p3, dz=1)
    b_p1, b_m1 = fetch(b_own, dz=1), fetch(b_own, dz=-1)

    a_own = jnp.broadcast_to(pair_a[None], (NZ,) + pair_a.shape)
    for dz, chunk in ((1, a_p1), (7, a_m1), (2, a_p2), (6, a_m2), (3, a_p3), (5, a_m3), (4, a_p4)):
        a_own = lax.dynamic_update_slice_in_dim(a_own, chunk[None], (z + dz) % NZ, 0)
    rings = [[first + j for j in range(NY)] for first in range(0, NZ * NX * NY, NY)]
    a_all = lax.all_gather(
        a_own[:, :, None], "dp", axis=2, tiled=True, axis_index_groups=rings
    ).reshape(depth, a_width)

    b_p1, b_m1, from_chip, head_later, own_rows = together(
        b_p1, b_m1, from_chip, head_outputs, output_gradient
    )
    b_p2, b_m2 = fetch(b_p1, dz=1), fetch(b_m1, dz=-1)
    from_core = swap_tensor(own_rows, 1)
    from_both = swap_tensor(from_chip, 1)
    partial = jnp.dot(head_later, adapter_down_factors, preferred_element_type=jnp.float32)
    core_partial = swap_tensor(partial, 1)

    b_p2, b_m2, from_both, from_core, partial, core_partial = together(
        b_p2, b_m2, from_both, from_core, partial, core_partial
    )
    b_p3, b_m3 = fetch(b_p2, dz=1), fetch(b_m2, dz=-1)
    chip_sum = partial + core_partial
    far_sum = swap_tensor(chip_sum, 2)

    b_p3, b_m3, far_sum = together(b_p3, b_m3, far_sum)
    cut = b_own.shape[0] // 2 // 16 * 16
    b_p4, b_m4 = fetch(b_p3[:cut], dz=1), fetch(b_m3[cut:], dz=-1)

    gradients = jnp.zeros((row_count, depth), output_gradient.dtype)
    for block, mask in ((own_rows, 0), (from_core, 1), (from_chip, 2), (from_both, 3)):
        gradients = lax.dynamic_update_slice_in_dim(
            gradients, block, (tensor ^ mask) * part_rows, 0
        )
    by_z = split_columns(gradients, z.reshape(1))

    position = jnp.arange(row_count, dtype=jnp.int32)
    active_rows = position < tenant_group_counts[0]
    slot_lookup = jnp.arange(adapter_down_factors.shape[1], dtype=jnp.int32) // ADAPTER_RANK
    select_rows = (
        active_rows[:, None] & (slot_lookup[None, :] == (tenant_index % TEN_DEV)[:, None])
    ).astype(jnp.float32)
    adapter_input = ((chip_sum + far_sum) * select_rows).astype(jnp.bfloat16)
    (adapter_input,) = together(adapter_input)
    adapter_backward = (contract(gradients, adapter_up_factors, 1, 1) * select_rows).astype(
        jnp.bfloat16
    )
    down_factor_gradient = ADAPTER_SCALE * contract(head_outputs, adapter_backward, 0, 0)
    up_factor_gradient = ADAPTER_SCALE * contract(adapter_input, gradients, 0, 0)

    b_total = ADAPTER_SCALE * contract(adapter_backward, adapter_down_factors[a_width:], 1, 1)
    chunks = (b_own, b_p1, b_p2, b_p3, jnp.concatenate([b_p4, b_m4], 0), b_m3, b_m2, b_m1)
    for slot in (0, 1, 7, 2, 6, 3, 5, 4):
        b_total = b_total + contract(by_z[slot], chunks[slot], 1, 0)
    b_out = jnp.where(active_rows[:, None], b_total, 0.0).astype(jnp.bfloat16)
    live = active_rows.astype(jnp.float32)[:, None]

    a_all, b_out, live, adapter_backward, down_factor_gradient, up_factor_gradient = together(
        a_all, b_out, live, adapter_backward, down_factor_gradient, up_factor_gradient
    )
    head_feature_gradient = last_product(
        gradients, a_all, adapter_backward, adapter_down_factors[:a_width], live, b_out
    )
    return (head_feature_gradient, down_factor_gradient, up_factor_gradient)


def solution(mesh):
    in_specs = (
        P("dp", "tensor"),
        P(("dp", "tensor"), None),
        P("dp", "tensor"),
        P("tensor", "dp"),
        P("dp", None),
        P("dp"),
        P("dp"),
    )
    out_specs = (P("dp", "tensor"), P("tensor", "dp"), P("dp", None))
    return jax.shard_map(body, mesh=mesh, in_specs=in_specs, out_specs=out_specs, check_vma=False)
```

time: 137 us -> 131 us (0.956)
  matrix products: 24.2 us -> 12.9 us
  waiting for transfers between devices: 49.8 us -> 54.9 us
  other arithmetic: 3.03 us -> 0.31 us
  starting transfers between devices: 25.8 us -> 28.4 us
  Pallas kernels: 4.99 us -> 6.87 us
  local copies, waits for them, and re-layouts: 12.3 us -> 10.9 us
    ppermute x12 -> x19, waiting for transfers between devices: 34 us -> 47.7 us  [fetch(): return lax.ppermute(x, 'dp', pairs)]
    ppermute x5, waiting for transfers between devices: 11.5 us -> 0.26 us  [swap_tensor(): return lax.ppermute(x, 'tensor', [(t, t ^ mask) for t in range(4)])]
    dot_general x14 -> x12, matrix products: 22.5 us -> 11.2 us  [contract(): lax.dot_general(left, right, (((left_dim,), (right_dim,)), ((), ())), pre...]
    unnamed x17 -> x19, local copies, waits for them, and re-layouts: 1.04 us -> 7.56 us
    dynamic_update_slice x4, local copies, waits for them, and re-layouts: 7.01 us -> 1.75 us  [body(): lax.dynamic_update_slice_in_dim(gradients, block, (tensor ^ mask) * part_...]
    pallas_call x0 -> x1, Pallas kernels: none -> 5.26 us  [last_product(): pl.pallas_call(last_kernel, grid=(steps,), in_specs=[pl.BlockSpec((rows,...]
    pallas_call x1, Pallas kernels: 4.99 us -> 1.61 us  [split_columns(): pl.pallas_call(split_kernel, grid_spec=pltpu.PrefetchScalarGridSpec(num_s...]
    all_gather x1, waiting for transfers between devices: 4.36 us -> 6.9 us  [body(): lax.all_gather(a_own[:, :, None], 'dp', axis=2, tiled=True, axis_index_gr...]
  transfers between devices with their start and end apart: 18 -> 25, of which waited for: 10 -> 18; matrix products, arithmetic and copies ran while one was open for 21% -> 13% of each run, Pallas kernels for 4% -> 1%
where the time goes in v2:
time: 131 us; the launch traced here: 130 us
  waiting for transfers between devices  54.9 us (42%)
  starting transfers between devices  28.4 us (22%)
  between operations  15.3 us (12%)
  matrix products  12.9 us (10%)
  local copies, waits for them, and re-layouts  10.9 us (8%)
  Pallas kernels  6.87 us (5%)
    ppermute x19, waiting for transfers between devices, fetch(): return lax.ppermute(x, 'dp', pairs)  47.7 us
    ppermute x19, starting transfers between devices, fetch(): return lax.ppermute(x, 'dp', pairs)  24.7 us
    dot_general x12, matrix products, contract(): lax.dot_general(left, right, (((left_dim,), (right_dim,)), ((), ())), pre...  11.2 us
    unnamed x19, local copies, waits for them, and re-layouts  7.56 us
    all_gather x1, waiting for transfers between devices, body(): lax.all_gather(a_own[:, :, None], 'dp', axis=2, tiled=True, axis_index_gr...  6.9 us
    pallas_call x1, Pallas kernels, last_product(): pl.pallas_call(last_kernel, grid=(steps,), in_specs=[pl.BlockSpec((rows,...  5.26 us
    ppermute x5, starting transfers between devices, swap_tensor(): return lax.ppermute(x, 'tensor', [(t, t ^ mask) for t in range(4)])  3.67 us
  transfers between devices with their start and end apart: 25, of which 18 were waited for; matrix products, arithmetic and copies ran while one was open for 13% of the time, Pallas kernels for 1%

profile of v2, /device:TPU:6, one launch (start us, length us, event | category | flops | bytes accessed | tf_op | source)
XLA Modules:
  0.0 129.6 jit_solution(549470164533461285)
XLA Ops:
  9.7 3.4 %collective-permute-done = bf16[72,1024]{1,0:T(8,128)(2,1)S(1)} collective-permute-done((bf16[72,1024]{1,0:T(8,128)(2,1)}, bf16[72,1024]{1,0:T(8,128)(2,1)S(1)}, u32[]{:S(2)}, u32[]{:S(2)}) %collective-permute-start) | collective-permute-done | bytes 147488 | tf_op jit(solution)/shard_map/ppermute | solution.py:27
  13.2 5.9 %collective-permute-start.1 = (bf16[2,72,512]{2,1,0:T(8,128)(2,1)S(1)}, bf16[2,72,512]{2,1,0:T(8,128)(2,1)S(1)}, u32[]{:S(2)}, u32[]{:S(2)}) collective-permute-start(bf16[2,72,512]{2,1,0:T(8,128)(2,1)S(1)} %maximum_select_fusion), channel_id=1, source_target_pairs={{32,0},{36,4},{40,8},{44,12},{48,16},{52,20},{56,24},{60,28},{64,3... | collective-permute-start | bytes 442376 | tf_op jit(solution)/shard_map/ppermute | solution.py:27
  19.3 1.5 %collective-permute-start.12 = (bf16[128,4608]{1,0:T(8,128)(2,1)}, bf16[128,4608]{1,0:T(8,128)(2,1)}, u32[]{:S(2)}, u32[]{:S(2)}) collective-permute-start(bf16[128,4608]{1,0:T(8,128)(2,1)} %param.8), channel_id=1, source_target_pairs={{0,2},{1,3},{2,0},{3,1},{4,6},{5,7},{6,4},{7,5},{8,10},{9,11},{10,... | collective-permute-start | bytes 3538952 | tf_op jit(solution)/shard_map/ppermute | solution.py:31
  21.8 3.7 %collective-permute-done.2 = bf16[2,72,512]{2,1,0:T(8,128)(2,1)S(1)} collective-permute-done((bf16[2,72,512]{2,1,0:T(8,128)(2,1)S(1)}, bf16[2,72,512]{2,1,0:T(8,128)(2,1)S(1)}, u32[]{:S(2)}, u32[]{:S(2)}) %collective-permute-start.2) | collective-permute-done | bytes 147488 | tf_op jit(solution)/shard_map/ppermute | solution.py:27
  25.4 2.0 %collective-permute-start.4 = (bf16[2,72,512]{2,1,0:T(8,128)(2,1)S(1)}, bf16[2,72,512]{2,1,0:T(8,128)(2,1)S(1)}, u32[]{:S(2)}, u32[]{:S(2)}) collective-permute-start(bf16[2,72,512]{2,1,0:T(8,128)(2,1)S(1)} %collective-permute-done.2), channel_id=1, source_target_pairs={{224,0},{228,4},{232,8},{236,12},{240,16},{244,20},{248,24},{252,2... | collective-permute-start | bytes 442376 | tf_op jit(solution)/shard_map/ppermute | solution.py:27
  27.6 3.0 %collective-permute-done.3 = bf16[2,72,512]{2,1,0:T(8,128)(2,1)S(1)} collective-permute-done((bf16[2,72,512]{2,1,0:T(8,128)(2,1)S(1)}, bf16[2,72,512]{2,1,0:T(8,128)(2,1)S(1)}, u32[]{:S(2)}, u32[]{:S(2)}) %collective-permute-start.3) | collective-permute-done | bytes 147488 | tf_op jit(solution)/shard_map/ppermute | solution.py:27
  31.8 3.0 %collective-permute-start.7 = (bf16[2,72,512]{2,1,0:T(8,128)(2,1)S(1)}, bf16[2,72,512]{2,1,0:T(8,128)(2,1)S(1)}, u32[]{:S(2)}, u32[]{:S(2)}) collective-permute-start(bf16[2,72,512]{2,1,0:T(8,128)(2,1)S(1)} %maximum_select_fusion.1), channel_id=1, source_target_pairs={{4,0},{8,4},{12,8},{0,12},{20,16},{24,20},{28,24},{16,28},{36,32},... | collective-permute-start | bytes 442376 | tf_op jit(solution)/shard_map/ppermute | solution.py:27
  34.8 2.2 %collective-permute-start.9 = (bf16[2,72,512]{2,1,0:T(8,128)(2,1)S(1)}, bf16[2,72,512]{2,1,0:T(8,128)(2,1)S(1)}, u32[]{:S(2)}, u32[]{:S(2)}) collective-permute-start(bf16[2,72,512]{2,1,0:T(8,128)(2,1)S(1)} %maximum_select_fusion.1), channel_id=1, source_target_pairs={{8,0},{12,4},{0,8},{4,12},{24,16},{28,20},{16,24},{20,28},{40,32},... | collective-permute-start | bytes 442376 | tf_op jit(solution)/shard_map/ppermute | solution.py:27
  39.3 3.5 %collective-permute-done.8 = bf16[2,72,512]{2,1,0:T(8,128)(2,1)S(1)} collective-permute-done((bf16[2,72,512]{2,1,0:T(8,128)(2,1)S(1)}, bf16[2,72,512]{2,1,0:T(8,128)(2,1)S(1)}, u32[]{:S(2)}, u32[]{:S(2)}) %collective-permute-start.8) | collective-permute-done | bytes 147488 | tf_op jit(solution)/shard_map/ppermute | solution.py:27
  42.9 3.4 %collective-permute-done.6 = bf16[2,72,512]{2,1,0:T(8,128)(2,1)S(1)} collective-permute-done((bf16[2,72,512]{2,1,0:T(8,128)(2,1)S(1)}, bf16[2,72,512]{2,1,0:T(8,128)(2,1)S(1)}, u32[]{:S(2)}, u32[]{:S(2)}) %collective-permute-start.6) | collective-permute-done | bytes 147488 | tf_op jit(solution)/shard_map/ppermute | solution.py:27
  46.3 2.0 %collective-permute-start.11 = (bf16[576,512]{1,0:T(8,128)(2,1)S(1)}, bf16[576,512]{1,0:T(8,128)(2,1)}, u32[]{:S(2)}, u32[]{:S(2)}) collective-permute-start(bf16[576,512]{1,0:T(8,128)(2,1)S(1)} %bitcast.96), channel_id=1, source_target_pairs={{224,0},{228,4},{232,8},{236,12},{240,16},{244,20},{248,24},{252,2... | collective-permute-start | bytes 1769480 | tf_op jit(solution)/shard_map/ppermute | solution.py:27
  49.7 8.4 %collective-permute-done.18 = bf16[2,72,512]{2,1,0:T(8,128)(2,1)S(1)} collective-permute-done((bf16[2,72,512]{2,1,0:T(8,128)(2,1)S(1)}, bf16[2,72,512]{2,1,0:T(8,128)(2,1)S(1)}, u32[]{:S(2)}, u32[]{:S(2)}) %collective-permute-start.18) | collective-permute-done | bytes 147488 | tf_op jit(solution)/shard_map/ppermute | solution.py:27
  59.8 1.5 %collective-permute-start.13 = (bf16[576,512]{1,0:T(8,128)(2,1)}, bf16[576,512]{1,0:T(8,128)(2,1)S(1)}, u32[]{:S(2)}, u32[]{:S(2)}) collective-permute-start(bf16[576,512]{1,0:T(8,128)(2,1)} %collective-permute-done.10), channel_id=1, source_target_pairs={{32,0},{36,4},{40,8},{44,12},{48,16},{52,20},{56,24},{60,28},{64,3... | collective-permute-start | bytes 1769480 | tf_op jit(solution)/shard_map/ppermute | solution.py:27
  62.1 1.7 %fusion.25 = f32[512,128]{1,0:T(8,128)S(1)} fusion(bf16[512,1024]{1,0:T(8,128)(2,1)} %param.7, bf16[1024,128]{1,0:T(8,128)(2,1)S(1)} %copy-done.7), kind=kOutput, calls=%fused_computation.69 | convolution fusion | flops 134217728 | bytes 1572864 | tf_op jit(solution)/shard_map/dot_general | solution.py:177
  65.4 10.2 %collective-permute-done.13 = bf16[576,512]{1,0:T(8,128)(2,1)S(1)} collective-permute-done((bf16[576,512]{1,0:T(8,128)(2,1)}, bf16[576,512]{1,0:T(8,128)(2,1)S(1)}, u32[]{:S(2)}, u32[]{:S(2)}) %collective-permute-start.13) | collective-permute-done | bytes 589856 | tf_op jit(solution)/shard_map/ppermute | solution.py:27
  75.6 2.1 %collective-permute-done.14 = bf16[576,512]{1,0:T(8,128)(2,1)S(1)} collective-permute-done((bf16[576,512]{1,0:T(8,128)(2,1)}, bf16[576,512]{1,0:T(8,128)(2,1)S(1)}, u32[]{:S(2)}, u32[]{:S(2)}) %collective-permute-start.14) | collective-permute-done | bytes 589856 | tf_op jit(solution)/shard_map/ppermute | solution.py:27
  77.8 1.5 %collective-permute-start.21 = (f32[512,128]{1,0:T(8,128)S(1)}, f32[512,128]{1,0:T(8,128)S(1)}, u32[]{:S(2)}, u32[]{:S(2)}) collective-permute-start(f32[512,128]{1,0:T(8,128)S(1)} %add.194), channel_id=1, source_target_pairs={{0,2},{1,3},{2,0},{3,1},{4,6},{5,7},{6,4},{7,5},{8,10},{9,11},{10,... | collective-permute-start | bytes 786440 | tf_op jit(solution)/shard_map/ppermute | solution.py:31
  79.6 1.7 %collective-permute-start.20 = (bf16[576,512]{1,0:T(8,128)(2,1)S(1)}, bf16[576,512]{1,0:T(8,128)(2,1)S(1)}, u32[]{:S(2)}, u32[]{:S(2)}) collective-permute-start(bf16[576,512]{1,0:T(8,128)(2,1)S(1)} %collective-permute-done.14), channel_id=1, source_target_pairs={{224,0},{228,4},{232,8},{236,12},{240,16},{244,20},{248,24},{252,2... | collective-permute-start | bytes 1769480 | tf_op jit(solution)/shard_map/ppermute | solution.py:27
  81.5 1.4 %constant_dynamic-update-slice_fusion.1 = bf16[512,4608]{1,0:T(8,128)(2,1)S(1)} fusion(bf16[512,4608]{1,0:T(8,128)(2,1)S(1)} %constant_dynamic-update-slice_fusion.2, bf16[128,4608]{1,0:T(8,128)(2,1)} %collective-permute-done.12, s32[]{:T(128)S(6)} %select_n.145), kind=kLoop, calls=%fused_computation.56 | loop fusion | bytes 2359300 | tf_op jit(solution)/shard_map/dynamic_update_slice | solution.py:193
  83.0 1.6 %shard_map.94 = bf16[8,512,576]{2,1,0:T(8,128)(2,1)S(1)} custom-call(s32[1]{0:T(128)} %bitcast.26.start_ref, bf16[512,4608]{1,0:T(8,128)(2,1)S(1)} %constant_dynamic-update-slice_fusion.g_ref), custom_call_target="tpu_custom_call" | custom-call | tf_op jit(solution)/shard_map/pallas_call | solution.py:49
  85.8 1.6 %fusion.16 = f32[512,512]{1,0:T(8,128)S(1)} fusion(bf16[576,512]{1,0:T(8,128)(2,1)} %collective-permute-done.11, bf16[8,512,576]{2,1,0:T(8,128)(2,1)S(1)} %shard_map.94), kind=kOutput, calls=%fused_computation.27 | convolution fusion | flops 301989888 | bytes 2293760 | tf_op jit(solution)/shard_map/dot_general | solution.py:15
  87.4 1.6 %fusion.17 = f32[512,512]{1,0:T(8,128)S(1)} fusion(bf16[576,512]{1,0:T(8,128)(2,1)} %collective-permute-done.10, bf16[8,512,576]{2,1,0:T(8,128)(2,1)S(1)} %shard_map.94), kind=kOutput, calls=%fused_computation.29 | convolution fusion | flops 301989888 | bytes 2293760 | tf_op jit(solution)/shard_map/dot_general | solution.py:15
  89.1 1.4 %fusion.10.back_ref = bf16[512,128]{1,0:T(8,128)(2,1)S(1)} fusion(bf16[512,4608]{1,0:T(8,128)(2,1)S(1)} %constant_dynamic-update-slice_fusion.g_ref, bf16[128,4608]{1,0:T(8,128)(2,1)S(1)} %copy-done, s32[128]{0:T(128)S(1)} %and_select_fusion, s32[512]{0:T(512)S(1)} %add_select_fusion, pred[512]{0:T(512)(128)(4,1)S(1)} %iota_compare_fusion.1), kind=kOutput, calls=%fused_computation.15 | convolution fusion | flops 604241920 | bytes 6032384 | tf_op jit(solution)/shard_map/dot_general | solution.py:15
  91.2 2.2 %collective-permute-done.19 = bf16[576,512]{1,0:T(8,128)(2,1)S(1)} collective-permute-done((bf16[576,512]{1,0:T(8,128)(2,1)S(1)}, bf16[576,512]{1,0:T(8,128)(2,1)S(1)}, u32[]{:S(2)}, u32[]{:S(2)}) %collective-permute-start.19) | collective-permute-done | bytes 589856 | tf_op jit(solution)/shard_map/ppermute | solution.py:27
  93.3 1.4 %collective-permute-done.20 = bf16[576,512]{1,0:T(8,128)(2,1)S(1)} collective-permute-done((bf16[576,512]{1,0:T(8,128)(2,1)S(1)}, bf16[576,512]{1,0:T(8,128)(2,1)S(1)}, u32[]{:S(2)}, u32[]{:S(2)}) %collective-permute-start.20) | collective-permute-done | bytes 589856 | tf_op jit(solution)/shard_map/ppermute | solution.py:27
  95.4 1.8 %collective-permute-start.23 = (bf16[288,512]{1,0:T(8,128)(2,1)S(1)}, bf16[288,512]{1,0:T(8,128)(2,1)S(1)}, u32[]{:S(2)}, u32[]{:S(2)}) collective-permute-start(bf16[288,512]{1,0:T(8,128)(2,1)S(1)} %slice.62), channel_id=1, source_target_pairs={{224,0},{228,4},{232,8},{236,12},{240,16},{244,20},{248,24},{252,2... | collective-permute-start | bytes 884744 | tf_op jit(solution)/shard_map/ppermute | solution.py:27
  97.2 2.2 %convolution_multiply_fusion = f32[128,4608]{1,0:T(8,128)} fusion(bf16[512,128]{1,0:T(8,128)(2,1)S(1)} %select_convert_fusion, bf16[512,4608]{1,0:T(8,128)(2,1)S(1)} %constant_dynamic-update-slice_fusion.g_ref), kind=kOutput, calls=%fused_computation | convolution fusion | flops 604569600 | bytes 7208960 | tf_op jit(solution)/shard_map/dot_general | solution.py:15
  101.9 1.6 %collective-permute-done.23 = bf16[288,512]{1,0:T(8,128)(2,1)S(1)} collective-permute-done((bf16[288,512]{1,0:T(8,128)(2,1)S(1)}, bf16[288,512]{1,0:T(8,128)(2,1)S(1)}, u32[]{:S(2)}, u32[]{:S(2)}) %collective-permute-start.23) | collective-permute-done | bytes 294944 | tf_op jit(solution)/shard_map/ppermute | solution.py:27
  104.9 6.9 %all-gather.2.cloned.1.call-done = bf16[8,2,4,72,512]{4,3,2,1,0:T(8,128)(2,1)} async-done(((bf16[8,2,1,72,512]{4,3,2,1,0:T(8,128)(2,1)}), bf16[8,2,4,72,512]{4,3,2,1,0:T(8,128)(2,1)}) %all-gather.2.cloned.1.call-update) | async-done | bytes 4718608 | tf_op jit(solution)/shard_map/all_gather | solution.py:167
  112.8 2.3 %copy-done.2 = bf16[512,4608]{1,0:T(8,128)(2,1)S(1)} copy-done((bf16[512,4608]{1,0:T(8,128)(2,1)S(1)}, bf16[512,4608]{1,0:T(8,128)(2,1)}, u32[]{:S(2)}) %copy-start.2) | copy-done | bytes 4718616
  115.1 2.3 %copy-done.3 = bf16[8,2,4,72,512]{4,3,2,1,0:T(8,128)(2,1)S(1)} copy-done((bf16[8,2,4,72,512]{4,3,2,1,0:T(8,128)(2,1)S(1)}, bf16[8,2,4,72,512]{4,3,2,1,0:T(8,128)(2,1)}, u32[]{:S(2)}) %copy-start.3) | copy-done | bytes 4718616
  117.5 5.3 %shard_map.95 = bf16[512,1024]{1,0:T(8,128)(2,1)} custom-call(bf16[512,4608]{1,0:T(8,128)(2,1)S(1)} %copy-done.2, bf16[4608,512]{1,0:T(8,128)(2,1)S(1)} %bitcast.94, bf16[512,128]{1,0:T(8,128)(2,1)S(1)} %fusion.10.back_ref, bf16[512,128]{1,0:T(8,128)(2,1)S(1)} %slice.63.down_ref, f32[512,1]{1,0:T(8,128)S(1)} %fusion.21.live_ref, ...), custom_call_target="tpu_custom_call" | custom-call | tf_op jit(solution)/shard_map/pallas_call | solution.py:89
  (83 shorter events, 19.8 us)
Async XLA Ops:
  7.2 81.9 %copy-start = (bf16[128,4608]{1,0:T(8,128)(2,1)S(1)}, bf16[128,4608]{1,0:T(8,128)(2,1)}, u32[]{:S(2)}) copy-start(bf16[128,4608]{1,0:T(8,128)(2,1)} %param.11) | copy-start | bytes 3538948
  7.2 104.6 %all-gather.2.cloned.1.call-start = ((), (), s32[]{:S(2)}) async-start(), calls=%async_computation | async-start | bytes 5898240 | tf_op jit(solution)/shard_map/all_gather | solution.py:167
  7.2 5.9 %collective-permute-start = (bf16[72,1024]{1,0:T(8,128)(2,1)}, bf16[72,1024]{1,0:T(8,128)(2,1)S(1)}, u32[]{:S(2)}, u32[]{:S(2)}) collective-permute-start(bf16[72,1024]{1,0:T(8,128)(2,1)} %param.9), channel_id=1, source_target_pairs={{16,0},{20,4},{24,8},{28,12},{0,16},{4,20},{8,24},{12,28},{48,32},... | collective-permute-start | bytes 442376 | tf_op jit(solution)/shard_map/ppermute | solution.py:27
  13.2 8.6 %collective-permute-start.1 = (bf16[2,72,512]{2,1,0:T(8,128)(2,1)S(1)}, bf16[2,72,512]{2,1,0:T(8,128)(2,1)S(1)}, u32[]{:S(2)}, u32[]{:S(2)}) collective-permute-start(bf16[2,72,512]{2,1,0:T(8,128)(2,1)S(1)} %maximum_select_fusion), channel_id=1, source_target_pairs={{32,0},{36,4},{40,8},{44,12},{48,16},{52,20},{56,24},{60,28},{64,3... | collective-permute-start | bytes 442376 | tf_op jit(solution)/shard_map/ppermute | solution.py:27
  19.1 6.4 %collective-permute-start.2 = (bf16[2,72,512]{2,1,0:T(8,128)(2,1)S(1)}, bf16[2,72,512]{2,1,0:T(8,128)(2,1)S(1)}, u32[]{:S(2)}, u32[]{:S(2)}) collective-permute-start(bf16[2,72,512]{2,1,0:T(8,128)(2,1)S(1)} %maximum_select_fusion), channel_id=1, source_target_pairs={{224,0},{228,4},{232,8},{236,12},{240,16},{244,20},{248,24},{252,2... | collective-permute-start | bytes 442376 | tf_op jit(solution)/shard_map/ppermute | solution.py:27
  19.3 39.9 %collective-permute-start.12 = (bf16[128,4608]{1,0:T(8,128)(2,1)}, bf16[128,4608]{1,0:T(8,128)(2,1)}, u32[]{:S(2)}, u32[]{:S(2)}) collective-permute-start(bf16[128,4608]{1,0:T(8,128)(2,1)} %param.8), channel_id=1, source_target_pairs={{0,2},{1,3},{2,0},{3,1},{4,6},{5,7},{6,4},{7,5},{8,10},{9,11},{10,... | collective-permute-start | bytes 3538952 | tf_op jit(solution)/shard_map/ppermute | solution.py:31
  25.4 5.1 %collective-permute-start.3 = (bf16[2,72,512]{2,1,0:T(8,128)(2,1)S(1)}, bf16[2,72,512]{2,1,0:T(8,128)(2,1)S(1)}, u32[]{:S(2)}, u32[]{:S(2)}) collective-permute-start(bf16[2,72,512]{2,1,0:T(8,128)(2,1)S(1)} %collective-permute-done.1), channel_id=1, source_target_pairs={{32,0},{36,4},{40,8},{44,12},{48,16},{52,20},{56,24},{60,28},{64,3... | collective-permute-start | bytes 442376 | tf_op jit(solution)/shard_map/ppermute | solution.py:27
  25.4 6.4 %collective-permute-start.4 = (bf16[2,72,512]{2,1,0:T(8,128)(2,1)S(1)}, bf16[2,72,512]{2,1,0:T(8,128)(2,1)S(1)}, u32[]{:S(2)}, u32[]{:S(2)}) collective-permute-start(bf16[2,72,512]{2,1,0:T(8,128)(2,1)S(1)} %collective-permute-done.2), channel_id=1, source_target_pairs={{224,0},{228,4},{232,8},{236,12},{240,16},{244,20},{248,24},{252,2... | collective-permute-start | bytes 442376 | tf_op jit(solution)/shard_map/ppermute | solution.py:27
  27.6 31.6 %copy-start.7 = (bf16[1024,128]{1,0:T(8,128)(2,1)S(1)}, bf16[1024,128]{1,0:T(8,128)(2,1)}, u32[]{:S(2)}) copy-start(bf16[1024,128]{1,0:T(8,128)(2,1)} %param.10) | copy-start | bytes 786436
  31.8 6.7 %collective-permute-start.7 = (bf16[2,72,512]{2,1,0:T(8,128)(2,1)S(1)}, bf16[2,72,512]{2,1,0:T(8,128)(2,1)S(1)}, u32[]{:S(2)}, u32[]{:S(2)}) collective-permute-start(bf16[2,72,512]{2,1,0:T(8,128)(2,1)S(1)} %maximum_select_fusion.1), channel_id=1, source_target_pairs={{4,0},{8,4},{12,8},{0,12},{20,16},{24,20},{28,24},{16,28},{36,32},... | collective-permute-start | bytes 442376 | tf_op jit(solution)/shard_map/ppermute | solution.py:27
  34.8 7.9 %collective-permute-start.8 = (bf16[2,72,512]{2,1,0:T(8,128)(2,1)S(1)}, bf16[2,72,512]{2,1,0:T(8,128)(2,1)S(1)}, u32[]{:S(2)}, u32[]{:S(2)}) collective-permute-start(bf16[2,72,512]{2,1,0:T(8,128)(2,1)S(1)} %maximum_select_fusion.1), channel_id=1, source_target_pairs={{12,0},{0,4},{4,8},{8,12},{28,16},{16,20},{20,24},{24,28},{44,32},... | collective-permute-start | bytes 442376 | tf_op jit(solution)/shard_map/ppermute | solution.py:27
  34.8 7.9 %collective-permute-start.9 = (bf16[2,72,512]{2,1,0:T(8,128)(2,1)S(1)}, bf16[2,72,512]{2,1,0:T(8,128)(2,1)S(1)}, u32[]{:S(2)}, u32[]{:S(2)}) collective-permute-start(bf16[2,72,512]{2,1,0:T(8,128)(2,1)S(1)} %maximum_select_fusion.1), channel_id=1, source_target_pairs={{8,0},{12,4},{0,8},{4,12},{24,16},{28,20},{16,24},{20,28},{40,32},... | collective-permute-start | bytes 442376 | tf_op jit(solution)/shard_map/ppermute | solution.py:27
  37.0 22.8 %copy-start.8 = (s32[512]{0:T(512)S(1)}, s32[512]{0:T(512)}, u32[]{:S(2)}) copy-start(s32[512]{0:T(512)} %param.12) | copy-start | bytes 6148
  37.0 5.9 %collective-permute-start.5 = (bf16[2,72,512]{2,1,0:T(8,128)(2,1)S(1)}, bf16[2,72,512]{2,1,0:T(8,128)(2,1)S(1)}, u32[]{:S(2)}, u32[]{:S(2)}) collective-permute-start(bf16[2,72,512]{2,1,0:T(8,128)(2,1)S(1)} %collective-permute-done.3), channel_id=1, source_target_pairs={{32,0},{36,4},{40,8},{44,12},{48,16},{52,20},{56,24},{60,28},{64,3... | collective-permute-start | bytes 442376 | tf_op jit(solution)/shard_map/ppermute | solution.py:27
  38.5 7.8 %collective-permute-start.6 = (bf16[2,72,512]{2,1,0:T(8,128)(2,1)S(1)}, bf16[2,72,512]{2,1,0:T(8,128)(2,1)S(1)}, u32[]{:S(2)}, u32[]{:S(2)}) collective-permute-start(bf16[2,72,512]{2,1,0:T(8,128)(2,1)S(1)} %collective-permute-done.4), channel_id=1, source_target_pairs={{224,0},{228,4},{232,8},{236,12},{240,16},{244,20},{248,24},{252,2... | collective-permute-start | bytes 442376 | tf_op jit(solution)/shard_map/ppermute | solution.py:27
  46.3 12.9 %collective-permute-start.10 = (bf16[576,512]{1,0:T(8,128)(2,1)S(1)}, bf16[576,512]{1,0:T(8,128)(2,1)}, u32[]{:S(2)}, u32[]{:S(2)}) collective-permute-start(bf16[576,512]{1,0:T(8,128)(2,1)S(1)} %bitcast.95), channel_id=1, source_target_pairs={{32,0},{36,4},{40,8},{44,12},{48,16},{52,20},{56,24},{60,28},{64,3... | collective-permute-start | bytes 1769480 | tf_op jit(solution)/shard_map/ppermute | solution.py:27
  46.3 12.9 %collective-permute-start.11 = (bf16[576,512]{1,0:T(8,128)(2,1)S(1)}, bf16[576,512]{1,0:T(8,128)(2,1)}, u32[]{:S(2)}, u32[]{:S(2)}) collective-permute-start(bf16[576,512]{1,0:T(8,128)(2,1)S(1)} %bitcast.96), channel_id=1, source_target_pairs={{224,0},{228,4},{232,8},{236,12},{240,16},{244,20},{248,24},{252,2... | collective-permute-start | bytes 1769480 | tf_op jit(solution)/shard_map/ppermute | solution.py:27
  48.4 9.7 %collective-permute-start.18 = (bf16[2,72,512]{2,1,0:T(8,128)(2,1)S(1)}, bf16[2,72,512]{2,1,0:T(8,128)(2,1)S(1)}, u32[]{:S(2)}, u32[]{:S(2)}) collective-permute-start(bf16[2,72,512]{2,1,0:T(8,128)(2,1)S(1)} %collective-permute-done.5), channel_id=1, source_target_pairs={{32,0},{36,4},{40,8},{44,12},{48,16},{52,20},{56,24},{60,28},{64,3... | collective-permute-start | bytes 442376 | tf_op jit(solution)/shard_map/ppermute | solution.py:27
  59.2 18.6 %collective-permute-start.15 = (bf16[128,4608]{1,0:T(8,128)(2,1)}, bf16[128,4608]{1,0:T(8,128)(2,1)S(1)}, u32[]{:S(2)}, u32[]{:S(2)}) collective-permute-start(bf16[128,4608]{1,0:T(8,128)(2,1)} %collective-permute-done.12), channel_id=1, source_target_pairs={{0,1},{1,0},{2,3},{3,2},{4,5},{5,4},{6,7},{7,6},{8,9},{9,8},{10,11... | collective-permute-start | bytes 3538952 | tf_op jit(solution)/shard_map/ppermute | solution.py:31
  59.3 18.5 %collective-permute-start.16 = (bf16[128,4608]{1,0:T(8,128)(2,1)}, bf16[128,4608]{1,0:T(8,128)(2,1)S(1)}, u32[]{:S(2)}, u32[]{:S(2)}) collective-permute-start(bf16[128,4608]{1,0:T(8,128)(2,1)} %param.8), channel_id=1, source_target_pairs={{0,1},{1,0},{2,3},{3,2},{4,5},{5,4},{6,7},{7,6},{8,9},{9,8},{10,11... | collective-permute-start | bytes 3538952 | tf_op jit(solution)/shard_map/ppermute | solution.py:31
  59.8 15.8 %collective-permute-start.13 = (bf16[576,512]{1,0:T(8,128)(2,1)}, bf16[576,512]{1,0:T(8,128)(2,1)S(1)}, u32[]{:S(2)}, u32[]{:S(2)}) collective-permute-start(bf16[576,512]{1,0:T(8,128)(2,1)} %collective-permute-done.10), channel_id=1, source_target_pairs={{32,0},{36,4},{40,8},{44,12},{48,16},{52,20},{56,24},{60,28},{64,3... | collective-permute-start | bytes 1769480 | tf_op jit(solution)/shard_map/ppermute | solution.py:27
  61.3 16.5 %collective-permute-start.14 = (bf16[576,512]{1,0:T(8,128)(2,1)}, bf16[576,512]{1,0:T(8,128)(2,1)S(1)}, u32[]{:S(2)}, u32[]{:S(2)}) collective-permute-start(bf16[576,512]{1,0:T(8,128)(2,1)} %collective-permute-done.11), channel_id=1, source_target_pairs={{224,0},{228,4},{232,8},{236,12},{240,16},{244,20},{248,24},{252,2... | collective-permute-start | bytes 1769480 | tf_op jit(solution)/shard_map/ppermute | solution.py:27
  63.8 1.6 %collective-permute-start.17 = (f32[512,128]{1,0:T(8,128)S(1)}, f32[512,128]{1,0:T(8,128)S(1)}, u32[]{:S(2)}, u32[]{:S(2)}) collective-permute-start(f32[512,128]{1,0:T(8,128)S(1)} %fusion.25), channel_id=1, source_target_pairs={{0,1},{1,0},{2,3},{3,2},{4,5},{5,4},{6,7},{7,6},{8,9},{9,8},{10,11... | collective-permute-start | bytes 786440 | tf_op jit(solution)/shard_map/ppermute | solution.py:31
  77.8 13.3 %collective-permute-start.21 = (f32[512,128]{1,0:T(8,128)S(1)}, f32[512,128]{1,0:T(8,128)S(1)}, u32[]{:S(2)}, u32[]{:S(2)}) collective-permute-start(f32[512,128]{1,0:T(8,128)S(1)} %add.194), channel_id=1, source_target_pairs={{0,2},{1,3},{2,0},{3,1},{4,6},{5,7},{6,4},{7,5},{8,10},{9,11},{10,... | collective-permute-start | bytes 786440 | tf_op jit(solution)/shard_map/ppermute | solution.py:31
  79.3 14.0 %collective-permute-start.19 = (bf16[576,512]{1,0:T(8,128)(2,1)S(1)}, bf16[576,512]{1,0:T(8,128)(2,1)S(1)}, u32[]{:S(2)}, u32[]{:S(2)}) collective-permute-start(bf16[576,512]{1,0:T(8,128)(2,1)S(1)} %collective-permute-done.13), channel_id=1, source_target_pairs={{32,0},{36,4},{40,8},{44,12},{48,16},{52,20},{56,24},{60,28},{64,3... | collective-permute-start | bytes 1769480 | tf_op jit(solution)/shard_map/ppermute | solution.py:27
  79.6 15.1 %collective-permute-start.20 = (bf16[576,512]{1,0:T(8,128)(2,1)S(1)}, bf16[576,512]{1,0:T(8,128)(2,1)S(1)}, u32[]{:S(2)}, u32[]{:S(2)}) collective-permute-start(bf16[576,512]{1,0:T(8,128)(2,1)S(1)} %collective-permute-done.14), channel_id=1, source_target_pairs={{224,0},{228,4},{232,8},{236,12},{240,16},{244,20},{248,24},{252,2... | collective-permute-start | bytes 1769480 | tf_op jit(solution)/shard_map/ppermute | solution.py:27
  83.0 14.2 %copy-start.1 = (bf16[512,4608]{1,0:T(8,128)(2,1)}, bf16[512,4608]{1,0:T(8,128)(2,1)S(1)}, u32[]{:S(2)}) copy-start(bf16[512,4608]{1,0:T(8,128)(2,1)S(1)} %constant_dynamic-update-slice_fusion.g_ref) | copy-start | bytes 14155780
  89.1 1.4 %copy-start.5 = (bf16[512,1024]{1,0:T(8,128)(2,1)S(1)}, bf16[512,1024]{1,0:T(8,128)(2,1)}, u32[]{:S(2)}) copy-start(bf16[512,1024]{1,0:T(8,128)(2,1)} %param.7) | copy-start | bytes 3145732
  95.0 6.9 %collective-permute-start.22 = (bf16[288,512]{1,0:T(8,128)(2,1)S(1)}, bf16[288,512]{1,0:T(8,128)(2,1)S(1)}, u32[]{:S(2)}, u32[]{:S(2)}) collective-permute-start(bf16[288,512]{1,0:T(8,128)(2,1)S(1)} %slice.61), channel_id=1, source_target_pairs={{32,0},{36,4},{40,8},{44,12},{48,16},{52,20},{56,24},{60,28},{64,3... | collective-permute-start | bytes 884744 | tf_op jit(solution)/shard_map/ppermute | solution.py:27
  95.4 8.1 %collective-permute-start.23 = (bf16[288,512]{1,0:T(8,128)(2,1)S(1)}, bf16[288,512]{1,0:T(8,128)(2,1)S(1)}, u32[]{:S(2)}, u32[]{:S(2)}) collective-permute-start(bf16[288,512]{1,0:T(8,128)(2,1)S(1)} %slice.62), channel_id=1, source_target_pairs={{224,0},{228,4},{232,8},{236,12},{240,16},{244,20},{248,24},{252,2... | collective-permute-start | bytes 884744 | tf_op jit(solution)/shard_map/ppermute | solution.py:27
  112.8 2.3 %copy-start.2 = (bf16[512,4608]{1,0:T(8,128)(2,1)S(1)}, bf16[512,4608]{1,0:T(8,128)(2,1)}, u32[]{:S(2)}) copy-start(bf16[512,4608]{1,0:T(8,128)(2,1)} %copy-done.1) | copy-start | bytes 14155780
  115.1 2.3 %copy-start.3 = (bf16[8,2,4,72,512]{4,3,2,1,0:T(8,128)(2,1)S(1)}, bf16[8,2,4,72,512]{4,3,2,1,0:T(8,128)(2,1)}, u32[]{:S(2)}) copy-start(bf16[8,2,4,72,512]{4,3,2,1,0:T(8,128)(2,1)} %all-gather.2.cloned.1.call-done) | copy-start | bytes 14155780
  (2 other events, 2.3 us)
Sparse Core Ops, SparseCore 0:
  59.2 52.5 all-gather.1

commit v3 on v1

v3 whole, which is shorter than its diff:
```python
import jax
import jax.numpy as jnp
from jax import lax
from jax.experimental import pallas as pl
from jax.experimental.pallas import tpu as pltpu
from jax.sharding import PartitionSpec as P

ADAPTER_RANK = 16
TEN_DEV = 8
ADAPTER_SCALE = 2.0
NZ, NX, NY = 8, 2, 4


def contract(left, right, left_dim, right_dim):
    return lax.dot_general(
        left, right, (((left_dim,), (right_dim,)), ((), ())), preferred_element_type=jnp.float32
    )


def fetch(x, dz=0, dx=0, dy=0):
    pairs = []
    for z in range(NZ):
        for a in range(NX):
            for y in range(NY):
                source = (((z + dz) % NZ) * NX + (a + dx) % NX) * NY + (y + dy) % NY
                pairs.append((source, (z * NX + a) * NY + y))
    return lax.ppermute(x, "dp", pairs)


def swap_tensor(x, mask):
    return lax.ppermute(x, "tensor", [(t, t ^ mask) for t in range(4)])


def together(*values):
    return lax.optimization_barrier(values)


def split_kernel(start_ref, g_ref, z_ref):
    width = z_ref.shape[2]
    for block in range(NZ):
        slot = lax.rem(block - start_ref[0] + NZ, NZ)
        z_ref[slot] = g_ref[:, block * width : (block + 1) * width]


def split_columns(gradients, start):
    rows, depth = gradients.shape
    step = rows // 4
    width = depth // NZ
    return pl.pallas_call(
        split_kernel,
        grid_spec=pltpu.PrefetchScalarGridSpec(
            num_scalar_prefetch=1,
            grid=(4,),
            in_specs=[pl.BlockSpec((step, depth), lambda i, s: (i, 0))],
            out_specs=pl.BlockSpec((NZ, step, width), lambda i, s: (0, i, 0)),
        ),
        out_shape=jax.ShapeDtypeStruct((NZ, rows, width), gradients.dtype),
        compiler_params=pltpu.CompilerParams(vmem_limit_bytes=32 * 1024 * 1024),
    )(start, gradients)


def last_kernel(g_ref, w_ref, back_ref, down_ref, live_ref, b_ref, out_ref):
    width = w_ref.shape[1]
    total = contract(g_ref[...], w_ref[...], 1, 0)
    total += ADAPTER_SCALE * contract(back_ref[...], down_ref[...], 1, 1)
    out_ref[:, :width] = jnp.where(live_ref[...] > 0, total, 0.0).astype(out_ref.dtype)
    out_ref[:, width:] = b_ref[...]


def down_kernel(head_ref, back_ref, out_ref):
    out_ref[...] = ADAPTER_SCALE * contract(head_ref[...], back_ref[...], 0, 0)


def in_vmem(kernel, shape, dtype, *arrays):
    return pl.pallas_call(
        kernel,
        in_specs=[pl.BlockSpec(memory_space=pltpu.VMEM)] * len(arrays),
        out_specs=pl.BlockSpec(memory_space=pltpu.VMEM),
        out_shape=jax.ShapeDtypeStruct(shape, dtype),
        compiler_params=pltpu.CompilerParams(vmem_limit_bytes=40 * 1024 * 1024),
    )(*arrays)


def body(
    head_outputs,
    output_gradient,
    frozen_weight,
    adapter_down_factors,
    adapter_up_factors,
    tenant_index,
    tenant_group_counts,
):
    row_count = head_outputs.shape[0]
    part_rows, depth = output_gradient.shape
    shard_rows, feature_width = frozen_weight.shape
    a_width = feature_width // 2
    group = lax.axis_index("dp").astype(jnp.int32)
    z, xl, y = group // (NX * NY), (group // NY) % NX, group % NY
    tensor = lax.axis_index("tensor").astype(jnp.int32)

    own_a, own_b = frozen_weight[:, :a_width], frozen_weight[:, a_width:]
    other = fetch(frozen_weight, dx=1)
    y_b = [fetch(own_b, dy=dy) for dy in (1, 2, 3)]
    from_core = swap_tensor(output_gradient, 1)
    other, from_core, *y_b = together(other, from_core, *y_b)

    far_a, far_b = other[:, :a_width], other[:, a_width:]
    pair_a = jnp.where(xl == 0, jnp.stack([own_a, far_a]), jnp.stack([far_a, own_a]))
    a_p1, a_m1 = fetch(pair_a, dz=1), fetch(pair_a, dz=-1)
    y_b = jnp.stack(y_b)
    x_b = fetch(y_b, dx=1)
    gradient_later, head_later, pair_a, y_b = together(
        output_gradient, head_outputs, pair_a, y_b
    )
    from_chip = swap_tensor(gradient_later, 2)
    partial = jnp.dot(head_later, adapter_down_factors, preferred_element_type=jnp.float32)
    core_partial = swap_tensor(partial, 1)
    a_p1, a_m1, x_b = together(a_p1, a_m1, x_b)
    a_p2, a_m2 = fetch(a_p1, dz=1), fetch(a_m1, dz=-1)
    b_own = jnp.broadcast_to(
        jnp.where(xl == 0, jnp.stack([own_b, far_b]), jnp.stack([far_b, own_b]))[:, None],
        (NX, NY, shard_rows, own_b.shape[1]),
    )
    zero = jnp.int32(0)
    for i, dy in enumerate((1, 2, 3)):
        for x, chunk in ((xl, y_b[i]), (1 - xl, x_b[i])):
            b_own = lax.dynamic_update_slice(
                b_own, chunk[None, None], (x, (y + dy) % NY, zero, zero)
            )
    b_own = b_own.reshape(NX * NY * shard_rows, -1)
    b_p1, b_m1 = fetch(b_own, dz=1), fetch(b_own, dz=-1)
    a_p2, a_m2, b_own = together(a_p2, a_m2, b_own)
    a_p3, a_m3 = fetch(a_p2, dz=1), fetch(a_m2, dz=-1)
    a_p3, a_m3 = together(a_p3, a_m3)
    a_p4 = fetch(a_p3, dz=1)

    b_p1, b_m1, a_p3, a_m3 = together(b_p1, b_m1, a_p3, a_m3)
    b_p2, b_m2 = fetch(b_p1, dz=1), fetch(b_m1, dz=-1)

    a_own = jnp.broadcast_to(pair_a[None], (NZ,) + pair_a.shape)
    for dz, chunk in ((1, a_p1), (7, a_m1), (2, a_p2), (6, a_m2), (3, a_p3), (5, a_m3), (4, a_p4)):
        a_own = lax.dynamic_update_slice_in_dim(a_own, chunk[None], (z + dz) % NZ, 0)
    half = NZ // 2
    a_low, a_high = together(a_own[:half], a_own[half:])
    low_p, low_m = fetch(a_low, dy=1), fetch(a_low, dy=-1)

    from_chip, a_low, a_high = together(from_chip, a_low, a_high)
    from_both = swap_tensor(from_chip, 1)

    b_p2, b_m2, low_p, low_m, from_both, partial, core_partial = together(
        b_p2, b_m2, low_p, low_m, from_both, partial, core_partial
    )
    b_p3, b_m3 = fetch(b_p2, dz=1), fetch(b_m2, dz=-1)
    high_p, high_m, low_o = fetch(a_high, dy=1), fetch(a_high, dy=-1), fetch(low_p, dy=1)

    gradients = jnp.zeros((row_count, depth), output_gradient.dtype)
    for block, mask in ((output_gradient, 0), (from_core, 1), (from_chip, 2), (from_both, 3)):
        gradients = lax.dynamic_update_slice_in_dim(
            gradients, block, (tensor ^ mask) * part_rows, 0
        )
    chip_sum = partial + core_partial
    far_sum = swap_tensor(chip_sum, 2)
    by_z = split_columns(gradients, z.reshape(1))

    b_p3, b_m3, high_p, high_m, low_o, by_z, far_sum = together(
        b_p3, b_m3, high_p, high_m, low_o, by_z, far_sum
    )
    cut = b_own.shape[0] // 2 // 16 * 16
    b_p4, b_m4 = fetch(b_p3[:cut], dz=1), fetch(b_m3[cut:], dz=-1)
    high_o = fetch(high_m, dy=-1)

    position = jnp.arange(row_count, dtype=jnp.int32)
    active_rows = position < tenant_group_counts[0]
    slot_lookup = jnp.arange(adapter_down_factors.shape[1], dtype=jnp.int32) // ADAPTER_RANK
    select_rows = (
        active_rows[:, None] & (slot_lookup[None, :] == (tenant_index % TEN_DEV)[:, None])
    ).astype(jnp.float32)
    adapter_input = ((chip_sum + far_sum) * select_rows).astype(jnp.bfloat16)
    adapter_backward = (contract(gradients, adapter_up_factors, 1, 1) * select_rows).astype(
        jnp.bfloat16
    )
    down_factor_gradient = in_vmem(
        down_kernel, adapter_down_factors.shape, jnp.float32, head_outputs, adapter_backward
    )

    b_total = ADAPTER_SCALE * contract(adapter_backward, adapter_down_factors[a_width:], 1, 1)
    chunks = (b_own, b_p1, b_p2, b_p3, None, b_m3, b_m2, b_m1)
    for slot in (0, 1, 7, 2, 6, 3, 5):
        b_total = b_total + contract(by_z[slot], chunks[slot], 1, 0)
    live = active_rows.astype(jnp.float32)[:, None]

    adapter_input, b_p4, b_m4, *arrived = together(
        adapter_input, b_p4, b_m4, a_low, low_p, low_m, low_o, a_high, high_p, high_m
    )
    up_factor_gradient = ADAPTER_SCALE * contract(adapter_input, gradients, 0, 0)
    b_total = b_total + contract(by_z[4], jnp.concatenate([b_p4, b_m4], 0), 1, 0)
    b_out = jnp.where(active_rows[:, None], b_total, 0.0).astype(jnp.bfloat16)
    a_all = jnp.zeros((NZ, NX, NY) + a_own.shape[2:], a_own.dtype)

    def placed(array, chunk, first, dy):
        at = (jnp.int32(first), zero, (y + dy) % NY, zero, zero)
        return lax.dynamic_update_slice(array, chunk[:, :, None], at)

    places = ((0, 0), (0, 1), (0, 3), (0, 2), (half, 0), (half, 1), (half, 3))
    for (first, dy), chunk in zip(places, arrived):
        a_all = placed(a_all, chunk, first, dy)

    high_o, a_all, b_out, down_factor_gradient, up_factor_gradient = together(
        high_o, a_all, b_out, down_factor_gradient, up_factor_gradient
    )
    a_all = placed(a_all, high_o, half, 2)
    head_feature_gradient = in_vmem(
        last_kernel,
        head_outputs.shape,
        jnp.bfloat16,
        gradients,
        a_all.reshape(depth, a_width),
        adapter_backward,
        adapter_down_factors[:a_width],
        live,
        b_out,
    )
    return (head_feature_gradient, down_factor_gradient, up_factor_gradient)


def solution(mesh):
    in_specs = (
        P("dp", "tensor"),
        P(("dp", "tensor"), None),
        P("dp", "tensor"),
        P("tensor", "dp"),
        P("dp", None),
        P("dp"),
        P("dp"),
    )
    out_specs = (P("dp", "tensor"), P("tensor", "dp"), P("dp", None))
    return jax.shard_map(body, mesh=mesh, in_specs=in_specs, out_specs=out_specs, check_vma=False)
```

time: 137 us -> 136 us (level)
  starting transfers between devices: 25.8 us -> 39.7 us
  between operations: 15 us -> 1.87 us
  matrix products: 24.2 us -> 13.8 us
  Pallas kernels: 4.99 us -> 11.2 us
  waiting for transfers between devices: 49.8 us -> 55.9 us
  other arithmetic: 3.03 us -> 1.11 us
  local copies, waits for them, and re-layouts: 12.3 us -> 10.6 us
    ppermute x12 -> x26, waiting for transfers between devices: 34 us -> 55.9 us  [fetch(): return lax.ppermute(x, 'dp', pairs)]
    ppermute x12 -> x26, starting transfers between devices: 22.2 us -> 37 us  [fetch(): return lax.ppermute(x, 'dp', pairs)]
    ppermute x5, waiting for transfers between devices: 11.5 us -> 0.01 us  [swap_tensor(): return lax.ppermute(x, 'tensor', [(t, t ^ mask) for t in range(4)])]
    dot_general x14 -> x11, matrix products: 22.5 us -> 13.4 us  [contract(): lax.dot_general(left, right, (((left_dim,), (right_dim,)), ((), ())), pre...]
    pallas_call x0 -> x2, Pallas kernels: none -> 7.36 us  [in_vmem(): pl.pallas_call(kernel, in_specs=[pl.BlockSpec(memory_space=pltpu.VMEM)] *...]
    all_gather x1 -> x0, waiting for transfers between devices: 4.36 us -> none  [body(): lax.all_gather(pair_a, 'dp', axis=1, tiled=True, axis_index_groups=rings)]
  transfers between devices with their start and end apart: 18 -> 31, of which waited for: 10 -> 13; matrix products, arithmetic and copies ran while one was open for 21% -> 17% of each run, Pallas kernels for 4% -> 4%
where the time goes in v3:
time: 136 us; the launch traced here: 134 us
  waiting for transfers between devices  55.9 us (41%)
  starting transfers between devices  39.7 us (29%)
  matrix products  13.8 us (10%)
  Pallas kernels  11.2 us (8%)
  local copies, waits for them, and re-layouts  10.6 us (8%)
  between operations  1.87 us (1%)
    ppermute x26, waiting for transfers between devices, fetch(): return lax.ppermute(x, 'dp', pairs)  55.9 us
    ppermute x26, starting transfers between devices, fetch(): return lax.ppermute(x, 'dp', pairs)  37 us
    dot_general x11, matrix products, contract(): lax.dot_general(left, right, (((left_dim,), (right_dim,)), ((), ())), pre...  13.4 us
    pallas_call x2, Pallas kernels, in_vmem(): pl.pallas_call(kernel, in_specs=[pl.BlockSpec(memory_space=pltpu.VMEM)] *...  7.36 us
    dynamic_update_slice x4, local copies, waits for them, and re-layouts, body(): lax.dynamic_update_slice_in_dim(gradients, block, (tensor ^ mask) * part_...  5.67 us
    pallas_call x1, Pallas kernels, split_columns(): pl.pallas_call(split_kernel, grid_spec=pltpu.PrefetchScalarGridSpec(num_s...  3.89 us
  transfers between devices with their start and end apart: 31, of which 13 were waited for; matrix products, arithmetic and copies ran while one was open for 17% of the time, Pallas kernels for 4%

profile of v3, /device:TPU:6, one launch (start us, length us, event | category | flops | bytes accessed | tf_op | source)
XLA Modules:
  0.0 134.3 jit_solution(9862199299438224180)
XLA Ops:
  1.9 3.1 %collective-permute-start.2 = (bf16[72,512]{1,0:T(8,128)(2,1)S(1)}, bf16[72,512]{1,0:T(8,128)(2,1)S(1)}, u32[]{:S(2)}, u32[]{:S(2)}) collective-permute-start(bf16[72,512]{1,0:T(8,128)(2,1)S(1)} %get-tuple-element.117), channel_id=1, source_target_pairs={{4,0},{8,4},{12,8},{0,12},{20,16},{24,20},{28,24},{16,28},{36,32},... | collective-permute-start | bytes 221192 | tf_op jit(solution)/shard_map/ppermute | solution.py:27
  8.9 2.4 %broadcast_in_dim.80 = bf16[512,4608]{1,0:T(8,128)(2,1)} broadcast(bf16[]{:T(256)} %constant.147.clone.1), dimensions={} | broadcast | bytes 4718594 | tf_op jit(solution)/shard_map/broadcast_in_dim | solution.py:156
  12.6 5.9 %collective-permute-start.6 = (bf16[2,72,512]{2,1,0:T(8,128)(2,1)S(1)}, bf16[2,72,512]{2,1,0:T(8,128)(2,1)S(1)}, u32[]{:S(2)}, u32[]{:S(2)}) collective-permute-start(bf16[2,72,512]{2,1,0:T(8,128)(2,1)S(1)} %maximum_select_fusion), channel_id=1, source_target_pairs={{32,0},{36,4},{40,8},{44,12},{48,16},{52,20},{56,24},{60,28},{64,3... | collective-permute-start | bytes 442376 | tf_op jit(solution)/shard_map/ppermute | solution.py:27
  18.6 1.3 collective-permute-start.8
  19.9 1.4 %collective-permute-start.5 = (bf16[128,4608]{1,0:T(8,128)(2,1)}, bf16[128,4608]{1,0:T(8,128)(2,1)S(1)}, u32[]{:S(2)}, u32[]{:S(2)}) collective-permute-start(bf16[128,4608]{1,0:T(8,128)(2,1)} %param.8), channel_id=1, source_target_pairs={{0,2},{1,3},{2,0},{3,1},{4,6},{5,7},{6,4},{7,5},{8,10},{9,11},{10,... | collective-permute-start | bytes 3538952 | tf_op jit(solution)/shard_map/ppermute | solution.py:31
  21.9 3.1 %collective-permute-done.7 = bf16[2,72,512]{2,1,0:T(8,128)(2,1)S(1)} collective-permute-done((bf16[2,72,512]{2,1,0:T(8,128)(2,1)S(1)}, bf16[2,72,512]{2,1,0:T(8,128)(2,1)S(1)}, u32[]{:S(2)}, u32[]{:S(2)}) %collective-permute-start.7) | collective-permute-done | bytes 147488 | tf_op jit(solution)/shard_map/ppermute | solution.py:27
  24.9 2.1 %collective-permute-done.8 = bf16[3,72,512]{2,1,0:T(8,128)(2,1)S(1)} collective-permute-done((bf16[3,72,512]{2,1,0:T(8,128)(2,1)S(1)}, bf16[3,72,512]{2,1,0:T(8,128)(2,1)S(1)}, u32[]{:S(2)}, u32[]{:S(2)}) %collective-permute-start.8) | collective-permute-done | bytes 221216 | tf_op jit(solution)/shard_map/ppermute | solution.py:27
  27.1 3.3 %collective-permute-start.11 = (bf16[576,512]{1,0:T(8,128)(2,1)S(1)}, bf16[576,512]{1,0:T(8,128)(2,1)S(1)}, u32[]{:S(2)}, u32[]{:S(2)}) collective-permute-start(bf16[576,512]{1,0:T(8,128)(2,1)S(1)} %bitcast.112), channel_id=1, source_target_pairs={{32,0},{36,4},{40,8},{44,12},{48,16},{52,20},{56,24},{60,28},{64,3... | collective-permute-start | bytes 1769480 | tf_op jit(solution)/shard_map/ppermute | solution.py:27
  30.5 3.3 %collective-permute-start.9 = (bf16[2,72,512]{2,1,0:T(8,128)(2,1)S(1)}, bf16[2,72,512]{2,1,0:T(8,128)(2,1)S(1)}, u32[]{:S(2)}, u32[]{:S(2)}) collective-permute-start(bf16[2,72,512]{2,1,0:T(8,128)(2,1)S(1)} %collective-permute-done.6), channel_id=1, source_target_pairs={{32,0},{36,4},{40,8},{44,12},{48,16},{52,20},{56,24},{60,28},{64,3... | collective-permute-start | bytes 442376 | tf_op jit(solution)/shard_map/ppermute | solution.py:27
  33.9 12.9 %collective-permute-done.10 = bf16[2,72,512]{2,1,0:T(8,128)(2,1)S(1)} collective-permute-done((bf16[2,72,512]{2,1,0:T(8,128)(2,1)S(1)}, bf16[2,72,512]{2,1,0:T(8,128)(2,1)S(1)}, u32[]{:S(2)}, u32[]{:S(2)}) %collective-permute-start.10) | collective-permute-done | bytes 147488 | tf_op jit(solution)/shard_map/ppermute | solution.py:27
  47.1 1.8 %collective-permute-start.14 = (bf16[2,72,512]{2,1,0:T(8,128)(2,1)S(1)}, bf16[2,72,512]{2,1,0:T(8,128)(2,1)S(1)}, u32[]{:S(2)}, u32[]{:S(2)}) collective-permute-start(bf16[2,72,512]{2,1,0:T(8,128)(2,1)S(1)} %collective-permute-done.10), channel_id=1, source_target_pairs={{224,0},{228,4},{232,8},{236,12},{240,16},{244,20},{248,24},{252,2... | collective-permute-start | bytes 442376 | tf_op jit(solution)/shard_map/ppermute | solution.py:27
  48.9 3.1 %collective-permute-done.13 = bf16[2,72,512]{2,1,0:T(8,128)(2,1)S(1)} collective-permute-done((bf16[2,72,512]{2,1,0:T(8,128)(2,1)S(1)}, bf16[2,72,512]{2,1,0:T(8,128)(2,1)S(1)}, u32[]{:S(2)}, u32[]{:S(2)}) %collective-permute-start.13) | collective-permute-done | bytes 147488 | tf_op jit(solution)/shard_map/ppermute | solution.py:27
  52.0 1.5 %collective-permute-done.14 = bf16[2,72,512]{2,1,0:T(8,128)(2,1)S(1)} collective-permute-done((bf16[2,72,512]{2,1,0:T(8,128)(2,1)S(1)}, bf16[2,72,512]{2,1,0:T(8,128)(2,1)S(1)}, u32[]{:S(2)}, u32[]{:S(2)}) %collective-permute-start.14) | collective-permute-done | bytes 147488 | tf_op jit(solution)/shard_map/ppermute | solution.py:27
  53.5 5.1 %collective-permute-done.15 = bf16[2,72,512]{2,1,0:T(8,128)(2,1)S(1)} collective-permute-done((bf16[2,72,512]{2,1,0:T(8,128)(2,1)S(1)}, bf16[2,72,512]{2,1,0:T(8,128)(2,1)S(1)}, u32[]{:S(2)}, u32[]{:S(2)}) %collective-permute-start.15) | collective-permute-done | bytes 147488 | tf_op jit(solution)/shard_map/ppermute | solution.py:27
  58.8 2.4 %constant_dynamic-update-slice_fusion.2 = bf16[512,4608]{1,0:T(8,128)(2,1)} fusion(bf16[512,4608]{1,0:T(8,128)(2,1)} %constant_dynamic-update-slice_fusion.3, bf16[128,4608]{1,0:T(8,128)(2,1)} %collective-permute-done.1, s32[]{:T(128)S(6)} %select_n.183), kind=kLoop, calls=%fused_computation.74 | loop fusion | bytes 2359300 | tf_op jit(solution)/shard_map/dynamic_update_slice | solution.py:158
  61.2 1.9 %collective-permute-start.18 = (bf16[4,2,72,512]{3,2,1,0:T(8,128)(2,1)S(1)}, bf16[4,2,72,512]{3,2,1,0:T(8,128)(2,1)S(1)}, u32[]{:S(2)}, u32[]{:S(2)}) collective-permute-start(bf16[4,2,72,512]{3,2,1,0:T(8,128)(2,1)S(1)} %get-tuple-element.96), channel_id=1, source_target_pairs={{4,0},{8,4},{12,8},{0,12},{20,16},{24,20},{28,24},{16,28},{36,32},... | collective-permute-start | bytes 1769480 | tf_op jit(solution)/shard_map/ppermute | solution.py:27
  63.2 2.3 %collective-permute-start.16 = (bf16[576,512]{1,0:T(8,128)(2,1)S(1)}, bf16[576,512]{1,0:T(8,128)(2,1)S(1)}, u32[]{:S(2)}, u32[]{:S(2)}) collective-permute-start(bf16[576,512]{1,0:T(8,128)(2,1)S(1)} %collective-permute-done.11), channel_id=1, source_target_pairs={{32,0},{36,4},{40,8},{44,12},{48,16},{52,20},{56,24},{60,28},{64,3... | collective-permute-start | bytes 1769480 | tf_op jit(solution)/shard_map/ppermute | solution.py:27
  66.7 10.2 %collective-permute-done.18 = bf16[4,2,72,512]{3,2,1,0:T(8,128)(2,1)S(1)} collective-permute-done((bf16[4,2,72,512]{3,2,1,0:T(8,128)(2,1)S(1)}, bf16[4,2,72,512]{3,2,1,0:T(8,128)(2,1)S(1)}, u32[]{:S(2)}, u32[]{:S(2)}) %collective-permute-start.18) | collective-permute-done | bytes 589856 | tf_op jit(solution)/shard_map/ppermute | solution.py:27
  76.9 3.1 %collective-permute-start.24 = (bf16[4,2,72,512]{3,2,1,0:T(8,128)(2,1)S(1)}, bf16[4,2,72,512]{3,2,1,0:T(8,128)(2,1)S(1)}, u32[]{:S(2)}, u32[]{:S(2)}) collective-permute-start(bf16[4,2,72,512]{3,2,1,0:T(8,128)(2,1)S(1)} %get-tuple-element.100), channel_id=1, source_target_pairs={{4,0},{8,4},{12,8},{0,12},{20,16},{24,20},{28,24},{16,28},{36,32},... | collective-permute-start | bytes 1769480 | tf_op jit(solution)/shard_map/ppermute | solution.py:27
  80.0 1.8 %collective-permute-done.17 = bf16[576,512]{1,0:T(8,128)(2,1)S(1)} collective-permute-done((bf16[576,512]{1,0:T(8,128)(2,1)S(1)}, bf16[576,512]{1,0:T(8,128)(2,1)S(1)}, u32[]{:S(2)}, u32[]{:S(2)}) %collective-permute-start.17) | collective-permute-done | bytes 589856 | tf_op jit(solution)/shard_map/ppermute | solution.py:27
  83.5 1.5 %collective-permute-start.23 = (bf16[576,512]{1,0:T(8,128)(2,1)S(1)}, bf16[576,512]{1,0:T(8,128)(2,1)S(1)}, u32[]{:S(2)}, u32[]{:S(2)}) collective-permute-start(bf16[576,512]{1,0:T(8,128)(2,1)S(1)} %collective-permute-done.17), channel_id=1, source_target_pairs={{224,0},{228,4},{232,8},{236,12},{240,16},{244,20},{248,24},{252,2... | collective-permute-start | bytes 1769480 | tf_op jit(solution)/shard_map/ppermute | solution.py:27
  86.1 6.4 %collective-permute-done.24 = bf16[4,2,72,512]{3,2,1,0:T(8,128)(2,1)S(1)} collective-permute-done((bf16[4,2,72,512]{3,2,1,0:T(8,128)(2,1)S(1)}, bf16[4,2,72,512]{3,2,1,0:T(8,128)(2,1)S(1)}, u32[]{:S(2)}, u32[]{:S(2)}) %collective-permute-start.24) | collective-permute-done | bytes 589856 | tf_op jit(solution)/shard_map/ppermute | solution.py:27
  92.5 3.7 %collective-permute-start.26 = (bf16[4,2,72,512]{3,2,1,0:T(8,128)(2,1)S(1)}, bf16[4,2,72,512]{3,2,1,0:T(8,128)(2,1)S(1)}, u32[]{:S(2)}, u32[]{:S(2)}) collective-permute-start(bf16[4,2,72,512]{3,2,1,0:T(8,128)(2,1)S(1)} %collective-permute-done.18), channel_id=1, source_target_pairs={{4,0},{8,4},{12,8},{0,12},{20,16},{24,20},{28,24},{16,28},{36,32},... | collective-permute-start | bytes 1769480 | tf_op jit(solution)/shard_map/ppermute | solution.py:27
  96.2 3.7 %fusion.9.back_ref = bf16[512,128]{1,0:T(8,128)(2,1)S(1)} fusion(bf16[512,4608]{1,0:T(8,128)(2,1)} %constant_dynamic-update-slice_fusion.g_ref, bf16[128,4608]{1,0:T(8,128)(2,1)S(1)} %copy-done, s32[128]{0:T(128)S(1)} %and_select_fusion, s32[512]{0:T(512)S(1)} %add_select_fusion, pred[512]{0:T(512)(128)(4,1)S(1)} %iota_compare_fusion.1), kind=kOutput, calls=%fused_computation.13 | convolution fusion | flops 604241920 | bytes 6032384 | tf_op jit(solution)/shard_map/dot_general | solution.py:15
  99.9 3.9 %shard_map.94 = bf16[8,512,576]{2,1,0:T(8,128)(2,1)S(1)} custom-call(s32[1]{0:T(128)} %bitcast.21.start_ref, bf16[512,4608]{1,0:T(8,128)(2,1)} %constant_dynamic-update-slice_fusion.g_ref), custom_call_target="tpu_custom_call" | custom-call | tf_op jit(solution)/shard_map/pallas_call | solution.py:49
  103.8 1.3 shard_map.95
  105.4 2.3 %collective-permute-done.26 = bf16[4,2,72,512]{3,2,1,0:T(8,128)(2,1)S(1)} collective-permute-done((bf16[4,2,72,512]{3,2,1,0:T(8,128)(2,1)S(1)}, bf16[4,2,72,512]{3,2,1,0:T(8,128)(2,1)S(1)}, u32[]{:S(2)}, u32[]{:S(2)}) %collective-permute-start.26) | collective-permute-done | bytes 589856 | tf_op jit(solution)/shard_map/ppermute | solution.py:27
  110.7 2.4 %collective-permute-start.29 = (bf16[288,512]{1,0:T(8,128)(2,1)S(1)}, bf16[288,512]{1,0:T(8,128)(2,1)S(1)}, u32[]{:S(2)}, u32[]{:S(2)}) collective-permute-start(bf16[288,512]{1,0:T(8,128)(2,1)S(1)} %slice.84), channel_id=1, source_target_pairs={{32,0},{36,4},{40,8},{44,12},{48,16},{52,20},{56,24},{60,28},{64,3... | collective-permute-start | bytes 884744 | tf_op jit(solution)/shard_map/ppermute | solution.py:27
  114.0 3.6 %collective-permute-done.29 = bf16[288,512]{1,0:T(8,128)(2,1)S(1)} collective-permute-done((bf16[288,512]{1,0:T(8,128)(2,1)S(1)}, bf16[288,512]{1,0:T(8,128)(2,1)S(1)}, u32[]{:S(2)}, u32[]{:S(2)}) %collective-permute-start.29) | collective-permute-done | bytes 294944 | tf_op jit(solution)/shard_map/ppermute | solution.py:27
  117.6 3.4 %collective-permute-done.30 = bf16[288,512]{1,0:T(8,128)(2,1)S(1)} collective-permute-done((bf16[288,512]{1,0:T(8,128)(2,1)S(1)}, bf16[288,512]{1,0:T(8,128)(2,1)S(1)}, u32[]{:S(2)}, u32[]{:S(2)}) %collective-permute-start.30) | collective-permute-done | bytes 294944 | tf_op jit(solution)/shard_map/ppermute | solution.py:27
  121.0 4.6 %convolution_multiply_fusion = f32[128,4608]{1,0:T(8,128)} fusion(bf16[512,128]{1,0:T(8,128)(2,1)S(1)} %select_convert_fusion, bf16[512,4608]{1,0:T(8,128)(2,1)} %constant_dynamic-update-slice_fusion.g_ref), kind=kOutput, calls=%fused_computation | convolution fusion | flops 604569600 | bytes 7208960 | tf_op jit(solution)/shard_map/dot_general | solution.py:15
  128.2 6.1 %shard_map.96 = bf16[512,1024]{1,0:T(8,128)(2,1)} custom-call(bf16[512,4608]{1,0:T(8,128)(2,1)} %constant_dynamic-update-slice_fusion.g_ref, bf16[4608,512]{1,0:T(8,128)(2,1)S(1)} %bitcast.111, bf16[512,128]{1,0:T(8,128)(2,1)S(1)} %fusion.9.back_ref, bf16[512,128]{1,0:T(8,128)(2,1)S(1)} %slice.95.down_ref, f32[512,1]{1,0:T(8,128)S(1)} %fusion.36.live_ref, ...), custom_call_target="tpu_custom_call" | custom-call | tf_op jit(solution)/shard_map/pallas_call | solution.py:75
  (97 shorter events, 17.6 us)
Async XLA Ops:
  0.6 95.5 %copy-start = (bf16[128,4608]{1,0:T(8,128)(2,1)S(1)}, bf16[128,4608]{1,0:T(8,128)(2,1)}, u32[]{:S(2)}) copy-start(bf16[128,4608]{1,0:T(8,128)(2,1)} %param.11) | copy-start | bytes 3538948
  0.7 11.9 %collective-permute-start.1 = (bf16[128,4608]{1,0:T(8,128)(2,1)}, bf16[128,4608]{1,0:T(8,128)(2,1)}, u32[]{:S(2)}, u32[]{:S(2)}) collective-permute-start(bf16[128,4608]{1,0:T(8,128)(2,1)} %param.8), channel_id=1, source_target_pairs={{0,1},{1,0},{2,3},{3,2},{4,5},{5,4},{6,7},{7,6},{8,9},{9,8},{10,11... | collective-permute-start | bytes 3538952 | tf_op jit(solution)/shard_map/ppermute | solution.py:31
  1.9 10.7 %collective-permute-start.2 = (bf16[72,512]{1,0:T(8,128)(2,1)S(1)}, bf16[72,512]{1,0:T(8,128)(2,1)S(1)}, u32[]{:S(2)}, u32[]{:S(2)}) collective-permute-start(bf16[72,512]{1,0:T(8,128)(2,1)S(1)} %get-tuple-element.117), channel_id=1, source_target_pairs={{4,0},{8,4},{12,8},{0,12},{20,16},{24,20},{28,24},{16,28},{36,32},... | collective-permute-start | bytes 221192 | tf_op jit(solution)/shard_map/ppermute | solution.py:27
  5.0 7.6 %collective-permute-start.3 = (bf16[72,512]{1,0:T(8,128)(2,1)S(1)}, bf16[72,512]{1,0:T(8,128)(2,1)S(1)}, u32[]{:S(2)}, u32[]{:S(2)}) collective-permute-start(bf16[72,512]{1,0:T(8,128)(2,1)S(1)} %get-tuple-element.117), channel_id=1, source_target_pairs={{8,0},{12,4},{0,8},{4,12},{24,16},{28,20},{16,24},{20,28},{40,32},... | collective-permute-start | bytes 221192 | tf_op jit(solution)/shard_map/ppermute | solution.py:27
  5.6 7.0 %collective-permute-start.4 = (bf16[72,512]{1,0:T(8,128)(2,1)S(1)}, bf16[72,512]{1,0:T(8,128)(2,1)S(1)}, u32[]{:S(2)}, u32[]{:S(2)}) collective-permute-start(bf16[72,512]{1,0:T(8,128)(2,1)S(1)} %get-tuple-element.117), channel_id=1, source_target_pairs={{12,0},{0,4},{4,8},{8,12},{28,16},{16,20},{20,24},{24,28},{44,32},... | collective-permute-start | bytes 221192 | tf_op jit(solution)/shard_map/ppermute | solution.py:27
  6.6 6.0 %collective-permute-start = (bf16[72,1024]{1,0:T(8,128)(2,1)}, bf16[72,1024]{1,0:T(8,128)(2,1)S(1)}, u32[]{:S(2)}, u32[]{:S(2)}) collective-permute-start(bf16[72,1024]{1,0:T(8,128)(2,1)} %param.9), channel_id=1, source_target_pairs={{16,0},{20,4},{24,8},{28,12},{0,16},{4,20},{8,24},{12,28},{48,32},... | collective-permute-start | bytes 442376 | tf_op jit(solution)/shard_map/ppermute | solution.py:27
  12.6 9.2 %collective-permute-start.6 = (bf16[2,72,512]{2,1,0:T(8,128)(2,1)S(1)}, bf16[2,72,512]{2,1,0:T(8,128)(2,1)S(1)}, u32[]{:S(2)}, u32[]{:S(2)}) collective-permute-start(bf16[2,72,512]{2,1,0:T(8,128)(2,1)S(1)} %maximum_select_fusion), channel_id=1, source_target_pairs={{32,0},{36,4},{40,8},{44,12},{48,16},{52,20},{56,24},{60,28},{64,3... | collective-permute-start | bytes 442376 | tf_op jit(solution)/shard_map/ppermute | solution.py:27
  18.6 6.4 %collective-permute-start.7 = (bf16[2,72,512]{2,1,0:T(8,128)(2,1)S(1)}, bf16[2,72,512]{2,1,0:T(8,128)(2,1)S(1)}, u32[]{:S(2)}, u32[]{:S(2)}) collective-permute-start(bf16[2,72,512]{2,1,0:T(8,128)(2,1)S(1)} %maximum_select_fusion), channel_id=1, source_target_pairs={{224,0},{228,4},{232,8},{236,12},{240,16},{244,20},{248,24},{252,2... | collective-permute-start | bytes 442376 | tf_op jit(solution)/shard_map/ppermute | solution.py:27
  18.6 8.5 %collective-permute-start.8 = (bf16[3,72,512]{2,1,0:T(8,128)(2,1)S(1)}, bf16[3,72,512]{2,1,0:T(8,128)(2,1)S(1)}, u32[]{:S(2)}, u32[]{:S(2)}) collective-permute-start(bf16[3,72,512]{2,1,0:T(8,128)(2,1)S(1)} %pad_maximum_fusion), channel_id=1, source_target_pairs={{16,0},{20,4},{24,8},{28,12},{0,16},{4,20},{8,24},{12,28},{48,32},... | collective-permute-start | bytes 663560 | tf_op jit(solution)/shard_map/ppermute | solution.py:27
  19.9 38.8 %collective-permute-start.5 = (bf16[128,4608]{1,0:T(8,128)(2,1)}, bf16[128,4608]{1,0:T(8,128)(2,1)S(1)}, u32[]{:S(2)}, u32[]{:S(2)}) collective-permute-start(bf16[128,4608]{1,0:T(8,128)(2,1)} %param.8), channel_id=1, source_target_pairs={{0,2},{1,3},{2,0},{3,1},{4,6},{5,7},{6,4},{7,5},{8,10},{9,11},{10,... | collective-permute-start | bytes 3538952 | tf_op jit(solution)/shard_map/ppermute | solution.py:31
  27.1 26.3 %collective-permute-start.11 = (bf16[576,512]{1,0:T(8,128)(2,1)S(1)}, bf16[576,512]{1,0:T(8,128)(2,1)S(1)}, u32[]{:S(2)}, u32[]{:S(2)}) collective-permute-start(bf16[576,512]{1,0:T(8,128)(2,1)S(1)} %bitcast.112), channel_id=1, source_target_pairs={{32,0},{36,4},{40,8},{44,12},{48,16},{52,20},{56,24},{60,28},{64,3... | collective-permute-start | bytes 1769480 | tf_op jit(solution)/shard_map/ppermute | solution.py:27
  30.5 23.0 %collective-permute-start.12 = (bf16[576,512]{1,0:T(8,128)(2,1)S(1)}, bf16[576,512]{1,0:T(8,128)(2,1)S(1)}, u32[]{:S(2)}, u32[]{:S(2)}) collective-permute-start(bf16[576,512]{1,0:T(8,128)(2,1)S(1)} %bitcast.113), channel_id=1, source_target_pairs={{224,0},{228,4},{232,8},{236,12},{240,16},{244,20},{248,24},{252,2... | collective-permute-start | bytes 1769480 | tf_op jit(solution)/shard_map/ppermute | solution.py:27
  30.5 16.4 %collective-permute-start.10 = (bf16[2,72,512]{2,1,0:T(8,128)(2,1)S(1)}, bf16[2,72,512]{2,1,0:T(8,128)(2,1)S(1)}, u32[]{:S(2)}, u32[]{:S(2)}) collective-permute-start(bf16[2,72,512]{2,1,0:T(8,128)(2,1)S(1)} %collective-permute-done.7), channel_id=1, source_target_pairs={{224,0},{228,4},{232,8},{236,12},{240,16},{244,20},{248,24},{252,2... | collective-permute-start | bytes 442376 | tf_op jit(solution)/shard_map/ppermute | solution.py:27
  30.5 16.4 %collective-permute-start.9 = (bf16[2,72,512]{2,1,0:T(8,128)(2,1)S(1)}, bf16[2,72,512]{2,1,0:T(8,128)(2,1)S(1)}, u32[]{:S(2)}, u32[]{:S(2)}) collective-permute-start(bf16[2,72,512]{2,1,0:T(8,128)(2,1)S(1)} %collective-permute-done.6), channel_id=1, source_target_pairs={{32,0},{36,4},{40,8},{44,12},{48,16},{52,20},{56,24},{60,28},{64,3... | collective-permute-start | bytes 442376 | tf_op jit(solution)/shard_map/ppermute | solution.py:27
  46.8 5.1 %collective-permute-start.13 = (bf16[2,72,512]{2,1,0:T(8,128)(2,1)S(1)}, bf16[2,72,512]{2,1,0:T(8,128)(2,1)S(1)}, u32[]{:S(2)}, u32[]{:S(2)}) collective-permute-start(bf16[2,72,512]{2,1,0:T(8,128)(2,1)S(1)} %collective-permute-done.9), channel_id=1, source_target_pairs={{32,0},{36,4},{40,8},{44,12},{48,16},{52,20},{56,24},{60,28},{64,3... | collective-permute-start | bytes 442376 | tf_op jit(solution)/shard_map/ppermute | solution.py:27
  47.1 6.4 %collective-permute-start.14 = (bf16[2,72,512]{2,1,0:T(8,128)(2,1)S(1)}, bf16[2,72,512]{2,1,0:T(8,128)(2,1)S(1)}, u32[]{:S(2)}, u32[]{:S(2)}) collective-permute-start(bf16[2,72,512]{2,1,0:T(8,128)(2,1)S(1)} %collective-permute-done.10), channel_id=1, source_target_pairs={{224,0},{228,4},{232,8},{236,12},{240,16},{244,20},{248,24},{252,2... | collective-permute-start | bytes 442376 | tf_op jit(solution)/shard_map/ppermute | solution.py:27
  52.0 13.6 %collective-permute-start.21 = (f32[512,128]{1,0:T(8,128)S(1)}, f32[512,128]{1,0:T(8,128)S(1)}, u32[]{:S(2)}, u32[]{:S(2)}) collective-permute-start(f32[512,128]{1,0:T(8,128)S(1)} %fusion.41), channel_id=1, source_target_pairs={{0,1},{1,0},{2,3},{3,2},{4,5},{5,4},{6,7},{7,6},{8,9},{9,8},{10,11... | collective-permute-start | bytes 786440 | tf_op jit(solution)/shard_map/ppermute | solution.py:31
  53.5 5.1 %collective-permute-start.15 = (bf16[2,72,512]{2,1,0:T(8,128)(2,1)S(1)}, bf16[2,72,512]{2,1,0:T(8,128)(2,1)S(1)}, u32[]{:S(2)}, u32[]{:S(2)}) collective-permute-start(bf16[2,72,512]{2,1,0:T(8,128)(2,1)S(1)} %collective-permute-done.13), channel_id=1, source_target_pairs={{32,0},{36,4},{40,8},{44,12},{48,16},{52,20},{56,24},{60,28},{64,3... | collective-permute-start | bytes 442376 | tf_op jit(solution)/shard_map/ppermute | solution.py:27
  58.7 23.1 %collective-permute-start.20 = (bf16[128,4608]{1,0:T(8,128)(2,1)S(1)}, bf16[128,4608]{1,0:T(8,128)(2,1)S(1)}, u32[]{:S(2)}, u32[]{:S(2)}) collective-permute-start(bf16[128,4608]{1,0:T(8,128)(2,1)S(1)} %collective-permute-done.5), channel_id=1, source_target_pairs={{0,1},{1,0},{2,3},{3,2},{4,5},{5,4},{6,7},{7,6},{8,9},{9,8},{10,11... | collective-permute-start | bytes 3538952 | tf_op jit(solution)/shard_map/ppermute | solution.py:31
  61.2 15.7 %collective-permute-start.18 = (bf16[4,2,72,512]{3,2,1,0:T(8,128)(2,1)S(1)}, bf16[4,2,72,512]{3,2,1,0:T(8,128)(2,1)S(1)}, u32[]{:S(2)}, u32[]{:S(2)}) collective-permute-start(bf16[4,2,72,512]{3,2,1,0:T(8,128)(2,1)S(1)} %get-tuple-element.96), channel_id=1, source_target_pairs={{4,0},{8,4},{12,8},{0,12},{20,16},{24,20},{28,24},{16,28},{36,32},... | collective-permute-start | bytes 1769480 | tf_op jit(solution)/shard_map/ppermute | solution.py:27
  63.1 16.9 %collective-permute-start.19 = (bf16[4,2,72,512]{3,2,1,0:T(8,128)(2,1)S(1)}, bf16[4,2,72,512]{3,2,1,0:T(8,128)(2,1)S(1)}, u32[]{:S(2)}, u32[]{:S(2)}) collective-permute-start(bf16[4,2,72,512]{3,2,1,0:T(8,128)(2,1)S(1)} %get-tuple-element.96), channel_id=1, source_target_pairs={{12,0},{0,4},{4,8},{8,12},{28,16},{16,20},{20,24},{24,28},{44,32},... | collective-permute-start | bytes 1769480 | tf_op jit(solution)/shard_map/ppermute | solution.py:27
  63.2 16.8 %collective-permute-start.16 = (bf16[576,512]{1,0:T(8,128)(2,1)S(1)}, bf16[576,512]{1,0:T(8,128)(2,1)S(1)}, u32[]{:S(2)}, u32[]{:S(2)}) collective-permute-start(bf16[576,512]{1,0:T(8,128)(2,1)S(1)} %collective-permute-done.11), channel_id=1, source_target_pairs={{32,0},{36,4},{40,8},{44,12},{48,16},{52,20},{56,24},{60,28},{64,3... | collective-permute-start | bytes 1769480 | tf_op jit(solution)/shard_map/ppermute | solution.py:27
  65.6 16.2 %collective-permute-start.17 = (bf16[576,512]{1,0:T(8,128)(2,1)S(1)}, bf16[576,512]{1,0:T(8,128)(2,1)S(1)}, u32[]{:S(2)}, u32[]{:S(2)}) collective-permute-start(bf16[576,512]{1,0:T(8,128)(2,1)S(1)} %collective-permute-done.12), channel_id=1, source_target_pairs={{224,0},{228,4},{232,8},{236,12},{240,16},{244,20},{248,24},{252,2... | collective-permute-start | bytes 1769480 | tf_op jit(solution)/shard_map/ppermute | solution.py:27
  76.9 15.6 %collective-permute-start.24 = (bf16[4,2,72,512]{3,2,1,0:T(8,128)(2,1)S(1)}, bf16[4,2,72,512]{3,2,1,0:T(8,128)(2,1)S(1)}, u32[]{:S(2)}, u32[]{:S(2)}) collective-permute-start(bf16[4,2,72,512]{3,2,1,0:T(8,128)(2,1)S(1)} %get-tuple-element.100), channel_id=1, source_target_pairs={{4,0},{8,4},{12,8},{0,12},{20,16},{24,20},{28,24},{16,28},{36,32},... | collective-permute-start | bytes 1769480 | tf_op jit(solution)/shard_map/ppermute | solution.py:27
  80.0 25.4 %collective-permute-start.25 = (bf16[4,2,72,512]{3,2,1,0:T(8,128)(2,1)S(1)}, bf16[4,2,72,512]{3,2,1,0:T(8,128)(2,1)S(1)}, u32[]{:S(2)}, u32[]{:S(2)}) collective-permute-start(bf16[4,2,72,512]{3,2,1,0:T(8,128)(2,1)S(1)} %get-tuple-element.100), channel_id=1, source_target_pairs={{12,0},{0,4},{4,8},{8,12},{28,16},{16,20},{20,24},{24,28},{44,32},... | collective-permute-start | bytes 1769480 | tf_op jit(solution)/shard_map/ppermute | solution.py:27
  81.8 23.6 %collective-permute-start.27 = (f32[512,128]{1,0:T(8,128)S(1)}, f32[512,128]{1,0:T(8,128)S(1)}, u32[]{:S(2)}, u32[]{:S(2)}) collective-permute-start(f32[512,128]{1,0:T(8,128)S(1)} %add.236), channel_id=1, source_target_pairs={{0,2},{1,3},{2,0},{3,1},{4,6},{5,7},{6,4},{7,5},{8,10},{9,11},{10,... | collective-permute-start | bytes 786440 | tf_op jit(solution)/shard_map/ppermute | solution.py:31
  82.9 22.5 %collective-permute-start.22 = (bf16[576,512]{1,0:T(8,128)(2,1)S(1)}, bf16[576,512]{1,0:T(8,128)(2,1)S(1)}, u32[]{:S(2)}, u32[]{:S(2)}) collective-permute-start(bf16[576,512]{1,0:T(8,128)(2,1)S(1)} %collective-permute-done.16), channel_id=1, source_target_pairs={{32,0},{36,4},{40,8},{44,12},{48,16},{52,20},{56,24},{60,28},{64,3... | collective-permute-start | bytes 1769480 | tf_op jit(solution)/shard_map/ppermute | solution.py:27
  83.5 21.9 %collective-permute-start.23 = (bf16[576,512]{1,0:T(8,128)(2,1)S(1)}, bf16[576,512]{1,0:T(8,128)(2,1)S(1)}, u32[]{:S(2)}, u32[]{:S(2)}) collective-permute-start(bf16[576,512]{1,0:T(8,128)(2,1)S(1)} %collective-permute-done.17), channel_id=1, source_target_pairs={{224,0},{228,4},{232,8},{236,12},{240,16},{244,20},{248,24},{252,2... | collective-permute-start | bytes 1769480 | tf_op jit(solution)/shard_map/ppermute | solution.py:27
  92.5 15.3 %collective-permute-start.26 = (bf16[4,2,72,512]{3,2,1,0:T(8,128)(2,1)S(1)}, bf16[4,2,72,512]{3,2,1,0:T(8,128)(2,1)S(1)}, u32[]{:S(2)}, u32[]{:S(2)}) collective-permute-start(bf16[4,2,72,512]{3,2,1,0:T(8,128)(2,1)S(1)} %collective-permute-done.18), channel_id=1, source_target_pairs={{4,0},{8,4},{12,8},{0,12},{20,16},{24,20},{28,24},{16,28},{36,32},... | collective-permute-start | bytes 1769480 | tf_op jit(solution)/shard_map/ppermute | solution.py:27
  110.7 6.9 %collective-permute-start.29 = (bf16[288,512]{1,0:T(8,128)(2,1)S(1)}, bf16[288,512]{1,0:T(8,128)(2,1)S(1)}, u32[]{:S(2)}, u32[]{:S(2)}) collective-permute-start(bf16[288,512]{1,0:T(8,128)(2,1)S(1)} %slice.84), channel_id=1, source_target_pairs={{32,0},{36,4},{40,8},{44,12},{48,16},{52,20},{56,24},{60,28},{64,3... | collective-permute-start | bytes 884744 | tf_op jit(solution)/shard_map/ppermute | solution.py:27
  113.1 7.9 %collective-permute-start.30 = (bf16[288,512]{1,0:T(8,128)(2,1)S(1)}, bf16[288,512]{1,0:T(8,128)(2,1)S(1)}, u32[]{:S(2)}, u32[]{:S(2)}) collective-permute-start(bf16[288,512]{1,0:T(8,128)(2,1)S(1)} %slice.85), channel_id=1, source_target_pairs={{224,0},{228,4},{232,8},{236,12},{240,16},{244,20},{248,24},{252,2... | collective-permute-start | bytes 884744 | tf_op jit(solution)/shard_map/ppermute | solution.py:27
  113.3 14.9 %collective-permute-start.28 = (bf16[4,2,72,512]{3,2,1,0:T(8,128)(2,1)S(1)}, bf16[4,2,72,512]{3,2,1,0:T(8,128)(2,1)S(1)}, u32[]{:S(2)}, u32[]{:S(2)}) collective-permute-start(bf16[4,2,72,512]{3,2,1,0:T(8,128)(2,1)S(1)} %collective-permute-done.25), channel_id=1, source_target_pairs={{12,0},{0,4},{4,8},{8,12},{28,16},{16,20},{20,24},{24,28},{44,32},... | collective-permute-start | bytes 1769480 | tf_op jit(solution)/shard_map/ppermute | solution.py:27
  (3 other events, 35.7 us)

commit v4 on v3

v4 whole, which is shorter than its diff:
```python
import jax
import jax.numpy as jnp
from jax import lax
from jax.experimental import pallas as pl
from jax.experimental.pallas import tpu as pltpu
from jax.sharding import PartitionSpec as P

ADAPTER_RANK = 16
TEN_DEV = 8
ADAPTER_SCALE = 2.0
NZ, NX, NY = 8, 2, 4


def contract(left, right, left_dim, right_dim):
    return lax.dot_general(
        left, right, (((left_dim,), (right_dim,)), ((), ())), preferred_element_type=jnp.float32
    )


def fetch(x, dz=0, dx=0, dy=0):
    pairs = []
    for z in range(NZ):
        for a in range(NX):
            for y in range(NY):
                source = (((z + dz) % NZ) * NX + (a + dx) % NX) * NY + (y + dy) % NY
                pairs.append((source, (z * NX + a) * NY + y))
    return lax.ppermute(x, "dp", pairs)


def swap_tensor(x, mask):
    return lax.ppermute(x, "tensor", [(t, t ^ mask) for t in range(4)])


def together(*values):
    return lax.optimization_barrier(values)


def split_kernel(start_ref, g_ref, z_ref):
    width = z_ref.shape[2]
    for block in range(NZ):
        slot = lax.rem(block - start_ref[0] + NZ, NZ)
        z_ref[slot] = g_ref[:, block * width : (block + 1) * width]


def split_columns(gradients, start):
    rows, depth = gradients.shape
    step = rows // 4
    width = depth // NZ
    return pl.pallas_call(
        split_kernel,
        grid_spec=pltpu.PrefetchScalarGridSpec(
            num_scalar_prefetch=1,
            grid=(4,),
            in_specs=[pl.BlockSpec((step, depth), lambda i, s: (i, 0))],
            out_specs=pl.BlockSpec((NZ, step, width), lambda i, s: (0, i, 0)),
        ),
        out_shape=jax.ShapeDtypeStruct((NZ, rows, width), gradients.dtype),
        compiler_params=pltpu.CompilerParams(vmem_limit_bytes=32 * 1024 * 1024),
    )(start, gradients)


def last_kernel(z_ref, w_ref, total_ref, live_ref, b_ref, out_ref):
    width = w_ref.shape[2]
    count = w_ref.shape[0]
    total = total_ref[...]
    for i in range(count):
        total += contract(z_ref[NZ - count + i], w_ref[i], 1, 0)
    out_ref[:, :width] = jnp.where(live_ref[...] > 0, total, 0.0).astype(out_ref.dtype)
    out_ref[:, width:] = b_ref[...]


def down_kernel(head_ref, back_ref, out_ref):
    out_ref[...] = ADAPTER_SCALE * contract(head_ref[...], back_ref[...], 0, 0)


def in_vmem(kernel, shape, dtype, *arrays):
    return pl.pallas_call(
        kernel,
        in_specs=[pl.BlockSpec(memory_space=pltpu.VMEM)] * len(arrays),
        out_specs=pl.BlockSpec(memory_space=pltpu.VMEM),
        out_shape=jax.ShapeDtypeStruct(shape, dtype),
        compiler_params=pltpu.CompilerParams(vmem_limit_bytes=40 * 1024 * 1024),
    )(*arrays)


def body(
    head_outputs,
    output_gradient,
    frozen_weight,
    adapter_down_factors,
    adapter_up_factors,
    tenant_index,
    tenant_group_counts,
):
    row_count = head_outputs.shape[0]
    part_rows, depth = output_gradient.shape
    shard_rows, feature_width = frozen_weight.shape
    a_width = feature_width * 5 // 8
    group = lax.axis_index("dp").astype(jnp.int32)
    z, xl, y = group // (NX * NY), (group // NY) % NX, group % NY
    tensor = lax.axis_index("tensor").astype(jnp.int32)
    zero = jnp.int32(0)

    own_a, own_b = frozen_weight[:, :a_width], frozen_weight[:, a_width:]
    other = fetch(frozen_weight, dx=1)
    y_b = [fetch(own_b, dy=dy) for dy in (1, 2, 3)]
    from_core = swap_tensor(output_gradient, 1)
    other, from_core, own_rows, head_later, index_later, *y_b = together(
        other, from_core, output_gradient, head_outputs, tenant_index, *y_b
    )

    far_a, far_b = other[:, :a_width], other[:, a_width:]
    pair_a = jnp.where(xl == 0, jnp.stack([own_a, far_a]), jnp.stack([far_a, own_a]))
    a_p1, a_m1 = fetch(pair_a, dz=1), fetch(pair_a, dz=-1)
    y_b = jnp.stack(y_b)
    x_b = fetch(y_b, dx=1)
    y_b, pair_a, gradient_later, head_later = together(y_b, pair_a, own_rows, head_later)
    from_chip = swap_tensor(gradient_later, 2)
    partial = jnp.dot(head_later, adapter_down_factors, preferred_element_type=jnp.float32)
    core_partial = swap_tensor(partial, 1)

    a_p1, a_m1, x_b, pair_a, partial, core_partial = together(
        a_p1, a_m1, x_b, pair_a, partial, core_partial
    )
    a_p2, a_m2 = fetch(a_p1, dz=1), fetch(a_m1, dz=-1)
    a_p4 = fetch(pair_a, dz=4)
    b_own = jnp.broadcast_to(
        jnp.where(xl == 0, jnp.stack([own_b, far_b]), jnp.stack([far_b, own_b]))[:, None],
        (NX, NY, shard_rows, own_b.shape[1]),
    )
    for i, dy in enumerate((1, 2, 3)):
        for x, chunk in ((xl, y_b[i]), (1 - xl, x_b[i])):
            b_own = lax.dynamic_update_slice(
                b_own, chunk[None, None], (x, (y + dy) % NY, zero, zero)
            )
    b_own = b_own.reshape(NX * NY * shard_rows, -1)

    a_p2, a_m2, b_own = together(a_p2, a_m2, b_own)
    a_p3, a_m3 = fetch(a_p2, dz=1), fetch(a_m2, dz=-1)
    low = jnp.stack([a_m1, pair_a, a_p1, a_p2])
    low_p, low_m = fetch(low, dy=1), fetch(low, dy=-1)

    a_p3, a_m3, a_p4, b_own = together(a_p3, a_m3, a_p4, b_own)
    high = jnp.stack([a_p3, a_p4, a_m3, a_m2])
    b_p1, b_m1 = fetch(b_own, dz=1), fetch(b_own, dz=-1)

    chip_sum = partial + core_partial
    far_sum = swap_tensor(chip_sum, 2)
    b_p1, b_m1, low_p, low_m, high, from_chip, own_rows, far_sum = together(
        b_p1, b_m1, low_p, low_m, high, from_chip, own_rows, far_sum
    )
    b_p2, b_m2 = fetch(b_p1, dz=1), fetch(b_m1, dz=-1)
    low_o, high_m = fetch(low_p, dy=1), fetch(high, dy=-1)

    from_both = swap_tensor(from_chip, 1)
    gradients = jnp.zeros((row_count, depth), output_gradient.dtype)
    for block, mask in ((own_rows, 0), (from_core, 1), (from_chip, 2), (from_both, 3)):
        gradients = lax.dynamic_update_slice_in_dim(
            gradients, block, (tensor ^ mask) * part_rows, 0
        )

    def placed(array, chunk, dy):
        return lax.dynamic_update_slice_in_dim(array, chunk[:, :, None], (y + dy) % NY, 2)

    def spread(chunk):
        return jnp.broadcast_to(chunk[:, :, None], (chunk.shape[0], NX, NY) + chunk.shape[2:])

    low_all = placed(placed(spread(low), low_p, 1), low_m, 3)

    b_p2, b_m2, gradients = together(b_p2, b_m2, gradients)
    b_p3, b_m3 = fetch(b_p2, dz=1), fetch(b_m2, dz=-1)
    low_o, high_m, high, low_all, b_p2 = together(low_o, high_m, high, low_all, b_p2)
    high_p, high_o = fetch(high, dy=1), fetch(high_m, dy=-1)
    by_z = split_columns(gradients, ((z + NZ - 1) % NZ).reshape(1))

    position = jnp.arange(row_count, dtype=jnp.int32)
    active_rows = position < tenant_group_counts[0]
    slot_lookup = jnp.arange(adapter_down_factors.shape[1], dtype=jnp.int32) // ADAPTER_RANK
    select_rows = (
        active_rows[:, None] & (slot_lookup[None, :] == (index_later % TEN_DEV)[:, None])
    ).astype(jnp.float32)
    adapter_backward = (contract(gradients, adapter_up_factors, 1, 1) * select_rows).astype(
        jnp.bfloat16
    )
    down_factor_gradient = in_vmem(
        down_kernel, adapter_down_factors.shape, jnp.float32, head_outputs, adapter_backward
    )
    live = active_rows.astype(jnp.float32)[:, None]

    b_p3, b_m3, by_z, adapter_backward, down_factor_gradient = together(
        b_p3, b_m3, by_z, adapter_backward, down_factor_gradient
    )
    cut = b_own.shape[0] // 2 // 16 * 16
    b_p4, b_m4 = fetch(b_p3[:cut], dz=1), fetch(b_m3[cut:], dz=-1)
    adapter_input = ((chip_sum + far_sum) * select_rows).astype(jnp.bfloat16)
    (adapter_input,) = together(adapter_input)
    up_factor_gradient = ADAPTER_SCALE * contract(adapter_input, gradients, 0, 0)

    def product(total, terms):
        for slot, chunk in terms:
            total = total + contract(by_z[slot], chunk.reshape(by_z.shape[2], -1), 1, 0)
        return total

    b_p4, b_m4, up_factor_gradient, low_all, high_m = together(
        b_p4, b_m4, up_factor_gradient, low_all, high_m
    )
    b_total = product(
        ADAPTER_SCALE * contract(adapter_backward, adapter_down_factors[a_width:], 1, 1),
        [(1, b_own), (0, b_m1), (2, b_p1), (7, b_m2), (3, b_p2), (6, b_m3), (4, b_p3)]
        + [(5, jnp.concatenate([b_p4, b_m4], 0))],
    )
    b_out = jnp.where(active_rows[:, None], b_total, 0.0).astype(jnp.bfloat16)
    low_all = placed(low_all, low_o, 2)
    a_total = product(
        ADAPTER_SCALE * contract(adapter_backward, adapter_down_factors[:a_width], 1, 1),
        [(i, low_all[i]) for i in range(4)],
    )
    high_all = placed(spread(high), high_m, 3)

    high_p, high_o, high_all, b_out, a_total = together(high_p, high_o, high_all, b_out, a_total)
    high_all = placed(placed(high_all, high_p, 1), high_o, 2)
    head_feature_gradient = in_vmem(
        last_kernel,
        head_outputs.shape,
        jnp.bfloat16,
        by_z,
        high_all.reshape(NZ // 2, by_z.shape[2], a_width),
        a_total,
        live,
        b_out,
    )
    return (head_feature_gradient, down_factor_gradient, up_factor_gradient)


def solution(mesh):
    in_specs = (
        P("dp", "tensor"),
        P(("dp", "tensor"), None),
        P("dp", "tensor"),
        P("tensor", "dp"),
        P("dp", None),
        P("dp"),
        P("dp"),
    )
    out_specs = (P("dp", "tensor"), P("tensor", "dp"), P("dp", None))
    return jax.shard_map(body, mesh=mesh, in_specs=in_specs, out_specs=out_specs, check_vma=False)
```

time: 136 us -> 119 us (0.88)
  waiting for transfers between devices: 55.9 us -> 39.9 us
  starting transfers between devices: 39.7 us -> 44.7 us
  Pallas kernels: 11.2 us -> 6.34 us
  other arithmetic: 1.11 us -> 2.49 us
    ppermute x26, waiting for transfers between devices: 55.9 us -> 37.1 us  [fetch(): return lax.ppermute(x, 'dp', pairs)]
    ppermute x26, starting transfers between devices: 37 us -> 42.4 us  [fetch(): return lax.ppermute(x, 'dp', pairs)]
    dynamic_update_slice x15 -> x5, local copies, waits for them, and re-layouts: 0.53 us -> 4.07 us  [placed(): lax.dynamic_update_slice_in_dim(array, chunk[:, :, None], (y + dy) % NY, 2)]
    ppermute x5, waiting for transfers between devices: 0.01 us -> 2.81 us  [swap_tensor(): return lax.ppermute(x, 'tensor', [(t, t ^ mask) for t in range(4)])]
    dynamic_update_slice x4, local copies, waits for them, and re-layouts: 5.67 us -> 3.04 us  [body(): lax.dynamic_update_slice_in_dim(gradients, block, (tensor ^ mask) * part_...]
    pallas_call x2, Pallas kernels: 7.36 us -> 4.76 us  [in_vmem(): pl.pallas_call(kernel, in_specs=[pl.BlockSpec(memory_space=pltpu.VMEM)] *...]
    pallas_call x1, Pallas kernels: 3.89 us -> 1.58 us  [split_columns(): pl.pallas_call(split_kernel, grid_spec=pltpu.PrefetchScalarGridSpec(num_s...]
    broadcast_in_dim x1, local copies, waits for them, and re-layouts: 2.44 us -> 0.31 us  [body(): gradients = jnp.zeros((row_count, depth), output_gradient.dtype)]
  transfers between devices with their start and end apart: 31 -> 31, of which waited for: 13 -> 15; matrix products, arithmetic and copies ran while one was open for 17% -> 21% of each run, Pallas kernels for 4% -> 2%
where the time goes in v4:
time: 119 us
  starting transfers between devices  44.7 us (38%)
  waiting for transfers between devices  39.9 us (34%)
  matrix products  13.2 us (11%)
  local copies, waits for them, and re-layouts  10.2 us (9%)
  Pallas kernels  6.34 us (5%)
  other arithmetic  2.49 us (2%)
  between operations  1.73 us (1%)
    ppermute x26, starting transfers between devices, fetch(): return lax.ppermute(x, 'dp', pairs)  42.4 us
    ppermute x26, waiting for transfers between devices, fetch(): return lax.ppermute(x, 'dp', pairs)  37.1 us
    dot_general x16, matrix products, contract(): lax.dot_general(left, right, (((left_dim,), (right_dim,)), ((), ())), pre...  11.5 us
    pallas_call x2, Pallas kernels, in_vmem(): pl.pallas_call(kernel, in_specs=[pl.BlockSpec(memory_space=pltpu.VMEM)] *...  4.76 us
    dynamic_update_slice x5, local copies, waits for them, and re-layouts, placed(): lax.dynamic_update_slice_in_dim(array, chunk[:, :, None], (y + dy) % NY, 2)  4.07 us
    dynamic_update_slice x4, local copies, waits for them, and re-layouts, body(): lax.dynamic_update_slice_in_dim(gradients, block, (tensor ^ mask) * part_...  3.04 us
    ppermute x5, waiting for transfers between devices, swap_tensor(): return lax.ppermute(x, 'tensor', [(t, t ^ mask) for t in range(4)])  2.81 us
  transfers between devices with their start and end apart: 31, of which 15 were waited for; matrix products, arithmetic and copies ran while one was open for 21% of the time, Pallas kernels for 2%

profile of v4, /device:TPU:6, one launch (start us, length us, event | category | flops | bytes accessed | tf_op | source)
XLA Modules:
  0.0 118.6 jit_solution(58605562073557248)
XLA Ops:
  1.7 1.7 %collective-permute-start.4 = (bf16[72,384]{1,0:T(8,128)(2,1)S(1)}, bf16[72,384]{1,0:T(8,128)(2,1)S(1)}, u32[]{:S(2)}, u32[]{:S(2)}) collective-permute-start(bf16[72,384]{1,0:T(8,128)(2,1)S(1)} %get-tuple-element.120), channel_id=1, source_target_pairs={{12,0},{0,4},{4,8},{8,12},{28,16},{16,20},{20,24},{24,28},{44,32},... | collective-permute-start | bytes 165896 | tf_op jit(solution)/shard_map/ppermute | solution.py:27
  3.3 2.9 %collective-permute-start.3 = (bf16[72,384]{1,0:T(8,128)(2,1)S(1)}, bf16[72,384]{1,0:T(8,128)(2,1)S(1)}, u32[]{:S(2)}, u32[]{:S(2)}) collective-permute-start(bf16[72,384]{1,0:T(8,128)(2,1)S(1)} %get-tuple-element.120), channel_id=1, source_target_pairs={{8,0},{12,4},{0,8},{4,12},{24,16},{28,20},{16,24},{20,28},{40,32},... | collective-permute-start | bytes 165896 | tf_op jit(solution)/shard_map/ppermute | solution.py:27
  10.4 2.7 %collective-permute-done = bf16[72,1024]{1,0:T(8,128)(2,1)S(1)} collective-permute-done((bf16[72,1024]{1,0:T(8,128)(2,1)}, bf16[72,1024]{1,0:T(8,128)(2,1)S(1)}, u32[]{:S(2)}, u32[]{:S(2)}) %collective-permute-start) | collective-permute-done | bytes 147488 | tf_op jit(solution)/shard_map/ppermute | solution.py:27
  13.2 2.0 %collective-permute-start.6 = (bf16[2,72,640]{2,1,0:T(8,128)(2,1)S(1)}, bf16[2,72,640]{2,1,0:T(8,128)(2,1)S(1)}, u32[]{:S(2)}, u32[]{:S(2)}) collective-permute-start(bf16[2,72,640]{2,1,0:T(8,128)(2,1)S(1)} %maximum_select_fusion), channel_id=1, source_target_pairs={{224,0},{228,4},{232,8},{236,12},{240,16},{244,20},{248,24},{252,2... | collective-permute-start | bytes 552968 | tf_op jit(solution)/shard_map/ppermute | solution.py:27
  15.2 4.0 %collective-permute-start.5 = (bf16[2,72,640]{2,1,0:T(8,128)(2,1)S(1)}, bf16[2,72,640]{2,1,0:T(8,128)(2,1)S(1)}, u32[]{:S(2)}, u32[]{:S(2)}) collective-permute-start(bf16[2,72,640]{2,1,0:T(8,128)(2,1)S(1)} %maximum_select_fusion), channel_id=1, source_target_pairs={{32,0},{36,4},{40,8},{44,12},{48,16},{52,20},{56,24},{60,28},{64,3... | collective-permute-start | bytes 552968 | tf_op jit(solution)/shard_map/ppermute | solution.py:27
  20.2 1.7 %fusion.54 = f32[512,128]{1,0:T(8,128)S(1)} fusion(bf16[512,1024]{1,0:T(8,128)(2,1)} %head_ref.1, bf16[1024,128]{1,0:T(8,128)(2,1)} %param.10), kind=kOutput, calls=%fused_computation.97 | convolution fusion | flops 134217728 | bytes 1572864 | tf_op jit(solution)/shard_map/dot_general | solution.py:119
  23.3 1.4 %collective-permute-done.7 = bf16[3,72,384]{2,1,0:T(8,128)(2,1)S(1)} collective-permute-done((bf16[3,72,384]{2,1,0:T(8,128)(2,1)S(1)}, bf16[3,72,384]{2,1,0:T(8,128)(2,1)S(1)}, u32[]{:S(2)}, u32[]{:S(2)}) %collective-permute-start.7) | collective-permute-done | bytes 165920 | tf_op jit(solution)/shard_map/ppermute | solution.py:27
  24.7 2.0 %collective-permute-start.9 = (bf16[2,72,640]{2,1,0:T(8,128)(2,1)S(1)}, bf16[2,72,640]{2,1,0:T(8,128)(2,1)}, u32[]{:S(2)}, u32[]{:S(2)}) collective-permute-start(bf16[2,72,640]{2,1,0:T(8,128)(2,1)S(1)} %collective-permute-done.5), channel_id=1, source_target_pairs={{32,0},{36,4},{40,8},{44,12},{48,16},{52,20},{56,24},{60,28},{64,3... | collective-permute-start | bytes 552968 | tf_op jit(solution)/shard_map/ppermute | solution.py:27
  26.8 4.5 %collective-permute-start.13 = (bf16[2,72,640]{2,1,0:T(8,128)(2,1)S(1)}, bf16[2,72,640]{2,1,0:T(8,128)(2,1)S(1)}, u32[]{:S(2)}, u32[]{:S(2)}) collective-permute-start(bf16[2,72,640]{2,1,0:T(8,128)(2,1)S(1)} %maximum_select_fusion), channel_id=1, source_target_pairs={{128,0},{132,4},{136,8},{140,12},{144,16},{148,20},{152,24},{156,2... | collective-permute-start | bytes 552968 | tf_op jit(solution)/shard_map/ppermute | solution.py:27
  31.4 4.8 %collective-permute-done.9 = bf16[2,72,640]{2,1,0:T(8,128)(2,1)} collective-permute-done((bf16[2,72,640]{2,1,0:T(8,128)(2,1)S(1)}, bf16[2,72,640]{2,1,0:T(8,128)(2,1)}, u32[]{:S(2)}, u32[]{:S(2)}) %collective-permute-start.9) | collective-permute-done | bytes 184352 | tf_op jit(solution)/shard_map/ppermute | solution.py:27
  36.2 3.0 %collective-permute-done.10 = bf16[2,72,640]{2,1,0:T(8,128)(2,1)S(1)} collective-permute-done((bf16[2,72,640]{2,1,0:T(8,128)(2,1)S(1)}, bf16[2,72,640]{2,1,0:T(8,128)(2,1)S(1)}, u32[]{:S(2)}, u32[]{:S(2)}) %collective-permute-start.10) | collective-permute-done | bytes 184352 | tf_op jit(solution)/shard_map/ppermute | solution.py:27
  39.3 1.5 %collective-permute-start.11 = (bf16[2,72,640]{2,1,0:T(8,128)(2,1)}, bf16[2,72,640]{2,1,0:T(8,128)(2,1)}, u32[]{:S(2)}, u32[]{:S(2)}) collective-permute-start(bf16[2,72,640]{2,1,0:T(8,128)(2,1)} %collective-permute-done.9), channel_id=1, source_target_pairs={{32,0},{36,4},{40,8},{44,12},{48,16},{52,20},{56,24},{60,28},{64,3... | collective-permute-start | bytes 552968 | tf_op jit(solution)/shard_map/ppermute | solution.py:27
  42.6 2.6 %collective-permute-start.16 = (bf16[4,2,72,640]{3,2,1,0:T(8,128)(2,1)S(1)}, bf16[4,2,72,640]{3,2,1,0:T(8,128)(2,1)}, u32[]{:S(2)}, u32[]{:S(2)}) collective-permute-start(bf16[4,2,72,640]{3,2,1,0:T(8,128)(2,1)S(1)} %pad_maximum_fusion), channel_id=1, source_target_pairs={{4,0},{8,4},{12,8},{0,12},{20,16},{24,20},{28,24},{16,28},{36,32},... | collective-permute-start | bytes 2211848 | tf_op jit(solution)/shard_map/ppermute | solution.py:27
  46.7 1.5 %collective-permute-start.12 = (bf16[2,72,640]{2,1,0:T(8,128)(2,1)S(1)}, bf16[2,72,640]{2,1,0:T(8,128)(2,1)S(1)}, u32[]{:S(2)}, u32[]{:S(2)}) collective-permute-start(bf16[2,72,640]{2,1,0:T(8,128)(2,1)S(1)} %collective-permute-done.10), channel_id=1, source_target_pairs={{224,0},{228,4},{232,8},{236,12},{240,16},{244,20},{248,24},{252,2... | collective-permute-start | bytes 552968 | tf_op jit(solution)/shard_map/ppermute | solution.py:27
  48.2 5.3 %collective-permute-done.12 = bf16[2,72,640]{2,1,0:T(8,128)(2,1)S(1)} collective-permute-done((bf16[2,72,640]{2,1,0:T(8,128)(2,1)S(1)}, bf16[2,72,640]{2,1,0:T(8,128)(2,1)S(1)}, u32[]{:S(2)}, u32[]{:S(2)}) %collective-permute-start.12) | collective-permute-done | bytes 184352 | tf_op jit(solution)/shard_map/ppermute | solution.py:27
  54.9 2.8 %collective-permute-done.19 = f32[512,128]{1,0:T(8,128)S(1)} collective-permute-done((f32[512,128]{1,0:T(8,128)S(1)}, f32[512,128]{1,0:T(8,128)S(1)}, u32[]{:S(2)}, u32[]{:S(2)}) %collective-permute-start.19) | collective-permute-done | bytes 262176 | tf_op jit(solution)/shard_map/ppermute | solution.py:31
  57.7 1.9 %collective-permute-start.14 = (bf16[576,384]{1,0:T(8,128)(2,1)S(1)}, bf16[576,384]{1,0:T(8,128)(2,1)S(1)}, u32[]{:S(2)}, u32[]{:S(2)}) collective-permute-start(bf16[576,384]{1,0:T(8,128)(2,1)S(1)} %bitcast.120), channel_id=1, source_target_pairs={{32,0},{36,4},{40,8},{44,12},{48,16},{52,20},{56,24},{60,28},{64,3... | collective-permute-start | bytes 1327112 | tf_op jit(solution)/shard_map/ppermute | solution.py:27
  60.7 2.4 %collective-permute-done.15 = bf16[576,384]{1,0:T(8,128)(2,1)S(1)} collective-permute-done((bf16[576,384]{1,0:T(8,128)(2,1)S(1)}, bf16[576,384]{1,0:T(8,128)(2,1)S(1)}, u32[]{:S(2)}, u32[]{:S(2)}) %collective-permute-start.15) | collective-permute-done | bytes 442400 | tf_op jit(solution)/shard_map/ppermute | solution.py:27
  63.1 6.3 %collective-permute-done.14 = bf16[576,384]{1,0:T(8,128)(2,1)S(1)} collective-permute-done((bf16[576,384]{1,0:T(8,128)(2,1)S(1)}, bf16[576,384]{1,0:T(8,128)(2,1)S(1)}, u32[]{:S(2)}, u32[]{:S(2)}) %collective-permute-start.14) | collective-permute-done | bytes 442400 | tf_op jit(solution)/shard_map/ppermute | solution.py:27
  69.6 3.2 %collective-permute-start.20 = (bf16[576,384]{1,0:T(8,128)(2,1)S(1)}, bf16[576,384]{1,0:T(8,128)(2,1)S(1)}, u32[]{:S(2)}, u32[]{:S(2)}) collective-permute-start(bf16[576,384]{1,0:T(8,128)(2,1)S(1)} %collective-permute-done.14), channel_id=1, source_target_pairs={{32,0},{36,4},{40,8},{44,12},{48,16},{52,20},{56,24},{60,28},{64,3... | collective-permute-start | bytes 1327112 | tf_op jit(solution)/shard_map/ppermute | solution.py:27
  73.1 1.7 %collective-permute-start.26 = (bf16[4,2,72,640]{3,2,1,0:T(8,128)(2,1)S(1)}, bf16[4,2,72,640]{3,2,1,0:T(8,128)(2,1)}, u32[]{:S(2)}, u32[]{:S(2)}) collective-permute-start(bf16[4,2,72,640]{3,2,1,0:T(8,128)(2,1)S(1)} %pad_maximum_fusion.1), channel_id=1, source_target_pairs={{12,0},{0,4},{4,8},{8,12},{28,16},{16,20},{20,24},{24,28},{44,32},... | collective-permute-start | bytes 2211848 | tf_op jit(solution)/shard_map/ppermute | solution.py:27
  77.9 1.4 %constant_dynamic-update-slice_fusion.3 = bf16[512,4608]{1,0:T(8,128)(2,1)S(1)} fusion(bf16[512,4608]{1,0:T(8,128)(2,1)S(1)} %broadcast_in_dim.57, bf16[128,4608]{1,0:T(8,128)(2,1)} %param.8, s32[]{:T(128)S(6)} %select_n.146), kind=kLoop, calls=%fused_computation.84 | loop fusion | bytes 2359300 | tf_op jit(solution)/shard_map/dynamic_update_slice | solution.py:158
  79.5 1.4 %constant_dynamic-update-slice_fusion.1 = bf16[512,4608]{1,0:T(8,128)(2,1)S(1)} fusion(bf16[512,4608]{1,0:T(8,128)(2,1)S(1)} %constant_dynamic-update-slice_fusion.2, bf16[128,4608]{1,0:T(8,128)(2,1)} %collective-permute-done.18, s32[]{:T(128)S(6)} %select_n.148), kind=kLoop, calls=%fused_computation.82 | loop fusion | bytes 2359300 | tf_op jit(solution)/shard_map/dynamic_update_slice | solution.py:158
  81.2 3.4 %collective-permute-done.21 = bf16[576,384]{1,0:T(8,128)(2,1)S(1)} collective-permute-done((bf16[576,384]{1,0:T(8,128)(2,1)S(1)}, bf16[576,384]{1,0:T(8,128)(2,1)S(1)}, u32[]{:S(2)}, u32[]{:S(2)}) %collective-permute-start.21) | collective-permute-done | bytes 442400 | tf_op jit(solution)/shard_map/ppermute | solution.py:27
  84.9 1.7 %collective-permute-start.24 = (bf16[576,384]{1,0:T(8,128)(2,1)S(1)}, bf16[576,384]{1,0:T(8,128)(2,1)S(1)}, u32[]{:S(2)}, u32[]{:S(2)}) collective-permute-start(bf16[576,384]{1,0:T(8,128)(2,1)S(1)} %collective-permute-done.21), channel_id=1, source_target_pairs={{224,0},{228,4},{232,8},{236,12},{240,16},{244,20},{248,24},{252,2... | collective-permute-start | bytes 1327112 | tf_op jit(solution)/shard_map/ppermute | solution.py:27
  88.0 1.9 %collective-permute-done.25 = bf16[4,2,72,640]{3,2,1,0:T(8,128)(2,1)S(1)} collective-permute-done((bf16[4,2,72,640]{3,2,1,0:T(8,128)(2,1)}, bf16[4,2,72,640]{3,2,1,0:T(8,128)(2,1)S(1)}, u32[]{:S(2)}, u32[]{:S(2)}) %collective-permute-start.25) | collective-permute-done | bytes 737312 | tf_op jit(solution)/shard_map/ppermute | solution.py:27
  92.7 1.6 %collective-permute-start.28 = (bf16[4,2,72,640]{3,2,1,0:T(8,128)(2,1)}, bf16[4,2,72,640]{3,2,1,0:T(8,128)(2,1)S(1)}, u32[]{:S(2)}, u32[]{:S(2)}) collective-permute-start(bf16[4,2,72,640]{3,2,1,0:T(8,128)(2,1)} %collective-permute-done.26), channel_id=1, source_target_pairs={{12,0},{0,4},{4,8},{8,12},{28,16},{16,20},{20,24},{24,28},{44,32},... | collective-permute-start | bytes 2211848 | tf_op jit(solution)/shard_map/ppermute | solution.py:27
  94.4 1.6 %shard_map.94.z_ref = bf16[8,512,576]{2,1,0:T(8,128)(2,1)S(1)} custom-call(s32[1]{0:T(128)} %bitcast.22.start_ref, bf16[512,4608]{1,0:T(8,128)(2,1)S(1)} %constant_dynamic-update-slice_fusion.g_ref), custom_call_target="tpu_custom_call" | custom-call | tf_op jit(solution)/shard_map/pallas_call | solution.py:49
  96.0 2.2 %convolution_multiply_fusion = f32[128,4608]{1,0:T(8,128)} fusion(bf16[512,128]{1,0:T(8,128)(2,1)S(1)} %select_convert_fusion, bf16[512,4608]{1,0:T(8,128)(2,1)S(1)} %constant_dynamic-update-slice_fusion.g_ref), kind=kOutput, calls=%fused_computation | convolution fusion | flops 604569600 | bytes 7208960 | tf_op jit(solution)/shard_map/dot_general | solution.py:15
  101.5 3.2 %collective-permute-start.29 = (bf16[288,384]{1,0:T(8,128)(2,1)S(1)}, bf16[288,384]{1,0:T(8,128)(2,1)S(1)}, u32[]{:S(2)}, u32[]{:S(2)}) collective-permute-start(bf16[288,384]{1,0:T(8,128)(2,1)S(1)} %slice.92), channel_id=1, source_target_pairs={{32,0},{36,4},{40,8},{44,12},{48,16},{52,20},{56,24},{60,28},{64,3... | collective-permute-start | bytes 663560 | tf_op jit(solution)/shard_map/ppermute | solution.py:27
  105.2 3.4 %collective-permute-done.30 = bf16[288,384]{1,0:T(8,128)(2,1)S(1)} collective-permute-done((bf16[288,384]{1,0:T(8,128)(2,1)S(1)}, bf16[288,384]{1,0:T(8,128)(2,1)S(1)}, u32[]{:S(2)}, u32[]{:S(2)}) %collective-permute-start.30) | collective-permute-done | bytes 221216 | tf_op jit(solution)/shard_map/ppermute | solution.py:27
  115.2 3.5 %shard_map.96 = bf16[512,1024]{1,0:T(8,128)(2,1)} custom-call(bf16[8,512,576]{2,1,0:T(8,128)(2,1)S(1)} %shard_map.94.z_ref, bf16[4,576,640]{2,1,0:T(8,128)(2,1)S(1)} %bitcast.114, f32[512,640]{1,0:T(8,128)S(1)} %convolution_add_fusion.total_ref, f32[512,1]{1,0:T(8,128)S(1)} %fusion.48.live_ref, bf16[512,384]{1,0:T(8,128)(2,1)S(1)} %fusion.10.b_ref), custom_call_target="tpu_custom_call" | custom-call | tf_op jit(solution)/shard_map/pallas_call | solution.py:77
  (99 shorter events, 31.5 us)
Async XLA Ops:
  0.6 86.0 %copy-start = (bf16[128,4608]{1,0:T(8,128)(2,1)S(1)}, bf16[128,4608]{1,0:T(8,128)(2,1)}, u32[]{:S(2)}) copy-start(bf16[128,4608]{1,0:T(8,128)(2,1)} %param.11) | copy-start | bytes 3538948
  0.6 12.5 %collective-permute-start.1 = (bf16[128,4608]{1,0:T(8,128)(2,1)}, bf16[128,4608]{1,0:T(8,128)(2,1)S(1)}, u32[]{:S(2)}, u32[]{:S(2)}) collective-permute-start(bf16[128,4608]{1,0:T(8,128)(2,1)} %param.8), channel_id=1, source_target_pairs={{0,1},{1,0},{2,3},{3,2},{4,5},{5,4},{6,7},{7,6},{8,9},{9,8},{10,11... | collective-permute-start | bytes 3538952 | tf_op jit(solution)/shard_map/ppermute | solution.py:31
  1.7 7.7 %collective-permute-start.4 = (bf16[72,384]{1,0:T(8,128)(2,1)S(1)}, bf16[72,384]{1,0:T(8,128)(2,1)S(1)}, u32[]{:S(2)}, u32[]{:S(2)}) collective-permute-start(bf16[72,384]{1,0:T(8,128)(2,1)S(1)} %get-tuple-element.120), channel_id=1, source_target_pairs={{12,0},{0,4},{4,8},{8,12},{28,16},{16,20},{20,24},{24,28},{44,32},... | collective-permute-start | bytes 165896 | tf_op jit(solution)/shard_map/ppermute | solution.py:27
  3.3 6.3 %collective-permute-start.3 = (bf16[72,384]{1,0:T(8,128)(2,1)S(1)}, bf16[72,384]{1,0:T(8,128)(2,1)S(1)}, u32[]{:S(2)}, u32[]{:S(2)}) collective-permute-start(bf16[72,384]{1,0:T(8,128)(2,1)S(1)} %get-tuple-element.120), channel_id=1, source_target_pairs={{8,0},{12,4},{0,8},{4,12},{24,16},{28,20},{16,24},{20,28},{40,32},... | collective-permute-start | bytes 165896 | tf_op jit(solution)/shard_map/ppermute | solution.py:27
  6.2 4.2 %collective-permute-start.2 = (bf16[72,384]{1,0:T(8,128)(2,1)S(1)}, bf16[72,384]{1,0:T(8,128)(2,1)S(1)}, u32[]{:S(2)}, u32[]{:S(2)}) collective-permute-start(bf16[72,384]{1,0:T(8,128)(2,1)S(1)} %get-tuple-element.120), channel_id=1, source_target_pairs={{4,0},{8,4},{12,8},{0,12},{20,16},{24,20},{28,24},{16,28},{36,32},... | collective-permute-start | bytes 165896 | tf_op jit(solution)/shard_map/ppermute | solution.py:27
  7.6 5.6 %collective-permute-start = (bf16[72,1024]{1,0:T(8,128)(2,1)}, bf16[72,1024]{1,0:T(8,128)(2,1)S(1)}, u32[]{:S(2)}, u32[]{:S(2)}) collective-permute-start(bf16[72,1024]{1,0:T(8,128)(2,1)} %param.9), channel_id=1, source_target_pairs={{16,0},{20,4},{24,8},{28,12},{0,16},{4,20},{8,24},{12,28},{48,32},... | collective-permute-start | bytes 442376 | tf_op jit(solution)/shard_map/ppermute | solution.py:27
  13.2 11.5 %collective-permute-start.6 = (bf16[2,72,640]{2,1,0:T(8,128)(2,1)S(1)}, bf16[2,72,640]{2,1,0:T(8,128)(2,1)S(1)}, u32[]{:S(2)}, u32[]{:S(2)}) collective-permute-start(bf16[2,72,640]{2,1,0:T(8,128)(2,1)S(1)} %maximum_select_fusion), channel_id=1, source_target_pairs={{224,0},{228,4},{232,8},{236,12},{240,16},{244,20},{248,24},{252,2... | collective-permute-start | bytes 552968 | tf_op jit(solution)/shard_map/ppermute | solution.py:27
  15.2 9.5 %collective-permute-start.5 = (bf16[2,72,640]{2,1,0:T(8,128)(2,1)S(1)}, bf16[2,72,640]{2,1,0:T(8,128)(2,1)S(1)}, u32[]{:S(2)}, u32[]{:S(2)}) collective-permute-start(bf16[2,72,640]{2,1,0:T(8,128)(2,1)S(1)} %maximum_select_fusion), channel_id=1, source_target_pairs={{32,0},{36,4},{40,8},{44,12},{48,16},{52,20},{56,24},{60,28},{64,3... | collective-permute-start | bytes 552968 | tf_op jit(solution)/shard_map/ppermute | solution.py:27
  19.3 5.4 %collective-permute-start.7 = (bf16[3,72,384]{2,1,0:T(8,128)(2,1)S(1)}, bf16[3,72,384]{2,1,0:T(8,128)(2,1)S(1)}, u32[]{:S(2)}, u32[]{:S(2)}) collective-permute-start(bf16[3,72,384]{2,1,0:T(8,128)(2,1)S(1)} %pad_maximum_fusion.2), channel_id=1, source_target_pairs={{16,0},{20,4},{24,8},{28,12},{0,16},{4,20},{8,24},{12,28},{48,32},... | collective-permute-start | bytes 497672 | tf_op jit(solution)/shard_map/ppermute | solution.py:27
  21.9 2.8 %collective-permute-start.8 = (f32[512,128]{1,0:T(8,128)S(1)}, f32[512,128]{1,0:T(8,128)S(1)}, u32[]{:S(2)}, u32[]{:S(2)}) collective-permute-start(f32[512,128]{1,0:T(8,128)S(1)} %fusion.54), channel_id=1, source_target_pairs={{0,1},{1,0},{2,3},{3,2},{4,5},{5,4},{6,7},{7,6},{8,9},{9,8},{10,11... | collective-permute-start | bytes 786440 | tf_op jit(solution)/shard_map/ppermute | solution.py:31
  22.0 47.4 %collective-permute-start.18 = (bf16[128,4608]{1,0:T(8,128)(2,1)}, bf16[128,4608]{1,0:T(8,128)(2,1)}, u32[]{:S(2)}, u32[]{:S(2)}) collective-permute-start(bf16[128,4608]{1,0:T(8,128)(2,1)} %param.8), channel_id=1, source_target_pairs={{0,2},{1,3},{2,0},{3,1},{4,6},{5,7},{6,4},{7,5},{8,10},{9,11},{10,... | collective-permute-start | bytes 3538952 | tf_op jit(solution)/shard_map/ppermute | solution.py:31
  24.7 11.5 %collective-permute-start.9 = (bf16[2,72,640]{2,1,0:T(8,128)(2,1)S(1)}, bf16[2,72,640]{2,1,0:T(8,128)(2,1)}, u32[]{:S(2)}, u32[]{:S(2)}) collective-permute-start(bf16[2,72,640]{2,1,0:T(8,128)(2,1)S(1)} %collective-permute-done.5), channel_id=1, source_target_pairs={{32,0},{36,4},{40,8},{44,12},{48,16},{52,20},{56,24},{60,28},{64,3... | collective-permute-start | bytes 552968 | tf_op jit(solution)/shard_map/ppermute | solution.py:27
  26.7 12.5 %collective-permute-start.10 = (bf16[2,72,640]{2,1,0:T(8,128)(2,1)S(1)}, bf16[2,72,640]{2,1,0:T(8,128)(2,1)S(1)}, u32[]{:S(2)}, u32[]{:S(2)}) collective-permute-start(bf16[2,72,640]{2,1,0:T(8,128)(2,1)S(1)} %collective-permute-done.6), channel_id=1, source_target_pairs={{224,0},{228,4},{232,8},{236,12},{240,16},{244,20},{248,24},{252,2... | collective-permute-start | bytes 552968 | tf_op jit(solution)/shard_map/ppermute | solution.py:27
  26.8 18.3 %collective-permute-start.13 = (bf16[2,72,640]{2,1,0:T(8,128)(2,1)S(1)}, bf16[2,72,640]{2,1,0:T(8,128)(2,1)S(1)}, u32[]{:S(2)}, u32[]{:S(2)}) collective-permute-start(bf16[2,72,640]{2,1,0:T(8,128)(2,1)S(1)} %maximum_select_fusion), channel_id=1, source_target_pairs={{128,0},{132,4},{136,8},{140,12},{144,16},{148,20},{152,24},{156,2... | collective-permute-start | bytes 552968 | tf_op jit(solution)/shard_map/ppermute | solution.py:27
  39.3 7.5 %collective-permute-start.11 = (bf16[2,72,640]{2,1,0:T(8,128)(2,1)}, bf16[2,72,640]{2,1,0:T(8,128)(2,1)}, u32[]{:S(2)}, u32[]{:S(2)}) collective-permute-start(bf16[2,72,640]{2,1,0:T(8,128)(2,1)} %collective-permute-done.9), channel_id=1, source_target_pairs={{32,0},{36,4},{40,8},{44,12},{48,16},{52,20},{56,24},{60,28},{64,3... | collective-permute-start | bytes 552968 | tf_op jit(solution)/shard_map/ppermute | solution.py:27
  41.8 27.6 %collective-permute-start.17 = (bf16[4,2,72,640]{3,2,1,0:T(8,128)(2,1)S(1)}, bf16[4,2,72,640]{3,2,1,0:T(8,128)(2,1)}, u32[]{:S(2)}, u32[]{:S(2)}) collective-permute-start(bf16[4,2,72,640]{3,2,1,0:T(8,128)(2,1)S(1)} %pad_maximum_fusion), channel_id=1, source_target_pairs={{12,0},{0,4},{4,8},{8,12},{28,16},{16,20},{20,24},{24,28},{44,32},... | collective-permute-start | bytes 2211848 | tf_op jit(solution)/shard_map/ppermute | solution.py:27
  42.6 26.9 %collective-permute-start.16 = (bf16[4,2,72,640]{3,2,1,0:T(8,128)(2,1)S(1)}, bf16[4,2,72,640]{3,2,1,0:T(8,128)(2,1)}, u32[]{:S(2)}, u32[]{:S(2)}) collective-permute-start(bf16[4,2,72,640]{3,2,1,0:T(8,128)(2,1)S(1)} %pad_maximum_fusion), channel_id=1, source_target_pairs={{4,0},{8,4},{12,8},{0,12},{20,16},{24,20},{28,24},{16,28},{36,32},... | collective-permute-start | bytes 2211848 | tf_op jit(solution)/shard_map/ppermute | solution.py:27
  45.2 12.5 %collective-permute-start.19 = (f32[512,128]{1,0:T(8,128)S(1)}, f32[512,128]{1,0:T(8,128)S(1)}, u32[]{:S(2)}, u32[]{:S(2)}) collective-permute-start(f32[512,128]{1,0:T(8,128)S(1)} %add.159), channel_id=1, source_target_pairs={{0,2},{1,3},{2,0},{3,1},{4,6},{5,7},{6,4},{7,5},{8,10},{9,11},{10,... | collective-permute-start | bytes 786440 | tf_op jit(solution)/shard_map/ppermute | solution.py:31
  46.7 6.8 %collective-permute-start.12 = (bf16[2,72,640]{2,1,0:T(8,128)(2,1)S(1)}, bf16[2,72,640]{2,1,0:T(8,128)(2,1)S(1)}, u32[]{:S(2)}, u32[]{:S(2)}) collective-permute-start(bf16[2,72,640]{2,1,0:T(8,128)(2,1)S(1)} %collective-permute-done.10), channel_id=1, source_target_pairs={{224,0},{228,4},{232,8},{236,12},{240,16},{244,20},{248,24},{252,2... | collective-permute-start | bytes 552968 | tf_op jit(solution)/shard_map/ppermute | solution.py:27
  53.6 9.5 %collective-permute-start.15 = (bf16[576,384]{1,0:T(8,128)(2,1)S(1)}, bf16[576,384]{1,0:T(8,128)(2,1)S(1)}, u32[]{:S(2)}, u32[]{:S(2)}) collective-permute-start(bf16[576,384]{1,0:T(8,128)(2,1)S(1)} %bitcast.119), channel_id=1, source_target_pairs={{224,0},{228,4},{232,8},{236,12},{240,16},{244,20},{248,24},{252,2... | collective-permute-start | bytes 1327112 | tf_op jit(solution)/shard_map/ppermute | solution.py:27
  57.7 11.7 %collective-permute-start.14 = (bf16[576,384]{1,0:T(8,128)(2,1)S(1)}, bf16[576,384]{1,0:T(8,128)(2,1)S(1)}, u32[]{:S(2)}, u32[]{:S(2)}) collective-permute-start(bf16[576,384]{1,0:T(8,128)(2,1)S(1)} %bitcast.120), channel_id=1, source_target_pairs={{32,0},{36,4},{40,8},{44,12},{48,16},{52,20},{56,24},{60,28},{64,3... | collective-permute-start | bytes 1327112 | tf_op jit(solution)/shard_map/ppermute | solution.py:27
  69.6 11.6 %collective-permute-start.20 = (bf16[576,384]{1,0:T(8,128)(2,1)S(1)}, bf16[576,384]{1,0:T(8,128)(2,1)S(1)}, u32[]{:S(2)}, u32[]{:S(2)}) collective-permute-start(bf16[576,384]{1,0:T(8,128)(2,1)S(1)} %collective-permute-done.14), channel_id=1, source_target_pairs={{32,0},{36,4},{40,8},{44,12},{48,16},{52,20},{56,24},{60,28},{64,3... | collective-permute-start | bytes 1327112 | tf_op jit(solution)/shard_map/ppermute | solution.py:27
  72.9 11.7 %collective-permute-start.21 = (bf16[576,384]{1,0:T(8,128)(2,1)S(1)}, bf16[576,384]{1,0:T(8,128)(2,1)S(1)}, u32[]{:S(2)}, u32[]{:S(2)}) collective-permute-start(bf16[576,384]{1,0:T(8,128)(2,1)S(1)} %collective-permute-done.15), channel_id=1, source_target_pairs={{224,0},{228,4},{232,8},{236,12},{240,16},{244,20},{248,24},{252,2... | collective-permute-start | bytes 1327112 | tf_op jit(solution)/shard_map/ppermute | solution.py:27
  72.9 17.1 %collective-permute-start.25 = (bf16[4,2,72,640]{3,2,1,0:T(8,128)(2,1)}, bf16[4,2,72,640]{3,2,1,0:T(8,128)(2,1)S(1)}, u32[]{:S(2)}, u32[]{:S(2)}) collective-permute-start(bf16[4,2,72,640]{3,2,1,0:T(8,128)(2,1)} %collective-permute-done.16), channel_id=1, source_target_pairs={{4,0},{8,4},{12,8},{0,12},{20,16},{24,20},{28,24},{16,28},{36,32},... | collective-permute-start | bytes 2211848 | tf_op jit(solution)/shard_map/ppermute | solution.py:27
  73.1 17.9 %collective-permute-start.26 = (bf16[4,2,72,640]{3,2,1,0:T(8,128)(2,1)S(1)}, bf16[4,2,72,640]{3,2,1,0:T(8,128)(2,1)}, u32[]{:S(2)}, u32[]{:S(2)}) collective-permute-start(bf16[4,2,72,640]{3,2,1,0:T(8,128)(2,1)S(1)} %pad_maximum_fusion.1), channel_id=1, source_target_pairs={{12,0},{0,4},{4,8},{8,12},{28,16},{16,20},{20,24},{24,28},{44,32},... | collective-permute-start | bytes 2211848 | tf_op jit(solution)/shard_map/ppermute | solution.py:27
  74.9 6.0 %collective-permute-start.22 = (bf16[128,4608]{1,0:T(8,128)(2,1)}, bf16[128,4608]{1,0:T(8,128)(2,1)S(1)}, u32[]{:S(2)}, u32[]{:S(2)}) collective-permute-start(bf16[128,4608]{1,0:T(8,128)(2,1)} %collective-permute-done.18), channel_id=1, source_target_pairs={{0,1},{1,0},{2,3},{3,2},{4,5},{5,4},{6,7},{7,6},{8,9},{9,8},{10,11... | collective-permute-start | bytes 3538952 | tf_op jit(solution)/shard_map/ppermute | solution.py:31
  84.6 13.6 %collective-permute-start.23 = (bf16[576,384]{1,0:T(8,128)(2,1)S(1)}, bf16[576,384]{1,0:T(8,128)(2,1)S(1)}, u32[]{:S(2)}, u32[]{:S(2)}) collective-permute-start(bf16[576,384]{1,0:T(8,128)(2,1)S(1)} %collective-permute-done.20), channel_id=1, source_target_pairs={{32,0},{36,4},{40,8},{44,12},{48,16},{52,20},{56,24},{60,28},{64,3... | collective-permute-start | bytes 1327112 | tf_op jit(solution)/shard_map/ppermute | solution.py:27
  84.9 13.3 %collective-permute-start.24 = (bf16[576,384]{1,0:T(8,128)(2,1)S(1)}, bf16[576,384]{1,0:T(8,128)(2,1)S(1)}, u32[]{:S(2)}, u32[]{:S(2)}) collective-permute-start(bf16[576,384]{1,0:T(8,128)(2,1)S(1)} %collective-permute-done.21), channel_id=1, source_target_pairs={{224,0},{228,4},{232,8},{236,12},{240,16},{244,20},{248,24},{252,2... | collective-permute-start | bytes 1327112 | tf_op jit(solution)/shard_map/ppermute | solution.py:27
  92.3 22.5 %collective-permute-start.27 = (bf16[4,2,72,640]{3,2,1,0:T(8,128)(2,1)S(1)}, bf16[4,2,72,640]{3,2,1,0:T(8,128)(2,1)S(1)}, u32[]{:S(2)}, u32[]{:S(2)}) collective-permute-start(bf16[4,2,72,640]{3,2,1,0:T(8,128)(2,1)S(1)} %pad_maximum_fusion.1), channel_id=1, source_target_pairs={{4,0},{8,4},{12,8},{0,12},{20,16},{24,20},{28,24},{16,28},{36,32},... | collective-permute-start | bytes 2211848 | tf_op jit(solution)/shard_map/ppermute | solution.py:27
  92.7 22.2 %collective-permute-start.28 = (bf16[4,2,72,640]{3,2,1,0:T(8,128)(2,1)}, bf16[4,2,72,640]{3,2,1,0:T(8,128)(2,1)S(1)}, u32[]{:S(2)}, u32[]{:S(2)}) collective-permute-start(bf16[4,2,72,640]{3,2,1,0:T(8,128)(2,1)} %collective-permute-done.26), channel_id=1, source_target_pairs={{12,0},{0,4},{4,8},{8,12},{28,16},{16,20},{20,24},{24,28},{44,32},... | collective-permute-start | bytes 2211848 | tf_op jit(solution)/shard_map/ppermute | solution.py:27
  101.4 7.2 %collective-permute-start.30 = (bf16[288,384]{1,0:T(8,128)(2,1)S(1)}, bf16[288,384]{1,0:T(8,128)(2,1)S(1)}, u32[]{:S(2)}, u32[]{:S(2)}) collective-permute-start(bf16[288,384]{1,0:T(8,128)(2,1)S(1)} %slice.93), channel_id=1, source_target_pairs={{224,0},{228,4},{232,8},{236,12},{240,16},{244,20},{248,24},{252,2... | collective-permute-start | bytes 663560 | tf_op jit(solution)/shard_map/ppermute | solution.py:27
  101.5 7.1 %collective-permute-start.29 = (bf16[288,384]{1,0:T(8,128)(2,1)S(1)}, bf16[288,384]{1,0:T(8,128)(2,1)S(1)}, u32[]{:S(2)}, u32[]{:S(2)}) collective-permute-start(bf16[288,384]{1,0:T(8,128)(2,1)S(1)} %slice.92), channel_id=1, source_target_pairs={{32,0},{36,4},{40,8},{44,12},{48,16},{52,20},{56,24},{60,28},{64,3... | collective-permute-start | bytes 663560 | tf_op jit(solution)/shard_map/ppermute | solution.py:27
  (5 other events, 80.9 us)

commit v5 on v4

--- a/solution.py
+++ b/solution.py
@@ -101,53 +101,55 @@
     tensor = lax.axis_index("tensor").astype(jnp.int32)
     zero = jnp.int32(0)
 
-    own_a, own_b = frozen_weight[:, :a_width], frozen_weight[:, a_width:]
     other = fetch(frozen_weight, dx=1)
-    y_b = [fetch(own_b, dy=dy) for dy in (1, 2, 3)]
     from_core = swap_tensor(output_gradient, 1)
-    other, from_core, own_rows, head_later, index_later, *y_b = together(
-        other, from_core, output_gradient, head_outputs, tenant_index, *y_b
-    )
-
-    far_a, far_b = other[:, :a_width], other[:, a_width:]
-    pair_a = jnp.where(xl == 0, jnp.stack([own_a, far_a]), jnp.stack([far_a, own_a]))
+    partial = jnp.dot(head_outputs, adapter_down_factors, preferred_element_type=jnp.float32)
+    core_partial = swap_tensor(partial, 1)
+    other, from_core, own_rows, index_later = together(
+        other, from_core, output_gradient, tenant_index
+    )
+
+    def pair(columns):
+        mine, far = frozen_weight[:, columns], other[:, columns]
+        return jnp.where(xl == 0, jnp.stack([mine, far]), jnp.stack([far, mine]))
+
+    pair_a, pair_b, own_rows = together(
+        pair(slice(0, a_width)), pair(slice(a_width, None)), own_rows
+    )
     a_p1, a_m1 = fetch(pair_a, dz=1), fetch(pair_a, dz=-1)
-    y_b = jnp.stack(y_b)
-    x_b = fetch(y_b, dx=1)
-    y_b, pair_a, gradient_later, head_later = together(y_b, pair_a, own_rows, head_later)
-    from_chip = swap_tensor(gradient_later, 2)
-    partial = jnp.dot(head_later, adapter_down_factors, preferred_element_type=jnp.float32)
-    core_partial = swap_tensor(partial, 1)
-
-    a_p1, a_m1, x_b, pair_a, partial, core_partial = together(
-        a_p1, a_m1, x_b, pair_a, partial, core_partial
-    )
+    y_b = [fetch(pair_b, dy=dy) for dy in (1, 2, 3)]
+    from_chip = swap_tensor(own_rows, 2)
+
+    a_p1, a_m1, pair_a, core_partial = together(a_p1, a_m1, pair_a, core_partial)
     a_p2, a_m2 = fetch(a_p1, dz=1), fetch(a_m1, dz=-1)
     a_p4 = fetch(pair_a, dz=4)
-    b_own = jnp.broadcast_to(
-        jnp.where(xl == 0, jnp.stack([own_b, far_b]), jnp.stack([far_b, own_b]))[:, None],
-        (NX, NY, shard_rows, own_b.shape[1]),
-    )
-    for i, dy in enumerate((1, 2, 3)):
-        for x, chunk in ((xl, y_b[i]), (1 - xl, x_b[i])):
-            b_own = lax.dynamic_update_slice(
-                b_own, chunk[None, None], (x, (y + dy) % NY, zero, zero)
-            )
+
+    def placed(array, chunk, dy):
+        at = array.ndim - 3
+        return lax.dynamic_update_slice_in_dim(
+            array, jnp.expand_dims(chunk, at), (y + dy) % NY, at
+        )
+
+    def spread(chunk):
+        at = chunk.ndim - 2
+        shape = chunk.shape[:at] + (NY,) + chunk.shape[at:]
+        return jnp.broadcast_to(jnp.expand_dims(chunk, at), shape)
+
+    *y_b, pair_b, a_p1 = together(*y_b, pair_b, a_p1)
+    b_own = spread(pair_b)
+    for dy, chunk in zip((1, 2, 3), y_b):
+        b_own = placed(b_own, chunk, dy)
     b_own = b_own.reshape(NX * NY * shard_rows, -1)
 
     a_p2, a_m2, b_own = together(a_p2, a_m2, b_own)
-    a_p3, a_m3 = fetch(a_p2, dz=1), fetch(a_m2, dz=-1)
     low = jnp.stack([a_m1, pair_a, a_p1, a_p2])
     low_p, low_m = fetch(low, dy=1), fetch(low, dy=-1)
-
-    a_p3, a_m3, a_p4, b_own = together(a_p3, a_m3, a_p4, b_own)
+    a_p3, a_m3 = fetch(a_p2, dz=1), fetch(a_m2, dz=-1)
+    b_p1, b_m1 = fetch(b_own, dz=1), fetch(b_own, dz=-1)
     high = jnp.stack([a_p3, a_p4, a_m3, a_m2])
-    b_p1, b_m1 = fetch(b_own, dz=1), fetch(b_own, dz=-1)
-
-    chip_sum = partial + core_partial
-    far_sum = swap_tensor(chip_sum, 2)
-    b_p1, b_m1, low_p, low_m, high, from_chip, own_rows, far_sum = together(
-        b_p1, b_m1, low_p, low_m, high, from_chip, own_rows, far_sum
+
+    b_p1, b_m1, low_p, low_m, high, from_chip, own_rows, partial, core_partial = together(
+        b_p1, b_m1, low_p, low_m, high, from_chip, own_rows, partial, core_partial
     )
     b_p2, b_m2 = fetch(b_p1, dz=1), fetch(b_m1, dz=-1)
     low_o, high_m = fetch(low_p, dy=1), fetch(high, dy=-1)
@@ -159,12 +161,9 @@
             gradients, block, (tensor ^ mask) * part_rows, 0
         )
 
-    def placed(array, chunk, dy):
-        return lax.dynamic_update_slice_in_dim(array, chunk[:, :, None], (y + dy) % NY, 2)
-
-    def spread(chunk):
-        return jnp.broadcast_to(chunk[:, :, None], (chunk.shape[0], NX, NY) + chunk.shape[2:])
-
+    from_both, partial, core_partial = together(from_both, partial, core_partial)
+    chip_sum = partial + core_partial
+    far_sum = swap_tensor(chip_sum, 2)
     low_all = placed(placed(spread(low), low_p, 1), low_m, 3)
 
     b_p2, b_m2, gradients = together(b_p2, b_m2, gradients)

time: 119 us -> 116 us (0.975); the launches traced: 119 us -> 114 us
  waiting for transfers between devices: 39.9 us -> 28.8 us
  starting transfers between devices: 44.7 us -> 48.7 us
  local copies, waits for them, and re-layouts: 10.2 us -> 12.6 us
    ppermute x26 -> x25, waiting for transfers between devices: 37.1 us -> 28.8 us  [fetch(): return lax.ppermute(x, 'dp', pairs)]
    ppermute x5, starting transfers between devices: 2.28 us -> 6.26 us  [swap_tensor(): return lax.ppermute(x, 'tensor', [(t, t ^ mask) for t in range(4)])]
    ppermute x5, waiting for transfers between devices: 2.81 us -> 0.01 us  [swap_tensor(): return lax.ppermute(x, 'tensor', [(t, t ^ mask) for t in range(4)])]
    dynamic_update_slice x11 -> x8, local copies, waits for them, and re-layouts: 4.19 us -> 6.87 us  [placed(): lax.dynamic_update_slice_in_dim(array, jnp.expand_dims(chunk, at), (y + d...]
    dynamic_update_slice x4, local copies, waits for them, and re-layouts: 3.04 us -> 1.73 us  [body(): lax.dynamic_update_slice_in_dim(gradients, block, (tensor ^ mask) * part_...]
    ppermute x26 -> x25, starting transfers between devices: 42.4 us -> 42.4 us  [fetch(): return lax.ppermute(x, 'dp', pairs)]
  transfers between devices with their start and end apart: 31 -> 30, of which waited for: 15 -> 11; matrix products, arithmetic and copies ran while one was open for 21% -> 24% of each run, Pallas kernels for 2% -> 3%
where the time goes in v5:
time: 116 us; the launch traced here: 114 us
  starting transfers between devices  48.7 us (42%)
  waiting for transfers between devices  28.8 us (25%)
  matrix products  13.2 us (11%)
  local copies, waits for them, and re-layouts  12.6 us (11%)
  Pallas kernels  6.34 us (5%)
  other arithmetic  2.62 us (2%)
  between operations  1.79 us (2%)
    ppermute x25, starting transfers between devices, fetch(): return lax.ppermute(x, 'dp', pairs)  42.4 us
    ppermute x25, waiting for transfers between devices, fetch(): return lax.ppermute(x, 'dp', pairs)  28.8 us
    dot_general x16, matrix products, contract(): lax.dot_general(left, right, (((left_dim,), (right_dim,)), ((), ())), pre...  11.5 us
    dynamic_update_slice x8, local copies, waits for them, and re-layouts, placed(): lax.dynamic_update_slice_in_dim(array, jnp.expand_dims(chunk, at), (y + d...  6.87 us
    ppermute x5, starting transfers between devices, swap_tensor(): return lax.ppermute(x, 'tensor', [(t, t ^ mask) for t in range(4)])  6.26 us
    pallas_call x2, Pallas kernels, in_vmem(): pl.pallas_call(kernel, in_specs=[pl.BlockSpec(memory_space=pltpu.VMEM)] *...  4.76 us
  transfers between devices with their start and end apart: 30, of which 11 were waited for; matrix products, arithmetic and copies ran while one was open for 24% of the time, Pallas kernels for 3%

profile of v5, /device:TPU:6, one launch (start us, length us, event | category | flops | bytes accessed | tf_op | source)
XLA Modules:
  0.0 114.1 jit_solution(15935220446878451039)
XLA Ops:
  1.7 1.7 %fusion.54 = f32[512,128]{1,0:T(8,128)S(1)} fusion(bf16[512,1024]{1,0:T(8,128)(2,1)} %head_ref.1, bf16[1024,128]{1,0:T(8,128)(2,1)} %param.10), kind=kOutput, calls=%fused_computation.93 | convolution fusion | flops 134217728 | bytes 1572864 | tf_op jit(solution)/shard_map/dot_general | solution.py:106
  5.3 1.9 %collective-permute-done = bf16[72,1024]{1,0:T(8,128)(2,1)S(1)} collective-permute-done((bf16[72,1024]{1,0:T(8,128)(2,1)}, bf16[72,1024]{1,0:T(8,128)(2,1)S(1)}, u32[]{:S(2)}, u32[]{:S(2)}) %collective-permute-start) | collective-permute-done | bytes 147488 | tf_op jit(solution)/shard_map/ppermute | solution.py:27
  7.4 2.0 %collective-permute-start.3 = (bf16[2,72,640]{2,1,0:T(8,128)(2,1)S(1)}, bf16[2,72,640]{2,1,0:T(8,128)(2,1)S(1)}, u32[]{:S(2)}, u32[]{:S(2)}) collective-permute-start(bf16[2,72,640]{2,1,0:T(8,128)(2,1)S(1)} %maximum_select_fusion), channel_id=1, source_target_pairs={{224,0},{228,4},{232,8},{236,12},{240,16},{244,20},{248,24},{252,2... | collective-permute-start | bytes 552968 | tf_op jit(solution)/shard_map/ppermute | solution.py:27
  9.4 4.0 %collective-permute-start.2 = (bf16[2,72,640]{2,1,0:T(8,128)(2,1)S(1)}, bf16[2,72,640]{2,1,0:T(8,128)(2,1)}, u32[]{:S(2)}, u32[]{:S(2)}) collective-permute-start(bf16[2,72,640]{2,1,0:T(8,128)(2,1)S(1)} %maximum_select_fusion), channel_id=1, source_target_pairs={{32,0},{36,4},{40,8},{44,12},{48,16},{52,20},{56,24},{60,28},{64,3... | collective-permute-start | bytes 552968 | tf_op jit(solution)/shard_map/ppermute | solution.py:27
  13.4 1.6 %collective-permute-start.9 = (bf16[2,72,384]{2,1,0:T(8,128)(2,1)S(1)}, bf16[2,72,384]{2,1,0:T(8,128)(2,1)S(1)}, u32[]{:S(2)}, u32[]{:S(2)}) collective-permute-start(bf16[2,72,384]{2,1,0:T(8,128)(2,1)S(1)} %maximum_select_fusion.1), channel_id=1, source_target_pairs={{12,0},{0,4},{4,8},{8,12},{28,16},{16,20},{20,24},{24,28},{44,32},... | collective-permute-start | bytes 331784 | tf_op jit(solution)/shard_map/ppermute | solution.py:27
  15.0 2.9 %collective-permute-start.8 = (bf16[2,72,384]{2,1,0:T(8,128)(2,1)S(1)}, bf16[2,72,384]{2,1,0:T(8,128)(2,1)}, u32[]{:S(2)}, u32[]{:S(2)}) collective-permute-start(bf16[2,72,384]{2,1,0:T(8,128)(2,1)S(1)} %maximum_select_fusion.1), channel_id=1, source_target_pairs={{8,0},{12,4},{0,8},{4,12},{24,16},{28,20},{16,24},{20,28},{40,32},... | collective-permute-start | bytes 331784 | tf_op jit(solution)/shard_map/ppermute | solution.py:27
  19.2 1.4 %collective-permute-start.17 = (bf16[128,4608]{1,0:T(8,128)(2,1)}, bf16[128,4608]{1,0:T(8,128)(2,1)}, u32[]{:S(2)}, u32[]{:S(2)}) collective-permute-start(bf16[128,4608]{1,0:T(8,128)(2,1)} %param.8), channel_id=1, source_target_pairs={{0,2},{1,3},{2,0},{3,1},{4,6},{5,7},{6,4},{7,5},{8,10},{9,11},{10,... | collective-permute-start | bytes 3538952 | tf_op jit(solution)/shard_map/ppermute | solution.py:31
  20.6 1.9 %collective-permute-start.5 = (bf16[2,72,640]{2,1,0:T(8,128)(2,1)}, bf16[2,72,640]{2,1,0:T(8,128)(2,1)S(1)}, u32[]{:S(2)}, u32[]{:S(2)}) collective-permute-start(bf16[2,72,640]{2,1,0:T(8,128)(2,1)} %collective-permute-done.2), channel_id=1, source_target_pairs={{32,0},{36,4},{40,8},{44,12},{48,16},{52,20},{56,24},{60,28},{64,3... | collective-permute-start | bytes 552968 | tf_op jit(solution)/shard_map/ppermute | solution.py:27
  23.2 4.1 %collective-permute-start.15 = (bf16[2,72,640]{2,1,0:T(8,128)(2,1)S(1)}, bf16[2,72,640]{2,1,0:T(8,128)(2,1)}, u32[]{:S(2)}, u32[]{:S(2)}) collective-permute-start(bf16[2,72,640]{2,1,0:T(8,128)(2,1)S(1)} %maximum_select_fusion), channel_id=1, source_target_pairs={{128,0},{132,4},{136,8},{140,12},{144,16},{148,20},{152,24},{156,2... | collective-permute-start | bytes 552968 | tf_op jit(solution)/shard_map/ppermute | solution.py:27
  30.2 2.4 %collective-permute-done.6 = bf16[2,72,640]{2,1,0:T(8,128)(2,1)S(1)} collective-permute-done((bf16[2,72,640]{2,1,0:T(8,128)(2,1)S(1)}, bf16[2,72,640]{2,1,0:T(8,128)(2,1)S(1)}, u32[]{:S(2)}, u32[]{:S(2)}) %collective-permute-start.6) | collective-permute-done | bytes 184352 | tf_op jit(solution)/shard_map/ppermute | solution.py:27
  34.3 1.4 %collective-permute-start.13 = (bf16[4,2,72,640]{3,2,1,0:T(8,128)(2,1)S(1)}, bf16[4,2,72,640]{3,2,1,0:T(8,128)(2,1)}, u32[]{:S(2)}, u32[]{:S(2)}) collective-permute-start(bf16[4,2,72,640]{3,2,1,0:T(8,128)(2,1)S(1)} %pad_maximum_fusion), channel_id=1, source_target_pairs={{12,0},{0,4},{4,8},{8,12},{28,16},{16,20},{20,24},{24,28},{44,32},... | collective-permute-start | bytes 2211848 | tf_op jit(solution)/shard_map/ppermute | solution.py:27
  35.7 2.0 %collective-permute-start.12 = (bf16[4,2,72,640]{3,2,1,0:T(8,128)(2,1)S(1)}, bf16[4,2,72,640]{3,2,1,0:T(8,128)(2,1)}, u32[]{:S(2)}, u32[]{:S(2)}) collective-permute-start(bf16[4,2,72,640]{3,2,1,0:T(8,128)(2,1)S(1)} %pad_maximum_fusion), channel_id=1, source_target_pairs={{4,0},{8,4},{12,8},{0,12},{20,16},{24,20},{28,24},{16,28},{36,32},... | collective-permute-start | bytes 2211848 | tf_op jit(solution)/shard_map/ppermute | solution.py:27
  40.5 3.7 %collective-permute-done.14 = bf16[2,72,640]{2,1,0:T(8,128)(2,1)S(1)} collective-permute-done((bf16[2,72,640]{2,1,0:T(8,128)(2,1)}, bf16[2,72,640]{2,1,0:T(8,128)(2,1)S(1)}, u32[]{:S(2)}, u32[]{:S(2)}) %collective-permute-start.14) | collective-permute-done | bytes 184352 | tf_op jit(solution)/shard_map/ppermute | solution.py:27
  44.1 4.2 %collective-permute-done.16 = bf16[2,72,640]{2,1,0:T(8,128)(2,1)S(1)} collective-permute-done((bf16[2,72,640]{2,1,0:T(8,128)(2,1)}, bf16[2,72,640]{2,1,0:T(8,128)(2,1)S(1)}, u32[]{:S(2)}, u32[]{:S(2)}) %collective-permute-start.16) | collective-permute-done | bytes 184352 | tf_op jit(solution)/shard_map/ppermute | solution.py:27
  49.7 5.7 %collective-permute-done.11 = bf16[576,384]{1,0:T(8,128)(2,1)S(1)} collective-permute-done((bf16[576,384]{1,0:T(8,128)(2,1)S(1)}, bf16[576,384]{1,0:T(8,128)(2,1)S(1)}, u32[]{:S(2)}, u32[]{:S(2)}) %collective-permute-start.11) | collective-permute-done | bytes 442400 | tf_op jit(solution)/shard_map/ppermute | solution.py:27
  55.3 4.5 %collective-permute-done.10 = bf16[576,384]{1,0:T(8,128)(2,1)S(1)} collective-permute-done((bf16[576,384]{1,0:T(8,128)(2,1)S(1)}, bf16[576,384]{1,0:T(8,128)(2,1)S(1)}, u32[]{:S(2)}, u32[]{:S(2)}) %collective-permute-start.10) | collective-permute-done | bytes 442400 | tf_op jit(solution)/shard_map/ppermute | solution.py:27
  59.8 2.2 %collective-permute-start.18 = (bf16[576,384]{1,0:T(8,128)(2,1)S(1)}, bf16[576,384]{1,0:T(8,128)(2,1)S(1)}, u32[]{:S(2)}, u32[]{:S(2)}) collective-permute-start(bf16[576,384]{1,0:T(8,128)(2,1)S(1)} %collective-permute-done.10), channel_id=1, source_target_pairs={{32,0},{36,4},{40,8},{44,12},{48,16},{52,20},{56,24},{60,28},{64,3... | collective-permute-start | bytes 1327112 | tf_op jit(solution)/shard_map/ppermute | solution.py:27
  62.1 1.9 %collective-permute-start.19 = (bf16[576,384]{1,0:T(8,128)(2,1)S(1)}, bf16[576,384]{1,0:T(8,128)(2,1)S(1)}, u32[]{:S(2)}, u32[]{:S(2)}) collective-permute-start(bf16[576,384]{1,0:T(8,128)(2,1)S(1)} %collective-permute-done.11), channel_id=1, source_target_pairs={{224,0},{228,4},{232,8},{236,12},{240,16},{244,20},{248,24},{252,2... | collective-permute-start | bytes 1327112 | tf_op jit(solution)/shard_map/ppermute | solution.py:27
  64.0 1.6 %collective-permute-start.23 = (bf16[4,2,72,640]{3,2,1,0:T(8,128)(2,1)}, bf16[4,2,72,640]{3,2,1,0:T(8,128)(2,1)S(1)}, u32[]{:S(2)}, u32[]{:S(2)}) collective-permute-start(bf16[4,2,72,640]{3,2,1,0:T(8,128)(2,1)} %collective-permute-done.12), channel_id=1, source_target_pairs={{4,0},{8,4},{12,8},{0,12},{20,16},{24,20},{28,24},{16,28},{36,32},... | collective-permute-start | bytes 2211848 | tf_op jit(solution)/shard_map/ppermute | solution.py:27
  68.1 1.4 %constant_dynamic-update-slice_fusion.1 = bf16[512,4608]{1,0:T(8,128)(2,1)S(1)} fusion(bf16[512,4608]{1,0:T(8,128)(2,1)S(1)} %constant_dynamic-update-slice_fusion.2, bf16[128,4608]{1,0:T(8,128)(2,1)} %collective-permute-done.17, s32[]{:T(128)S(6)} %select_n.123), kind=kLoop, calls=%fused_computation.79 | loop fusion | bytes 2359300 | tf_op jit(solution)/shard_map/dynamic_update_slice | solution.py:160
  70.8 4.5 %collective-permute-start.29 = (f32[512,128]{1,0:T(8,128)S(1)}, f32[512,128]{1,0:T(8,128)S(1)}, u32[]{:S(2)}, u32[]{:S(2)}) collective-permute-start(f32[512,128]{1,0:T(8,128)S(1)} %add.143), channel_id=1, source_target_pairs={{0,2},{1,3},{2,0},{3,1},{4,6},{5,7},{6,4},{7,5},{8,10},{9,11},{10,... | collective-permute-start | bytes 786440 | tf_op jit(solution)/shard_map/ppermute | solution.py:31
  75.5 3.2 %collective-permute-start.21 = (bf16[576,384]{1,0:T(8,128)(2,1)S(1)}, bf16[576,384]{1,0:T(8,128)(2,1)S(1)}, u32[]{:S(2)}, u32[]{:S(2)}) collective-permute-start(bf16[576,384]{1,0:T(8,128)(2,1)S(1)} %collective-permute-done.18), channel_id=1, source_target_pairs={{32,0},{36,4},{40,8},{44,12},{48,16},{52,20},{56,24},{60,28},{64,3... | collective-permute-start | bytes 1327112 | tf_op jit(solution)/shard_map/ppermute | solution.py:27
  78.7 3.4 %collective-permute-start.22 = (bf16[576,384]{1,0:T(8,128)(2,1)S(1)}, bf16[576,384]{1,0:T(8,128)(2,1)S(1)}, u32[]{:S(2)}, u32[]{:S(2)}) collective-permute-start(bf16[576,384]{1,0:T(8,128)(2,1)S(1)} %collective-permute-done.19), channel_id=1, source_target_pairs={{224,0},{228,4},{232,8},{236,12},{240,16},{244,20},{248,24},{252,2... | collective-permute-start | bytes 1327112 | tf_op jit(solution)/shard_map/ppermute | solution.py:27
  82.1 1.4 %fusion.11.back_ref = bf16[512,128]{1,0:T(8,128)(2,1)S(1)} fusion(bf16[512,4608]{1,0:T(8,128)(2,1)S(1)} %constant_dynamic-update-slice_fusion.g_ref, bf16[128,4608]{1,0:T(8,128)(2,1)S(1)} %copy-done, s32[128]{0:T(128)S(1)} %and_select_fusion, s32[512]{0:T(512)S(1)} %add_select_fusion, pred[512]{0:T(512)(128)(4,1)S(1)} %iota_compare_fusion.1), kind=kOutput, calls=%fused_computation.18 | convolution fusion | flops 604241920 | bytes 6032384 | tf_op jit(solution)/shard_map/dot_general | solution.py:15
  84.9 1.9 %collective-permute-start.26 = (bf16[4,2,72,640]{3,2,1,0:T(8,128)(2,1)}, bf16[4,2,72,640]{3,2,1,0:T(8,128)(2,1)S(1)}, u32[]{:S(2)}, u32[]{:S(2)}) collective-permute-start(bf16[4,2,72,640]{3,2,1,0:T(8,128)(2,1)} %collective-permute-done.24), channel_id=1, source_target_pairs={{12,0},{0,4},{4,8},{8,12},{28,16},{16,20},{20,24},{24,28},{44,32},... | collective-permute-start | bytes 2211848 | tf_op jit(solution)/shard_map/ppermute | solution.py:27
  86.8 1.6 %shard_map.94.z_ref = bf16[8,512,576]{2,1,0:T(8,128)(2,1)S(1)} custom-call(s32[1]{0:T(128)} %bitcast.18.start_ref, bf16[512,4608]{1,0:T(8,128)(2,1)S(1)} %constant_dynamic-update-slice_fusion.g_ref), custom_call_target="tpu_custom_call" | custom-call | tf_op jit(solution)/shard_map/pallas_call | solution.py:49
  88.6 2.2 %convolution_multiply_fusion = f32[128,4608]{1,0:T(8,128)} fusion(bf16[512,128]{1,0:T(8,128)(2,1)S(1)} %select_convert_fusion, bf16[512,4608]{1,0:T(8,128)(2,1)S(1)} %constant_dynamic-update-slice_fusion.g_ref), kind=kOutput, calls=%fused_computation | convolution fusion | flops 604569600 | bytes 7208960 | tf_op jit(solution)/shard_map/dot_general | solution.py:15
  95.1 1.9 %collective-permute-start.28 = (bf16[288,384]{1,0:T(8,128)(2,1)S(1)}, bf16[288,384]{1,0:T(8,128)(2,1)S(1)}, u32[]{:S(2)}, u32[]{:S(2)}) collective-permute-start(bf16[288,384]{1,0:T(8,128)(2,1)S(1)} %slice.69), channel_id=1, source_target_pairs={{224,0},{228,4},{232,8},{236,12},{240,16},{244,20},{248,24},{252,2... | collective-permute-start | bytes 663560 | tf_op jit(solution)/shard_map/ppermute | solution.py:27
  97.1 1.4 %collective-permute-start.27 = (bf16[288,384]{1,0:T(8,128)(2,1)S(1)}, bf16[288,384]{1,0:T(8,128)(2,1)S(1)}, u32[]{:S(2)}, u32[]{:S(2)}) collective-permute-start(bf16[288,384]{1,0:T(8,128)(2,1)S(1)} %slice.68), channel_id=1, source_target_pairs={{32,0},{36,4},{40,8},{44,12},{48,16},{52,20},{56,24},{60,28},{64,3... | collective-permute-start | bytes 663560 | tf_op jit(solution)/shard_map/ppermute | solution.py:27
  99.0 3.9 %collective-permute-done.28 = bf16[288,384]{1,0:T(8,128)(2,1)S(1)} collective-permute-done((bf16[288,384]{1,0:T(8,128)(2,1)S(1)}, bf16[288,384]{1,0:T(8,128)(2,1)S(1)}, u32[]{:S(2)}, u32[]{:S(2)}) %collective-permute-start.28) | collective-permute-done | bytes 221216 | tf_op jit(solution)/shard_map/ppermute | solution.py:27
  104.3 1.4 %bitcast_dynamic-update-slice_fusion.2 = (bf16[4,2,4,72,640]{4,3,2,1,0:T(8,128)(2,1)S(1)}, bf16[4,2,4,72,640]{4,3,2,1,0:T(8,128)(2,1)S(1)}) fusion(bf16[4,2,4,72,640]{4,3,2,1,0:T(8,128)(2,1)S(1)} %bitcast_dynamic-update-slice_fusion.4, s32[]{:T(128)S(6)} %select_n.118, bf16[4,2,72,640]{3,2,1,0:T(8,128)(2,1)S(1)} %collective-permute-done.23, ...), kind=kLoop, calls=%fused_computation.23 | loop fusion | bytes 2949128 | tf_op jit(solution)/shard_map/dynamic_update_slice | solution.py:129
  110.6 3.5 %shard_map.96 = bf16[512,1024]{1,0:T(8,128)(2,1)} custom-call(bf16[8,512,576]{2,1,0:T(8,128)(2,1)S(1)} %shard_map.94.z_ref, bf16[4,576,640]{2,1,0:T(8,128)(2,1)S(1)} %bitcast.111, f32[512,640]{1,0:T(8,128)S(1)} %convolution_add_fusion.total_ref, f32[512,1]{1,0:T(8,128)S(1)} %fusion.48.live_ref, bf16[512,384]{1,0:T(8,128)(2,1)S(1)} %fusion.10.b_ref), custom_call_target="tpu_custom_call" | custom-call | tf_op jit(solution)/shard_map/pallas_call | solution.py:77
  (105 shorter events, 29.6 us)
Async XLA Ops:
  0.6 81.4 %copy-start = (bf16[128,4608]{1,0:T(8,128)(2,1)S(1)}, bf16[128,4608]{1,0:T(8,128)(2,1)}, u32[]{:S(2)}) copy-start(bf16[128,4608]{1,0:T(8,128)(2,1)} %param.11) | copy-start | bytes 3538948
  0.6 47.7 %copy-start.11 = (s32[512]{0:T(512)S(1)}, s32[512]{0:T(512)}, u32[]{:S(2)}) copy-start(s32[512]{0:T(512)} %param.12) | copy-start | bytes 6148
  0.7 6.6 %collective-permute-start.1 = (bf16[128,4608]{1,0:T(8,128)(2,1)}, bf16[128,4608]{1,0:T(8,128)(2,1)S(1)}, u32[]{:S(2)}, u32[]{:S(2)}) collective-permute-start(bf16[128,4608]{1,0:T(8,128)(2,1)} %param.8), channel_id=1, source_target_pairs={{0,1},{1,0},{2,3},{3,2},{4,5},{5,4},{6,7},{7,6},{8,9},{9,8},{10,11... | collective-permute-start | bytes 3538952 | tf_op jit(solution)/shard_map/ppermute | solution.py:31
  0.8 6.5 %collective-permute-start = (bf16[72,1024]{1,0:T(8,128)(2,1)}, bf16[72,1024]{1,0:T(8,128)(2,1)S(1)}, u32[]{:S(2)}, u32[]{:S(2)}) collective-permute-start(bf16[72,1024]{1,0:T(8,128)(2,1)} %param.9), channel_id=1, source_target_pairs={{16,0},{20,4},{24,8},{28,12},{0,16},{4,20},{8,24},{12,28},{48,32},... | collective-permute-start | bytes 442376 | tf_op jit(solution)/shard_map/ppermute | solution.py:27
  3.4 14.5 %collective-permute-start.4 = (f32[512,128]{1,0:T(8,128)S(1)}, f32[512,128]{1,0:T(8,128)S(1)}, u32[]{:S(2)}, u32[]{:S(2)}) collective-permute-start(f32[512,128]{1,0:T(8,128)S(1)} %fusion.54), channel_id=1, source_target_pairs={{0,1},{1,0},{2,3},{3,2},{4,5},{5,4},{6,7},{7,6},{8,9},{9,8},{10,11... | collective-permute-start | bytes 786440 | tf_op jit(solution)/shard_map/ppermute | solution.py:31
  7.4 11.9 %collective-permute-start.3 = (bf16[2,72,640]{2,1,0:T(8,128)(2,1)S(1)}, bf16[2,72,640]{2,1,0:T(8,128)(2,1)S(1)}, u32[]{:S(2)}, u32[]{:S(2)}) collective-permute-start(bf16[2,72,640]{2,1,0:T(8,128)(2,1)S(1)} %maximum_select_fusion), channel_id=1, source_target_pairs={{224,0},{228,4},{232,8},{236,12},{240,16},{244,20},{248,24},{252,2... | collective-permute-start | bytes 552968 | tf_op jit(solution)/shard_map/ppermute | solution.py:27
  9.4 11.3 %collective-permute-start.2 = (bf16[2,72,640]{2,1,0:T(8,128)(2,1)S(1)}, bf16[2,72,640]{2,1,0:T(8,128)(2,1)}, u32[]{:S(2)}, u32[]{:S(2)}) collective-permute-start(bf16[2,72,640]{2,1,0:T(8,128)(2,1)S(1)} %maximum_select_fusion), channel_id=1, source_target_pairs={{32,0},{36,4},{40,8},{44,12},{48,16},{52,20},{56,24},{60,28},{64,3... | collective-permute-start | bytes 552968 | tf_op jit(solution)/shard_map/ppermute | solution.py:27
  13.4 9.2 %collective-permute-start.9 = (bf16[2,72,384]{2,1,0:T(8,128)(2,1)S(1)}, bf16[2,72,384]{2,1,0:T(8,128)(2,1)S(1)}, u32[]{:S(2)}, u32[]{:S(2)}) collective-permute-start(bf16[2,72,384]{2,1,0:T(8,128)(2,1)S(1)} %maximum_select_fusion.1), channel_id=1, source_target_pairs={{12,0},{0,4},{4,8},{8,12},{28,16},{16,20},{20,24},{24,28},{44,32},... | collective-permute-start | bytes 331784 | tf_op jit(solution)/shard_map/ppermute | solution.py:27
  15.0 7.7 %collective-permute-start.8 = (bf16[2,72,384]{2,1,0:T(8,128)(2,1)S(1)}, bf16[2,72,384]{2,1,0:T(8,128)(2,1)}, u32[]{:S(2)}, u32[]{:S(2)}) collective-permute-start(bf16[2,72,384]{2,1,0:T(8,128)(2,1)S(1)} %maximum_select_fusion.1), channel_id=1, source_target_pairs={{8,0},{12,4},{0,8},{4,12},{24,16},{28,20},{16,24},{20,28},{40,32},... | collective-permute-start | bytes 331784 | tf_op jit(solution)/shard_map/ppermute | solution.py:27
  17.9 4.9 %collective-permute-start.7 = (bf16[2,72,384]{2,1,0:T(8,128)(2,1)S(1)}, bf16[2,72,384]{2,1,0:T(8,128)(2,1)}, u32[]{:S(2)}, u32[]{:S(2)}) collective-permute-start(bf16[2,72,384]{2,1,0:T(8,128)(2,1)S(1)} %maximum_select_fusion.1), channel_id=1, source_target_pairs={{4,0},{8,4},{12,8},{0,12},{20,16},{24,20},{28,24},{16,28},{36,32},... | collective-permute-start | bytes 331784 | tf_op jit(solution)/shard_map/ppermute | solution.py:27
  19.2 40.6 %collective-permute-start.17 = (bf16[128,4608]{1,0:T(8,128)(2,1)}, bf16[128,4608]{1,0:T(8,128)(2,1)}, u32[]{:S(2)}, u32[]{:S(2)}) collective-permute-start(bf16[128,4608]{1,0:T(8,128)(2,1)} %param.8), channel_id=1, source_target_pairs={{0,2},{1,3},{2,0},{3,1},{4,6},{5,7},{6,4},{7,5},{8,10},{9,11},{10,... | collective-permute-start | bytes 3538952 | tf_op jit(solution)/shard_map/ppermute | solution.py:31
  20.6 9.5 %collective-permute-start.5 = (bf16[2,72,640]{2,1,0:T(8,128)(2,1)}, bf16[2,72,640]{2,1,0:T(8,128)(2,1)S(1)}, u32[]{:S(2)}, u32[]{:S(2)}) collective-permute-start(bf16[2,72,640]{2,1,0:T(8,128)(2,1)} %collective-permute-done.2), channel_id=1, source_target_pairs={{32,0},{36,4},{40,8},{44,12},{48,16},{52,20},{56,24},{60,28},{64,3... | collective-permute-start | bytes 552968 | tf_op jit(solution)/shard_map/ppermute | solution.py:27
  22.7 9.8 %collective-permute-start.6 = (bf16[2,72,640]{2,1,0:T(8,128)(2,1)S(1)}, bf16[2,72,640]{2,1,0:T(8,128)(2,1)S(1)}, u32[]{:S(2)}, u32[]{:S(2)}) collective-permute-start(bf16[2,72,640]{2,1,0:T(8,128)(2,1)S(1)} %collective-permute-done.3), channel_id=1, source_target_pairs={{224,0},{228,4},{232,8},{236,12},{240,16},{244,20},{248,24},{252,2... | collective-permute-start | bytes 552968 | tf_op jit(solution)/shard_map/ppermute | solution.py:27
  23.2 16.3 %collective-permute-start.15 = (bf16[2,72,640]{2,1,0:T(8,128)(2,1)S(1)}, bf16[2,72,640]{2,1,0:T(8,128)(2,1)}, u32[]{:S(2)}, u32[]{:S(2)}) collective-permute-start(bf16[2,72,640]{2,1,0:T(8,128)(2,1)S(1)} %maximum_select_fusion), channel_id=1, source_target_pairs={{128,0},{132,4},{136,8},{140,12},{144,16},{148,20},{152,24},{156,2... | collective-permute-start | bytes 552968 | tf_op jit(solution)/shard_map/ppermute | solution.py:27
  34.3 25.5 %collective-permute-start.13 = (bf16[4,2,72,640]{3,2,1,0:T(8,128)(2,1)S(1)}, bf16[4,2,72,640]{3,2,1,0:T(8,128)(2,1)}, u32[]{:S(2)}, u32[]{:S(2)}) collective-permute-start(bf16[4,2,72,640]{3,2,1,0:T(8,128)(2,1)S(1)} %pad_maximum_fusion), channel_id=1, source_target_pairs={{12,0},{0,4},{4,8},{8,12},{28,16},{16,20},{20,24},{24,28},{44,32},... | collective-permute-start | bytes 2211848 | tf_op jit(solution)/shard_map/ppermute | solution.py:27
  35.7 24.1 %collective-permute-start.12 = (bf16[4,2,72,640]{3,2,1,0:T(8,128)(2,1)S(1)}, bf16[4,2,72,640]{3,2,1,0:T(8,128)(2,1)}, u32[]{:S(2)}, u32[]{:S(2)}) collective-permute-start(bf16[4,2,72,640]{3,2,1,0:T(8,128)(2,1)S(1)} %pad_maximum_fusion), channel_id=1, source_target_pairs={{4,0},{8,4},{12,8},{0,12},{20,16},{24,20},{28,24},{16,28},{36,32},... | collective-permute-start | bytes 2211848 | tf_op jit(solution)/shard_map/ppermute | solution.py:27
  38.3 5.8 %collective-permute-start.14 = (bf16[2,72,640]{2,1,0:T(8,128)(2,1)}, bf16[2,72,640]{2,1,0:T(8,128)(2,1)S(1)}, u32[]{:S(2)}, u32[]{:S(2)}) collective-permute-start(bf16[2,72,640]{2,1,0:T(8,128)(2,1)} %copy-done.9), channel_id=1, source_target_pairs={{32,0},{36,4},{40,8},{44,12},{48,16},{52,20},{56,24},{60,28},{64,3... | collective-permute-start | bytes 552968 | tf_op jit(solution)/shard_map/ppermute | solution.py:27
  39.5 8.9 %collective-permute-start.16 = (bf16[2,72,640]{2,1,0:T(8,128)(2,1)}, bf16[2,72,640]{2,1,0:T(8,128)(2,1)S(1)}, u32[]{:S(2)}, u32[]{:S(2)}) collective-permute-start(bf16[2,72,640]{2,1,0:T(8,128)(2,1)} %copy-done.8), channel_id=1, source_target_pairs={{224,0},{228,4},{232,8},{236,12},{240,16},{244,20},{248,24},{252,2... | collective-permute-start | bytes 552968 | tf_op jit(solution)/shard_map/ppermute | solution.py:27
  44.1 11.2 %collective-permute-start.11 = (bf16[576,384]{1,0:T(8,128)(2,1)S(1)}, bf16[576,384]{1,0:T(8,128)(2,1)S(1)}, u32[]{:S(2)}, u32[]{:S(2)}) collective-permute-start(bf16[576,384]{1,0:T(8,128)(2,1)S(1)} %bitcast.116), channel_id=1, source_target_pairs={{224,0},{228,4},{232,8},{236,12},{240,16},{244,20},{248,24},{252,2... | collective-permute-start | bytes 1327112 | tf_op jit(solution)/shard_map/ppermute | solution.py:27
  48.4 11.4 %collective-permute-start.10 = (bf16[576,384]{1,0:T(8,128)(2,1)S(1)}, bf16[576,384]{1,0:T(8,128)(2,1)S(1)}, u32[]{:S(2)}, u32[]{:S(2)}) collective-permute-start(bf16[576,384]{1,0:T(8,128)(2,1)S(1)} %bitcast.117), channel_id=1, source_target_pairs={{32,0},{36,4},{40,8},{44,12},{48,16},{52,20},{56,24},{60,28},{64,3... | collective-permute-start | bytes 1327112 | tf_op jit(solution)/shard_map/ppermute | solution.py:27
  59.8 15.7 %collective-permute-start.18 = (bf16[576,384]{1,0:T(8,128)(2,1)S(1)}, bf16[576,384]{1,0:T(8,128)(2,1)S(1)}, u32[]{:S(2)}, u32[]{:S(2)}) collective-permute-start(bf16[576,384]{1,0:T(8,128)(2,1)S(1)} %collective-permute-done.10), channel_id=1, source_target_pairs={{32,0},{36,4},{40,8},{44,12},{48,16},{52,20},{56,24},{60,28},{64,3... | collective-permute-start | bytes 1327112 | tf_op jit(solution)/shard_map/ppermute | solution.py:27
  62.1 13.4 %collective-permute-start.19 = (bf16[576,384]{1,0:T(8,128)(2,1)S(1)}, bf16[576,384]{1,0:T(8,128)(2,1)S(1)}, u32[]{:S(2)}, u32[]{:S(2)}) collective-permute-start(bf16[576,384]{1,0:T(8,128)(2,1)S(1)} %collective-permute-done.11), channel_id=1, source_target_pairs={{224,0},{228,4},{232,8},{236,12},{240,16},{244,20},{248,24},{252,2... | collective-permute-start | bytes 1327112 | tf_op jit(solution)/shard_map/ppermute | solution.py:27
  64.0 14.7 %collective-permute-start.23 = (bf16[4,2,72,640]{3,2,1,0:T(8,128)(2,1)}, bf16[4,2,72,640]{3,2,1,0:T(8,128)(2,1)S(1)}, u32[]{:S(2)}, u32[]{:S(2)}) collective-permute-start(bf16[4,2,72,640]{3,2,1,0:T(8,128)(2,1)} %collective-permute-done.12), channel_id=1, source_target_pairs={{4,0},{8,4},{12,8},{0,12},{20,16},{24,20},{28,24},{16,28},{36,32},... | collective-permute-start | bytes 2211848 | tf_op jit(solution)/shard_map/ppermute | solution.py:27
  65.6 13.1 %collective-permute-start.24 = (bf16[4,2,72,640]{3,2,1,0:T(8,128)(2,1)S(1)}, bf16[4,2,72,640]{3,2,1,0:T(8,128)(2,1)}, u32[]{:S(2)}, u32[]{:S(2)}) collective-permute-start(bf16[4,2,72,640]{3,2,1,0:T(8,128)(2,1)S(1)} %pad_maximum_fusion.1), channel_id=1, source_target_pairs={{12,0},{0,4},{4,8},{8,12},{28,16},{16,20},{20,24},{24,28},{44,32},... | collective-permute-start | bytes 2211848 | tf_op jit(solution)/shard_map/ppermute | solution.py:27
  66.0 4.7 %collective-permute-start.20 = (bf16[128,4608]{1,0:T(8,128)(2,1)}, bf16[128,4608]{1,0:T(8,128)(2,1)S(1)}, u32[]{:S(2)}, u32[]{:S(2)}) collective-permute-start(bf16[128,4608]{1,0:T(8,128)(2,1)} %collective-permute-done.17), channel_id=1, source_target_pairs={{0,1},{1,0},{2,3},{3,2},{4,5},{5,4},{6,7},{7,6},{8,9},{9,8},{10,11... | collective-permute-start | bytes 3538952 | tf_op jit(solution)/shard_map/ppermute | solution.py:31
  70.8 17.6 %collective-permute-start.29 = (f32[512,128]{1,0:T(8,128)S(1)}, f32[512,128]{1,0:T(8,128)S(1)}, u32[]{:S(2)}, u32[]{:S(2)}) collective-permute-start(f32[512,128]{1,0:T(8,128)S(1)} %add.143), channel_id=1, source_target_pairs={{0,2},{1,3},{2,0},{3,1},{4,6},{5,7},{6,4},{7,5},{8,10},{9,11},{10,... | collective-permute-start | bytes 786440 | tf_op jit(solution)/shard_map/ppermute | solution.py:31
  75.5 15.3 %collective-permute-start.21 = (bf16[576,384]{1,0:T(8,128)(2,1)S(1)}, bf16[576,384]{1,0:T(8,128)(2,1)S(1)}, u32[]{:S(2)}, u32[]{:S(2)}) collective-permute-start(bf16[576,384]{1,0:T(8,128)(2,1)S(1)} %collective-permute-done.18), channel_id=1, source_target_pairs={{32,0},{36,4},{40,8},{44,12},{48,16},{52,20},{56,24},{60,28},{64,3... | collective-permute-start | bytes 1327112 | tf_op jit(solution)/shard_map/ppermute | solution.py:27
  78.7 13.2 %collective-permute-start.22 = (bf16[576,384]{1,0:T(8,128)(2,1)S(1)}, bf16[576,384]{1,0:T(8,128)(2,1)S(1)}, u32[]{:S(2)}, u32[]{:S(2)}) collective-permute-start(bf16[576,384]{1,0:T(8,128)(2,1)S(1)} %collective-permute-done.19), channel_id=1, source_target_pairs={{224,0},{228,4},{232,8},{236,12},{240,16},{244,20},{248,24},{252,2... | collective-permute-start | bytes 1327112 | tf_op jit(solution)/shard_map/ppermute | solution.py:27
  84.8 25.6 %collective-permute-start.25 = (bf16[4,2,72,640]{3,2,1,0:T(8,128)(2,1)S(1)}, bf16[4,2,72,640]{3,2,1,0:T(8,128)(2,1)S(1)}, u32[]{:S(2)}, u32[]{:S(2)}) collective-permute-start(bf16[4,2,72,640]{3,2,1,0:T(8,128)(2,1)S(1)} %pad_maximum_fusion.1), channel_id=1, source_target_pairs={{4,0},{8,4},{12,8},{0,12},{20,16},{24,20},{28,24},{16,28},{36,32},... | collective-permute-start | bytes 2211848 | tf_op jit(solution)/shard_map/ppermute | solution.py:27
  84.9 25.5 %collective-permute-start.26 = (bf16[4,2,72,640]{3,2,1,0:T(8,128)(2,1)}, bf16[4,2,72,640]{3,2,1,0:T(8,128)(2,1)S(1)}, u32[]{:S(2)}, u32[]{:S(2)}) collective-permute-start(bf16[4,2,72,640]{3,2,1,0:T(8,128)(2,1)} %collective-permute-done.24), channel_id=1, source_target_pairs={{12,0},{0,4},{4,8},{8,12},{28,16},{16,20},{20,24},{24,28},{44,32},... | collective-permute-start | bytes 2211848 | tf_op jit(solution)/shard_map/ppermute | solution.py:27
  95.1 7.7 %collective-permute-start.28 = (bf16[288,384]{1,0:T(8,128)(2,1)S(1)}, bf16[288,384]{1,0:T(8,128)(2,1)S(1)}, u32[]{:S(2)}, u32[]{:S(2)}) collective-permute-start(bf16[288,384]{1,0:T(8,128)(2,1)S(1)} %slice.69), channel_id=1, source_target_pairs={{224,0},{228,4},{232,8},{236,12},{240,16},{244,20},{248,24},{252,2... | collective-permute-start | bytes 663560 | tf_op jit(solution)/shard_map/ppermute | solution.py:27
  97.1 7.0 %collective-permute-start.27 = (bf16[288,384]{1,0:T(8,128)(2,1)S(1)}, bf16[288,384]{1,0:T(8,128)(2,1)S(1)}, u32[]{:S(2)}, u32[]{:S(2)}) collective-permute-start(bf16[288,384]{1,0:T(8,128)(2,1)S(1)} %slice.68), channel_id=1, source_target_pairs={{32,0},{36,4},{40,8},{44,12},{48,16},{52,20},{56,24},{60,28},{64,3... | collective-permute-start | bytes 663560 | tf_op jit(solution)/shard_map/ppermute | solution.py:27
  (10 other events, 83.4 us)

commit v6 on v5

--- a/solution.py
+++ b/solution.py
@@ -105,24 +105,22 @@
     from_core = swap_tensor(output_gradient, 1)
     partial = jnp.dot(head_outputs, adapter_down_factors, preferred_element_type=jnp.float32)
     core_partial = swap_tensor(partial, 1)
-    other, from_core, own_rows, index_later = together(
-        other, from_core, output_gradient, tenant_index
-    )
+    partial, own_rows = together(partial, output_gradient)
+    from_chip = swap_tensor(own_rows, 2)
+    other, from_core, index_later = together(other, from_core, tenant_index)
 
     def pair(columns):
         mine, far = frozen_weight[:, columns], other[:, columns]
         return jnp.where(xl == 0, jnp.stack([mine, far]), jnp.stack([far, mine]))
 
-    pair_a, pair_b, own_rows = together(
-        pair(slice(0, a_width)), pair(slice(a_width, None)), own_rows
-    )
+    pair_a = pair(slice(0, a_width))
+    pair_b = pair(slice(a_width, None))
     a_p1, a_m1 = fetch(pair_a, dz=1), fetch(pair_a, dz=-1)
-    y_b = [fetch(pair_b, dy=dy) for dy in (1, 2, 3)]
-    from_chip = swap_tensor(own_rows, 2)
-
-    a_p1, a_m1, pair_a, core_partial = together(a_p1, a_m1, pair_a, core_partial)
+    y_b1, y_b3 = fetch(pair_b, dy=1), fetch(pair_b, dy=-1)
+
+    a_p1, a_m1, pair_a, pair_b, core_partial = together(a_p1, a_m1, pair_a, pair_b, core_partial)
     a_p2, a_m2 = fetch(a_p1, dz=1), fetch(a_m1, dz=-1)
-    a_p4 = fetch(pair_a, dz=4)
+    y_b = [y_b1, fetch(pair_b, dy=2), y_b3]
 
     def placed(array, chunk, dy):
         at = array.ndim - 3
@@ -135,24 +133,24 @@
         shape = chunk.shape[:at] + (NY,) + chunk.shape[at:]
         return jnp.broadcast_to(jnp.expand_dims(chunk, at), shape)
 
-    *y_b, pair_b, a_p1 = together(*y_b, pair_b, a_p1)
+    a_p2, a_m2, pair_b, *y_b = together(a_p2, a_m2, pair_b, *y_b)
+    low = jnp.stack([a_m1, pair_a, a_p1, a_p2])
+    low_p, low_m = fetch(low, dy=1), fetch(low, dy=-1)
+    a_p3, a_m3 = fetch(a_p2, dz=1), fetch(a_m2, dz=-1)
     b_own = spread(pair_b)
     for dy, chunk in zip((1, 2, 3), y_b):
         b_own = placed(b_own, chunk, dy)
     b_own = b_own.reshape(NX * NY * shard_rows, -1)
 
-    a_p2, a_m2, b_own = together(a_p2, a_m2, b_own)
-    low = jnp.stack([a_m1, pair_a, a_p1, a_p2])
-    low_p, low_m = fetch(low, dy=1), fetch(low, dy=-1)
-    a_p3, a_m3 = fetch(a_p2, dz=1), fetch(a_m2, dz=-1)
+    a_p3, a_m3, b_own, from_chip = together(a_p3, a_m3, b_own, from_chip)
+    a_p4 = fetch(a_p3, dz=1)
     b_p1, b_m1 = fetch(b_own, dz=1), fetch(b_own, dz=-1)
     high = jnp.stack([a_p3, a_p4, a_m3, a_m2])
 
-    b_p1, b_m1, low_p, low_m, high, from_chip, own_rows, partial, core_partial = together(
-        b_p1, b_m1, low_p, low_m, high, from_chip, own_rows, partial, core_partial
-    )
+    low_p, low_m, high = together(low_p, low_m, high)
+    low_o, high_m = fetch(low_p, dy=1), fetch(high, dy=-1)
+    b_p1, b_m1, low_p = together(b_p1, b_m1, low_p)
     b_p2, b_m2 = fetch(b_p1, dz=1), fetch(b_m1, dz=-1)
-    low_o, high_m = fetch(low_p, dy=1), fetch(high, dy=-1)
 
     from_both = swap_tensor(from_chip, 1)
     gradients = jnp.zeros((row_count, depth), output_gradient.dtype)
@@ -166,10 +164,6 @@
     far_sum = swap_tensor(chip_sum, 2)
     low_all = placed(placed(spread(low), low_p, 1), low_m, 3)
 
-    b_p2, b_m2, gradients = together(b_p2, b_m2, gradients)
-    b_p3, b_m3 = fetch(b_p2, dz=1), fetch(b_m2, dz=-1)
-    low_o, high_m, high, low_all, b_p2 = together(low_o, high_m, high, low_all, b_p2)
-    high_p, high_o = fetch(high, dy=1), fetch(high_m, dy=-1)
     by_z = split_columns(gradients, ((z + NZ - 1) % NZ).reshape(1))
 
     position = jnp.arange(row_count, dtype=jnp.int32)
@@ -186,27 +180,38 @@
     )
     live = active_rows.astype(jnp.float32)[:, None]
 
-    b_p3, b_m3, by_z, adapter_backward, down_factor_gradient = together(
-        b_p3, b_m3, by_z, adapter_backward, down_factor_gradient
-    )
+    def product(total, terms):
+        for slot, chunk in terms:
+            total = total + contract(by_z[slot], chunk.reshape(by_z.shape[2], -1), 1, 0)
+        return total
+
+    b_total = product(
+        ADAPTER_SCALE * contract(adapter_backward, adapter_down_factors[a_width:], 1, 1),
+        [(1, b_own), (0, b_m1), (2, b_p1)],
+    )
+
+    (
+        b_p2, b_m2, low_o, high_m, high, low_all, far_sum, by_z, adapter_backward,
+        down_factor_gradient, b_total,
+    ) = together(
+        b_p2, b_m2, low_o, high_m, high, low_all, far_sum, by_z, adapter_backward,
+        down_factor_gradient, b_total,
+    )
+    high_p, high_o = fetch(high, dy=1), fetch(high_m, dy=-1)
+    b_p3, b_m3 = fetch(b_p2, dz=1), fetch(b_m2, dz=-1)
+    b_p3, b_m3 = together(b_p3, b_m3)
     cut = b_own.shape[0] // 2 // 16 * 16
     b_p4, b_m4 = fetch(b_p3[:cut], dz=1), fetch(b_m3[cut:], dz=-1)
     adapter_input = ((chip_sum + far_sum) * select_rows).astype(jnp.bfloat16)
     (adapter_input,) = together(adapter_input)
     up_factor_gradient = ADAPTER_SCALE * contract(adapter_input, gradients, 0, 0)
 
-    def product(total, terms):
-        for slot, chunk in terms:
-            total = total + contract(by_z[slot], chunk.reshape(by_z.shape[2], -1), 1, 0)
-        return total
-
     b_p4, b_m4, up_factor_gradient, low_all, high_m = together(
         b_p4, b_m4, up_factor_gradient, low_all, high_m
     )
     b_total = product(
-        ADAPTER_SCALE * contract(adapter_backward, adapter_down_factors[a_width:], 1, 1),
-        [(1, b_own), (0, b_m1), (2, b_p1), (7, b_m2), (3, b_p2), (6, b_m3), (4, b_p3)]
-        + [(5, jnp.concatenate([b_p4, b_m4], 0))],
+        b_total,
+        [(7, b_m2), (3, b_p2), (6, b_m3), (4, b_p3), (5, jnp.concatenate([b_p4, b_m4], 0))],
     )
     b_out = jnp.where(active_rows[:, None], b_total, 0.0).astype(jnp.bfloat16)
     low_all = placed(low_all, low_o, 2)

time: 116 us -> 119 us (1.026)
  the two profiles are of different devices: /device:TPU:6 before, /device:TPU:24 now
where the time goes in v6:
time: 119 us
  starting transfers between devices  40.9 us (34%)
  waiting for transfers between devices  30.6 us (26%)
  matrix products  18.6 us (16%)
  local copies, waits for them, and re-layouts  14.9 us (13%)
  Pallas kernels  8.64 us (7%)
  other arithmetic  3.46 us (3%)
  between operations  1.74 us (1%)
    ppermute x25, starting transfers between devices, fetch(): return lax.ppermute(x, 'dp', pairs)  36.9 us
    ppermute x25, waiting for transfers between devices, fetch(): return lax.ppermute(x, 'dp', pairs)  23.9 us
    dot_general x16, matrix products, contract(): lax.dot_general(left, right, (((left_dim,), (right_dim,)), ((), ())), pre...  16.2 us
    ppermute x5, waiting for transfers between devices, swap_tensor(): return lax.ppermute(x, 'tensor', [(t, t ^ mask) for t in range(4)])  6.66 us
    dynamic_update_slice x4, local copies, waits for them, and re-layouts, body(): lax.dynamic_update_slice_in_dim(gradients, block, (tensor ^ mask) * part_...  5.67 us
    pallas_call x2, Pallas kernels, in_vmem(): pl.pallas_call(kernel, in_specs=[pl.BlockSpec(memory_space=pltpu.VMEM)] *...  4.76 us
    another operation x4, local copies, waits for them, and re-layouts, pair(): return jnp.where(xl == 0, jnp.stack([mine, far]), jnp.stack([far, mine]))  4.7 us
    ppermute x5, starting transfers between devices, swap_tensor(): return lax.ppermute(x, 'tensor', [(t, t ^ mask) for t in range(4)])  3.98 us
  transfers between devices with their start and end apart: 30, of which 11 were waited for; matrix products, arithmetic and copies ran while one was open for 31% of the time, Pallas kernels for 4%

profile of v6, /device:TPU:24, one launch (start us, length us, event | category | flops | bytes accessed | tf_op | source)
XLA Modules:
  0.0 118.7 jit_solution(6074003952480949260)
XLA Ops:
  0.7 1.6 %collective-permute-start = (bf16[72,1024]{1,0:T(8,128)(2,1)}, bf16[72,1024]{1,0:T(8,128)(2,1)}, u32[]{:S(2)}, u32[]{:S(2)}) collective-permute-start(bf16[72,1024]{1,0:T(8,128)(2,1)} %param.9), channel_id=1, source_target_pairs={{16,0},{20,4},{24,8},{28,12},{0,16},{4,20},{8,24},{12,28},{48,32},... | collective-permute-start | bytes 442376 | tf_op jit(solution)/shard_map/ppermute | solution.py:27
  2.2 2.4 %fusion.41 = f32[512,128]{1,0:T(8,128)} fusion(bf16[512,1024]{1,0:T(8,128)(2,1)} %head_ref.1, bf16[1024,128]{1,0:T(8,128)(2,1)} %param.10), kind=kOutput, calls=%fused_computation.83 | convolution fusion | flops 134217728 | bytes 1572864 | tf_op jit(solution)/shard_map/dot_general | solution.py:106
  5.2 2.7 %collective-permute-start.12 = (bf16[128,4608]{1,0:T(8,128)(2,1)}, bf16[128,4608]{1,0:T(8,128)(2,1)S(1)}, u32[]{:S(2)}, u32[]{:S(2)}) collective-permute-start(bf16[128,4608]{1,0:T(8,128)(2,1)} %param.8), channel_id=1, source_target_pairs={{0,2},{1,3},{2,0},{3,1},{4,6},{5,7},{6,4},{7,5},{8,10},{9,11},{10,... | collective-permute-start | bytes 3538952 | tf_op jit(solution)/shard_map/ppermute | solution.py:31
  7.9 1.4 %slice_bitcast_fusion.9 = bf16[1,72,384]{2,1,0:T(8,128)(2,1)} fusion(bf16[72,1024]{1,0:T(8,128)(2,1)} %param.9), kind=kLoop, calls=%fused_computation.67 | loop fusion | bytes 110592 | tf_op jit(solution)/shard_map/stack | solution.py:114
  9.3 1.5 %slice_bitcast_fusion.7 = bf16[1,72,640]{2,1,0:T(8,128)(2,1)} fusion(bf16[72,1024]{1,0:T(8,128)(2,1)} %param.9), kind=kLoop, calls=%fused_computation.65 | loop fusion | bytes 184320 | tf_op jit(solution)/shard_map/stack | solution.py:114
  10.9 2.4 %broadcast_in_dim.72 = bf16[512,4608]{1,0:T(8,128)(2,1)} broadcast(bf16[]{:T(256)} %constant.119.clone.1), dimensions={} | broadcast | bytes 4718594 | tf_op jit(solution)/shard_map/broadcast_in_dim | solution.py:156
  17.9 2.0 %collective-permute-start.3 = (bf16[2,72,640]{2,1,0:T(8,128)(2,1)S(1)}, bf16[2,72,640]{2,1,0:T(8,128)(2,1)S(1)}, u32[]{:S(2)}, u32[]{:S(2)}) collective-permute-start(bf16[2,72,640]{2,1,0:T(8,128)(2,1)S(1)} %maximum_select_fusion), channel_id=1, source_target_pairs={{224,0},{228,4},{232,8},{236,12},{240,16},{244,20},{248,24},{252,2... | collective-permute-start | bytes 552968 | tf_op jit(solution)/shard_map/ppermute | solution.py:27
  19.9 4.0 %collective-permute-start.2 = (bf16[2,72,640]{2,1,0:T(8,128)(2,1)S(1)}, bf16[2,72,640]{2,1,0:T(8,128)(2,1)S(1)}, u32[]{:S(2)}, u32[]{:S(2)}) collective-permute-start(bf16[2,72,640]{2,1,0:T(8,128)(2,1)S(1)} %maximum_select_fusion), channel_id=1, source_target_pairs={{32,0},{36,4},{40,8},{44,12},{48,16},{52,20},{56,24},{60,28},{64,3... | collective-permute-start | bytes 552968 | tf_op jit(solution)/shard_map/ppermute | solution.py:27
  25.1 1.9 %collective-permute-start.7 = (bf16[2,72,384]{2,1,0:T(8,128)(2,1)S(1)}, bf16[2,72,384]{2,1,0:T(8,128)(2,1)S(1)}, u32[]{:S(2)}, u32[]{:S(2)}) collective-permute-start(bf16[2,72,384]{2,1,0:T(8,128)(2,1)S(1)} %maximum_select_fusion.1), channel_id=1, source_target_pairs={{4,0},{8,4},{12,8},{0,12},{20,16},{24,20},{28,24},{16,28},{36,32},... | collective-permute-start | bytes 331784 | tf_op jit(solution)/shard_map/ppermute | solution.py:27
  27.0 1.3 %collective-permute-done.3 = bf16[2,72,640]{2,1,0:T(8,128)(2,1)S(1)} collective-permute-done((bf16[2,72,640]{2,1,0:T(8,128)(2,1)S(1)}, bf16[2,72,640]{2,1,0:T(8,128)(2,1)S(1)}, u32[]{:S(2)}, u32[]{:S(2)}) %collective-permute-start.3) | collective-permute-done | bytes 184352 | tf_op jit(solution)/shard_map/ppermute | solution.py:27
  29.6 3.0 %collective-permute-start.5 = (bf16[2,72,640]{2,1,0:T(8,128)(2,1)S(1)}, bf16[2,72,640]{2,1,0:T(8,128)(2,1)S(1)}, u32[]{:S(2)}, u32[]{:S(2)}) collective-permute-start(bf16[2,72,640]{2,1,0:T(8,128)(2,1)S(1)} %collective-permute-done.2), channel_id=1, source_target_pairs={{32,0},{36,4},{40,8},{44,12},{48,16},{52,20},{56,24},{60,28},{64,3... | collective-permute-start | bytes 552968 | tf_op jit(solution)/shard_map/ppermute | solution.py:27
  32.6 2.4 %constant_dynamic-update-slice_fusion.2 = bf16[512,4608]{1,0:T(8,128)(2,1)} fusion(bf16[512,4608]{1,0:T(8,128)(2,1)} %constant_dynamic-update-slice_fusion.3, bf16[128,4608]{1,0:T(8,128)(2,1)} %collective-permute-done.1, s32[]{:T(128)S(6)} %select_n.124), kind=kLoop, calls=%fused_computation.70 | loop fusion | bytes 2359300 | tf_op jit(solution)/shard_map/dynamic_update_slice | solution.py:158
  35.7 3.7 %collective-permute-done.6 = bf16[2,72,640]{2,1,0:T(8,128)(2,1)S(1)} collective-permute-done((bf16[2,72,640]{2,1,0:T(8,128)(2,1)S(1)}, bf16[2,72,640]{2,1,0:T(8,128)(2,1)S(1)}, u32[]{:S(2)}, u32[]{:S(2)}) %collective-permute-start.6) | collective-permute-done | bytes 184352 | tf_op jit(solution)/shard_map/ppermute | solution.py:27
  39.5 2.3 %collective-permute-start.16 = (bf16[4,2,72,640]{3,2,1,0:T(8,128)(2,1)S(1)}, bf16[4,2,72,640]{3,2,1,0:T(8,128)(2,1)S(1)}, u32[]{:S(2)}, u32[]{:S(2)}) collective-permute-start(bf16[4,2,72,640]{3,2,1,0:T(8,128)(2,1)S(1)} %pad_maximum_fusion), channel_id=1, source_target_pairs={{12,0},{0,4},{4,8},{8,12},{28,16},{16,20},{20,24},{24,28},{44,32},... | collective-permute-start | bytes 2211848 | tf_op jit(solution)/shard_map/ppermute | solution.py:27
  41.8 2.0 %collective-permute-start.11 = (bf16[2,72,640]{2,1,0:T(8,128)(2,1)S(1)}, bf16[2,72,640]{2,1,0:T(8,128)(2,1)S(1)}, u32[]{:S(2)}, u32[]{:S(2)}) collective-permute-start(bf16[2,72,640]{2,1,0:T(8,128)(2,1)S(1)} %collective-permute-done.6), channel_id=1, source_target_pairs={{224,0},{228,4},{232,8},{236,12},{240,16},{244,20},{248,24},{252,2... | collective-permute-start | bytes 552968 | tf_op jit(solution)/shard_map/ppermute | solution.py:27
  44.9 3.6 %collective-permute-done.11 = bf16[2,72,640]{2,1,0:T(8,128)(2,1)S(1)} collective-permute-done((bf16[2,72,640]{2,1,0:T(8,128)(2,1)S(1)}, bf16[2,72,640]{2,1,0:T(8,128)(2,1)S(1)}, u32[]{:S(2)}, u32[]{:S(2)}) %collective-permute-start.11) | collective-permute-done | bytes 184352 | tf_op jit(solution)/shard_map/ppermute | solution.py:27
  48.6 2.1 %collective-permute-start.14 = (bf16[576,384]{1,0:T(8,128)(2,1)S(1)}, bf16[576,384]{1,0:T(8,128)(2,1)S(1)}, u32[]{:S(2)}, u32[]{:S(2)}) collective-permute-start(bf16[576,384]{1,0:T(8,128)(2,1)S(1)} %bitcast.121), channel_id=1, source_target_pairs={{224,0},{228,4},{232,8},{236,12},{240,16},{244,20},{248,24},{252,2... | collective-permute-start | bytes 1327112 | tf_op jit(solution)/shard_map/ppermute | solution.py:27
  51.9 3.9 %collective-permute-done.17 = bf16[2,72,640]{2,1,0:T(8,128)(2,1)S(1)} collective-permute-done((bf16[2,72,640]{2,1,0:T(8,128)(2,1)S(1)}, bf16[2,72,640]{2,1,0:T(8,128)(2,1)S(1)}, u32[]{:S(2)}, u32[]{:S(2)}) %collective-permute-start.17) | collective-permute-done | bytes 184352 | tf_op jit(solution)/shard_map/ppermute | solution.py:27
  57.0 1.5 %collective-permute-done.15 = bf16[4,2,72,640]{3,2,1,0:T(8,128)(2,1)S(1)} collective-permute-done((bf16[4,2,72,640]{3,2,1,0:T(8,128)(2,1)S(1)}, bf16[4,2,72,640]{3,2,1,0:T(8,128)(2,1)S(1)}, u32[]{:S(2)}, u32[]{:S(2)}) %collective-permute-start.15) | collective-permute-done | bytes 737312 | tf_op jit(solution)/shard_map/ppermute | solution.py:27
  58.5 2.2 %collective-permute-done.13 = bf16[576,384]{1,0:T(8,128)(2,1)S(1)} collective-permute-done((bf16[576,384]{1,0:T(8,128)(2,1)S(1)}, bf16[576,384]{1,0:T(8,128)(2,1)S(1)}, u32[]{:S(2)}, u32[]{:S(2)}) %collective-permute-start.13) | collective-permute-done | bytes 442400 | tf_op jit(solution)/shard_map/ppermute | solution.py:27
  60.7 2.1 %collective-permute-start.18 = (bf16[576,384]{1,0:T(8,128)(2,1)S(1)}, bf16[576,384]{1,0:T(8,128)(2,1)S(1)}, u32[]{:S(2)}, u32[]{:S(2)}) collective-permute-start(bf16[576,384]{1,0:T(8,128)(2,1)S(1)} %collective-permute-done.13), channel_id=1, source_target_pairs={{32,0},{36,4},{40,8},{44,12},{48,16},{52,20},{56,24},{60,28},{64,3... | collective-permute-start | bytes 1327112 | tf_op jit(solution)/shard_map/ppermute | solution.py:27
  62.8 3.2 %collective-permute-start.21 = (bf16[4,2,72,640]{3,2,1,0:T(8,128)(2,1)S(1)}, bf16[4,2,72,640]{3,2,1,0:T(8,128)(2,1)S(1)}, u32[]{:S(2)}, u32[]{:S(2)}) collective-permute-start(bf16[4,2,72,640]{3,2,1,0:T(8,128)(2,1)S(1)} %pad_maximum_fusion.1), channel_id=1, source_target_pairs={{12,0},{0,4},{4,8},{8,12},{28,16},{16,20},{20,24},{24,28},{44,32},... | collective-permute-start | bytes 2211848 | tf_op jit(solution)/shard_map/ppermute | solution.py:27
  67.6 3.9 %shard_map.94.z_ref = bf16[8,512,576]{2,1,0:T(8,128)(2,1)S(1)} custom-call(s32[1]{0:T(128)} %bitcast.22.start_ref, bf16[512,4608]{1,0:T(8,128)(2,1)} %constant_dynamic-update-slice_fusion.g_ref), custom_call_target="tpu_custom_call" | custom-call | tf_op jit(solution)/shard_map/pallas_call | solution.py:49
  72.1 3.8 %fusion.3.back_ref = bf16[512,128]{1,0:T(8,128)(2,1)S(1)} fusion(bf16[512,4608]{1,0:T(8,128)(2,1)} %constant_dynamic-update-slice_fusion.g_ref, bf16[128,4608]{1,0:T(8,128)(2,1)S(1)} %copy-done, s32[128]{0:T(128)S(1)} %and_select_fusion, s32[512]{0:T(512)S(1)} %add_select_fusion, pred[512]{0:T(512)(128)(4,1)S(1)} %iota_compare_fusion.1), kind=kOutput, calls=%fused_computation.11 | convolution fusion | flops 604241920 | bytes 6032384 | tf_op jit(solution)/shard_map/dot_general | solution.py:15
  80.8 6.6 %collective-permute-done.23 = f32[512,128]{1,0:T(8,128)S(1)} collective-permute-done((f32[512,128]{1,0:T(8,128)S(1)}, f32[512,128]{1,0:T(8,128)S(1)}, u32[]{:S(2)}, u32[]{:S(2)}) %collective-permute-start.23) | collective-permute-done | bytes 262176 | tf_op jit(solution)/shard_map/ppermute | solution.py:31
  87.4 3.2 %collective-permute-start.26 = (bf16[576,384]{1,0:T(8,128)(2,1)S(1)}, bf16[576,384]{1,0:T(8,128)(2,1)S(1)}, u32[]{:S(2)}, u32[]{:S(2)}) collective-permute-start(bf16[576,384]{1,0:T(8,128)(2,1)S(1)} %collective-permute-done.18), channel_id=1, source_target_pairs={{32,0},{36,4},{40,8},{44,12},{48,16},{52,20},{56,24},{60,28},{64,3... | collective-permute-start | bytes 1327112 | tf_op jit(solution)/shard_map/ppermute | solution.py:27
  92.0 3.2 %collective-permute-start.25 = (bf16[4,2,72,640]{3,2,1,0:T(8,128)(2,1)S(1)}, bf16[4,2,72,640]{3,2,1,0:T(8,128)(2,1)S(1)}, u32[]{:S(2)}, u32[]{:S(2)}) collective-permute-start(bf16[4,2,72,640]{3,2,1,0:T(8,128)(2,1)S(1)} %collective-permute-done.21), channel_id=1, source_target_pairs={{12,0},{0,4},{4,8},{8,12},{28,16},{16,20},{20,24},{24,28},{44,32},... | collective-permute-start | bytes 2211848 | tf_op jit(solution)/shard_map/ppermute | solution.py:27
  95.2 4.6 %convolution_multiply_fusion = f32[128,4608]{1,0:T(8,128)} fusion(bf16[512,128]{1,0:T(8,128)(2,1)S(1)} %select_convert_fusion.1, bf16[512,4608]{1,0:T(8,128)(2,1)} %constant_dynamic-update-slice_fusion.g_ref), kind=kOutput, calls=%fused_computation | convolution fusion | flops 604569600 | bytes 7208960 | tf_op jit(solution)/shard_map/dot_general | solution.py:15
  99.8 2.6 %collective-permute-done.27 = bf16[576,384]{1,0:T(8,128)(2,1)S(1)} collective-permute-done((bf16[576,384]{1,0:T(8,128)(2,1)S(1)}, bf16[576,384]{1,0:T(8,128)(2,1)S(1)}, u32[]{:S(2)}, u32[]{:S(2)}) %collective-permute-start.27) | collective-permute-done | bytes 442400 | tf_op jit(solution)/shard_map/ppermute | solution.py:27
  103.1 3.2 %collective-permute-start.28 = (bf16[288,384]{1,0:T(8,128)(2,1)S(1)}, bf16[288,384]{1,0:T(8,128)(2,1)S(1)}, u32[]{:S(2)}, u32[]{:S(2)}) collective-permute-start(bf16[288,384]{1,0:T(8,128)(2,1)S(1)} %slice.78), channel_id=1, source_target_pairs={{32,0},{36,4},{40,8},{44,12},{48,16},{52,20},{56,24},{60,28},{64,3... | collective-permute-start | bytes 663560 | tf_op jit(solution)/shard_map/ppermute | solution.py:27
  106.8 3.4 %collective-permute-done.29 = bf16[288,384]{1,0:T(8,128)(2,1)S(1)} collective-permute-done((bf16[288,384]{1,0:T(8,128)(2,1)S(1)}, bf16[288,384]{1,0:T(8,128)(2,1)S(1)}, u32[]{:S(2)}, u32[]{:S(2)}) %collective-permute-start.29) | collective-permute-done | bytes 221216 | tf_op jit(solution)/shard_map/ppermute | solution.py:27
  115.3 3.5 %shard_map.96 = bf16[512,1024]{1,0:T(8,128)(2,1)} custom-call(bf16[8,512,576]{2,1,0:T(8,128)(2,1)S(1)} %shard_map.94.z_ref, bf16[4,576,640]{2,1,0:T(8,128)(2,1)S(1)} %bitcast.116, f32[512,640]{1,0:T(8,128)S(1)} %convolution_add_fusion.total_ref, f32[512,1]{1,0:T(8,128)S(1)} %fusion.35.live_ref, bf16[512,384]{1,0:T(8,128)(2,1)S(1)} %select_convert_fusion.b_ref), custom_call_target="tpu_custom_call" | custom-call | tf_op jit(solution)/shard_map/pallas_call | solution.py:77
  (91 shorter events, 25.6 us)
Async XLA Ops:
  0.6 71.4 %copy-start = (bf16[128,4608]{1,0:T(8,128)(2,1)S(1)}, bf16[128,4608]{1,0:T(8,128)(2,1)}, u32[]{:S(2)}) copy-start(bf16[128,4608]{1,0:T(8,128)(2,1)} %param.11) | copy-start | bytes 3538948
  0.7 14.5 %collective-permute-start = (bf16[72,1024]{1,0:T(8,128)(2,1)}, bf16[72,1024]{1,0:T(8,128)(2,1)}, u32[]{:S(2)}, u32[]{:S(2)}) collective-permute-start(bf16[72,1024]{1,0:T(8,128)(2,1)} %param.9), channel_id=1, source_target_pairs={{16,0},{20,4},{24,8},{28,12},{0,16},{4,20},{8,24},{12,28},{48,32},... | collective-permute-start | bytes 442376 | tf_op jit(solution)/shard_map/ppermute | solution.py:27
  4.6 20.5 %collective-permute-start.4 = (f32[512,128]{1,0:T(8,128)}, f32[512,128]{1,0:T(8,128)}, u32[]{:S(2)}, u32[]{:S(2)}) collective-permute-start(f32[512,128]{1,0:T(8,128)} %fusion.41), channel_id=1, source_target_pairs={{0,1},{1,0},{2,3},{3,2},{4,5},{5,4},{6,7},{7,6},{8,9},{9,8},{10,11... | collective-permute-start | bytes 786440 | tf_op jit(solution)/shard_map/ppermute | solution.py:31
  4.6 10.5 %collective-permute-start.1 = (bf16[128,4608]{1,0:T(8,128)(2,1)}, bf16[128,4608]{1,0:T(8,128)(2,1)}, u32[]{:S(2)}, u32[]{:S(2)}) collective-permute-start(bf16[128,4608]{1,0:T(8,128)(2,1)} %param.8), channel_id=1, source_target_pairs={{0,1},{1,0},{2,3},{3,2},{4,5},{5,4},{6,7},{7,6},{8,9},{9,8},{10,11... | collective-permute-start | bytes 3538952 | tf_op jit(solution)/shard_map/ppermute | solution.py:31
  5.2 38.8 %collective-permute-start.12 = (bf16[128,4608]{1,0:T(8,128)(2,1)}, bf16[128,4608]{1,0:T(8,128)(2,1)S(1)}, u32[]{:S(2)}, u32[]{:S(2)}) collective-permute-start(bf16[128,4608]{1,0:T(8,128)(2,1)} %param.8), channel_id=1, source_target_pairs={{0,2},{1,3},{2,0},{3,1},{4,6},{5,7},{6,4},{7,5},{8,10},{9,11},{10,... | collective-permute-start | bytes 3538952 | tf_op jit(solution)/shard_map/ppermute | solution.py:31
  15.1 33.4 %copy-start.4 = (s32[512]{0:T(512)S(1)}, s32[512]{0:T(512)}, u32[]{:S(2)}) copy-start(s32[512]{0:T(512)} %param.12) | copy-start | bytes 6148
  17.9 10.5 %collective-permute-start.3 = (bf16[2,72,640]{2,1,0:T(8,128)(2,1)S(1)}, bf16[2,72,640]{2,1,0:T(8,128)(2,1)S(1)}, u32[]{:S(2)}, u32[]{:S(2)}) collective-permute-start(bf16[2,72,640]{2,1,0:T(8,128)(2,1)S(1)} %maximum_select_fusion), channel_id=1, source_target_pairs={{224,0},{228,4},{232,8},{236,12},{240,16},{244,20},{248,24},{252,2... | collective-permute-start | bytes 552968 | tf_op jit(solution)/shard_map/ppermute | solution.py:27
  19.9 8.5 %collective-permute-start.2 = (bf16[2,72,640]{2,1,0:T(8,128)(2,1)S(1)}, bf16[2,72,640]{2,1,0:T(8,128)(2,1)S(1)}, u32[]{:S(2)}, u32[]{:S(2)}) collective-permute-start(bf16[2,72,640]{2,1,0:T(8,128)(2,1)S(1)} %maximum_select_fusion), channel_id=1, source_target_pairs={{32,0},{36,4},{40,8},{44,12},{48,16},{52,20},{56,24},{60,28},{64,3... | collective-permute-start | bytes 552968 | tf_op jit(solution)/shard_map/ppermute | solution.py:27
  24.8 7.8 %collective-permute-start.9 = (bf16[2,72,384]{2,1,0:T(8,128)(2,1)S(1)}, bf16[2,72,384]{2,1,0:T(8,128)(2,1)S(1)}, u32[]{:S(2)}, u32[]{:S(2)}) collective-permute-start(bf16[2,72,384]{2,1,0:T(8,128)(2,1)S(1)} %maximum_select_fusion.1), channel_id=1, source_target_pairs={{12,0},{0,4},{4,8},{8,12},{28,16},{16,20},{20,24},{24,28},{44,32},... | collective-permute-start | bytes 331784 | tf_op jit(solution)/shard_map/ppermute | solution.py:27
  25.1 9.9 %collective-permute-start.7 = (bf16[2,72,384]{2,1,0:T(8,128)(2,1)S(1)}, bf16[2,72,384]{2,1,0:T(8,128)(2,1)S(1)}, u32[]{:S(2)}, u32[]{:S(2)}) collective-permute-start(bf16[2,72,384]{2,1,0:T(8,128)(2,1)S(1)} %maximum_select_fusion.1), channel_id=1, source_target_pairs={{4,0},{8,4},{12,8},{0,12},{20,16},{24,20},{28,24},{16,28},{36,32},... | collective-permute-start | bytes 331784 | tf_op jit(solution)/shard_map/ppermute | solution.py:27
  28.3 6.7 %collective-permute-start.8 = (bf16[2,72,384]{2,1,0:T(8,128)(2,1)S(1)}, bf16[2,72,384]{2,1,0:T(8,128)(2,1)S(1)}, u32[]{:S(2)}, u32[]{:S(2)}) collective-permute-start(bf16[2,72,384]{2,1,0:T(8,128)(2,1)S(1)} %maximum_select_fusion.1), channel_id=1, source_target_pairs={{8,0},{12,4},{0,8},{4,12},{24,16},{28,20},{16,24},{20,28},{40,32},... | collective-permute-start | bytes 331784 | tf_op jit(solution)/shard_map/ppermute | solution.py:27
  29.6 6.1 %collective-permute-start.5 = (bf16[2,72,640]{2,1,0:T(8,128)(2,1)S(1)}, bf16[2,72,640]{2,1,0:T(8,128)(2,1)S(1)}, u32[]{:S(2)}, u32[]{:S(2)}) collective-permute-start(bf16[2,72,640]{2,1,0:T(8,128)(2,1)S(1)} %collective-permute-done.2), channel_id=1, source_target_pairs={{32,0},{36,4},{40,8},{44,12},{48,16},{52,20},{56,24},{60,28},{64,3... | collective-permute-start | bytes 552968 | tf_op jit(solution)/shard_map/ppermute | solution.py:27
  32.6 6.7 %collective-permute-start.6 = (bf16[2,72,640]{2,1,0:T(8,128)(2,1)S(1)}, bf16[2,72,640]{2,1,0:T(8,128)(2,1)S(1)}, u32[]{:S(2)}, u32[]{:S(2)}) collective-permute-start(bf16[2,72,640]{2,1,0:T(8,128)(2,1)S(1)} %collective-permute-done.3), channel_id=1, source_target_pairs={{224,0},{228,4},{232,8},{236,12},{240,16},{244,20},{248,24},{252,2... | collective-permute-start | bytes 552968 | tf_op jit(solution)/shard_map/ppermute | solution.py:27
  39.4 5.5 %collective-permute-start.10 = (bf16[2,72,640]{2,1,0:T(8,128)(2,1)S(1)}, bf16[2,72,640]{2,1,0:T(8,128)(2,1)S(1)}, u32[]{:S(2)}, u32[]{:S(2)}) collective-permute-start(bf16[2,72,640]{2,1,0:T(8,128)(2,1)S(1)} %collective-permute-done.5), channel_id=1, source_target_pairs={{32,0},{36,4},{40,8},{44,12},{48,16},{52,20},{56,24},{60,28},{64,3... | collective-permute-start | bytes 552968 | tf_op jit(solution)/shard_map/ppermute | solution.py:27
  39.5 17.5 %collective-permute-start.16 = (bf16[4,2,72,640]{3,2,1,0:T(8,128)(2,1)S(1)}, bf16[4,2,72,640]{3,2,1,0:T(8,128)(2,1)S(1)}, u32[]{:S(2)}, u32[]{:S(2)}) collective-permute-start(bf16[4,2,72,640]{3,2,1,0:T(8,128)(2,1)S(1)} %pad_maximum_fusion), channel_id=1, source_target_pairs={{12,0},{0,4},{4,8},{8,12},{28,16},{16,20},{20,24},{24,28},{44,32},... | collective-permute-start | bytes 2211848 | tf_op jit(solution)/shard_map/ppermute | solution.py:27
  41.8 16.7 %collective-permute-start.15 = (bf16[4,2,72,640]{3,2,1,0:T(8,128)(2,1)S(1)}, bf16[4,2,72,640]{3,2,1,0:T(8,128)(2,1)S(1)}, u32[]{:S(2)}, u32[]{:S(2)}) collective-permute-start(bf16[4,2,72,640]{3,2,1,0:T(8,128)(2,1)S(1)} %pad_maximum_fusion), channel_id=1, source_target_pairs={{4,0},{8,4},{12,8},{0,12},{20,16},{24,20},{28,24},{16,28},{36,32},... | collective-permute-start | bytes 2211848 | tf_op jit(solution)/shard_map/ppermute | solution.py:27
  41.8 6.8 %collective-permute-start.11 = (bf16[2,72,640]{2,1,0:T(8,128)(2,1)S(1)}, bf16[2,72,640]{2,1,0:T(8,128)(2,1)S(1)}, u32[]{:S(2)}, u32[]{:S(2)}) collective-permute-start(bf16[2,72,640]{2,1,0:T(8,128)(2,1)S(1)} %collective-permute-done.6), channel_id=1, source_target_pairs={{224,0},{228,4},{232,8},{236,12},{240,16},{244,20},{248,24},{252,2... | collective-permute-start | bytes 552968 | tf_op jit(solution)/shard_map/ppermute | solution.py:27
  48.6 7.2 %collective-permute-start.17 = (bf16[2,72,640]{2,1,0:T(8,128)(2,1)S(1)}, bf16[2,72,640]{2,1,0:T(8,128)(2,1)S(1)}, u32[]{:S(2)}, u32[]{:S(2)}) collective-permute-start(bf16[2,72,640]{2,1,0:T(8,128)(2,1)S(1)} %collective-permute-done.10), channel_id=1, source_target_pairs={{32,0},{36,4},{40,8},{44,12},{48,16},{52,20},{56,24},{60,28},{64,3... | collective-permute-start | bytes 552968 | tf_op jit(solution)/shard_map/ppermute | solution.py:27
  48.6 9.9 %collective-permute-start.14 = (bf16[576,384]{1,0:T(8,128)(2,1)S(1)}, bf16[576,384]{1,0:T(8,128)(2,1)S(1)}, u32[]{:S(2)}, u32[]{:S(2)}) collective-permute-start(bf16[576,384]{1,0:T(8,128)(2,1)S(1)} %bitcast.121), channel_id=1, source_target_pairs={{224,0},{228,4},{232,8},{236,12},{240,16},{244,20},{248,24},{252,2... | collective-permute-start | bytes 1327112 | tf_op jit(solution)/shard_map/ppermute | solution.py:27
  50.7 10.0 %collective-permute-start.13 = (bf16[576,384]{1,0:T(8,128)(2,1)S(1)}, bf16[576,384]{1,0:T(8,128)(2,1)S(1)}, u32[]{:S(2)}, u32[]{:S(2)}) collective-permute-start(bf16[576,384]{1,0:T(8,128)(2,1)S(1)} %bitcast.122), channel_id=1, source_target_pairs={{32,0},{36,4},{40,8},{44,12},{48,16},{52,20},{56,24},{60,28},{64,3... | collective-permute-start | bytes 1327112 | tf_op jit(solution)/shard_map/ppermute | solution.py:27
  55.8 10.8 %collective-permute-start.22 = (bf16[128,4608]{1,0:T(8,128)(2,1)S(1)}, bf16[128,4608]{1,0:T(8,128)(2,1)S(1)}, u32[]{:S(2)}, u32[]{:S(2)}) collective-permute-start(bf16[128,4608]{1,0:T(8,128)(2,1)S(1)} %collective-permute-done.12), channel_id=1, source_target_pairs={{0,1},{1,0},{2,3},{3,2},{4,5},{5,4},{6,7},{7,6},{8,9},{9,8},{10,11... | collective-permute-start | bytes 3538952 | tf_op jit(solution)/shard_map/ppermute | solution.py:31
  58.5 22.2 %collective-permute-start.20 = (bf16[4,2,72,640]{3,2,1,0:T(8,128)(2,1)S(1)}, bf16[4,2,72,640]{3,2,1,0:T(8,128)(2,1)S(1)}, u32[]{:S(2)}, u32[]{:S(2)}) collective-permute-start(bf16[4,2,72,640]{3,2,1,0:T(8,128)(2,1)S(1)} %collective-permute-done.15), channel_id=1, source_target_pairs={{4,0},{8,4},{12,8},{0,12},{20,16},{24,20},{28,24},{16,28},{36,32},... | collective-permute-start | bytes 2211848 | tf_op jit(solution)/shard_map/ppermute | solution.py:27
  60.7 20.1 %collective-permute-start.18 = (bf16[576,384]{1,0:T(8,128)(2,1)S(1)}, bf16[576,384]{1,0:T(8,128)(2,1)S(1)}, u32[]{:S(2)}, u32[]{:S(2)}) collective-permute-start(bf16[576,384]{1,0:T(8,128)(2,1)S(1)} %collective-permute-done.13), channel_id=1, source_target_pairs={{32,0},{36,4},{40,8},{44,12},{48,16},{52,20},{56,24},{60,28},{64,3... | collective-permute-start | bytes 1327112 | tf_op jit(solution)/shard_map/ppermute | solution.py:27
  62.8 17.9 %collective-permute-start.19 = (bf16[576,384]{1,0:T(8,128)(2,1)S(1)}, bf16[576,384]{1,0:T(8,128)(2,1)S(1)}, u32[]{:S(2)}, u32[]{:S(2)}) collective-permute-start(bf16[576,384]{1,0:T(8,128)(2,1)S(1)} %collective-permute-done.14), channel_id=1, source_target_pairs={{224,0},{228,4},{232,8},{236,12},{240,16},{244,20},{248,24},{252,2... | collective-permute-start | bytes 1327112 | tf_op jit(solution)/shard_map/ppermute | solution.py:27
  62.8 17.9 %collective-permute-start.21 = (bf16[4,2,72,640]{3,2,1,0:T(8,128)(2,1)S(1)}, bf16[4,2,72,640]{3,2,1,0:T(8,128)(2,1)S(1)}, u32[]{:S(2)}, u32[]{:S(2)}) collective-permute-start(bf16[4,2,72,640]{3,2,1,0:T(8,128)(2,1)S(1)} %pad_maximum_fusion.1), channel_id=1, source_target_pairs={{12,0},{0,4},{4,8},{8,12},{28,16},{16,20},{20,24},{24,28},{44,32},... | collective-permute-start | bytes 2211848 | tf_op jit(solution)/shard_map/ppermute | solution.py:27
  79.4 8.0 %collective-permute-start.23 = (f32[512,128]{1,0:T(8,128)S(1)}, f32[512,128]{1,0:T(8,128)S(1)}, u32[]{:S(2)}, u32[]{:S(2)}) collective-permute-start(f32[512,128]{1,0:T(8,128)S(1)} %add.137), channel_id=1, source_target_pairs={{0,2},{1,3},{2,0},{3,1},{4,6},{5,7},{6,4},{7,5},{8,10},{9,11},{10,... | collective-permute-start | bytes 786440 | tf_op jit(solution)/shard_map/ppermute | solution.py:31
  87.4 12.4 %collective-permute-start.26 = (bf16[576,384]{1,0:T(8,128)(2,1)S(1)}, bf16[576,384]{1,0:T(8,128)(2,1)S(1)}, u32[]{:S(2)}, u32[]{:S(2)}) collective-permute-start(bf16[576,384]{1,0:T(8,128)(2,1)S(1)} %collective-permute-done.18), channel_id=1, source_target_pairs={{32,0},{36,4},{40,8},{44,12},{48,16},{52,20},{56,24},{60,28},{64,3... | collective-permute-start | bytes 1327112 | tf_op jit(solution)/shard_map/ppermute | solution.py:27
  90.6 11.7 %collective-permute-start.27 = (bf16[576,384]{1,0:T(8,128)(2,1)S(1)}, bf16[576,384]{1,0:T(8,128)(2,1)S(1)}, u32[]{:S(2)}, u32[]{:S(2)}) collective-permute-start(bf16[576,384]{1,0:T(8,128)(2,1)S(1)} %collective-permute-done.19), channel_id=1, source_target_pairs={{224,0},{228,4},{232,8},{236,12},{240,16},{244,20},{248,24},{252,2... | collective-permute-start | bytes 1327112 | tf_op jit(solution)/shard_map/ppermute | solution.py:27
  91.9 23.1 %collective-permute-start.24 = (bf16[4,2,72,640]{3,2,1,0:T(8,128)(2,1)S(1)}, bf16[4,2,72,640]{3,2,1,0:T(8,128)(2,1)S(1)}, u32[]{:S(2)}, u32[]{:S(2)}) collective-permute-start(bf16[4,2,72,640]{3,2,1,0:T(8,128)(2,1)S(1)} %pad_maximum_fusion.1), channel_id=1, source_target_pairs={{4,0},{8,4},{12,8},{0,12},{20,16},{24,20},{28,24},{16,28},{36,32},... | collective-permute-start | bytes 2211848 | tf_op jit(solution)/shard_map/ppermute | solution.py:27
  92.0 23.0 %collective-permute-start.25 = (bf16[4,2,72,640]{3,2,1,0:T(8,128)(2,1)S(1)}, bf16[4,2,72,640]{3,2,1,0:T(8,128)(2,1)S(1)}, u32[]{:S(2)}, u32[]{:S(2)}) collective-permute-start(bf16[4,2,72,640]{3,2,1,0:T(8,128)(2,1)S(1)} %collective-permute-done.21), channel_id=1, source_target_pairs={{12,0},{0,4},{4,8},{8,12},{28,16},{16,20},{20,24},{24,28},{44,32},... | collective-permute-start | bytes 2211848 | tf_op jit(solution)/shard_map/ppermute | solution.py:27
  103.0 7.2 %collective-permute-start.29 = (bf16[288,384]{1,0:T(8,128)(2,1)S(1)}, bf16[288,384]{1,0:T(8,128)(2,1)S(1)}, u32[]{:S(2)}, u32[]{:S(2)}) collective-permute-start(bf16[288,384]{1,0:T(8,128)(2,1)S(1)} %slice.79), channel_id=1, source_target_pairs={{224,0},{228,4},{232,8},{236,12},{240,16},{244,20},{248,24},{252,2... | collective-permute-start | bytes 663560 | tf_op jit(solution)/shard_map/ppermute | solution.py:27
  103.1 7.1 %collective-permute-start.28 = (bf16[288,384]{1,0:T(8,128)(2,1)S(1)}, bf16[288,384]{1,0:T(8,128)(2,1)S(1)}, u32[]{:S(2)}, u32[]{:S(2)}) collective-permute-start(bf16[288,384]{1,0:T(8,128)(2,1)S(1)} %slice.78), channel_id=1, source_target_pairs={{32,0},{36,4},{40,8},{44,12},{48,16},{52,20},{56,24},{60,28},{64,3... | collective-permute-start | bytes 663560 | tf_op jit(solution)/shard_map/ppermute | solution.py:27
  (3 other events, 18.2 us)

commit v7 on v6

--- a/solution.py
+++ b/solution.py
@@ -67,6 +67,26 @@
         total += contract(z_ref[NZ - count + i], w_ref[i], 1, 0)
     out_ref[:, :width] = jnp.where(live_ref[...] > 0, total, 0.0).astype(out_ref.dtype)
     out_ref[:, width:] = b_ref[...]
+
+
+def pair_kernel(x_ref, mine_ref, far_ref, a_ref, b_ref):
+    width = a_ref.shape[2]
+    x = x_ref[0]
+    for slot, ref in ((x, mine_ref), (1 - x, far_ref)):
+        a_ref[slot] = ref[:, :width]
+        b_ref[slot] = ref[:, width:]
+
+
+def pairs(x, mine, far, a_width):
+    rows, width = mine.shape
+    shapes = [(NX, rows, a_width), (NX, rows, width - a_width)]
+    vmem = pl.BlockSpec(memory_space=pltpu.VMEM)
+    return pl.pallas_call(
+        pair_kernel,
+        in_specs=[pl.BlockSpec(memory_space=pltpu.SMEM), vmem, vmem],
+        out_specs=[vmem, vmem],
+        out_shape=[jax.ShapeDtypeStruct(shape, mine.dtype) for shape in shapes],
+    )(x, mine, far)
 
 
 def down_kernel(head_ref, back_ref, out_ref):
@@ -109,12 +129,7 @@
     from_chip = swap_tensor(own_rows, 2)
     other, from_core, index_later = together(other, from_core, tenant_index)
 
-    def pair(columns):
-        mine, far = frozen_weight[:, columns], other[:, columns]
-        return jnp.where(xl == 0, jnp.stack([mine, far]), jnp.stack([far, mine]))
-
-    pair_a = pair(slice(0, a_width))
-    pair_b = pair(slice(a_width, None))
+    pair_a, pair_b = pairs(xl.reshape(1), frozen_weight, other, a_width)
     a_p1, a_m1 = fetch(pair_a, dz=1), fetch(pair_a, dz=-1)
     y_b1, y_b3 = fetch(pair_b, dy=1), fetch(pair_b, dy=-1)
 
@@ -142,14 +157,20 @@
         b_own = placed(b_own, chunk, dy)
     b_own = b_own.reshape(NX * NY * shard_rows, -1)
 
-    a_p3, a_m3, b_own, from_chip = together(a_p3, a_m3, b_own, from_chip)
+    a_p3, a_m3, b_own, from_chip, partial, core_partial = together(
+        a_p3, a_m3, b_own, from_chip, partial, core_partial
+    )
+    chip_sum = partial + core_partial
+    far_sum = swap_tensor(chip_sum, 2)
     a_p4 = fetch(a_p3, dz=1)
     b_p1, b_m1 = fetch(b_own, dz=1), fetch(b_own, dz=-1)
     high = jnp.stack([a_p3, a_p4, a_m3, a_m2])
 
     low_p, low_m, high = together(low_p, low_m, high)
     low_o, high_m = fetch(low_p, dy=1), fetch(high, dy=-1)
-    b_p1, b_m1, low_p = together(b_p1, b_m1, low_p)
+    b_p1, b_m1, low_p, far_sum, own_rows, from_core = together(
+        b_p1, b_m1, low_p, far_sum, own_rows, from_core
+    )
     b_p2, b_m2 = fetch(b_p1, dz=1), fetch(b_m1, dz=-1)
 
     from_both = swap_tensor(from_chip, 1)
@@ -159,9 +180,6 @@
             gradients, block, (tensor ^ mask) * part_rows, 0
         )
 
-    from_both, partial, core_partial = together(from_both, partial, core_partial)
-    chip_sum = partial + core_partial
-    far_sum = swap_tensor(chip_sum, 2)
     low_all = placed(placed(spread(low), low_p, 1), low_m, 3)
 
     by_z = split_columns(gradients, ((z + NZ - 1) % NZ).reshape(1))
@@ -191,10 +209,10 @@
     )
 
     (
-        b_p2, b_m2, low_o, high_m, high, low_all, far_sum, by_z, adapter_backward,
+        b_p2, b_m2, low_o, high_m, high, low_all, by_z, adapter_backward,
         down_factor_gradient, b_total,
     ) = together(
-        b_p2, b_m2, low_o, high_m, high, low_all, far_sum, by_z, adapter_backward,
+        b_p2, b_m2, low_o, high_m, high, low_all, by_z, adapter_backward,
         down_factor_gradient, b_total,
     )
     high_p, high_o = fetch(high, dy=1), fetch(high_m, dy=-1)

time: 119 us -> 113 us (0.950)
  the two profiles are of different devices: /device:TPU:24 before, /device:TPU:6 now
where the time goes in v7:
time: 113 us; the launch traced here: 112 us
  starting transfers between devices  40.6 us (36%)
  waiting for transfers between devices  31.5 us (28%)
  matrix products  18 us (16%)
  local copies, waits for them, and re-layouts  8.53 us (8%)
  Pallas kernels  8.07 us (7%)
  other arithmetic  3.65 us (3%)
  between operations  1.71 us (2%)
    ppermute x25, starting transfers between devices, fetch(): return lax.ppermute(x, 'dp', pairs)  37.8 us
    ppermute x25, waiting for transfers between devices, fetch(): return lax.ppermute(x, 'dp', pairs)  26 us
    dot_general x16, matrix products, contract(): lax.dot_general(left, right, (((left_dim,), (right_dim,)), ((), ())), pre...  15.6 us
    ppermute x5, waiting for transfers between devices, swap_tensor(): return lax.ppermute(x, 'tensor', [(t, t ^ mask) for t in range(4)])  5.49 us
    pallas_call x2, Pallas kernels, in_vmem(): pl.pallas_call(kernel, in_specs=[pl.BlockSpec(memory_space=pltpu.VMEM)] *...  4.76 us
    dynamic_update_slice x8, local copies, waits for them, and re-layouts, placed(): lax.dynamic_update_slice_in_dim(array, jnp.expand_dims(chunk, at), (y + d...  4.15 us
    ppermute x5, starting transfers between devices, swap_tensor(): return lax.ppermute(x, 'tensor', [(t, t ^ mask) for t in range(4)])  2.85 us
    dot_general x1, matrix products, body(): jnp.dot(head_outputs, adapter_down_factors, preferred_element_type=jnp.fl...  2.41 us
  transfers between devices with their start and end apart: 30, of which 12 were waited for; matrix products, arithmetic and copies ran while one was open for 25% of the time, Pallas kernels for 4%

profile of v7, /device:TPU:6, one launch (start us, length us, event | category | flops | bytes accessed | tf_op | source)
XLA Modules:
  0.0 112.0 jit_solution(3037098510151542514)
XLA Ops:
  1.7 2.4 %fusion.41 = f32[512,128]{1,0:T(8,128)} fusion(bf16[512,1024]{1,0:T(8,128)(2,1)} %head_ref.1, bf16[1024,128]{1,0:T(8,128)(2,1)} %param.10), kind=kOutput, calls=%fused_computation.77 | convolution fusion | flops 134217728 | bytes 1572864 | tf_op jit(solution)/shard_map/dot_general | solution.py:126
  4.2 3.0 %collective-permute-done.far_ref = bf16[72,1024]{1,0:T(8,128)(2,1)S(1)} collective-permute-done((bf16[72,1024]{1,0:T(8,128)(2,1)}, bf16[72,1024]{1,0:T(8,128)(2,1)S(1)}, u32[]{:S(2)}, u32[]{:S(2)}) %collective-permute-start) | collective-permute-done | bytes 147488 | tf_op jit(solution)/shard_map/ppermute | solution.py:27
  7.9 1.7 %shard_map.94 = (bf16[2,72,640]{2,1,0:T(8,128)(2,1)}, bf16[2,72,384]{2,1,0:T(8,128)(2,1)}) custom-call(s32[1]{0:T(128)} %bitcast.x_ref, bf16[72,1024]{1,0:T(8,128)(2,1)} %mine_ref.1, bf16[72,1024]{1,0:T(8,128)(2,1)} %copy-done.4), custom_call_target="tpu_custom_call" | custom-call | tf_op jit(solution)/shard_map/pallas_call | solution.py:84
  9.6 1.9 %collective-permute-start.3 = (bf16[2,72,640]{2,1,0:T(8,128)(2,1)}, bf16[2,72,640]{2,1,0:T(8,128)(2,1)}, u32[]{:S(2)}, u32[]{:S(2)}) collective-permute-start(bf16[2,72,640]{2,1,0:T(8,128)(2,1)} %get-tuple-element.74), channel_id=1, source_target_pairs={{224,0},{228,4},{232,8},{236,12},{240,16},{244,20},{248,24},{252,2... | collective-permute-start | bytes 552968 | tf_op jit(solution)/shard_map/ppermute | solution.py:27
  11.5 3.9 %collective-permute-start.2 = (bf16[2,72,640]{2,1,0:T(8,128)(2,1)}, bf16[2,72,640]{2,1,0:T(8,128)(2,1)}, u32[]{:S(2)}, u32[]{:S(2)}) collective-permute-start(bf16[2,72,640]{2,1,0:T(8,128)(2,1)} %get-tuple-element.74), channel_id=1, source_target_pairs={{32,0},{36,4},{40,8},{44,12},{48,16},{52,20},{56,24},{60,28},{64,3... | collective-permute-start | bytes 552968 | tf_op jit(solution)/shard_map/ppermute | solution.py:27
  15.5 1.4 %collective-permute-start.12 = (bf16[128,4608]{1,0:T(8,128)(2,1)}, bf16[128,4608]{1,0:T(8,128)(2,1)S(1)}, u32[]{:S(2)}, u32[]{:S(2)}) collective-permute-start(bf16[128,4608]{1,0:T(8,128)(2,1)} %param.8), channel_id=1, source_target_pairs={{0,2},{1,3},{2,0},{3,1},{4,6},{5,7},{6,4},{7,5},{8,10},{9,11},{10,... | collective-permute-start | bytes 3538952 | tf_op jit(solution)/shard_map/ppermute | solution.py:31
  16.9 1.6 %collective-permute-start.9 = (bf16[2,72,384]{2,1,0:T(8,128)(2,1)}, bf16[2,72,384]{2,1,0:T(8,128)(2,1)}, u32[]{:S(2)}, u32[]{:S(2)}) collective-permute-start(bf16[2,72,384]{2,1,0:T(8,128)(2,1)} %get-tuple-element.66), channel_id=1, source_target_pairs={{12,0},{0,4},{4,8},{8,12},{28,16},{16,20},{20,24},{24,28},{44,32},... | collective-permute-start | bytes 331784 | tf_op jit(solution)/shard_map/ppermute | solution.py:27
  18.4 1.8 %collective-permute-done.3 = bf16[2,72,640]{2,1,0:T(8,128)(2,1)} collective-permute-done((bf16[2,72,640]{2,1,0:T(8,128)(2,1)}, bf16[2,72,640]{2,1,0:T(8,128)(2,1)}, u32[]{:S(2)}, u32[]{:S(2)}) %collective-permute-start.3) | collective-permute-done | bytes 184352 | tf_op jit(solution)/shard_map/ppermute | solution.py:27
  20.2 3.0 %collective-permute-start.5 = (bf16[2,72,640]{2,1,0:T(8,128)(2,1)}, bf16[2,72,640]{2,1,0:T(8,128)(2,1)}, u32[]{:S(2)}, u32[]{:S(2)}) collective-permute-start(bf16[2,72,640]{2,1,0:T(8,128)(2,1)} %collective-permute-done.2), channel_id=1, source_target_pairs={{32,0},{36,4},{40,8},{44,12},{48,16},{52,20},{56,24},{60,28},{64,3... | collective-permute-start | bytes 552968 | tf_op jit(solution)/shard_map/ppermute | solution.py:27
  23.8 3.1 %collective-permute-start.7 = (bf16[2,72,384]{2,1,0:T(8,128)(2,1)}, bf16[2,72,384]{2,1,0:T(8,128)(2,1)S(1)}, u32[]{:S(2)}, u32[]{:S(2)}) collective-permute-start(bf16[2,72,384]{2,1,0:T(8,128)(2,1)} %get-tuple-element.66), channel_id=1, source_target_pairs={{4,0},{8,4},{12,8},{0,12},{20,16},{24,20},{28,24},{16,28},{36,32},... | collective-permute-start | bytes 331784 | tf_op jit(solution)/shard_map/ppermute | solution.py:27
  27.6 3.3 %collective-permute-done.7 = bf16[2,72,384]{2,1,0:T(8,128)(2,1)S(1)} collective-permute-done((bf16[2,72,384]{2,1,0:T(8,128)(2,1)}, bf16[2,72,384]{2,1,0:T(8,128)(2,1)S(1)}, u32[]{:S(2)}, u32[]{:S(2)}) %collective-permute-start.7) | collective-permute-done | bytes 110624 | tf_op jit(solution)/shard_map/ppermute | solution.py:27
  30.9 2.5 %collective-permute-done.8 = bf16[2,72,384]{2,1,0:T(8,128)(2,1)S(1)} collective-permute-done((bf16[2,72,384]{2,1,0:T(8,128)(2,1)}, bf16[2,72,384]{2,1,0:T(8,128)(2,1)S(1)}, u32[]{:S(2)}, u32[]{:S(2)}) %collective-permute-start.8) | collective-permute-done | bytes 110624 | tf_op jit(solution)/shard_map/ppermute | solution.py:27
  33.4 3.2 %collective-permute-start.10 = (bf16[2,72,640]{2,1,0:T(8,128)(2,1)}, bf16[2,72,640]{2,1,0:T(8,128)(2,1)S(1)}, u32[]{:S(2)}, u32[]{:S(2)}) collective-permute-start(bf16[2,72,640]{2,1,0:T(8,128)(2,1)} %collective-permute-done.5), channel_id=1, source_target_pairs={{32,0},{36,4},{40,8},{44,12},{48,16},{52,20},{56,24},{60,28},{64,3... | collective-permute-start | bytes 552968 | tf_op jit(solution)/shard_map/ppermute | solution.py:27
  38.0 3.2 %collective-permute-start.15 = (bf16[4,2,72,640]{3,2,1,0:T(8,128)(2,1)S(1)}, bf16[4,2,72,640]{3,2,1,0:T(8,128)(2,1)}, u32[]{:S(2)}, u32[]{:S(2)}) collective-permute-start(bf16[4,2,72,640]{3,2,1,0:T(8,128)(2,1)S(1)} %pad_maximum_fusion), channel_id=1, source_target_pairs={{4,0},{8,4},{12,8},{0,12},{20,16},{24,20},{28,24},{16,28},{36,32},... | collective-permute-start | bytes 2211848 | tf_op jit(solution)/shard_map/ppermute | solution.py:27
  44.4 4.1 %collective-permute-done.11 = bf16[2,72,640]{2,1,0:T(8,128)(2,1)S(1)} collective-permute-done((bf16[2,72,640]{2,1,0:T(8,128)(2,1)}, bf16[2,72,640]{2,1,0:T(8,128)(2,1)S(1)}, u32[]{:S(2)}, u32[]{:S(2)}) %collective-permute-start.11) | collective-permute-done | bytes 184352 | tf_op jit(solution)/shard_map/ppermute | solution.py:27
  48.6 2.0 %collective-permute-start.14 = (bf16[576,384]{1,0:T(8,128)(2,1)S(1)}, bf16[576,384]{1,0:T(8,128)(2,1)}, u32[]{:S(2)}, u32[]{:S(2)}) collective-permute-start(bf16[576,384]{1,0:T(8,128)(2,1)S(1)} %bitcast.116), channel_id=1, source_target_pairs={{224,0},{228,4},{232,8},{236,12},{240,16},{244,20},{248,24},{252,2... | collective-permute-start | bytes 1327112 | tf_op jit(solution)/shard_map/ppermute | solution.py:27
  52.9 2.0 %collective-permute-done.17 = bf16[2,72,640]{2,1,0:T(8,128)(2,1)S(1)} collective-permute-done((bf16[2,72,640]{2,1,0:T(8,128)(2,1)S(1)}, bf16[2,72,640]{2,1,0:T(8,128)(2,1)S(1)}, u32[]{:S(2)}, u32[]{:S(2)}) %collective-permute-start.17) | collective-permute-done | bytes 184352 | tf_op jit(solution)/shard_map/ppermute | solution.py:27
  58.5 4.3 %collective-permute-done.18 = f32[512,128]{1,0:T(8,128)S(1)} collective-permute-done((f32[512,128]{1,0:T(8,128)S(1)}, f32[512,128]{1,0:T(8,128)S(1)}, u32[]{:S(2)}, u32[]{:S(2)}) %collective-permute-start.18) | collective-permute-done | bytes 262176 | tf_op jit(solution)/shard_map/ppermute | solution.py:31
  63.0 2.6 %collective-permute-start.19 = (bf16[576,384]{1,0:T(8,128)(2,1)}, bf16[576,384]{1,0:T(8,128)(2,1)}, u32[]{:S(2)}, u32[]{:S(2)}) collective-permute-start(bf16[576,384]{1,0:T(8,128)(2,1)} %collective-permute-done.13), channel_id=1, source_target_pairs={{32,0},{36,4},{40,8},{44,12},{48,16},{52,20},{56,24},{60,28},{64,3... | collective-permute-start | bytes 1327112 | tf_op jit(solution)/shard_map/ppermute | solution.py:27
  68.8 1.6 %shard_map.95.z_ref = bf16[8,512,576]{2,1,0:T(8,128)(2,1)S(1)} custom-call(s32[1]{0:T(128)} %bitcast.20.start_ref, bf16[512,4608]{1,0:T(8,128)(2,1)S(1)} %constant_dynamic-update-slice_fusion.g_ref), custom_call_target="tpu_custom_call" | custom-call | tf_op jit(solution)/shard_map/pallas_call | solution.py:49
  70.4 1.5 %fusion.4 = f32[512,384]{1,0:T(8,128)S(1)} fusion(bf16[576,384]{1,0:T(8,128)(2,1)} %collective-permute-done.13, bf16[8,512,576]{2,1,0:T(8,128)(2,1)S(1)} %shard_map.95.z_ref), kind=kOutput, calls=%fused_computation.22 | convolution fusion | flops 226492416 | bytes 1884160 | tf_op jit(solution)/shard_map/dot_general | solution.py:15
  71.9 1.5 %fusion.5 = f32[512,384]{1,0:T(8,128)S(1)} fusion(bf16[576,384]{1,0:T(8,128)(2,1)} %collective-permute-done.14, bf16[8,512,576]{2,1,0:T(8,128)(2,1)S(1)} %shard_map.95.z_ref), kind=kOutput, calls=%fused_computation.24 | convolution fusion | flops 226492416 | bytes 1884160 | tf_op jit(solution)/shard_map/dot_general | solution.py:15
  77.4 2.2 %convolution_multiply_fusion = f32[128,4608]{1,0:T(8,128)} fusion(bf16[512,128]{1,0:T(8,128)(2,1)S(1)} %select_convert_fusion.1, bf16[512,4608]{1,0:T(8,128)(2,1)S(1)} %constant_dynamic-update-slice_fusion.g_ref), kind=kOutput, calls=%fused_computation | convolution fusion | flops 604569600 | bytes 7208960 | tf_op jit(solution)/shard_map/dot_general | solution.py:15
  80.4 3.0 %collective-permute-start.26 = (bf16[576,384]{1,0:T(8,128)(2,1)}, bf16[576,384]{1,0:T(8,128)(2,1)S(1)}, u32[]{:S(2)}, u32[]{:S(2)}) collective-permute-start(bf16[576,384]{1,0:T(8,128)(2,1)} %collective-permute-done.19), channel_id=1, source_target_pairs={{32,0},{36,4},{40,8},{44,12},{48,16},{52,20},{56,24},{60,28},{64,3... | collective-permute-start | bytes 1327112 | tf_op jit(solution)/shard_map/ppermute | solution.py:27
  83.4 2.8 %collective-permute-start.24 = (bf16[4,2,72,640]{3,2,1,0:T(8,128)(2,1)S(1)}, bf16[4,2,72,640]{3,2,1,0:T(8,128)(2,1)S(1)}, u32[]{:S(2)}, u32[]{:S(2)}) collective-permute-start(bf16[4,2,72,640]{3,2,1,0:T(8,128)(2,1)S(1)} %pad_maximum_fusion.1), channel_id=1, source_target_pairs={{4,0},{8,4},{12,8},{0,12},{20,16},{24,20},{28,24},{16,28},{36,32},... | collective-permute-start | bytes 2211848 | tf_op jit(solution)/shard_map/ppermute | solution.py:27
  86.2 1.5 %fusion.19 = f32[512,384]{1,0:T(8,128)S(1)} fusion(bf16[576,384]{1,0:T(8,128)(2,1)} %collective-permute-done.19, bf16[8,512,576]{2,1,0:T(8,128)(2,1)S(1)} %shard_map.95.z_ref), kind=kOutput, calls=%fused_computation.37 | convolution fusion | flops 226492416 | bytes 1884160 | tf_op jit(solution)/shard_map/dot_general | solution.py:15
  87.7 1.5 %fusion.21 = f32[512,384]{1,0:T(8,128)S(1)} fusion(bf16[576,384]{1,0:T(8,128)(2,1)} %collective-permute-done.20, bf16[8,512,576]{2,1,0:T(8,128)(2,1)S(1)} %shard_map.95.z_ref), kind=kOutput, calls=%fused_computation.39 | convolution fusion | flops 226492416 | bytes 1884160 | tf_op jit(solution)/shard_map/dot_general | solution.py:15
  89.5 4.8 %collective-permute-done.27 = bf16[576,384]{1,0:T(8,128)(2,1)S(1)} collective-permute-done((bf16[576,384]{1,0:T(8,128)(2,1)}, bf16[576,384]{1,0:T(8,128)(2,1)S(1)}, u32[]{:S(2)}, u32[]{:S(2)}) %collective-permute-start.27) | collective-permute-done | bytes 442400 | tf_op jit(solution)/shard_map/ppermute | solution.py:27
  95.0 3.2 %collective-permute-start.28 = (bf16[288,384]{1,0:T(8,128)(2,1)S(1)}, bf16[288,384]{1,0:T(8,128)(2,1)S(1)}, u32[]{:S(2)}, u32[]{:S(2)}) collective-permute-start(bf16[288,384]{1,0:T(8,128)(2,1)S(1)} %slice.62), channel_id=1, source_target_pairs={{32,0},{36,4},{40,8},{44,12},{48,16},{52,20},{56,24},{60,28},{64,3... | collective-permute-start | bytes 663560 | tf_op jit(solution)/shard_map/ppermute | solution.py:27
  98.7 3.4 %collective-permute-done.29 = bf16[288,384]{1,0:T(8,128)(2,1)S(1)} collective-permute-done((bf16[288,384]{1,0:T(8,128)(2,1)S(1)}, bf16[288,384]{1,0:T(8,128)(2,1)S(1)}, u32[]{:S(2)}, u32[]{:S(2)}) %collective-permute-start.29) | collective-permute-done | bytes 221216 | tf_op jit(solution)/shard_map/ppermute | solution.py:27
  102.4 1.6 %bitcast_dynamic-update-slice_fusion.2 = (bf16[4,2,4,72,640]{4,3,2,1,0:T(8,128)(2,1)S(1)}, bf16[4,2,4,72,640]{4,3,2,1,0:T(8,128)(2,1)S(1)}) fusion(bf16[4,2,4,72,640]{4,3,2,1,0:T(8,128)(2,1)S(1)} %bitcast_dynamic-update-slice_fusion.4, s32[]{:T(128)S(6)} %select_n.98, bf16[4,2,72,640]{3,2,1,0:T(8,128)(2,1)} %collective-permute-done.21, ...), kind=kLoop, calls=%fused_computation.17 | loop fusion | bytes 2949128 | tf_op jit(solution)/shard_map/dynamic_update_slice | solution.py:142
  108.5 3.5 %shard_map.97 = bf16[512,1024]{1,0:T(8,128)(2,1)} custom-call(bf16[8,512,576]{2,1,0:T(8,128)(2,1)S(1)} %shard_map.95.z_ref, bf16[4,576,640]{2,1,0:T(8,128)(2,1)S(1)} %bitcast.111, f32[512,640]{1,0:T(8,128)S(1)} %convolution_add_fusion.total_ref, f32[512,1]{1,0:T(8,128)S(1)} %fusion.35.live_ref, bf16[512,384]{1,0:T(8,128)(2,1)S(1)} %select_convert_fusion.b_ref), custom_call_target="tpu_custom_call" | custom-call | tf_op jit(solution)/shard_map/pallas_call | solution.py:97
  (88 shorter events, 27.1 us)
Async XLA Ops:
  0.6 72.8 %copy-start = (bf16[128,4608]{1,0:T(8,128)(2,1)S(1)}, bf16[128,4608]{1,0:T(8,128)(2,1)}, u32[]{:S(2)}) copy-start(bf16[128,4608]{1,0:T(8,128)(2,1)} %param.11) | copy-start | bytes 3538948
  0.6 55.3 %copy-start.5 = (s32[512]{0:T(512)S(1)}, s32[512]{0:T(512)}, u32[]{:S(2)}) copy-start(s32[512]{0:T(512)} %param.12) | copy-start | bytes 6148
  0.7 6.6 %collective-permute-start.1 = (bf16[128,4608]{1,0:T(8,128)(2,1)}, bf16[128,4608]{1,0:T(8,128)(2,1)S(1)}, u32[]{:S(2)}, u32[]{:S(2)}) collective-permute-start(bf16[128,4608]{1,0:T(8,128)(2,1)} %param.8), channel_id=1, source_target_pairs={{0,1},{1,0},{2,3},{3,2},{4,5},{5,4},{6,7},{7,6},{8,9},{9,8},{10,11... | collective-permute-start | bytes 3538952 | tf_op jit(solution)/shard_map/ppermute | solution.py:31
  0.8 6.5 %collective-permute-start = (bf16[72,1024]{1,0:T(8,128)(2,1)}, bf16[72,1024]{1,0:T(8,128)(2,1)S(1)}, u32[]{:S(2)}, u32[]{:S(2)}) collective-permute-start(bf16[72,1024]{1,0:T(8,128)(2,1)} %mine_ref.1), channel_id=1, source_target_pairs={{16,0},{20,4},{24,8},{28,12},{0,16},{4,20},{8,24},{12,28},{48,32},... | collective-permute-start | bytes 442376 | tf_op jit(solution)/shard_map/ppermute | solution.py:27
  4.1 14.4 %collective-permute-start.4 = (f32[512,128]{1,0:T(8,128)}, f32[512,128]{1,0:T(8,128)}, u32[]{:S(2)}, u32[]{:S(2)}) collective-permute-start(f32[512,128]{1,0:T(8,128)} %fusion.41), channel_id=1, source_target_pairs={{0,1},{1,0},{2,3},{3,2},{4,5},{5,4},{6,7},{7,6},{8,9},{9,8},{10,11... | collective-permute-start | bytes 786440 | tf_op jit(solution)/shard_map/ppermute | solution.py:31
  9.6 10.6 %collective-permute-start.3 = (bf16[2,72,640]{2,1,0:T(8,128)(2,1)}, bf16[2,72,640]{2,1,0:T(8,128)(2,1)}, u32[]{:S(2)}, u32[]{:S(2)}) collective-permute-start(bf16[2,72,640]{2,1,0:T(8,128)(2,1)} %get-tuple-element.74), channel_id=1, source_target_pairs={{224,0},{228,4},{232,8},{236,12},{240,16},{244,20},{248,24},{252,2... | collective-permute-start | bytes 552968 | tf_op jit(solution)/shard_map/ppermute | solution.py:27
  11.5 8.7 %collective-permute-start.2 = (bf16[2,72,640]{2,1,0:T(8,128)(2,1)}, bf16[2,72,640]{2,1,0:T(8,128)(2,1)}, u32[]{:S(2)}, u32[]{:S(2)}) collective-permute-start(bf16[2,72,640]{2,1,0:T(8,128)(2,1)} %get-tuple-element.74), channel_id=1, source_target_pairs={{32,0},{36,4},{40,8},{44,12},{48,16},{52,20},{56,24},{60,28},{64,3... | collective-permute-start | bytes 552968 | tf_op jit(solution)/shard_map/ppermute | solution.py:27
  15.5 28.9 %collective-permute-start.12 = (bf16[128,4608]{1,0:T(8,128)(2,1)}, bf16[128,4608]{1,0:T(8,128)(2,1)S(1)}, u32[]{:S(2)}, u32[]{:S(2)}) collective-permute-start(bf16[128,4608]{1,0:T(8,128)(2,1)} %param.8), channel_id=1, source_target_pairs={{0,2},{1,3},{2,0},{3,1},{4,6},{5,7},{6,4},{7,5},{8,10},{9,11},{10,... | collective-permute-start | bytes 3538952 | tf_op jit(solution)/shard_map/ppermute | solution.py:31
  16.9 10.1 %collective-permute-start.9 = (bf16[2,72,384]{2,1,0:T(8,128)(2,1)}, bf16[2,72,384]{2,1,0:T(8,128)(2,1)}, u32[]{:S(2)}, u32[]{:S(2)}) collective-permute-start(bf16[2,72,384]{2,1,0:T(8,128)(2,1)} %get-tuple-element.66), channel_id=1, source_target_pairs={{12,0},{0,4},{4,8},{8,12},{28,16},{16,20},{20,24},{24,28},{44,32},... | collective-permute-start | bytes 331784 | tf_op jit(solution)/shard_map/ppermute | solution.py:27
  20.2 13.2 %collective-permute-start.5 = (bf16[2,72,640]{2,1,0:T(8,128)(2,1)}, bf16[2,72,640]{2,1,0:T(8,128)(2,1)}, u32[]{:S(2)}, u32[]{:S(2)}) collective-permute-start(bf16[2,72,640]{2,1,0:T(8,128)(2,1)} %collective-permute-done.2), channel_id=1, source_target_pairs={{32,0},{36,4},{40,8},{44,12},{48,16},{52,20},{56,24},{60,28},{64,3... | collective-permute-start | bytes 552968 | tf_op jit(solution)/shard_map/ppermute | solution.py:27
  23.2 10.2 %collective-permute-start.6 = (bf16[2,72,640]{2,1,0:T(8,128)(2,1)}, bf16[2,72,640]{2,1,0:T(8,128)(2,1)}, u32[]{:S(2)}, u32[]{:S(2)}) collective-permute-start(bf16[2,72,640]{2,1,0:T(8,128)(2,1)} %collective-permute-done.3), channel_id=1, source_target_pairs={{224,0},{228,4},{232,8},{236,12},{240,16},{244,20},{248,24},{252,2... | collective-permute-start | bytes 552968 | tf_op jit(solution)/shard_map/ppermute | solution.py:27
  23.8 7.1 %collective-permute-start.7 = (bf16[2,72,384]{2,1,0:T(8,128)(2,1)}, bf16[2,72,384]{2,1,0:T(8,128)(2,1)S(1)}, u32[]{:S(2)}, u32[]{:S(2)}) collective-permute-start(bf16[2,72,384]{2,1,0:T(8,128)(2,1)} %get-tuple-element.66), channel_id=1, source_target_pairs={{4,0},{8,4},{12,8},{0,12},{20,16},{24,20},{28,24},{16,28},{36,32},... | collective-permute-start | bytes 331784 | tf_op jit(solution)/shard_map/ppermute | solution.py:27
  26.9 6.5 %collective-permute-start.8 = (bf16[2,72,384]{2,1,0:T(8,128)(2,1)}, bf16[2,72,384]{2,1,0:T(8,128)(2,1)S(1)}, u32[]{:S(2)}, u32[]{:S(2)}) collective-permute-start(bf16[2,72,384]{2,1,0:T(8,128)(2,1)} %get-tuple-element.66), channel_id=1, source_target_pairs={{8,0},{12,4},{0,8},{4,12},{24,16},{28,20},{16,24},{20,28},{40,32},... | collective-permute-start | bytes 331784 | tf_op jit(solution)/shard_map/ppermute | solution.py:27
  33.4 11.0 %collective-permute-start.10 = (bf16[2,72,640]{2,1,0:T(8,128)(2,1)}, bf16[2,72,640]{2,1,0:T(8,128)(2,1)S(1)}, u32[]{:S(2)}, u32[]{:S(2)}) collective-permute-start(bf16[2,72,640]{2,1,0:T(8,128)(2,1)} %collective-permute-done.5), channel_id=1, source_target_pairs={{32,0},{36,4},{40,8},{44,12},{48,16},{52,20},{56,24},{60,28},{64,3... | collective-permute-start | bytes 552968 | tf_op jit(solution)/shard_map/ppermute | solution.py:27
  38.0 19.1 %collective-permute-start.16 = (bf16[4,2,72,640]{3,2,1,0:T(8,128)(2,1)S(1)}, bf16[4,2,72,640]{3,2,1,0:T(8,128)(2,1)S(1)}, u32[]{:S(2)}, u32[]{:S(2)}) collective-permute-start(bf16[4,2,72,640]{3,2,1,0:T(8,128)(2,1)S(1)} %pad_maximum_fusion), channel_id=1, source_target_pairs={{12,0},{0,4},{4,8},{8,12},{28,16},{16,20},{20,24},{24,28},{44,32},... | collective-permute-start | bytes 2211848 | tf_op jit(solution)/shard_map/ppermute | solution.py:27
  38.0 19.1 %collective-permute-start.15 = (bf16[4,2,72,640]{3,2,1,0:T(8,128)(2,1)S(1)}, bf16[4,2,72,640]{3,2,1,0:T(8,128)(2,1)}, u32[]{:S(2)}, u32[]{:S(2)}) collective-permute-start(bf16[4,2,72,640]{3,2,1,0:T(8,128)(2,1)S(1)} %pad_maximum_fusion), channel_id=1, source_target_pairs={{4,0},{8,4},{12,8},{0,12},{20,16},{24,20},{28,24},{16,28},{36,32},... | collective-permute-start | bytes 2211848 | tf_op jit(solution)/shard_map/ppermute | solution.py:27
  41.3 7.3 %collective-permute-start.11 = (bf16[2,72,640]{2,1,0:T(8,128)(2,1)}, bf16[2,72,640]{2,1,0:T(8,128)(2,1)S(1)}, u32[]{:S(2)}, u32[]{:S(2)}) collective-permute-start(bf16[2,72,640]{2,1,0:T(8,128)(2,1)} %collective-permute-done.6), channel_id=1, source_target_pairs={{224,0},{228,4},{232,8},{236,12},{240,16},{244,20},{248,24},{252,2... | collective-permute-start | bytes 552968 | tf_op jit(solution)/shard_map/ppermute | solution.py:27
  48.5 6.3 %collective-permute-start.17 = (bf16[2,72,640]{2,1,0:T(8,128)(2,1)S(1)}, bf16[2,72,640]{2,1,0:T(8,128)(2,1)S(1)}, u32[]{:S(2)}, u32[]{:S(2)}) collective-permute-start(bf16[2,72,640]{2,1,0:T(8,128)(2,1)S(1)} %collective-permute-done.10), channel_id=1, source_target_pairs={{32,0},{36,4},{40,8},{44,12},{48,16},{52,20},{56,24},{60,28},{64,3... | collective-permute-start | bytes 552968 | tf_op jit(solution)/shard_map/ppermute | solution.py:27
  48.6 14.2 %collective-permute-start.14 = (bf16[576,384]{1,0:T(8,128)(2,1)S(1)}, bf16[576,384]{1,0:T(8,128)(2,1)}, u32[]{:S(2)}, u32[]{:S(2)}) collective-permute-start(bf16[576,384]{1,0:T(8,128)(2,1)S(1)} %bitcast.116), channel_id=1, source_target_pairs={{224,0},{228,4},{232,8},{236,12},{240,16},{244,20},{248,24},{252,2... | collective-permute-start | bytes 1327112 | tf_op jit(solution)/shard_map/ppermute | solution.py:27
  50.6 12.2 %collective-permute-start.13 = (bf16[576,384]{1,0:T(8,128)(2,1)S(1)}, bf16[576,384]{1,0:T(8,128)(2,1)}, u32[]{:S(2)}, u32[]{:S(2)}) collective-permute-start(bf16[576,384]{1,0:T(8,128)(2,1)S(1)} %bitcast.117), channel_id=1, source_target_pairs={{32,0},{36,4},{40,8},{44,12},{48,16},{52,20},{56,24},{60,28},{64,3... | collective-permute-start | bytes 1327112 | tf_op jit(solution)/shard_map/ppermute | solution.py:27
  54.9 7.9 %collective-permute-start.18 = (f32[512,128]{1,0:T(8,128)S(1)}, f32[512,128]{1,0:T(8,128)S(1)}, u32[]{:S(2)}, u32[]{:S(2)}) collective-permute-start(f32[512,128]{1,0:T(8,128)S(1)} %add.137), channel_id=1, source_target_pairs={{0,2},{1,3},{2,0},{3,1},{4,6},{5,7},{6,4},{7,5},{8,10},{9,11},{10,... | collective-permute-start | bytes 786440 | tf_op jit(solution)/shard_map/ppermute | solution.py:31
  57.0 11.6 %collective-permute-start.23 = (bf16[128,4608]{1,0:T(8,128)(2,1)S(1)}, bf16[128,4608]{1,0:T(8,128)(2,1)S(1)}, u32[]{:S(2)}, u32[]{:S(2)}) collective-permute-start(bf16[128,4608]{1,0:T(8,128)(2,1)S(1)} %collective-permute-done.12), channel_id=1, source_target_pairs={{0,1},{1,0},{2,3},{3,2},{4,5},{5,4},{6,7},{7,6},{8,9},{9,8},{10,11... | collective-permute-start | bytes 3538952 | tf_op jit(solution)/shard_map/ppermute | solution.py:31
  57.1 22.5 %collective-permute-start.21 = (bf16[4,2,72,640]{3,2,1,0:T(8,128)(2,1)}, bf16[4,2,72,640]{3,2,1,0:T(8,128)(2,1)}, u32[]{:S(2)}, u32[]{:S(2)}) collective-permute-start(bf16[4,2,72,640]{3,2,1,0:T(8,128)(2,1)} %collective-permute-done.15), channel_id=1, source_target_pairs={{4,0},{8,4},{12,8},{0,12},{20,16},{24,20},{28,24},{16,28},{36,32},... | collective-permute-start | bytes 2211848 | tf_op jit(solution)/shard_map/ppermute | solution.py:27
  63.0 16.7 %collective-permute-start.19 = (bf16[576,384]{1,0:T(8,128)(2,1)}, bf16[576,384]{1,0:T(8,128)(2,1)}, u32[]{:S(2)}, u32[]{:S(2)}) collective-permute-start(bf16[576,384]{1,0:T(8,128)(2,1)} %collective-permute-done.13), channel_id=1, source_target_pairs={{32,0},{36,4},{40,8},{44,12},{48,16},{52,20},{56,24},{60,28},{64,3... | collective-permute-start | bytes 1327112 | tf_op jit(solution)/shard_map/ppermute | solution.py:27
  65.5 14.1 %collective-permute-start.20 = (bf16[576,384]{1,0:T(8,128)(2,1)}, bf16[576,384]{1,0:T(8,128)(2,1)}, u32[]{:S(2)}, u32[]{:S(2)}) collective-permute-start(bf16[576,384]{1,0:T(8,128)(2,1)} %collective-permute-done.14), channel_id=1, source_target_pairs={{224,0},{228,4},{232,8},{236,12},{240,16},{244,20},{248,24},{252,2... | collective-permute-start | bytes 1327112 | tf_op jit(solution)/shard_map/ppermute | solution.py:27
  65.5 14.9 %collective-permute-start.22 = (bf16[4,2,72,640]{3,2,1,0:T(8,128)(2,1)S(1)}, bf16[4,2,72,640]{3,2,1,0:T(8,128)(2,1)}, u32[]{:S(2)}, u32[]{:S(2)}) collective-permute-start(bf16[4,2,72,640]{3,2,1,0:T(8,128)(2,1)S(1)} %pad_maximum_fusion.1), channel_id=1, source_target_pairs={{12,0},{0,4},{4,8},{8,12},{28,16},{16,20},{20,24},{24,28},{44,32},... | collective-permute-start | bytes 2211848 | tf_op jit(solution)/shard_map/ppermute | solution.py:27
  80.4 9.1 %collective-permute-start.26 = (bf16[576,384]{1,0:T(8,128)(2,1)}, bf16[576,384]{1,0:T(8,128)(2,1)S(1)}, u32[]{:S(2)}, u32[]{:S(2)}) collective-permute-start(bf16[576,384]{1,0:T(8,128)(2,1)} %collective-permute-done.19), channel_id=1, source_target_pairs={{32,0},{36,4},{40,8},{44,12},{48,16},{52,20},{56,24},{60,28},{64,3... | collective-permute-start | bytes 1327112 | tf_op jit(solution)/shard_map/ppermute | solution.py:27
  83.4 10.9 %collective-permute-start.27 = (bf16[576,384]{1,0:T(8,128)(2,1)}, bf16[576,384]{1,0:T(8,128)(2,1)S(1)}, u32[]{:S(2)}, u32[]{:S(2)}) collective-permute-start(bf16[576,384]{1,0:T(8,128)(2,1)} %collective-permute-done.20), channel_id=1, source_target_pairs={{224,0},{228,4},{232,8},{236,12},{240,16},{244,20},{248,24},{252,2... | collective-permute-start | bytes 1327112 | tf_op jit(solution)/shard_map/ppermute | solution.py:27
  83.4 24.9 %collective-permute-start.24 = (bf16[4,2,72,640]{3,2,1,0:T(8,128)(2,1)S(1)}, bf16[4,2,72,640]{3,2,1,0:T(8,128)(2,1)S(1)}, u32[]{:S(2)}, u32[]{:S(2)}) collective-permute-start(bf16[4,2,72,640]{3,2,1,0:T(8,128)(2,1)S(1)} %pad_maximum_fusion.1), channel_id=1, source_target_pairs={{4,0},{8,4},{12,8},{0,12},{20,16},{24,20},{28,24},{16,28},{36,32},... | collective-permute-start | bytes 2211848 | tf_op jit(solution)/shard_map/ppermute | solution.py:27
  86.2 22.1 %collective-permute-start.25 = (bf16[4,2,72,640]{3,2,1,0:T(8,128)(2,1)}, bf16[4,2,72,640]{3,2,1,0:T(8,128)(2,1)S(1)}, u32[]{:S(2)}, u32[]{:S(2)}) collective-permute-start(bf16[4,2,72,640]{3,2,1,0:T(8,128)(2,1)} %collective-permute-done.22), channel_id=1, source_target_pairs={{12,0},{0,4},{4,8},{8,12},{28,16},{16,20},{20,24},{24,28},{44,32},... | collective-permute-start | bytes 2211848 | tf_op jit(solution)/shard_map/ppermute | solution.py:27
  94.9 7.2 %collective-permute-start.29 = (bf16[288,384]{1,0:T(8,128)(2,1)S(1)}, bf16[288,384]{1,0:T(8,128)(2,1)S(1)}, u32[]{:S(2)}, u32[]{:S(2)}) collective-permute-start(bf16[288,384]{1,0:T(8,128)(2,1)S(1)} %slice.63), channel_id=1, source_target_pairs={{224,0},{228,4},{232,8},{236,12},{240,16},{244,20},{248,24},{252,2... | collective-permute-start | bytes 663560 | tf_op jit(solution)/shard_map/ppermute | solution.py:27
  95.0 7.1 %collective-permute-start.28 = (bf16[288,384]{1,0:T(8,128)(2,1)S(1)}, bf16[288,384]{1,0:T(8,128)(2,1)S(1)}, u32[]{:S(2)}, u32[]{:S(2)}) collective-permute-start(bf16[288,384]{1,0:T(8,128)(2,1)S(1)} %slice.62), channel_id=1, source_target_pairs={{32,0},{36,4},{40,8},{44,12},{48,16},{52,20},{56,24},{60,28},{64,3... | collective-permute-start | bytes 663560 | tf_op jit(solution)/shard_map/ppermute | solution.py:27
  (4 other events, 4.6 us)

commit v8 on v7

--- a/solution.py
+++ b/solution.py
@@ -148,7 +148,7 @@
         shape = chunk.shape[:at] + (NY,) + chunk.shape[at:]
         return jnp.broadcast_to(jnp.expand_dims(chunk, at), shape)
 
-    a_p2, a_m2, pair_b, *y_b = together(a_p2, a_m2, pair_b, *y_b)
+    a_p2, a_m2 = together(a_p2, a_m2)
     low = jnp.stack([a_m1, pair_a, a_p1, a_p2])
     low_p, low_m = fetch(low, dy=1), fetch(low, dy=-1)
     a_p3, a_m3 = fetch(a_p2, dz=1), fetch(a_m2, dz=-1)
@@ -157,19 +157,15 @@
         b_own = placed(b_own, chunk, dy)
     b_own = b_own.reshape(NX * NY * shard_rows, -1)
 
-    a_p3, a_m3, b_own, from_chip, partial, core_partial = together(
-        a_p3, a_m3, b_own, from_chip, partial, core_partial
-    )
-    chip_sum = partial + core_partial
-    far_sum = swap_tensor(chip_sum, 2)
+    a_p3, a_m3, b_own = together(a_p3, a_m3, b_own)
     a_p4 = fetch(a_p3, dz=1)
     b_p1, b_m1 = fetch(b_own, dz=1), fetch(b_own, dz=-1)
     high = jnp.stack([a_p3, a_p4, a_m3, a_m2])
 
     low_p, low_m, high = together(low_p, low_m, high)
     low_o, high_m = fetch(low_p, dy=1), fetch(high, dy=-1)
-    b_p1, b_m1, low_p, far_sum, own_rows, from_core = together(
-        b_p1, b_m1, low_p, far_sum, own_rows, from_core
+    b_p1, b_m1, low_p, own_rows, from_core, from_chip = together(
+        b_p1, b_m1, low_p, own_rows, from_core, from_chip
     )
     b_p2, b_m2 = fetch(b_p1, dz=1), fetch(b_m1, dz=-1)
 
@@ -209,35 +205,38 @@
     )
 
     (
-        b_p2, b_m2, low_o, high_m, high, low_all, by_z, adapter_backward,
-        down_factor_gradient, b_total,
+        b_p2, b_m2, low_o, high_m, high, low_all, by_z, adapter_backward, partial,
+        core_partial, down_factor_gradient, b_total,
     ) = together(
-        b_p2, b_m2, low_o, high_m, high, low_all, by_z, adapter_backward,
-        down_factor_gradient, b_total,
+        b_p2, b_m2, low_o, high_m, high, low_all, by_z, adapter_backward, partial,
+        core_partial, down_factor_gradient, b_total,
     )
     high_p, high_o = fetch(high, dy=1), fetch(high_m, dy=-1)
     b_p3, b_m3 = fetch(b_p2, dz=1), fetch(b_m2, dz=-1)
-    b_p3, b_m3 = together(b_p3, b_m3)
+    chip_sum = partial + core_partial
+    far_sum = swap_tensor(chip_sum, 2)
+    low_all, low_o, far_sum, chip_sum = together(low_all, low_o, far_sum, chip_sum)
+    low_all = placed(low_all, low_o, 2)
+    a_total = product(
+        ADAPTER_SCALE * contract(adapter_backward, adapter_down_factors[:a_width], 1, 1),
+        [(i, low_all[i]) for i in range(4)],
+    )
+    b_p2, b_m2, b_p3, b_m3, a_total, b_total = together(
+        b_p2, b_m2, b_p3, b_m3, a_total, b_total
+    )
     cut = b_own.shape[0] // 2 // 16 * 16
     b_p4, b_m4 = fetch(b_p3[:cut], dz=1), fetch(b_m3[cut:], dz=-1)
     adapter_input = ((chip_sum + far_sum) * select_rows).astype(jnp.bfloat16)
     (adapter_input,) = together(adapter_input)
     up_factor_gradient = ADAPTER_SCALE * contract(adapter_input, gradients, 0, 0)
-
-    b_p4, b_m4, up_factor_gradient, low_all, high_m = together(
-        b_p4, b_m4, up_factor_gradient, low_all, high_m
-    )
-    b_total = product(
-        b_total,
-        [(7, b_m2), (3, b_p2), (6, b_m3), (4, b_p3), (5, jnp.concatenate([b_p4, b_m4], 0))],
-    )
+    high_all = placed(spread(high), high_m, 3)
+    b_total = product(b_total, [(7, b_m2), (3, b_p2), (6, b_m3), (4, b_p3)])
+
+    b_p4, b_m4, high_all, b_total, up_factor_gradient = together(
+        b_p4, b_m4, high_all, b_total, up_factor_gradient
+    )
+    b_total = product(b_total, [(5, jnp.concatenate([b_p4, b_m4], 0))])
     b_out = jnp.where(active_rows[:, None], b_total, 0.0).astype(jnp.bfloat16)
-    low_all = placed(low_all, low_o, 2)
-    a_total = product(
-        ADAPTER_SCALE * contract(adapter_backward, adapter_down_factors[:a_width], 1, 1),
-        [(i, low_all[i]) for i in range(4)],
-    )
-    high_all = placed(spread(high), high_m, 3)
 
     high_p, high_o, high_all, b_out, a_total = together(high_p, high_o, high_all, b_out, a_total)
     high_all = placed(placed(high_all, high_p, 1), high_o, 2)

time: 113 us -> 116 us (1.027)
  waiting for transfers between devices: 31.5 us -> 41.6 us
  starting transfers between devices: 40.6 us -> 34.6 us
  matrix products: 18 us -> 15.1 us
  local copies, waits for them, and re-layouts: 8.53 us -> 10.6 us
    ppermute x25, waiting for transfers between devices: 26 us -> 39.5 us  [fetch(): return lax.ppermute(x, 'dp', pairs)]
    ppermute x25, starting transfers between devices: 37.8 us -> 31.7 us  [fetch(): return lax.ppermute(x, 'dp', pairs)]
    ppermute x5, waiting for transfers between devices: 5.49 us -> 2.09 us  [swap_tensor(): return lax.ppermute(x, 'tensor', [(t, t ^ mask) for t in range(4)])]
    dot_general x16, matrix products: 15.6 us -> 13.4 us  [contract(): lax.dot_general(left, right, (((left_dim,), (right_dim,)), ((), ())), pre...]
    dynamic_update_slice x4, local copies, waits for them, and re-layouts: 0.46 us -> 1.74 us  [body(): lax.dynamic_update_slice_in_dim(gradients, block, (tensor ^ mask) * part_...]
    dynamic_update_slice x8 -> x9, local copies, waits for them, and re-layouts: 4.15 us -> 5.1 us  [placed(): lax.dynamic_update_slice_in_dim(array, jnp.expand_dims(chunk, at), (y + d...]
  transfers between devices with their start and end apart: 30 -> 30, of which waited for: 12 -> 13; matrix products, arithmetic and copies ran while one was open for 25% -> 23% of each run, Pallas kernels for 4% -> 4%
where the time goes in v8:
time: 116 us; the launch traced here: 115 us
  waiting for transfers between devices  41.6 us (36%)
  starting transfers between devices  34.6 us (30%)
  matrix products  15.1 us (13%)
  local copies, waits for them, and re-layouts  10.6 us (9%)
  Pallas kernels  8.08 us (7%)
  other arithmetic  3.04 us (3%)
  between operations  1.79 us (2%)
    ppermute x25, waiting for transfers between devices, fetch(): return lax.ppermute(x, 'dp', pairs)  39.5 us
    ppermute x25, starting transfers between devices, fetch(): return lax.ppermute(x, 'dp', pairs)  31.7 us
    dot_general x16, matrix products, contract(): lax.dot_general(left, right, (((left_dim,), (right_dim,)), ((), ())), pre...  13.4 us
    dynamic_update_slice x9, local copies, waits for them, and re-layouts, placed(): lax.dynamic_update_slice_in_dim(array, jnp.expand_dims(chunk, at), (y + d...  5.1 us
    pallas_call x2, Pallas kernels, in_vmem(): pl.pallas_call(kernel, in_specs=[pl.BlockSpec(memory_space=pltpu.VMEM)] *...  4.76 us
    ppermute x5, starting transfers between devices, swap_tensor(): return lax.ppermute(x, 'tensor', [(t, t ^ mask) for t in range(4)])  2.92 us
  transfers between devices with their start and end apart: 30, of which 13 were waited for; matrix products, arithmetic and copies ran while one was open for 23% of the time, Pallas kernels for 4%

profile of v8, /device:TPU:6, one launch (start us, length us, event | category | flops | bytes accessed | tf_op | source)
XLA Modules:
  0.0 114.9 jit_solution(10174625705866581570)
XLA Ops:
  1.7 1.7 %fusion.41 = f32[512,128]{1,0:T(8,128)S(1)} fusion(bf16[512,1024]{1,0:T(8,128)(2,1)} %head_ref.1, bf16[1024,128]{1,0:T(8,128)(2,1)} %param.10), kind=kOutput, calls=%fused_computation.78 | convolution fusion | flops 134217728 | bytes 1572864 | tf_op jit(solution)/shard_map/dot_general | solution.py:126
  3.6 3.6 %collective-permute-done.far_ref = bf16[72,1024]{1,0:T(8,128)(2,1)S(1)} collective-permute-done((bf16[72,1024]{1,0:T(8,128)(2,1)}, bf16[72,1024]{1,0:T(8,128)(2,1)S(1)}, u32[]{:S(2)}, u32[]{:S(2)}) %collective-permute-start) | collective-permute-done | bytes 147488 | tf_op jit(solution)/shard_map/ppermute | solution.py:27
  7.9 1.7 %shard_map.94 = (bf16[2,72,640]{2,1,0:T(8,128)(2,1)}, bf16[2,72,384]{2,1,0:T(8,128)(2,1)}) custom-call(s32[1]{0:T(128)} %bitcast.x_ref, bf16[72,1024]{1,0:T(8,128)(2,1)} %mine_ref.1, bf16[72,1024]{1,0:T(8,128)(2,1)} %copy-done.10), custom_call_target="tpu_custom_call" | custom-call | tf_op jit(solution)/shard_map/pallas_call | solution.py:84
  9.6 5.9 %collective-permute-start.2 = (bf16[2,72,640]{2,1,0:T(8,128)(2,1)}, bf16[2,72,640]{2,1,0:T(8,128)(2,1)S(1)}, u32[]{:S(2)}, u32[]{:S(2)}) collective-permute-start(bf16[2,72,640]{2,1,0:T(8,128)(2,1)} %get-tuple-element.70), channel_id=1, source_target_pairs={{32,0},{36,4},{40,8},{44,12},{48,16},{52,20},{56,24},{60,28},{64,3... | collective-permute-start | bytes 552968 | tf_op jit(solution)/shard_map/ppermute | solution.py:27
  15.5 3.0 %collective-permute-start.9 = (bf16[2,72,384]{2,1,0:T(8,128)(2,1)}, bf16[2,72,384]{2,1,0:T(8,128)(2,1)S(1)}, u32[]{:S(2)}, u32[]{:S(2)}) collective-permute-start(bf16[2,72,384]{2,1,0:T(8,128)(2,1)} %get-tuple-element.68), channel_id=1, source_target_pairs={{4,0},{8,4},{12,8},{0,12},{20,16},{24,20},{28,24},{16,28},{36,32},... | collective-permute-start | bytes 331784 | tf_op jit(solution)/shard_map/ppermute | solution.py:27
  18.5 1.4 %collective-permute-start.17 = (bf16[128,4608]{1,0:T(8,128)(2,1)}, bf16[128,4608]{1,0:T(8,128)(2,1)}, u32[]{:S(2)}, u32[]{:S(2)}) collective-permute-start(bf16[128,4608]{1,0:T(8,128)(2,1)} %param.8), channel_id=1, source_target_pairs={{0,2},{1,3},{2,0},{3,1},{4,6},{5,7},{6,4},{7,5},{8,10},{9,11},{10,... | collective-permute-start | bytes 3538952 | tf_op jit(solution)/shard_map/ppermute | solution.py:31
  19.9 3.0 %collective-permute-done.3 = bf16[2,72,640]{2,1,0:T(8,128)(2,1)} collective-permute-done((bf16[2,72,640]{2,1,0:T(8,128)(2,1)}, bf16[2,72,640]{2,1,0:T(8,128)(2,1)}, u32[]{:S(2)}, u32[]{:S(2)}) %collective-permute-start.3) | collective-permute-done | bytes 184352 | tf_op jit(solution)/shard_map/ppermute | solution.py:27
  22.9 3.2 %collective-permute-start.10 = (bf16[2,72,384]{2,1,0:T(8,128)(2,1)}, bf16[2,72,384]{2,1,0:T(8,128)(2,1)S(1)}, u32[]{:S(2)}, u32[]{:S(2)}) collective-permute-start(bf16[2,72,384]{2,1,0:T(8,128)(2,1)} %get-tuple-element.68), channel_id=1, source_target_pairs={{8,0},{12,4},{0,8},{4,12},{24,16},{28,20},{16,24},{20,28},{40,32},... | collective-permute-start | bytes 331784 | tf_op jit(solution)/shard_map/ppermute | solution.py:27
  26.9 1.8 %collective-permute-start.6 = (bf16[2,72,640]{2,1,0:T(8,128)(2,1)}, bf16[2,72,640]{2,1,0:T(8,128)(2,1)S(1)}, u32[]{:S(2)}, u32[]{:S(2)}) collective-permute-start(bf16[2,72,640]{2,1,0:T(8,128)(2,1)} %collective-permute-done.3), channel_id=1, source_target_pairs={{224,0},{228,4},{232,8},{236,12},{240,16},{244,20},{248,24},{252,2... | collective-permute-start | bytes 552968 | tf_op jit(solution)/shard_map/ppermute | solution.py:27
  31.6 2.2 %collective-permute-done.6 = bf16[2,72,640]{2,1,0:T(8,128)(2,1)S(1)} collective-permute-done((bf16[2,72,640]{2,1,0:T(8,128)(2,1)}, bf16[2,72,640]{2,1,0:T(8,128)(2,1)S(1)}, u32[]{:S(2)}, u32[]{:S(2)}) %collective-permute-start.6) | collective-permute-done | bytes 184352 | tf_op jit(solution)/shard_map/ppermute | solution.py:27
  37.3 2.0 %collective-permute-start.8 = (bf16[2,72,640]{2,1,0:T(8,128)(2,1)S(1)}, bf16[2,72,640]{2,1,0:T(8,128)(2,1)}, u32[]{:S(2)}, u32[]{:S(2)}) collective-permute-start(bf16[2,72,640]{2,1,0:T(8,128)(2,1)S(1)} %collective-permute-done.6), channel_id=1, source_target_pairs={{224,0},{228,4},{232,8},{236,12},{240,16},{244,20},{248,24},{252,2... | collective-permute-start | bytes 552968 | tf_op jit(solution)/shard_map/ppermute | solution.py:27
  39.5 4.6 %collective-permute-done.8 = bf16[2,72,640]{2,1,0:T(8,128)(2,1)} collective-permute-done((bf16[2,72,640]{2,1,0:T(8,128)(2,1)S(1)}, bf16[2,72,640]{2,1,0:T(8,128)(2,1)}, u32[]{:S(2)}, u32[]{:S(2)}) %collective-permute-start.8) | collective-permute-done | bytes 184352 | tf_op jit(solution)/shard_map/ppermute | solution.py:27
  45.7 6.1 %collective-permute-done.16 = bf16[2,72,640]{2,1,0:T(8,128)(2,1)} collective-permute-done((bf16[2,72,640]{2,1,0:T(8,128)(2,1)}, bf16[2,72,640]{2,1,0:T(8,128)(2,1)}, u32[]{:S(2)}, u32[]{:S(2)}) %collective-permute-start.16) | collective-permute-done | bytes 184352 | tf_op jit(solution)/shard_map/ppermute | solution.py:27
  52.3 1.3 %pad_maximum_fusion.1 = bf16[4,2,72,640]{3,2,1,0:T(8,128)(2,1)S(1)} fusion(bf16[1,2,72,640]{3,2,1,0:T(8,128)(2,1)} %bitcast.120, bf16[1,2,72,640]{3,2,1,0:T(8,128)(2,1)} %bitcast.14, bf16[1,2,72,640]{3,2,1,0:T(8,128)(2,1)} %bitcast.13, bf16[1,2,72,640]{3,2,1,0:T(8,128)(2,1)} %bitcast.12), kind=kLoop, calls=%fused_computation.15 | loop fusion | flops 1105920 | bytes 1474560 | tf_op jit(solution)/shard_map/stack | solution.py:163
  53.6 2.3 %collective-permute-start.20 = (bf16[4,2,72,640]{3,2,1,0:T(8,128)(2,1)}, bf16[4,2,72,640]{3,2,1,0:T(8,128)(2,1)S(1)}, u32[]{:S(2)}, u32[]{:S(2)}) collective-permute-start(bf16[4,2,72,640]{3,2,1,0:T(8,128)(2,1)} %collective-permute-done.14), channel_id=1, source_target_pairs={{4,0},{8,4},{12,8},{0,12},{20,16},{24,20},{28,24},{16,28},{36,32},... | collective-permute-start | bytes 2211848 | tf_op jit(solution)/shard_map/ppermute | solution.py:27
  56.4 4.9 %collective-permute-done.13 = bf16[576,384]{1,0:T(8,128)(2,1)S(1)} collective-permute-done((bf16[576,384]{1,0:T(8,128)(2,1)S(1)}, bf16[576,384]{1,0:T(8,128)(2,1)S(1)}, u32[]{:S(2)}, u32[]{:S(2)}) %collective-permute-start.13) | collective-permute-done | bytes 442400 | tf_op jit(solution)/shard_map/ppermute | solution.py:27
  61.6 1.7 %collective-permute-start.19 = (bf16[576,384]{1,0:T(8,128)(2,1)S(1)}, bf16[576,384]{1,0:T(8,128)(2,1)}, u32[]{:S(2)}, u32[]{:S(2)}) collective-permute-start(bf16[576,384]{1,0:T(8,128)(2,1)S(1)} %collective-permute-done.13), channel_id=1, source_target_pairs={{224,0},{228,4},{232,8},{236,12},{240,16},{244,20},{248,24},{252,2... | collective-permute-start | bytes 1327112 | tf_op jit(solution)/shard_map/ppermute | solution.py:27
  65.5 1.3 %bitcast_dynamic-update-slice_fusion.4 = bf16[4,2,4,72,640]{4,3,2,1,0:T(8,128)(2,1)S(1)} fusion(bf16[4,2,4,72,640]{4,3,2,1,0:T(8,128)(2,1)S(1)} %bitcast_dynamic-update-slice_fusion.5, s32[]{:T(128)S(6)} %select_n.100, bf16[4,2,72,640]{3,2,1,0:T(8,128)(2,1)} %collective-permute-done.15), kind=kLoop, calls=%fused_computation.20 | loop fusion | bytes 1474564 | tf_op jit(solution)/shard_map/dynamic_update_slice | solution.py:142
  67.4 1.4 %constant_dynamic-update-slice_fusion.1 = bf16[512,4608]{1,0:T(8,128)(2,1)S(1)} fusion(bf16[512,4608]{1,0:T(8,128)(2,1)S(1)} %constant_dynamic-update-slice_fusion.2, bf16[128,4608]{1,0:T(8,128)(2,1)} %collective-permute-done.17, s32[]{:T(128)S(6)} %select_n.105), kind=kLoop, calls=%fused_computation.64 | loop fusion | bytes 2359300 | tf_op jit(solution)/shard_map/dynamic_update_slice | solution.py:175
  68.9 1.6 %shard_map.95.z_ref = bf16[8,512,576]{2,1,0:T(8,128)(2,1)S(1)} custom-call(s32[1]{0:T(128)} %bitcast.20.start_ref, bf16[512,4608]{1,0:T(8,128)(2,1)S(1)} %constant_dynamic-update-slice_fusion.g_ref), custom_call_target="tpu_custom_call" | custom-call | tf_op jit(solution)/shard_map/pallas_call | solution.py:49
  71.0 1.4 %fusion.3.back_ref = bf16[512,128]{1,0:T(8,128)(2,1)S(1)} fusion(bf16[512,4608]{1,0:T(8,128)(2,1)S(1)} %constant_dynamic-update-slice_fusion.g_ref, bf16[128,4608]{1,0:T(8,128)(2,1)S(1)} %copy-done, s32[128]{0:T(128)S(1)} %and_select_fusion, s32[512]{0:T(512)S(1)} %add_select_fusion, pred[512]{0:T(512)(128)(4,1)S(1)} %iota_compare_fusion.1), kind=kOutput, calls=%fused_computation.11 | convolution fusion | flops 604241920 | bytes 6032384 | tf_op jit(solution)/shard_map/dot_general | solution.py:15
  73.7 1.3 %shard_map.96 = f32[1024,128]{1,0:T(8,128)} custom-call(bf16[512,1024]{1,0:T(8,128)(2,1)S(1)} %copy-done.1, bf16[512,128]{1,0:T(8,128)(2,1)S(1)} %fusion.3.back_ref), custom_call_target="tpu_custom_call" | custom-call | tf_op jit(solution)/shard_map/pallas_call | solution.py:97
  75.5 7.4 %collective-permute-done.21 = bf16[4,2,72,640]{3,2,1,0:T(8,128)(2,1)} collective-permute-done((bf16[4,2,72,640]{3,2,1,0:T(8,128)(2,1)S(1)}, bf16[4,2,72,640]{3,2,1,0:T(8,128)(2,1)}, u32[]{:S(2)}, u32[]{:S(2)}) %collective-permute-start.21) | collective-permute-done | bytes 737312 | tf_op jit(solution)/shard_map/ppermute | solution.py:27
  84.2 1.6 %collective-permute-start.25 = (bf16[576,384]{1,0:T(8,128)(2,1)}, bf16[576,384]{1,0:T(8,128)(2,1)S(1)}, u32[]{:S(2)}, u32[]{:S(2)}) collective-permute-start(bf16[576,384]{1,0:T(8,128)(2,1)} %collective-permute-done.18), channel_id=1, source_target_pairs={{32,0},{36,4},{40,8},{44,12},{48,16},{52,20},{56,24},{60,28},{64,3... | collective-permute-start | bytes 1327112 | tf_op jit(solution)/shard_map/ppermute | solution.py:27
  89.8 2.1 %collective-permute-done.27 = f32[512,128]{1,0:T(8,128)S(1)} collective-permute-done((f32[512,128]{1,0:T(8,128)S(1)}, f32[512,128]{1,0:T(8,128)S(1)}, u32[]{:S(2)}, u32[]{:S(2)}) %collective-permute-start.27) | collective-permute-done | bytes 262176 | tf_op jit(solution)/shard_map/ppermute | solution.py:31
  95.8 2.2 %convolution_multiply_fusion = f32[128,4608]{1,0:T(8,128)} fusion(bf16[512,128]{1,0:T(8,128)(2,1)S(1)} %select_convert_fusion.1, bf16[512,4608]{1,0:T(8,128)(2,1)S(1)} %constant_dynamic-update-slice_fusion.g_ref), kind=kOutput, calls=%fused_computation | convolution fusion | flops 604569600 | bytes 7208960 | tf_op jit(solution)/shard_map/dot_general | solution.py:15
  98.6 1.5 %fusion.14 = f32[512,384]{1,0:T(8,128)S(1)} fusion(bf16[576,384]{1,0:T(8,128)(2,1)} %collective-permute-done.19, bf16[8,512,576]{2,1,0:T(8,128)(2,1)S(1)} %shard_map.95.z_ref), kind=kOutput, calls=%fused_computation.33 | convolution fusion | flops 226492416 | bytes 1884160 | tf_op jit(solution)/shard_map/dot_general | solution.py:15
  100.2 1.5 %fusion.16 = f32[512,384]{1,0:T(8,128)S(1)} fusion(bf16[576,384]{1,0:T(8,128)(2,1)} %collective-permute-done.18, bf16[8,512,576]{2,1,0:T(8,128)(2,1)S(1)} %shard_map.95.z_ref), kind=kOutput, calls=%fused_computation.35 | convolution fusion | flops 226492416 | bytes 1884160 | tf_op jit(solution)/shard_map/dot_general | solution.py:15
  101.7 1.6 %collective-permute-start.28 = (bf16[288,384]{1,0:T(8,128)(2,1)S(1)}, bf16[288,384]{1,0:T(8,128)(2,1)S(1)}, u32[]{:S(2)}, u32[]{:S(2)}) collective-permute-start(bf16[288,384]{1,0:T(8,128)(2,1)S(1)} %slice.71), channel_id=1, source_target_pairs={{32,0},{36,4},{40,8},{44,12},{48,16},{52,20},{56,24},{60,28},{64,3... | collective-permute-start | bytes 663560 | tf_op jit(solution)/shard_map/ppermute | solution.py:27
  104.4 3.4 %collective-permute-done.28 = bf16[288,384]{1,0:T(8,128)(2,1)S(1)} collective-permute-done((bf16[288,384]{1,0:T(8,128)(2,1)S(1)}, bf16[288,384]{1,0:T(8,128)(2,1)S(1)}, u32[]{:S(2)}, u32[]{:S(2)}) %collective-permute-start.28) | collective-permute-done | bytes 221216 | tf_op jit(solution)/shard_map/ppermute | solution.py:27
  107.7 2.7 %collective-permute-done.29 = bf16[288,384]{1,0:T(8,128)(2,1)S(1)} collective-permute-done((bf16[288,384]{1,0:T(8,128)(2,1)S(1)}, bf16[288,384]{1,0:T(8,128)(2,1)S(1)}, u32[]{:S(2)}, u32[]{:S(2)}) %collective-permute-start.29) | collective-permute-done | bytes 221216 | tf_op jit(solution)/shard_map/ppermute | solution.py:27
  111.4 3.5 %shard_map.97 = bf16[512,1024]{1,0:T(8,128)(2,1)} custom-call(bf16[8,512,576]{2,1,0:T(8,128)(2,1)S(1)} %shard_map.95.z_ref, bf16[4,576,640]{2,1,0:T(8,128)(2,1)S(1)} %bitcast.111, f32[512,640]{1,0:T(8,128)S(1)} %convolution_add_fusion.total_ref, f32[512,1]{1,0:T(8,128)S(1)} %fusion.35.live_ref, bf16[512,384]{1,0:T(8,128)(2,1)S(1)} %select_convert_fusion.b_ref), custom_call_target="tpu_custom_call" | custom-call | tf_op jit(solution)/shard_map/pallas_call | solution.py:97
  (104 shorter events, 28.2 us)
Async XLA Ops:
  0.6 70.4 %copy-start = (bf16[128,4608]{1,0:T(8,128)(2,1)S(1)}, bf16[128,4608]{1,0:T(8,128)(2,1)}, u32[]{:S(2)}) copy-start(bf16[128,4608]{1,0:T(8,128)(2,1)} %param.11) | copy-start | bytes 3538948
  0.6 51.6 %copy-start.12 = (s32[512]{0:T(512)S(1)}, s32[512]{0:T(512)}, u32[]{:S(2)}) copy-start(s32[512]{0:T(512)} %param.12) | copy-start | bytes 6148
  0.7 6.6 %collective-permute-start.1 = (bf16[128,4608]{1,0:T(8,128)(2,1)}, bf16[128,4608]{1,0:T(8,128)(2,1)S(1)}, u32[]{:S(2)}, u32[]{:S(2)}) collective-permute-start(bf16[128,4608]{1,0:T(8,128)(2,1)} %param.8), channel_id=1, source_target_pairs={{0,1},{1,0},{2,3},{3,2},{4,5},{5,4},{6,7},{7,6},{8,9},{9,8},{10,11... | collective-permute-start | bytes 3538952 | tf_op jit(solution)/shard_map/ppermute | solution.py:31
  0.8 6.5 %collective-permute-start = (bf16[72,1024]{1,0:T(8,128)(2,1)}, bf16[72,1024]{1,0:T(8,128)(2,1)S(1)}, u32[]{:S(2)}, u32[]{:S(2)}) collective-permute-start(bf16[72,1024]{1,0:T(8,128)(2,1)} %mine_ref.1), channel_id=1, source_target_pairs={{16,0},{20,4},{24,8},{28,12},{0,16},{4,20},{8,24},{12,28},{48,32},... | collective-permute-start | bytes 442376 | tf_op jit(solution)/shard_map/ppermute | solution.py:27
  3.4 16.5 %collective-permute-start.4 = (f32[512,128]{1,0:T(8,128)S(1)}, f32[512,128]{1,0:T(8,128)S(1)}, u32[]{:S(2)}, u32[]{:S(2)}) collective-permute-start(f32[512,128]{1,0:T(8,128)S(1)} %fusion.41), channel_id=1, source_target_pairs={{0,1},{1,0},{2,3},{3,2},{4,5},{5,4},{6,7},{7,6},{8,9},{9,8},{10,11... | collective-permute-start | bytes 786440 | tf_op jit(solution)/shard_map/ppermute | solution.py:31
  9.6 10.3 %collective-permute-start.2 = (bf16[2,72,640]{2,1,0:T(8,128)(2,1)}, bf16[2,72,640]{2,1,0:T(8,128)(2,1)S(1)}, u32[]{:S(2)}, u32[]{:S(2)}) collective-permute-start(bf16[2,72,640]{2,1,0:T(8,128)(2,1)} %get-tuple-element.70), channel_id=1, source_target_pairs={{32,0},{36,4},{40,8},{44,12},{48,16},{52,20},{56,24},{60,28},{64,3... | collective-permute-start | bytes 552968 | tf_op jit(solution)/shard_map/ppermute | solution.py:27
  15.5 7.4 %collective-permute-start.3 = (bf16[2,72,640]{2,1,0:T(8,128)(2,1)}, bf16[2,72,640]{2,1,0:T(8,128)(2,1)}, u32[]{:S(2)}, u32[]{:S(2)}) collective-permute-start(bf16[2,72,640]{2,1,0:T(8,128)(2,1)} %get-tuple-element.70), channel_id=1, source_target_pairs={{224,0},{228,4},{232,8},{236,12},{240,16},{244,20},{248,24},{252,2... | collective-permute-start | bytes 552968 | tf_op jit(solution)/shard_map/ppermute | solution.py:27
  15.5 10.8 %collective-permute-start.9 = (bf16[2,72,384]{2,1,0:T(8,128)(2,1)}, bf16[2,72,384]{2,1,0:T(8,128)(2,1)S(1)}, u32[]{:S(2)}, u32[]{:S(2)}) collective-permute-start(bf16[2,72,384]{2,1,0:T(8,128)(2,1)} %get-tuple-element.68), channel_id=1, source_target_pairs={{4,0},{8,4},{12,8},{0,12},{20,16},{24,20},{28,24},{16,28},{36,32},... | collective-permute-start | bytes 331784 | tf_op jit(solution)/shard_map/ppermute | solution.py:27
  18.5 37.5 %collective-permute-start.17 = (bf16[128,4608]{1,0:T(8,128)(2,1)}, bf16[128,4608]{1,0:T(8,128)(2,1)}, u32[]{:S(2)}, u32[]{:S(2)}) collective-permute-start(bf16[128,4608]{1,0:T(8,128)(2,1)} %param.8), channel_id=1, source_target_pairs={{0,2},{1,3},{2,0},{3,1},{4,6},{5,7},{6,4},{7,5},{8,10},{9,11},{10,... | collective-permute-start | bytes 3538952 | tf_op jit(solution)/shard_map/ppermute | solution.py:31
  19.9 17.4 %collective-permute-start.11 = (bf16[2,72,384]{2,1,0:T(8,128)(2,1)}, bf16[2,72,384]{2,1,0:T(8,128)(2,1)S(1)}, u32[]{:S(2)}, u32[]{:S(2)}) collective-permute-start(bf16[2,72,384]{2,1,0:T(8,128)(2,1)} %get-tuple-element.68), channel_id=1, source_target_pairs={{12,0},{0,4},{4,8},{8,12},{28,16},{16,20},{20,24},{24,28},{44,32},... | collective-permute-start | bytes 331784 | tf_op jit(solution)/shard_map/ppermute | solution.py:27
  22.9 7.7 %collective-permute-start.10 = (bf16[2,72,384]{2,1,0:T(8,128)(2,1)}, bf16[2,72,384]{2,1,0:T(8,128)(2,1)S(1)}, u32[]{:S(2)}, u32[]{:S(2)}) collective-permute-start(bf16[2,72,384]{2,1,0:T(8,128)(2,1)} %get-tuple-element.68), channel_id=1, source_target_pairs={{8,0},{12,4},{0,8},{4,12},{24,16},{28,20},{16,24},{20,28},{40,32},... | collective-permute-start | bytes 331784 | tf_op jit(solution)/shard_map/ppermute | solution.py:27
  26.1 5.5 %collective-permute-start.5 = (bf16[2,72,640]{2,1,0:T(8,128)(2,1)S(1)}, bf16[2,72,640]{2,1,0:T(8,128)(2,1)S(1)}, u32[]{:S(2)}, u32[]{:S(2)}) collective-permute-start(bf16[2,72,640]{2,1,0:T(8,128)(2,1)S(1)} %collective-permute-done.2), channel_id=1, source_target_pairs={{32,0},{36,4},{40,8},{44,12},{48,16},{52,20},{56,24},{60,28},{64,3... | collective-permute-start | bytes 552968 | tf_op jit(solution)/shard_map/ppermute | solution.py:27
  26.9 7.0 %collective-permute-start.6 = (bf16[2,72,640]{2,1,0:T(8,128)(2,1)}, bf16[2,72,640]{2,1,0:T(8,128)(2,1)S(1)}, u32[]{:S(2)}, u32[]{:S(2)}) collective-permute-start(bf16[2,72,640]{2,1,0:T(8,128)(2,1)} %collective-permute-done.3), channel_id=1, source_target_pairs={{224,0},{228,4},{232,8},{236,12},{240,16},{244,20},{248,24},{252,2... | collective-permute-start | bytes 552968 | tf_op jit(solution)/shard_map/ppermute | solution.py:27
  33.9 5.6 %collective-permute-start.7 = (bf16[2,72,640]{2,1,0:T(8,128)(2,1)S(1)}, bf16[2,72,640]{2,1,0:T(8,128)(2,1)}, u32[]{:S(2)}, u32[]{:S(2)}) collective-permute-start(bf16[2,72,640]{2,1,0:T(8,128)(2,1)S(1)} %collective-permute-done.5), channel_id=1, source_target_pairs={{32,0},{36,4},{40,8},{44,12},{48,16},{52,20},{56,24},{60,28},{64,3... | collective-permute-start | bytes 552968 | tf_op jit(solution)/shard_map/ppermute | solution.py:27
  35.2 18.4 %collective-permute-start.14 = (bf16[4,2,72,640]{3,2,1,0:T(8,128)(2,1)S(1)}, bf16[4,2,72,640]{3,2,1,0:T(8,128)(2,1)}, u32[]{:S(2)}, u32[]{:S(2)}) collective-permute-start(bf16[4,2,72,640]{3,2,1,0:T(8,128)(2,1)S(1)} %pad_maximum_fusion), channel_id=1, source_target_pairs={{4,0},{8,4},{12,8},{0,12},{20,16},{24,20},{28,24},{16,28},{36,32},... | collective-permute-start | bytes 2211848 | tf_op jit(solution)/shard_map/ppermute | solution.py:27
  36.3 17.3 %collective-permute-start.15 = (bf16[4,2,72,640]{3,2,1,0:T(8,128)(2,1)S(1)}, bf16[4,2,72,640]{3,2,1,0:T(8,128)(2,1)}, u32[]{:S(2)}, u32[]{:S(2)}) collective-permute-start(bf16[4,2,72,640]{3,2,1,0:T(8,128)(2,1)S(1)} %pad_maximum_fusion), channel_id=1, source_target_pairs={{12,0},{0,4},{4,8},{8,12},{28,16},{16,20},{20,24},{24,28},{44,32},... | collective-permute-start | bytes 2211848 | tf_op jit(solution)/shard_map/ppermute | solution.py:27
  37.3 6.9 %collective-permute-start.8 = (bf16[2,72,640]{2,1,0:T(8,128)(2,1)S(1)}, bf16[2,72,640]{2,1,0:T(8,128)(2,1)}, u32[]{:S(2)}, u32[]{:S(2)}) collective-permute-start(bf16[2,72,640]{2,1,0:T(8,128)(2,1)S(1)} %collective-permute-done.6), channel_id=1, source_target_pairs={{224,0},{228,4},{232,8},{236,12},{240,16},{244,20},{248,24},{252,2... | collective-permute-start | bytes 552968 | tf_op jit(solution)/shard_map/ppermute | solution.py:27
  44.1 7.6 %collective-permute-start.16 = (bf16[2,72,640]{2,1,0:T(8,128)(2,1)}, bf16[2,72,640]{2,1,0:T(8,128)(2,1)}, u32[]{:S(2)}, u32[]{:S(2)}) collective-permute-start(bf16[2,72,640]{2,1,0:T(8,128)(2,1)} %collective-permute-done.7), channel_id=1, source_target_pairs={{32,0},{36,4},{40,8},{44,12},{48,16},{52,20},{56,24},{60,28},{64,3... | collective-permute-start | bytes 552968 | tf_op jit(solution)/shard_map/ppermute | solution.py:27
  44.8 11.6 %collective-permute-start.12 = (bf16[576,384]{1,0:T(8,128)(2,1)S(1)}, bf16[576,384]{1,0:T(8,128)(2,1)S(1)}, u32[]{:S(2)}, u32[]{:S(2)}) collective-permute-start(bf16[576,384]{1,0:T(8,128)(2,1)S(1)} %bitcast.116), channel_id=1, source_target_pairs={{32,0},{36,4},{40,8},{44,12},{48,16},{52,20},{56,24},{60,28},{64,3... | collective-permute-start | bytes 1327112 | tf_op jit(solution)/shard_map/ppermute | solution.py:27
  51.8 9.5 %collective-permute-start.13 = (bf16[576,384]{1,0:T(8,128)(2,1)S(1)}, bf16[576,384]{1,0:T(8,128)(2,1)S(1)}, u32[]{:S(2)}, u32[]{:S(2)}) collective-permute-start(bf16[576,384]{1,0:T(8,128)(2,1)S(1)} %bitcast.117), channel_id=1, source_target_pairs={{224,0},{228,4},{232,8},{236,12},{240,16},{244,20},{248,24},{252,2... | collective-permute-start | bytes 1327112 | tf_op jit(solution)/shard_map/ppermute | solution.py:27
  53.6 21.9 %collective-permute-start.20 = (bf16[4,2,72,640]{3,2,1,0:T(8,128)(2,1)}, bf16[4,2,72,640]{3,2,1,0:T(8,128)(2,1)S(1)}, u32[]{:S(2)}, u32[]{:S(2)}) collective-permute-start(bf16[4,2,72,640]{3,2,1,0:T(8,128)(2,1)} %collective-permute-done.14), channel_id=1, source_target_pairs={{4,0},{8,4},{12,8},{0,12},{20,16},{24,20},{28,24},{16,28},{36,32},... | collective-permute-start | bytes 2211848 | tf_op jit(solution)/shard_map/ppermute | solution.py:27
  61.3 7.5 %collective-permute-start.22 = (bf16[128,4608]{1,0:T(8,128)(2,1)}, bf16[128,4608]{1,0:T(8,128)(2,1)S(1)}, u32[]{:S(2)}, u32[]{:S(2)}) collective-permute-start(bf16[128,4608]{1,0:T(8,128)(2,1)} %collective-permute-done.17), channel_id=1, source_target_pairs={{0,1},{1,0},{2,3},{3,2},{4,5},{5,4},{6,7},{7,6},{8,9},{9,8},{10,11... | collective-permute-start | bytes 3538952 | tf_op jit(solution)/shard_map/ppermute | solution.py:31
  61.3 14.2 %collective-permute-start.18 = (bf16[576,384]{1,0:T(8,128)(2,1)S(1)}, bf16[576,384]{1,0:T(8,128)(2,1)}, u32[]{:S(2)}, u32[]{:S(2)}) collective-permute-start(bf16[576,384]{1,0:T(8,128)(2,1)S(1)} %collective-permute-done.12), channel_id=1, source_target_pairs={{32,0},{36,4},{40,8},{44,12},{48,16},{52,20},{56,24},{60,28},{64,3... | collective-permute-start | bytes 1327112 | tf_op jit(solution)/shard_map/ppermute | solution.py:27
  61.6 14.0 %collective-permute-start.19 = (bf16[576,384]{1,0:T(8,128)(2,1)S(1)}, bf16[576,384]{1,0:T(8,128)(2,1)}, u32[]{:S(2)}, u32[]{:S(2)}) collective-permute-start(bf16[576,384]{1,0:T(8,128)(2,1)S(1)} %collective-permute-done.13), channel_id=1, source_target_pairs={{224,0},{228,4},{232,8},{236,12},{240,16},{244,20},{248,24},{252,2... | collective-permute-start | bytes 1327112 | tf_op jit(solution)/shard_map/ppermute | solution.py:27
  63.3 19.7 %collective-permute-start.21 = (bf16[4,2,72,640]{3,2,1,0:T(8,128)(2,1)S(1)}, bf16[4,2,72,640]{3,2,1,0:T(8,128)(2,1)}, u32[]{:S(2)}, u32[]{:S(2)}) collective-permute-start(bf16[4,2,72,640]{3,2,1,0:T(8,128)(2,1)S(1)} %pad_maximum_fusion.1), channel_id=1, source_target_pairs={{12,0},{0,4},{4,8},{8,12},{28,16},{16,20},{20,24},{24,28},{44,32},... | collective-permute-start | bytes 2211848 | tf_op jit(solution)/shard_map/ppermute | solution.py:27
  83.0 8.9 %collective-permute-start.27 = (f32[512,128]{1,0:T(8,128)S(1)}, f32[512,128]{1,0:T(8,128)S(1)}, u32[]{:S(2)}, u32[]{:S(2)}) collective-permute-start(f32[512,128]{1,0:T(8,128)S(1)} %add.146), channel_id=1, source_target_pairs={{0,2},{1,3},{2,0},{3,1},{4,6},{5,7},{6,4},{7,5},{8,10},{9,11},{10,... | collective-permute-start | bytes 786440 | tf_op jit(solution)/shard_map/ppermute | solution.py:31
  84.2 13.9 %collective-permute-start.25 = (bf16[576,384]{1,0:T(8,128)(2,1)}, bf16[576,384]{1,0:T(8,128)(2,1)S(1)}, u32[]{:S(2)}, u32[]{:S(2)}) collective-permute-start(bf16[576,384]{1,0:T(8,128)(2,1)} %collective-permute-done.18), channel_id=1, source_target_pairs={{32,0},{36,4},{40,8},{44,12},{48,16},{52,20},{56,24},{60,28},{64,3... | collective-permute-start | bytes 1327112 | tf_op jit(solution)/shard_map/ppermute | solution.py:27
  85.8 12.3 %collective-permute-start.26 = (bf16[576,384]{1,0:T(8,128)(2,1)}, bf16[576,384]{1,0:T(8,128)(2,1)S(1)}, u32[]{:S(2)}, u32[]{:S(2)}) collective-permute-start(bf16[576,384]{1,0:T(8,128)(2,1)} %collective-permute-done.19), channel_id=1, source_target_pairs={{224,0},{228,4},{232,8},{236,12},{240,16},{244,20},{248,24},{252,2... | collective-permute-start | bytes 1327112 | tf_op jit(solution)/shard_map/ppermute | solution.py:27
  86.3 24.9 %collective-permute-start.23 = (bf16[4,2,72,640]{3,2,1,0:T(8,128)(2,1)S(1)}, bf16[4,2,72,640]{3,2,1,0:T(8,128)(2,1)S(1)}, u32[]{:S(2)}, u32[]{:S(2)}) collective-permute-start(bf16[4,2,72,640]{3,2,1,0:T(8,128)(2,1)S(1)} %pad_maximum_fusion.1), channel_id=1, source_target_pairs={{4,0},{8,4},{12,8},{0,12},{20,16},{24,20},{28,24},{16,28},{36,32},... | collective-permute-start | bytes 2211848 | tf_op jit(solution)/shard_map/ppermute | solution.py:27
  87.6 23.6 %collective-permute-start.24 = (bf16[4,2,72,640]{3,2,1,0:T(8,128)(2,1)}, bf16[4,2,72,640]{3,2,1,0:T(8,128)(2,1)S(1)}, u32[]{:S(2)}, u32[]{:S(2)}) collective-permute-start(bf16[4,2,72,640]{3,2,1,0:T(8,128)(2,1)} %collective-permute-done.21), channel_id=1, source_target_pairs={{12,0},{0,4},{4,8},{8,12},{28,16},{16,20},{20,24},{24,28},{44,32},... | collective-permute-start | bytes 2211848 | tf_op jit(solution)/shard_map/ppermute | solution.py:27
  101.7 6.0 %collective-permute-start.28 = (bf16[288,384]{1,0:T(8,128)(2,1)S(1)}, bf16[288,384]{1,0:T(8,128)(2,1)S(1)}, u32[]{:S(2)}, u32[]{:S(2)}) collective-permute-start(bf16[288,384]{1,0:T(8,128)(2,1)S(1)} %slice.71), channel_id=1, source_target_pairs={{32,0},{36,4},{40,8},{44,12},{48,16},{52,20},{56,24},{60,28},{64,3... | collective-permute-start | bytes 663560 | tf_op jit(solution)/shard_map/ppermute | solution.py:27
  103.3 7.1 %collective-permute-start.29 = (bf16[288,384]{1,0:T(8,128)(2,1)S(1)}, bf16[288,384]{1,0:T(8,128)(2,1)S(1)}, u32[]{:S(2)}, u32[]{:S(2)}) collective-permute-start(bf16[288,384]{1,0:T(8,128)(2,1)S(1)} %slice.72), channel_id=1, source_target_pairs={{224,0},{228,4},{232,8},{236,12},{240,16},{244,20},{248,24},{252,2... | collective-permute-start | bytes 663560 | tf_op jit(solution)/shard_map/ppermute | solution.py:27
  (11 other events, 88.6 us)

commit v9 on v8

--- a/solution.py
+++ b/solution.py
@@ -162,7 +162,7 @@
     b_p1, b_m1 = fetch(b_own, dz=1), fetch(b_own, dz=-1)
     high = jnp.stack([a_p3, a_p4, a_m3, a_m2])
 
-    low_p, low_m, high = together(low_p, low_m, high)
+    low_p, low_m, high, from_chip = together(low_p, low_m, high, from_chip)
     low_o, high_m = fetch(low_p, dy=1), fetch(high, dy=-1)
     b_p1, b_m1, low_p, own_rows, from_core, from_chip = together(
         b_p1, b_m1, low_p, own_rows, from_core, from_chip
@@ -215,22 +215,22 @@
     b_p3, b_m3 = fetch(b_p2, dz=1), fetch(b_m2, dz=-1)
     chip_sum = partial + core_partial
     far_sum = swap_tensor(chip_sum, 2)
-    low_all, low_o, far_sum, chip_sum = together(low_all, low_o, far_sum, chip_sum)
+    low_all, low_o, far_sum, chip_sum, b_q2, b_n2 = together(
+        low_all, low_o, far_sum, chip_sum, b_p2, b_m2
+    )
     low_all = placed(low_all, low_o, 2)
     a_total = product(
         ADAPTER_SCALE * contract(adapter_backward, adapter_down_factors[:a_width], 1, 1),
         [(i, low_all[i]) for i in range(4)],
     )
-    b_p2, b_m2, b_p3, b_m3, a_total, b_total = together(
-        b_p2, b_m2, b_p3, b_m3, a_total, b_total
-    )
+    b_p3, b_m3, a_total, chip_sum, far_sum = together(b_p3, b_m3, a_total, chip_sum, far_sum)
     cut = b_own.shape[0] // 2 // 16 * 16
     b_p4, b_m4 = fetch(b_p3[:cut], dz=1), fetch(b_m3[cut:], dz=-1)
     adapter_input = ((chip_sum + far_sum) * select_rows).astype(jnp.bfloat16)
     (adapter_input,) = together(adapter_input)
     up_factor_gradient = ADAPTER_SCALE * contract(adapter_input, gradients, 0, 0)
     high_all = placed(spread(high), high_m, 3)
-    b_total = product(b_total, [(7, b_m2), (3, b_p2), (6, b_m3), (4, b_p3)])
+    b_total = product(b_total, [(7, b_n2), (3, b_q2), (6, b_m3), (4, b_p3)])
 
     b_p4, b_m4, high_all, b_total, up_factor_gradient = together(
         b_p4, b_m4, high_all, b_total, up_factor_gradient

time: 116 us -> 113 us (0.974)
  waiting for transfers between devices: 41.6 us -> 39.7 us
    ppermute x25, waiting for transfers between devices: 39.5 us -> 36.9 us  [fetch(): return lax.ppermute(x, 'dp', pairs)]
  transfers between devices with their start and end apart: 30 -> 30, of which waited for: 13 -> 14; matrix products, arithmetic and copies ran while one was open for 23% -> 24% of each run, Pallas kernels for 4% -> 4%
where the time goes in v9:
time: 113 us
  waiting for transfers between devices  39.7 us (35%)
  starting transfers between devices  34.6 us (31%)
  matrix products  15.1 us (13%)
  local copies, waits for them, and re-layouts  10.6 us (9%)
  Pallas kernels  8.08 us (7%)
  other arithmetic  3.04 us (3%)
  between operations  1.8 us (2%)
    ppermute x25, waiting for transfers between devices, fetch(): return lax.ppermute(x, 'dp', pairs)  36.9 us
    ppermute x25, starting transfers between devices, fetch(): return lax.ppermute(x, 'dp', pairs)  31.7 us
    dot_general x16, matrix products, contract(): lax.dot_general(left, right, (((left_dim,), (right_dim,)), ((), ())), pre...  13.4 us
    dynamic_update_slice x9, local copies, waits for them, and re-layouts, placed(): lax.dynamic_update_slice_in_dim(array, jnp.expand_dims(chunk, at), (y + d...  5.1 us
    pallas_call x2, Pallas kernels, in_vmem(): pl.pallas_call(kernel, in_specs=[pl.BlockSpec(memory_space=pltpu.VMEM)] *...  4.76 us
    ppermute x5, starting transfers between devices, swap_tensor(): return lax.ppermute(x, 'tensor', [(t, t ^ mask) for t in range(4)])  2.92 us
    ppermute x5, waiting for transfers between devices, swap_tensor(): return lax.ppermute(x, 'tensor', [(t, t ^ mask) for t in range(4)])  2.73 us
  transfers between devices with their start and end apart: 30, of which 14 were waited for; matrix products, arithmetic and copies ran while one was open for 24% of the time, Pallas kernels for 4%

profile of v9, /device:TPU:6, one launch (start us, length us, event | category | flops | bytes accessed | tf_op | source)
XLA Modules:
  0.0 112.9 jit_solution(31532440871900859)
XLA Ops:
  1.7 1.7 %fusion.41 = f32[512,128]{1,0:T(8,128)S(1)} fusion(bf16[512,1024]{1,0:T(8,128)(2,1)} %head_ref.1, bf16[1024,128]{1,0:T(8,128)(2,1)} %param.10), kind=kOutput, calls=%fused_computation.78 | convolution fusion | flops 134217728 | bytes 1572864 | tf_op jit(solution)/shard_map/dot_general | solution.py:126
  3.6 3.6 %collective-permute-done.far_ref = bf16[72,1024]{1,0:T(8,128)(2,1)S(1)} collective-permute-done((bf16[72,1024]{1,0:T(8,128)(2,1)}, bf16[72,1024]{1,0:T(8,128)(2,1)S(1)}, u32[]{:S(2)}, u32[]{:S(2)}) %collective-permute-start) | collective-permute-done | bytes 147488 | tf_op jit(solution)/shard_map/ppermute | solution.py:27
  7.9 1.7 %shard_map.94 = (bf16[2,72,640]{2,1,0:T(8,128)(2,1)}, bf16[2,72,384]{2,1,0:T(8,128)(2,1)}) custom-call(s32[1]{0:T(128)} %bitcast.x_ref, bf16[72,1024]{1,0:T(8,128)(2,1)} %mine_ref.1, bf16[72,1024]{1,0:T(8,128)(2,1)} %copy-done.10), custom_call_target="tpu_custom_call" | custom-call | tf_op jit(solution)/shard_map/pallas_call | solution.py:84
  9.6 5.9 %collective-permute-start.2 = (bf16[2,72,640]{2,1,0:T(8,128)(2,1)}, bf16[2,72,640]{2,1,0:T(8,128)(2,1)S(1)}, u32[]{:S(2)}, u32[]{:S(2)}) collective-permute-start(bf16[2,72,640]{2,1,0:T(8,128)(2,1)} %get-tuple-element.72), channel_id=1, source_target_pairs={{32,0},{36,4},{40,8},{44,12},{48,16},{52,20},{56,24},{60,28},{64,3... | collective-permute-start | bytes 552968 | tf_op jit(solution)/shard_map/ppermute | solution.py:27
  15.5 3.0 %collective-permute-start.9 = (bf16[2,72,384]{2,1,0:T(8,128)(2,1)}, bf16[2,72,384]{2,1,0:T(8,128)(2,1)S(1)}, u32[]{:S(2)}, u32[]{:S(2)}) collective-permute-start(bf16[2,72,384]{2,1,0:T(8,128)(2,1)} %get-tuple-element.70), channel_id=1, source_target_pairs={{4,0},{8,4},{12,8},{0,12},{20,16},{24,20},{28,24},{16,28},{36,32},... | collective-permute-start | bytes 331784 | tf_op jit(solution)/shard_map/ppermute | solution.py:27
  18.5 1.4 %collective-permute-start.17 = (bf16[128,4608]{1,0:T(8,128)(2,1)}, bf16[128,4608]{1,0:T(8,128)(2,1)}, u32[]{:S(2)}, u32[]{:S(2)}) collective-permute-start(bf16[128,4608]{1,0:T(8,128)(2,1)} %param.8), channel_id=1, source_target_pairs={{0,2},{1,3},{2,0},{3,1},{4,6},{5,7},{6,4},{7,5},{8,10},{9,11},{10,... | collective-permute-start | bytes 3538952 | tf_op jit(solution)/shard_map/ppermute | solution.py:31
  19.9 3.0 %collective-permute-done.3 = bf16[2,72,640]{2,1,0:T(8,128)(2,1)} collective-permute-done((bf16[2,72,640]{2,1,0:T(8,128)(2,1)}, bf16[2,72,640]{2,1,0:T(8,128)(2,1)}, u32[]{:S(2)}, u32[]{:S(2)}) %collective-permute-start.3) | collective-permute-done | bytes 184352 | tf_op jit(solution)/shard_map/ppermute | solution.py:27
  22.9 3.2 %collective-permute-start.10 = (bf16[2,72,384]{2,1,0:T(8,128)(2,1)}, bf16[2,72,384]{2,1,0:T(8,128)(2,1)S(1)}, u32[]{:S(2)}, u32[]{:S(2)}) collective-permute-start(bf16[2,72,384]{2,1,0:T(8,128)(2,1)} %get-tuple-element.70), channel_id=1, source_target_pairs={{8,0},{12,4},{0,8},{4,12},{24,16},{28,20},{16,24},{20,28},{40,32},... | collective-permute-start | bytes 331784 | tf_op jit(solution)/shard_map/ppermute | solution.py:27
  26.9 1.8 %collective-permute-start.6 = (bf16[2,72,640]{2,1,0:T(8,128)(2,1)}, bf16[2,72,640]{2,1,0:T(8,128)(2,1)S(1)}, u32[]{:S(2)}, u32[]{:S(2)}) collective-permute-start(bf16[2,72,640]{2,1,0:T(8,128)(2,1)} %collective-permute-done.3), channel_id=1, source_target_pairs={{224,0},{228,4},{232,8},{236,12},{240,16},{244,20},{248,24},{252,2... | collective-permute-start | bytes 552968 | tf_op jit(solution)/shard_map/ppermute | solution.py:27
  31.6 2.2 %collective-permute-done.6 = bf16[2,72,640]{2,1,0:T(8,128)(2,1)S(1)} collective-permute-done((bf16[2,72,640]{2,1,0:T(8,128)(2,1)}, bf16[2,72,640]{2,1,0:T(8,128)(2,1)S(1)}, u32[]{:S(2)}, u32[]{:S(2)}) %collective-permute-start.6) | collective-permute-done | bytes 184352 | tf_op jit(solution)/shard_map/ppermute | solution.py:27
  37.3 2.0 %collective-permute-start.8 = (bf16[2,72,640]{2,1,0:T(8,128)(2,1)S(1)}, bf16[2,72,640]{2,1,0:T(8,128)(2,1)}, u32[]{:S(2)}, u32[]{:S(2)}) collective-permute-start(bf16[2,72,640]{2,1,0:T(8,128)(2,1)S(1)} %collective-permute-done.6), channel_id=1, source_target_pairs={{224,0},{228,4},{232,8},{236,12},{240,16},{244,20},{248,24},{252,2... | collective-permute-start | bytes 552968 | tf_op jit(solution)/shard_map/ppermute | solution.py:27
  39.5 4.6 %collective-permute-done.8 = bf16[2,72,640]{2,1,0:T(8,128)(2,1)} collective-permute-done((bf16[2,72,640]{2,1,0:T(8,128)(2,1)S(1)}, bf16[2,72,640]{2,1,0:T(8,128)(2,1)}, u32[]{:S(2)}, u32[]{:S(2)}) %collective-permute-start.8) | collective-permute-done | bytes 184352 | tf_op jit(solution)/shard_map/ppermute | solution.py:27
  45.7 6.1 %collective-permute-done.16 = bf16[2,72,640]{2,1,0:T(8,128)(2,1)} collective-permute-done((bf16[2,72,640]{2,1,0:T(8,128)(2,1)}, bf16[2,72,640]{2,1,0:T(8,128)(2,1)}, u32[]{:S(2)}, u32[]{:S(2)}) %collective-permute-start.16) | collective-permute-done | bytes 184352 | tf_op jit(solution)/shard_map/ppermute | solution.py:27
  52.3 1.3 %pad_maximum_fusion.1 = bf16[4,2,72,640]{3,2,1,0:T(8,128)(2,1)S(1)} fusion(bf16[1,2,72,640]{3,2,1,0:T(8,128)(2,1)} %bitcast.120, bf16[1,2,72,640]{3,2,1,0:T(8,128)(2,1)} %bitcast.14, bf16[1,2,72,640]{3,2,1,0:T(8,128)(2,1)} %bitcast.13, bf16[1,2,72,640]{3,2,1,0:T(8,128)(2,1)} %bitcast.12), kind=kLoop, calls=%fused_computation.15 | loop fusion | flops 1105920 | bytes 1474560 | tf_op jit(solution)/shard_map/stack | solution.py:163
  53.6 2.3 %collective-permute-start.20 = (bf16[4,2,72,640]{3,2,1,0:T(8,128)(2,1)}, bf16[4,2,72,640]{3,2,1,0:T(8,128)(2,1)S(1)}, u32[]{:S(2)}, u32[]{:S(2)}) collective-permute-start(bf16[4,2,72,640]{3,2,1,0:T(8,128)(2,1)} %collective-permute-done.14), channel_id=1, source_target_pairs={{4,0},{8,4},{12,8},{0,12},{20,16},{24,20},{28,24},{16,28},{36,32},... | collective-permute-start | bytes 2211848 | tf_op jit(solution)/shard_map/ppermute | solution.py:27
  56.4 4.9 %collective-permute-done.13 = bf16[576,384]{1,0:T(8,128)(2,1)S(1)} collective-permute-done((bf16[576,384]{1,0:T(8,128)(2,1)S(1)}, bf16[576,384]{1,0:T(8,128)(2,1)S(1)}, u32[]{:S(2)}, u32[]{:S(2)}) %collective-permute-start.13) | collective-permute-done | bytes 442400 | tf_op jit(solution)/shard_map/ppermute | solution.py:27
  62.2 1.7 %collective-permute-start.19 = (bf16[576,384]{1,0:T(8,128)(2,1)S(1)}, bf16[576,384]{1,0:T(8,128)(2,1)}, u32[]{:S(2)}, u32[]{:S(2)}) collective-permute-start(bf16[576,384]{1,0:T(8,128)(2,1)S(1)} %collective-permute-done.13), channel_id=1, source_target_pairs={{224,0},{228,4},{232,8},{236,12},{240,16},{244,20},{248,24},{252,2... | collective-permute-start | bytes 1327112 | tf_op jit(solution)/shard_map/ppermute | solution.py:27
  65.5 1.3 %bitcast_dynamic-update-slice_fusion.4 = bf16[4,2,4,72,640]{4,3,2,1,0:T(8,128)(2,1)S(1)} fusion(bf16[4,2,4,72,640]{4,3,2,1,0:T(8,128)(2,1)S(1)} %bitcast_dynamic-update-slice_fusion.5, s32[]{:T(128)S(6)} %select_n.100, bf16[4,2,72,640]{3,2,1,0:T(8,128)(2,1)} %collective-permute-done.15), kind=kLoop, calls=%fused_computation.20 | loop fusion | bytes 1474564 | tf_op jit(solution)/shard_map/dynamic_update_slice | solution.py:142
  67.4 1.4 %constant_dynamic-update-slice_fusion.1 = bf16[512,4608]{1,0:T(8,128)(2,1)S(1)} fusion(bf16[512,4608]{1,0:T(8,128)(2,1)S(1)} %constant_dynamic-update-slice_fusion.2, bf16[128,4608]{1,0:T(8,128)(2,1)} %collective-permute-done.17, s32[]{:T(128)S(6)} %select_n.105), kind=kLoop, calls=%fused_computation.64 | loop fusion | bytes 2359300 | tf_op jit(solution)/shard_map/dynamic_update_slice | solution.py:175
  68.9 1.6 %shard_map.95.z_ref = bf16[8,512,576]{2,1,0:T(8,128)(2,1)S(1)} custom-call(s32[1]{0:T(128)} %bitcast.20.start_ref, bf16[512,4608]{1,0:T(8,128)(2,1)S(1)} %constant_dynamic-update-slice_fusion.g_ref), custom_call_target="tpu_custom_call" | custom-call | tf_op jit(solution)/shard_map/pallas_call | solution.py:49
  71.0 1.4 %fusion.3.back_ref = bf16[512,128]{1,0:T(8,128)(2,1)S(1)} fusion(bf16[512,4608]{1,0:T(8,128)(2,1)S(1)} %constant_dynamic-update-slice_fusion.g_ref, bf16[128,4608]{1,0:T(8,128)(2,1)S(1)} %copy-done, s32[128]{0:T(128)S(1)} %and_select_fusion, s32[512]{0:T(512)S(1)} %add_select_fusion, pred[512]{0:T(512)(128)(4,1)S(1)} %iota_compare_fusion.1), kind=kOutput, calls=%fused_computation.11 | convolution fusion | flops 604241920 | bytes 6032384 | tf_op jit(solution)/shard_map/dot_general | solution.py:15
  73.7 1.3 %shard_map.96 = f32[1024,128]{1,0:T(8,128)} custom-call(bf16[512,1024]{1,0:T(8,128)(2,1)S(1)} %copy-done.1, bf16[512,128]{1,0:T(8,128)(2,1)S(1)} %fusion.3.back_ref), custom_call_target="tpu_custom_call" | custom-call | tf_op jit(solution)/shard_map/pallas_call | solution.py:97
  75.6 5.9 %collective-permute-done.21 = bf16[4,2,72,640]{3,2,1,0:T(8,128)(2,1)} collective-permute-done((bf16[4,2,72,640]{3,2,1,0:T(8,128)(2,1)S(1)}, bf16[4,2,72,640]{3,2,1,0:T(8,128)(2,1)}, u32[]{:S(2)}, u32[]{:S(2)}) %collective-permute-start.21) | collective-permute-done | bytes 737312 | tf_op jit(solution)/shard_map/ppermute | solution.py:27
  83.1 1.7 %collective-permute-start.26 = (bf16[576,384]{1,0:T(8,128)(2,1)}, bf16[576,384]{1,0:T(8,128)(2,1)S(1)}, u32[]{:S(2)}, u32[]{:S(2)}) collective-permute-start(bf16[576,384]{1,0:T(8,128)(2,1)} %collective-permute-done.19), channel_id=1, source_target_pairs={{224,0},{228,4},{232,8},{236,12},{240,16},{244,20},{248,24},{252,2... | collective-permute-start | bytes 1327112 | tf_op jit(solution)/shard_map/ppermute | solution.py:27
  88.3 2.7 %collective-permute-done.27 = f32[512,128]{1,0:T(8,128)S(1)} collective-permute-done((f32[512,128]{1,0:T(8,128)S(1)}, f32[512,128]{1,0:T(8,128)S(1)}, u32[]{:S(2)}, u32[]{:S(2)}) %collective-permute-start.27) | collective-permute-done | bytes 262176 | tf_op jit(solution)/shard_map/ppermute | solution.py:31
  92.2 1.5 %fusion.14 = f32[512,384]{1,0:T(8,128)S(1)} fusion(bf16[576,384]{1,0:T(8,128)(2,1)} %collective-permute-done.19, bf16[8,512,576]{2,1,0:T(8,128)(2,1)S(1)} %shard_map.95.z_ref), kind=kOutput, calls=%fused_computation.33 | convolution fusion | flops 226492416 | bytes 1884160 | tf_op jit(solution)/shard_map/dot_general | solution.py:15
  95.6 1.5 %fusion.16 = f32[512,384]{1,0:T(8,128)S(1)} fusion(bf16[576,384]{1,0:T(8,128)(2,1)} %collective-permute-done.18, bf16[8,512,576]{2,1,0:T(8,128)(2,1)S(1)} %shard_map.95.z_ref), kind=kOutput, calls=%fused_computation.35 | convolution fusion | flops 226492416 | bytes 1884160 | tf_op jit(solution)/shard_map/dot_general | solution.py:15
  98.7 2.2 %convolution_multiply_fusion = f32[128,4608]{1,0:T(8,128)} fusion(bf16[512,128]{1,0:T(8,128)(2,1)S(1)} %select_convert_fusion.1, bf16[512,4608]{1,0:T(8,128)(2,1)S(1)} %constant_dynamic-update-slice_fusion.g_ref), kind=kOutput, calls=%fused_computation | convolution fusion | flops 604569600 | bytes 7208960 | tf_op jit(solution)/shard_map/dot_general | solution.py:15
  101.3 1.7 %collective-permute-start.29 = (bf16[288,384]{1,0:T(8,128)(2,1)S(1)}, bf16[288,384]{1,0:T(8,128)(2,1)S(1)}, u32[]{:S(2)}, u32[]{:S(2)}) collective-permute-start(bf16[288,384]{1,0:T(8,128)(2,1)S(1)} %slice.72), channel_id=1, source_target_pairs={{224,0},{228,4},{232,8},{236,12},{240,16},{244,20},{248,24},{252,2... | collective-permute-start | bytes 663560 | tf_op jit(solution)/shard_map/ppermute | solution.py:27
  103.6 3.6 %collective-permute-done.28 = bf16[288,384]{1,0:T(8,128)(2,1)S(1)} collective-permute-done((bf16[288,384]{1,0:T(8,128)(2,1)S(1)}, bf16[288,384]{1,0:T(8,128)(2,1)S(1)}, u32[]{:S(2)}, u32[]{:S(2)}) %collective-permute-start.28) | collective-permute-done | bytes 221216 | tf_op jit(solution)/shard_map/ppermute | solution.py:27
  107.2 1.3 %collective-permute-done.29 = bf16[288,384]{1,0:T(8,128)(2,1)S(1)} collective-permute-done((bf16[288,384]{1,0:T(8,128)(2,1)S(1)}, bf16[288,384]{1,0:T(8,128)(2,1)S(1)}, u32[]{:S(2)}, u32[]{:S(2)}) %collective-permute-start.29) | collective-permute-done | bytes 221216 | tf_op jit(solution)/shard_map/ppermute | solution.py:27
  109.5 3.5 %shard_map.97 = bf16[512,1024]{1,0:T(8,128)(2,1)} custom-call(bf16[8,512,576]{2,1,0:T(8,128)(2,1)S(1)} %shard_map.95.z_ref, bf16[4,576,640]{2,1,0:T(8,128)(2,1)S(1)} %bitcast.111, f32[512,640]{1,0:T(8,128)S(1)} %convolution_add_fusion.total_ref, f32[512,1]{1,0:T(8,128)S(1)} %fusion.35.live_ref, bf16[512,384]{1,0:T(8,128)(2,1)S(1)} %select_convert_fusion.b_ref), custom_call_target="tpu_custom_call" | custom-call | tf_op jit(solution)/shard_map/pallas_call | solution.py:97
  (104 shorter events, 27.9 us)
Async XLA Ops:
  0.6 70.4 %copy-start = (bf16[128,4608]{1,0:T(8,128)(2,1)S(1)}, bf16[128,4608]{1,0:T(8,128)(2,1)}, u32[]{:S(2)}) copy-start(bf16[128,4608]{1,0:T(8,128)(2,1)} %param.11) | copy-start | bytes 3538948
  0.6 51.6 %copy-start.12 = (s32[512]{0:T(512)S(1)}, s32[512]{0:T(512)}, u32[]{:S(2)}) copy-start(s32[512]{0:T(512)} %param.12) | copy-start | bytes 6148
  0.7 6.6 %collective-permute-start.1 = (bf16[128,4608]{1,0:T(8,128)(2,1)}, bf16[128,4608]{1,0:T(8,128)(2,1)S(1)}, u32[]{:S(2)}, u32[]{:S(2)}) collective-permute-start(bf16[128,4608]{1,0:T(8,128)(2,1)} %param.8), channel_id=1, source_target_pairs={{0,1},{1,0},{2,3},{3,2},{4,5},{5,4},{6,7},{7,6},{8,9},{9,8},{10,11... | collective-permute-start | bytes 3538952 | tf_op jit(solution)/shard_map/ppermute | solution.py:31
  0.8 6.5 %collective-permute-start = (bf16[72,1024]{1,0:T(8,128)(2,1)}, bf16[72,1024]{1,0:T(8,128)(2,1)S(1)}, u32[]{:S(2)}, u32[]{:S(2)}) collective-permute-start(bf16[72,1024]{1,0:T(8,128)(2,1)} %mine_ref.1), channel_id=1, source_target_pairs={{16,0},{20,4},{24,8},{28,12},{0,16},{4,20},{8,24},{12,28},{48,32},... | collective-permute-start | bytes 442376 | tf_op jit(solution)/shard_map/ppermute | solution.py:27
  3.4 16.5 %collective-permute-start.4 = (f32[512,128]{1,0:T(8,128)S(1)}, f32[512,128]{1,0:T(8,128)S(1)}, u32[]{:S(2)}, u32[]{:S(2)}) collective-permute-start(f32[512,128]{1,0:T(8,128)S(1)} %fusion.41), channel_id=1, source_target_pairs={{0,1},{1,0},{2,3},{3,2},{4,5},{5,4},{6,7},{7,6},{8,9},{9,8},{10,11... | collective-permute-start | bytes 786440 | tf_op jit(solution)/shard_map/ppermute | solution.py:31
  9.6 10.3 %collective-permute-start.2 = (bf16[2,72,640]{2,1,0:T(8,128)(2,1)}, bf16[2,72,640]{2,1,0:T(8,128)(2,1)S(1)}, u32[]{:S(2)}, u32[]{:S(2)}) collective-permute-start(bf16[2,72,640]{2,1,0:T(8,128)(2,1)} %get-tuple-element.72), channel_id=1, source_target_pairs={{32,0},{36,4},{40,8},{44,12},{48,16},{52,20},{56,24},{60,28},{64,3... | collective-permute-start | bytes 552968 | tf_op jit(solution)/shard_map/ppermute | solution.py:27
  15.5 7.4 %collective-permute-start.3 = (bf16[2,72,640]{2,1,0:T(8,128)(2,1)}, bf16[2,72,640]{2,1,0:T(8,128)(2,1)}, u32[]{:S(2)}, u32[]{:S(2)}) collective-permute-start(bf16[2,72,640]{2,1,0:T(8,128)(2,1)} %get-tuple-element.72), channel_id=1, source_target_pairs={{224,0},{228,4},{232,8},{236,12},{240,16},{244,20},{248,24},{252,2... | collective-permute-start | bytes 552968 | tf_op jit(solution)/shard_map/ppermute | solution.py:27
  15.5 10.8 %collective-permute-start.9 = (bf16[2,72,384]{2,1,0:T(8,128)(2,1)}, bf16[2,72,384]{2,1,0:T(8,128)(2,1)S(1)}, u32[]{:S(2)}, u32[]{:S(2)}) collective-permute-start(bf16[2,72,384]{2,1,0:T(8,128)(2,1)} %get-tuple-element.70), channel_id=1, source_target_pairs={{4,0},{8,4},{12,8},{0,12},{20,16},{24,20},{28,24},{16,28},{36,32},... | collective-permute-start | bytes 331784 | tf_op jit(solution)/shard_map/ppermute | solution.py:27
  18.5 35.1 %collective-permute-start.17 = (bf16[128,4608]{1,0:T(8,128)(2,1)}, bf16[128,4608]{1,0:T(8,128)(2,1)}, u32[]{:S(2)}, u32[]{:S(2)}) collective-permute-start(bf16[128,4608]{1,0:T(8,128)(2,1)} %param.8), channel_id=1, source_target_pairs={{0,2},{1,3},{2,0},{3,1},{4,6},{5,7},{6,4},{7,5},{8,10},{9,11},{10,... | collective-permute-start | bytes 3538952 | tf_op jit(solution)/shard_map/ppermute | solution.py:31
  19.9 17.4 %collective-permute-start.11 = (bf16[2,72,384]{2,1,0:T(8,128)(2,1)}, bf16[2,72,384]{2,1,0:T(8,128)(2,1)S(1)}, u32[]{:S(2)}, u32[]{:S(2)}) collective-permute-start(bf16[2,72,384]{2,1,0:T(8,128)(2,1)} %get-tuple-element.70), channel_id=1, source_target_pairs={{12,0},{0,4},{4,8},{8,12},{28,16},{16,20},{20,24},{24,28},{44,32},... | collective-permute-start | bytes 331784 | tf_op jit(solution)/shard_map/ppermute | solution.py:27
  22.9 7.7 %collective-permute-start.10 = (bf16[2,72,384]{2,1,0:T(8,128)(2,1)}, bf16[2,72,384]{2,1,0:T(8,128)(2,1)S(1)}, u32[]{:S(2)}, u32[]{:S(2)}) collective-permute-start(bf16[2,72,384]{2,1,0:T(8,128)(2,1)} %get-tuple-element.70), channel_id=1, source_target_pairs={{8,0},{12,4},{0,8},{4,12},{24,16},{28,20},{16,24},{20,28},{40,32},... | collective-permute-start | bytes 331784 | tf_op jit(solution)/shard_map/ppermute | solution.py:27
  26.1 5.5 %collective-permute-start.5 = (bf16[2,72,640]{2,1,0:T(8,128)(2,1)S(1)}, bf16[2,72,640]{2,1,0:T(8,128)(2,1)S(1)}, u32[]{:S(2)}, u32[]{:S(2)}) collective-permute-start(bf16[2,72,640]{2,1,0:T(8,128)(2,1)S(1)} %collective-permute-done.2), channel_id=1, source_target_pairs={{32,0},{36,4},{40,8},{44,12},{48,16},{52,20},{56,24},{60,28},{64,3... | collective-permute-start | bytes 552968 | tf_op jit(solution)/shard_map/ppermute | solution.py:27
  26.9 7.0 %collective-permute-start.6 = (bf16[2,72,640]{2,1,0:T(8,128)(2,1)}, bf16[2,72,640]{2,1,0:T(8,128)(2,1)S(1)}, u32[]{:S(2)}, u32[]{:S(2)}) collective-permute-start(bf16[2,72,640]{2,1,0:T(8,128)(2,1)} %collective-permute-done.3), channel_id=1, source_target_pairs={{224,0},{228,4},{232,8},{236,12},{240,16},{244,20},{248,24},{252,2... | collective-permute-start | bytes 552968 | tf_op jit(solution)/shard_map/ppermute | solution.py:27
  33.9 5.6 %collective-permute-start.7 = (bf16[2,72,640]{2,1,0:T(8,128)(2,1)S(1)}, bf16[2,72,640]{2,1,0:T(8,128)(2,1)}, u32[]{:S(2)}, u32[]{:S(2)}) collective-permute-start(bf16[2,72,640]{2,1,0:T(8,128)(2,1)S(1)} %collective-permute-done.5), channel_id=1, source_target_pairs={{32,0},{36,4},{40,8},{44,12},{48,16},{52,20},{56,24},{60,28},{64,3... | collective-permute-start | bytes 552968 | tf_op jit(solution)/shard_map/ppermute | solution.py:27
  35.2 18.4 %collective-permute-start.14 = (bf16[4,2,72,640]{3,2,1,0:T(8,128)(2,1)S(1)}, bf16[4,2,72,640]{3,2,1,0:T(8,128)(2,1)}, u32[]{:S(2)}, u32[]{:S(2)}) collective-permute-start(bf16[4,2,72,640]{3,2,1,0:T(8,128)(2,1)S(1)} %pad_maximum_fusion), channel_id=1, source_target_pairs={{4,0},{8,4},{12,8},{0,12},{20,16},{24,20},{28,24},{16,28},{36,32},... | collective-permute-start | bytes 2211848 | tf_op jit(solution)/shard_map/ppermute | solution.py:27
  36.3 17.3 %collective-permute-start.15 = (bf16[4,2,72,640]{3,2,1,0:T(8,128)(2,1)S(1)}, bf16[4,2,72,640]{3,2,1,0:T(8,128)(2,1)}, u32[]{:S(2)}, u32[]{:S(2)}) collective-permute-start(bf16[4,2,72,640]{3,2,1,0:T(8,128)(2,1)S(1)} %pad_maximum_fusion), channel_id=1, source_target_pairs={{12,0},{0,4},{4,8},{8,12},{28,16},{16,20},{20,24},{24,28},{44,32},... | collective-permute-start | bytes 2211848 | tf_op jit(solution)/shard_map/ppermute | solution.py:27
  37.3 6.9 %collective-permute-start.8 = (bf16[2,72,640]{2,1,0:T(8,128)(2,1)S(1)}, bf16[2,72,640]{2,1,0:T(8,128)(2,1)}, u32[]{:S(2)}, u32[]{:S(2)}) collective-permute-start(bf16[2,72,640]{2,1,0:T(8,128)(2,1)S(1)} %collective-permute-done.6), channel_id=1, source_target_pairs={{224,0},{228,4},{232,8},{236,12},{240,16},{244,20},{248,24},{252,2... | collective-permute-start | bytes 552968 | tf_op jit(solution)/shard_map/ppermute | solution.py:27
  44.1 7.6 %collective-permute-start.16 = (bf16[2,72,640]{2,1,0:T(8,128)(2,1)}, bf16[2,72,640]{2,1,0:T(8,128)(2,1)}, u32[]{:S(2)}, u32[]{:S(2)}) collective-permute-start(bf16[2,72,640]{2,1,0:T(8,128)(2,1)} %collective-permute-done.7), channel_id=1, source_target_pairs={{32,0},{36,4},{40,8},{44,12},{48,16},{52,20},{56,24},{60,28},{64,3... | collective-permute-start | bytes 552968 | tf_op jit(solution)/shard_map/ppermute | solution.py:27
  44.8 11.6 %collective-permute-start.12 = (bf16[576,384]{1,0:T(8,128)(2,1)S(1)}, bf16[576,384]{1,0:T(8,128)(2,1)S(1)}, u32[]{:S(2)}, u32[]{:S(2)}) collective-permute-start(bf16[576,384]{1,0:T(8,128)(2,1)S(1)} %bitcast.116), channel_id=1, source_target_pairs={{32,0},{36,4},{40,8},{44,12},{48,16},{52,20},{56,24},{60,28},{64,3... | collective-permute-start | bytes 1327112 | tf_op jit(solution)/shard_map/ppermute | solution.py:27
  51.8 9.5 %collective-permute-start.13 = (bf16[576,384]{1,0:T(8,128)(2,1)S(1)}, bf16[576,384]{1,0:T(8,128)(2,1)S(1)}, u32[]{:S(2)}, u32[]{:S(2)}) collective-permute-start(bf16[576,384]{1,0:T(8,128)(2,1)S(1)} %bitcast.117), channel_id=1, source_target_pairs={{224,0},{228,4},{232,8},{236,12},{240,16},{244,20},{248,24},{252,2... | collective-permute-start | bytes 1327112 | tf_op jit(solution)/shard_map/ppermute | solution.py:27
  53.6 22.0 %collective-permute-start.20 = (bf16[4,2,72,640]{3,2,1,0:T(8,128)(2,1)}, bf16[4,2,72,640]{3,2,1,0:T(8,128)(2,1)S(1)}, u32[]{:S(2)}, u32[]{:S(2)}) collective-permute-start(bf16[4,2,72,640]{3,2,1,0:T(8,128)(2,1)} %collective-permute-done.14), channel_id=1, source_target_pairs={{4,0},{8,4},{12,8},{0,12},{20,16},{24,20},{28,24},{16,28},{36,32},... | collective-permute-start | bytes 2211848 | tf_op jit(solution)/shard_map/ppermute | solution.py:27
  61.3 7.5 %collective-permute-start.22 = (bf16[128,4608]{1,0:T(8,128)(2,1)}, bf16[128,4608]{1,0:T(8,128)(2,1)S(1)}, u32[]{:S(2)}, u32[]{:S(2)}) collective-permute-start(bf16[128,4608]{1,0:T(8,128)(2,1)} %collective-permute-done.17), channel_id=1, source_target_pairs={{0,1},{1,0},{2,3},{3,2},{4,5},{5,4},{6,7},{7,6},{8,9},{9,8},{10,11... | collective-permute-start | bytes 3538952 | tf_op jit(solution)/shard_map/ppermute | solution.py:31
  61.3 20.2 %collective-permute-start.21 = (bf16[4,2,72,640]{3,2,1,0:T(8,128)(2,1)S(1)}, bf16[4,2,72,640]{3,2,1,0:T(8,128)(2,1)}, u32[]{:S(2)}, u32[]{:S(2)}) collective-permute-start(bf16[4,2,72,640]{3,2,1,0:T(8,128)(2,1)S(1)} %pad_maximum_fusion.1), channel_id=1, source_target_pairs={{12,0},{0,4},{4,8},{8,12},{28,16},{16,20},{20,24},{24,28},{44,32},... | collective-permute-start | bytes 2211848 | tf_op jit(solution)/shard_map/ppermute | solution.py:27
  62.0 13.6 %collective-permute-start.18 = (bf16[576,384]{1,0:T(8,128)(2,1)S(1)}, bf16[576,384]{1,0:T(8,128)(2,1)}, u32[]{:S(2)}, u32[]{:S(2)}) collective-permute-start(bf16[576,384]{1,0:T(8,128)(2,1)S(1)} %collective-permute-done.12), channel_id=1, source_target_pairs={{32,0},{36,4},{40,8},{44,12},{48,16},{52,20},{56,24},{60,28},{64,3... | collective-permute-start | bytes 1327112 | tf_op jit(solution)/shard_map/ppermute | solution.py:27
  62.2 13.3 %collective-permute-start.19 = (bf16[576,384]{1,0:T(8,128)(2,1)S(1)}, bf16[576,384]{1,0:T(8,128)(2,1)}, u32[]{:S(2)}, u32[]{:S(2)}) collective-permute-start(bf16[576,384]{1,0:T(8,128)(2,1)S(1)} %collective-permute-done.13), channel_id=1, source_target_pairs={{224,0},{228,4},{232,8},{236,12},{240,16},{244,20},{248,24},{252,2... | collective-permute-start | bytes 1327112 | tf_op jit(solution)/shard_map/ppermute | solution.py:27
  81.5 9.5 %collective-permute-start.27 = (f32[512,128]{1,0:T(8,128)S(1)}, f32[512,128]{1,0:T(8,128)S(1)}, u32[]{:S(2)}, u32[]{:S(2)}) collective-permute-start(f32[512,128]{1,0:T(8,128)S(1)} %add.146), channel_id=1, source_target_pairs={{0,2},{1,3},{2,0},{3,1},{4,6},{5,7},{6,4},{7,5},{8,10},{9,11},{10,... | collective-permute-start | bytes 786440 | tf_op jit(solution)/shard_map/ppermute | solution.py:31
  82.7 15.1 %collective-permute-start.25 = (bf16[576,384]{1,0:T(8,128)(2,1)}, bf16[576,384]{1,0:T(8,128)(2,1)S(1)}, u32[]{:S(2)}, u32[]{:S(2)}) collective-permute-start(bf16[576,384]{1,0:T(8,128)(2,1)} %collective-permute-done.18), channel_id=1, source_target_pairs={{32,0},{36,4},{40,8},{44,12},{48,16},{52,20},{56,24},{60,28},{64,3... | collective-permute-start | bytes 1327112 | tf_op jit(solution)/shard_map/ppermute | solution.py:27
  83.1 14.8 %collective-permute-start.26 = (bf16[576,384]{1,0:T(8,128)(2,1)}, bf16[576,384]{1,0:T(8,128)(2,1)S(1)}, u32[]{:S(2)}, u32[]{:S(2)}) collective-permute-start(bf16[576,384]{1,0:T(8,128)(2,1)} %collective-permute-done.19), channel_id=1, source_target_pairs={{224,0},{228,4},{232,8},{236,12},{240,16},{244,20},{248,24},{252,2... | collective-permute-start | bytes 1327112 | tf_op jit(solution)/shard_map/ppermute | solution.py:27
  84.8 24.3 %collective-permute-start.23 = (bf16[4,2,72,640]{3,2,1,0:T(8,128)(2,1)S(1)}, bf16[4,2,72,640]{3,2,1,0:T(8,128)(2,1)S(1)}, u32[]{:S(2)}, u32[]{:S(2)}) collective-permute-start(bf16[4,2,72,640]{3,2,1,0:T(8,128)(2,1)S(1)} %pad_maximum_fusion.1), channel_id=1, source_target_pairs={{4,0},{8,4},{12,8},{0,12},{20,16},{24,20},{28,24},{16,28},{36,32},... | collective-permute-start | bytes 2211848 | tf_op jit(solution)/shard_map/ppermute | solution.py:27
  86.1 23.1 %collective-permute-start.24 = (bf16[4,2,72,640]{3,2,1,0:T(8,128)(2,1)}, bf16[4,2,72,640]{3,2,1,0:T(8,128)(2,1)S(1)}, u32[]{:S(2)}, u32[]{:S(2)}) collective-permute-start(bf16[4,2,72,640]{3,2,1,0:T(8,128)(2,1)} %collective-permute-done.21), channel_id=1, source_target_pairs={{12,0},{0,4},{4,8},{8,12},{28,16},{16,20},{20,24},{24,28},{44,32},... | collective-permute-start | bytes 2211848 | tf_op jit(solution)/shard_map/ppermute | solution.py:27
  100.9 6.2 %collective-permute-start.28 = (bf16[288,384]{1,0:T(8,128)(2,1)S(1)}, bf16[288,384]{1,0:T(8,128)(2,1)S(1)}, u32[]{:S(2)}, u32[]{:S(2)}) collective-permute-start(bf16[288,384]{1,0:T(8,128)(2,1)S(1)} %slice.71), channel_id=1, source_target_pairs={{32,0},{36,4},{40,8},{44,12},{48,16},{52,20},{56,24},{60,28},{64,3... | collective-permute-start | bytes 663560 | tf_op jit(solution)/shard_map/ppermute | solution.py:27
  101.3 7.2 %collective-permute-start.29 = (bf16[288,384]{1,0:T(8,128)(2,1)S(1)}, bf16[288,384]{1,0:T(8,128)(2,1)S(1)}, u32[]{:S(2)}, u32[]{:S(2)}) collective-permute-start(bf16[288,384]{1,0:T(8,128)(2,1)S(1)} %slice.72), channel_id=1, source_target_pairs={{224,0},{228,4},{232,8},{236,12},{240,16},{244,20},{248,24},{252,2... | collective-permute-start | bytes 663560 | tf_op jit(solution)/shard_map/ppermute | solution.py:27
  (11 other events, 85.7 us)

commit v10 on v9

--- a/solution.py
+++ b/solution.py
@@ -131,11 +131,10 @@
 
     pair_a, pair_b = pairs(xl.reshape(1), frozen_weight, other, a_width)
     a_p1, a_m1 = fetch(pair_a, dz=1), fetch(pair_a, dz=-1)
-    y_b1, y_b3 = fetch(pair_b, dy=1), fetch(pair_b, dy=-1)
 
     a_p1, a_m1, pair_a, pair_b, core_partial = together(a_p1, a_m1, pair_a, pair_b, core_partial)
     a_p2, a_m2 = fetch(a_p1, dz=1), fetch(a_m1, dz=-1)
-    y_b = [y_b1, fetch(pair_b, dy=2), y_b3]
+    y_b = [fetch(pair_b, dy=dy) for dy in (1, 2, 3)]
 
     def placed(array, chunk, dy):
         at = array.ndim - 3
@@ -148,7 +147,8 @@
         shape = chunk.shape[:at] + (NY,) + chunk.shape[at:]
         return jnp.broadcast_to(jnp.expand_dims(chunk, at), shape)
 
-    a_p2, a_m2 = together(a_p2, a_m2)
+    a_p2, a_m2, pair_b = together(a_p2, a_m2, pair_b)
+    *y_b, a_p2 = together(*y_b, a_p2)
     low = jnp.stack([a_m1, pair_a, a_p1, a_p2])
     low_p, low_m = fetch(low, dy=1), fetch(low, dy=-1)
     a_p3, a_m3 = fetch(a_p2, dz=1), fetch(a_m2, dz=-1)

time: 113 us -> 116 us (1.027)
  waiting for transfers between devices: 39.7 us -> 43.7 us
  starting transfers between devices: 34.6 us -> 32.2 us
  local copies, waits for them, and re-layouts: 10.6 us -> 11.8 us
    ppermute x25, waiting for transfers between devices: 36.9 us -> 40.8 us  [fetch(): return lax.ppermute(x, 'dp', pairs)]
    ppermute x25, starting transfers between devices: 31.7 us -> 29.1 us  [fetch(): return lax.ppermute(x, 'dp', pairs)]
    dynamic_update_slice x9, local copies, waits for them, and re-layouts: 5.1 us -> 6.89 us  [placed(): lax.dynamic_update_slice_in_dim(array, jnp.expand_dims(chunk, at), (y + d...]
  transfers between devices with their start and end apart: 30 -> 30, of which waited for: 14 -> 15; matrix products, arithmetic and copies ran while one was open for 24% -> 25% of each run, Pallas kernels for 4% -> 4%
where the time goes in v10:
time: 116 us; the launch traced here: 115 us
  waiting for transfers between devices  43.7 us (38%)
  starting transfers between devices  32.2 us (28%)
  matrix products  15.1 us (13%)
  local copies, waits for them, and re-layouts  11.8 us (10%)
  Pallas kernels  8.09 us (7%)
  other arithmetic  2.89 us (2%)
  between operations  1.73 us (1%)
    ppermute x25, waiting for transfers between devices, fetch(): return lax.ppermute(x, 'dp', pairs)  40.8 us
    ppermute x25, starting transfers between devices, fetch(): return lax.ppermute(x, 'dp', pairs)  29.1 us
    dot_general x16, matrix products, contract(): lax.dot_general(left, right, (((left_dim,), (right_dim,)), ((), ())), pre...  13.4 us
    dynamic_update_slice x9, local copies, waits for them, and re-layouts, placed(): lax.dynamic_update_slice_in_dim(array, jnp.expand_dims(chunk, at), (y + d...  6.89 us
    pallas_call x2, Pallas kernels, in_vmem(): pl.pallas_call(kernel, in_specs=[pl.BlockSpec(memory_space=pltpu.VMEM)] *...  4.76 us
    ppermute x5, starting transfers between devices, swap_tensor(): return lax.ppermute(x, 'tensor', [(t, t ^ mask) for t in range(4)])  3.07 us
    ppermute x5, waiting for transfers between devices, swap_tensor(): return lax.ppermute(x, 'tensor', [(t, t ^ mask) for t in range(4)])  2.88 us
  transfers between devices with their start and end apart: 30, of which 15 were waited for; matrix products, arithmetic and copies ran while one was open for 25% of the time, Pallas kernels for 4%

profile of v10, /device:TPU:6, one launch (start us, length us, event | category | flops | bytes accessed | tf_op | source)
XLA Modules:
  0.0 115.4 jit_solution(8340456229492490804)
XLA Ops:
  1.7 1.7 %fusion.41 = f32[512,128]{1,0:T(8,128)S(1)} fusion(bf16[512,1024]{1,0:T(8,128)(2,1)} %head_ref.1, bf16[1024,128]{1,0:T(8,128)(2,1)} %param.10), kind=kOutput, calls=%fused_computation.78 | convolution fusion | flops 134217728 | bytes 1572864 | tf_op jit(solution)/shard_map/dot_general | solution.py:126
  3.6 3.6 %collective-permute-done.far_ref = bf16[72,1024]{1,0:T(8,128)(2,1)S(1)} collective-permute-done((bf16[72,1024]{1,0:T(8,128)(2,1)}, bf16[72,1024]{1,0:T(8,128)(2,1)S(1)}, u32[]{:S(2)}, u32[]{:S(2)}) %collective-permute-start) | collective-permute-done | bytes 147488 | tf_op jit(solution)/shard_map/ppermute | solution.py:27
  7.9 1.7 %shard_map.94 = (bf16[2,72,640]{2,1,0:T(8,128)(2,1)}, bf16[2,72,384]{2,1,0:T(8,128)(2,1)}) custom-call(s32[1]{0:T(128)} %bitcast.x_ref, bf16[72,1024]{1,0:T(8,128)(2,1)} %mine_ref.1, bf16[72,1024]{1,0:T(8,128)(2,1)} %copy-done.8), custom_call_target="tpu_custom_call" | custom-call | tf_op jit(solution)/shard_map/pallas_call | solution.py:84
  9.6 5.9 %collective-permute-start.2 = (bf16[2,72,640]{2,1,0:T(8,128)(2,1)}, bf16[2,72,640]{2,1,0:T(8,128)(2,1)S(1)}, u32[]{:S(2)}, u32[]{:S(2)}) collective-permute-start(bf16[2,72,640]{2,1,0:T(8,128)(2,1)} %get-tuple-element.82), channel_id=1, source_target_pairs={{32,0},{36,4},{40,8},{44,12},{48,16},{52,20},{56,24},{60,28},{64,3... | collective-permute-start | bytes 552968 | tf_op jit(solution)/shard_map/ppermute | solution.py:27
  15.5 4.0 %collective-permute-done.2 = bf16[2,72,640]{2,1,0:T(8,128)(2,1)S(1)} collective-permute-done((bf16[2,72,640]{2,1,0:T(8,128)(2,1)}, bf16[2,72,640]{2,1,0:T(8,128)(2,1)S(1)}, u32[]{:S(2)}, u32[]{:S(2)}) %collective-permute-start.2) | collective-permute-done | bytes 184352 | tf_op jit(solution)/shard_map/ppermute | solution.py:27
  19.5 3.3 %collective-permute-done.3 = bf16[2,72,640]{2,1,0:T(8,128)(2,1)S(1)} collective-permute-done((bf16[2,72,640]{2,1,0:T(8,128)(2,1)}, bf16[2,72,640]{2,1,0:T(8,128)(2,1)S(1)}, u32[]{:S(2)}, u32[]{:S(2)}) %collective-permute-start.3) | collective-permute-done | bytes 184352 | tf_op jit(solution)/shard_map/ppermute | solution.py:27
  23.1 1.7 %collective-permute-start.9 = (bf16[2,72,640]{2,1,0:T(8,128)(2,1)S(1)}, bf16[2,72,640]{2,1,0:T(8,128)(2,1)}, u32[]{:S(2)}, u32[]{:S(2)}) collective-permute-start(bf16[2,72,640]{2,1,0:T(8,128)(2,1)S(1)} %collective-permute-done.3), channel_id=1, source_target_pairs={{224,0},{228,4},{232,8},{236,12},{240,16},{244,20},{248,24},{252,2... | collective-permute-start | bytes 552968 | tf_op jit(solution)/shard_map/ppermute | solution.py:27
  24.8 3.0 %collective-permute-start.5 = (bf16[2,72,384]{2,1,0:T(8,128)(2,1)}, bf16[2,72,384]{2,1,0:T(8,128)(2,1)}, u32[]{:S(2)}, u32[]{:S(2)}) collective-permute-start(bf16[2,72,384]{2,1,0:T(8,128)(2,1)} %get-tuple-element.77), channel_id=1, source_target_pairs={{4,0},{8,4},{12,8},{0,12},{20,16},{24,20},{28,24},{16,28},{36,32},... | collective-permute-start | bytes 331784 | tf_op jit(solution)/shard_map/ppermute | solution.py:27
  29.4 1.4 %collective-permute-start.17 = (bf16[128,4608]{1,0:T(8,128)(2,1)}, bf16[128,4608]{1,0:T(8,128)(2,1)}, u32[]{:S(2)}, u32[]{:S(2)}) collective-permute-start(bf16[128,4608]{1,0:T(8,128)(2,1)} %param.8), channel_id=1, source_target_pairs={{0,2},{1,3},{2,0},{3,1},{4,6},{5,7},{6,4},{7,5},{8,10},{9,11},{10,... | collective-permute-start | bytes 3538952 | tf_op jit(solution)/shard_map/ppermute | solution.py:31
  30.9 3.6 %collective-permute-done.6 = bf16[2,72,384]{2,1,0:T(8,128)(2,1)} collective-permute-done((bf16[2,72,384]{2,1,0:T(8,128)(2,1)}, bf16[2,72,384]{2,1,0:T(8,128)(2,1)}, u32[]{:S(2)}, u32[]{:S(2)}) %collective-permute-start.6) | collective-permute-done | bytes 110624 | tf_op jit(solution)/shard_map/ppermute | solution.py:27
  35.6 1.5 %collective-permute-start.10 = (bf16[2,72,640]{2,1,0:T(8,128)(2,1)}, bf16[2,72,640]{2,1,0:T(8,128)(2,1)}, u32[]{:S(2)}, u32[]{:S(2)}) collective-permute-start(bf16[2,72,640]{2,1,0:T(8,128)(2,1)} %collective-permute-done.8), channel_id=1, source_target_pairs={{32,0},{36,4},{40,8},{44,12},{48,16},{52,20},{56,24},{60,28},{64,3... | collective-permute-start | bytes 552968 | tf_op jit(solution)/shard_map/ppermute | solution.py:27
  38.9 1.5 %collective-permute-start.15 = (bf16[4,2,72,640]{3,2,1,0:T(8,128)(2,1)S(1)}, bf16[4,2,72,640]{3,2,1,0:T(8,128)(2,1)}, u32[]{:S(2)}, u32[]{:S(2)}) collective-permute-start(bf16[4,2,72,640]{3,2,1,0:T(8,128)(2,1)S(1)} %pad_maximum_fusion), channel_id=1, source_target_pairs={{12,0},{0,4},{4,8},{8,12},{28,16},{16,20},{20,24},{24,28},{44,32},... | collective-permute-start | bytes 2211848 | tf_op jit(solution)/shard_map/ppermute | solution.py:27
  44.6 2.8 %collective-permute-done.11 = bf16[2,72,640]{2,1,0:T(8,128)(2,1)} collective-permute-done((bf16[2,72,640]{2,1,0:T(8,128)(2,1)}, bf16[2,72,640]{2,1,0:T(8,128)(2,1)}, u32[]{:S(2)}, u32[]{:S(2)}) %collective-permute-start.11) | collective-permute-done | bytes 184352 | tf_op jit(solution)/shard_map/ppermute | solution.py:27
  48.3 5.7 %collective-permute-done.16 = bf16[2,72,640]{2,1,0:T(8,128)(2,1)} collective-permute-done((bf16[2,72,640]{2,1,0:T(8,128)(2,1)}, bf16[2,72,640]{2,1,0:T(8,128)(2,1)}, u32[]{:S(2)}, u32[]{:S(2)}) %collective-permute-start.16) | collective-permute-done | bytes 184352 | tf_op jit(solution)/shard_map/ppermute | solution.py:27
  56.2 2.3 %collective-permute-start.20 = (bf16[4,2,72,640]{3,2,1,0:T(8,128)(2,1)}, bf16[4,2,72,640]{3,2,1,0:T(8,128)(2,1)S(1)}, u32[]{:S(2)}, u32[]{:S(2)}) collective-permute-start(bf16[4,2,72,640]{3,2,1,0:T(8,128)(2,1)} %collective-permute-done.14), channel_id=1, source_target_pairs={{4,0},{8,4},{12,8},{0,12},{20,16},{24,20},{28,24},{16,28},{36,32},... | collective-permute-start | bytes 2211848 | tf_op jit(solution)/shard_map/ppermute | solution.py:27
  58.7 4.9 %collective-permute-done.13 = bf16[576,384]{1,0:T(8,128)(2,1)S(1)} collective-permute-done((bf16[576,384]{1,0:T(8,128)(2,1)S(1)}, bf16[576,384]{1,0:T(8,128)(2,1)S(1)}, u32[]{:S(2)}, u32[]{:S(2)}) %collective-permute-start.13) | collective-permute-done | bytes 442400 | tf_op jit(solution)/shard_map/ppermute | solution.py:27
  64.4 1.5 %collective-permute-start.19 = (bf16[576,384]{1,0:T(8,128)(2,1)S(1)}, bf16[576,384]{1,0:T(8,128)(2,1)}, u32[]{:S(2)}, u32[]{:S(2)}) collective-permute-start(bf16[576,384]{1,0:T(8,128)(2,1)S(1)} %collective-permute-done.13), channel_id=1, source_target_pairs={{224,0},{228,4},{232,8},{236,12},{240,16},{244,20},{248,24},{252,2... | collective-permute-start | bytes 1327112 | tf_op jit(solution)/shard_map/ppermute | solution.py:27
  67.3 1.3 %bitcast_dynamic-update-slice_fusion.4 = bf16[4,2,4,72,640]{4,3,2,1,0:T(8,128)(2,1)S(1)} fusion(bf16[4,2,4,72,640]{4,3,2,1,0:T(8,128)(2,1)S(1)} %bitcast_dynamic-update-slice_fusion.5, s32[]{:T(128)S(6)} %select_n.100, bf16[4,2,72,640]{3,2,1,0:T(8,128)(2,1)} %collective-permute-done.15), kind=kLoop, calls=%fused_computation.20 | loop fusion | bytes 1474564 | tf_op jit(solution)/shard_map/dynamic_update_slice | solution.py:141
  69.2 1.4 %constant_dynamic-update-slice_fusion.1 = bf16[512,4608]{1,0:T(8,128)(2,1)S(1)} fusion(bf16[512,4608]{1,0:T(8,128)(2,1)S(1)} %constant_dynamic-update-slice_fusion.2, bf16[128,4608]{1,0:T(8,128)(2,1)} %collective-permute-done.17, s32[]{:T(128)S(6)} %select_n.105), kind=kLoop, calls=%fused_computation.64 | loop fusion | bytes 2359300 | tf_op jit(solution)/shard_map/dynamic_update_slice | solution.py:175
  70.8 1.6 %shard_map.95.z_ref = bf16[8,512,576]{2,1,0:T(8,128)(2,1)S(1)} custom-call(s32[1]{0:T(128)} %bitcast.20.start_ref, bf16[512,4608]{1,0:T(8,128)(2,1)S(1)} %constant_dynamic-update-slice_fusion.g_ref), custom_call_target="tpu_custom_call" | custom-call | tf_op jit(solution)/shard_map/pallas_call | solution.py:49
  72.9 1.4 %fusion.3.back_ref = bf16[512,128]{1,0:T(8,128)(2,1)S(1)} fusion(bf16[512,4608]{1,0:T(8,128)(2,1)S(1)} %constant_dynamic-update-slice_fusion.g_ref, bf16[128,4608]{1,0:T(8,128)(2,1)S(1)} %copy-done, s32[128]{0:T(128)S(1)} %and_select_fusion, s32[512]{0:T(512)S(1)} %add_select_fusion, pred[512]{0:T(512)(128)(4,1)S(1)} %iota_compare_fusion.1), kind=kOutput, calls=%fused_computation.11 | convolution fusion | flops 604241920 | bytes 6032384 | tf_op jit(solution)/shard_map/dot_general | solution.py:15
  77.7 6.0 %collective-permute-done.21 = bf16[4,2,72,640]{3,2,1,0:T(8,128)(2,1)} collective-permute-done((bf16[4,2,72,640]{3,2,1,0:T(8,128)(2,1)S(1)}, bf16[4,2,72,640]{3,2,1,0:T(8,128)(2,1)}, u32[]{:S(2)}, u32[]{:S(2)}) %collective-permute-start.21) | collective-permute-done | bytes 737312 | tf_op jit(solution)/shard_map/ppermute | solution.py:27
  83.8 1.3 %collective-permute-start.27 = (f32[512,128]{1,0:T(8,128)S(1)}, f32[512,128]{1,0:T(8,128)S(1)}, u32[]{:S(2)}, u32[]{:S(2)}) collective-permute-start(f32[512,128]{1,0:T(8,128)S(1)} %add.146), channel_id=1, source_target_pairs={{0,2},{1,3},{2,0},{3,1},{4,6},{5,7},{6,4},{7,5},{8,10},{9,11},{10,... | collective-permute-start | bytes 786440 | tf_op jit(solution)/shard_map/ppermute | solution.py:31
  86.0 1.3 %collective-permute-start.26 = (bf16[576,384]{1,0:T(8,128)(2,1)}, bf16[576,384]{1,0:T(8,128)(2,1)S(1)}, u32[]{:S(2)}, u32[]{:S(2)}) collective-permute-start(bf16[576,384]{1,0:T(8,128)(2,1)} %collective-permute-done.19), channel_id=1, source_target_pairs={{224,0},{228,4},{232,8},{236,12},{240,16},{244,20},{248,24},{252,2... | collective-permute-start | bytes 1327112 | tf_op jit(solution)/shard_map/ppermute | solution.py:27
  90.8 2.6 %collective-permute-done.27 = f32[512,128]{1,0:T(8,128)S(1)} collective-permute-done((f32[512,128]{1,0:T(8,128)S(1)}, f32[512,128]{1,0:T(8,128)S(1)}, u32[]{:S(2)}, u32[]{:S(2)}) %collective-permute-start.27) | collective-permute-done | bytes 262176 | tf_op jit(solution)/shard_map/ppermute | solution.py:31
  94.5 1.5 %fusion.14 = f32[512,384]{1,0:T(8,128)S(1)} fusion(bf16[576,384]{1,0:T(8,128)(2,1)} %collective-permute-done.19, bf16[8,512,576]{2,1,0:T(8,128)(2,1)S(1)} %shard_map.95.z_ref), kind=kOutput, calls=%fused_computation.33 | convolution fusion | flops 226492416 | bytes 1884160 | tf_op jit(solution)/shard_map/dot_general | solution.py:15
  97.9 1.5 %fusion.16 = f32[512,384]{1,0:T(8,128)S(1)} fusion(bf16[576,384]{1,0:T(8,128)(2,1)} %collective-permute-done.18, bf16[8,512,576]{2,1,0:T(8,128)(2,1)S(1)} %shard_map.95.z_ref), kind=kOutput, calls=%fused_computation.35 | convolution fusion | flops 226492416 | bytes 1884160 | tf_op jit(solution)/shard_map/dot_general | solution.py:15
  101.0 2.2 %convolution_multiply_fusion = f32[128,4608]{1,0:T(8,128)} fusion(bf16[512,128]{1,0:T(8,128)(2,1)S(1)} %select_convert_fusion.1, bf16[512,4608]{1,0:T(8,128)(2,1)S(1)} %constant_dynamic-update-slice_fusion.g_ref), kind=kOutput, calls=%fused_computation | convolution fusion | flops 604569600 | bytes 7208960 | tf_op jit(solution)/shard_map/dot_general | solution.py:15
  103.8 1.5 %collective-permute-start.29 = (bf16[288,384]{1,0:T(8,128)(2,1)S(1)}, bf16[288,384]{1,0:T(8,128)(2,1)S(1)}, u32[]{:S(2)}, u32[]{:S(2)}) collective-permute-start(bf16[288,384]{1,0:T(8,128)(2,1)S(1)} %slice.72), channel_id=1, source_target_pairs={{224,0},{228,4},{232,8},{236,12},{240,16},{244,20},{248,24},{252,2... | collective-permute-start | bytes 663560 | tf_op jit(solution)/shard_map/ppermute | solution.py:27
  105.8 3.6 %collective-permute-done.28 = bf16[288,384]{1,0:T(8,128)(2,1)S(1)} collective-permute-done((bf16[288,384]{1,0:T(8,128)(2,1)S(1)}, bf16[288,384]{1,0:T(8,128)(2,1)S(1)}, u32[]{:S(2)}, u32[]{:S(2)}) %collective-permute-start.28) | collective-permute-done | bytes 221216 | tf_op jit(solution)/shard_map/ppermute | solution.py:27
  109.5 1.5 %collective-permute-done.29 = bf16[288,384]{1,0:T(8,128)(2,1)S(1)} collective-permute-done((bf16[288,384]{1,0:T(8,128)(2,1)S(1)}, bf16[288,384]{1,0:T(8,128)(2,1)S(1)}, u32[]{:S(2)}, u32[]{:S(2)}) %collective-permute-start.29) | collective-permute-done | bytes 221216 | tf_op jit(solution)/shard_map/ppermute | solution.py:27
  112.0 3.5 %shard_map.97 = bf16[512,1024]{1,0:T(8,128)(2,1)} custom-call(bf16[8,512,576]{2,1,0:T(8,128)(2,1)S(1)} %shard_map.95.z_ref, bf16[4,576,640]{2,1,0:T(8,128)(2,1)S(1)} %bitcast.111, f32[512,640]{1,0:T(8,128)S(1)} %convolution_add_fusion.total_ref, f32[512,1]{1,0:T(8,128)S(1)} %fusion.35.live_ref, bf16[512,384]{1,0:T(8,128)(2,1)S(1)} %select_convert_fusion.b_ref), custom_call_target="tpu_custom_call" | custom-call | tf_op jit(solution)/shard_map/pallas_call | solution.py:97
  (98 shorter events, 31.3 us)
Async XLA Ops:
  0.6 72.3 %copy-start = (bf16[128,4608]{1,0:T(8,128)(2,1)S(1)}, bf16[128,4608]{1,0:T(8,128)(2,1)}, u32[]{:S(2)}) copy-start(bf16[128,4608]{1,0:T(8,128)(2,1)} %param.11) | copy-start | bytes 3538948
  0.6 53.9 %copy-start.9 = (s32[512]{0:T(512)S(1)}, s32[512]{0:T(512)}, u32[]{:S(2)}) copy-start(s32[512]{0:T(512)} %param.12) | copy-start | bytes 6148
  0.7 6.6 %collective-permute-start.1 = (bf16[128,4608]{1,0:T(8,128)(2,1)}, bf16[128,4608]{1,0:T(8,128)(2,1)S(1)}, u32[]{:S(2)}, u32[]{:S(2)}) collective-permute-start(bf16[128,4608]{1,0:T(8,128)(2,1)} %param.8), channel_id=1, source_target_pairs={{0,1},{1,0},{2,3},{3,2},{4,5},{5,4},{6,7},{7,6},{8,9},{9,8},{10,11... | collective-permute-start | bytes 3538952 | tf_op jit(solution)/shard_map/ppermute | solution.py:31
  0.8 6.5 %collective-permute-start = (bf16[72,1024]{1,0:T(8,128)(2,1)}, bf16[72,1024]{1,0:T(8,128)(2,1)S(1)}, u32[]{:S(2)}, u32[]{:S(2)}) collective-permute-start(bf16[72,1024]{1,0:T(8,128)(2,1)} %mine_ref.1), channel_id=1, source_target_pairs={{16,0},{20,4},{24,8},{28,12},{0,16},{4,20},{8,24},{12,28},{48,32},... | collective-permute-start | bytes 442376 | tf_op jit(solution)/shard_map/ppermute | solution.py:27
  3.4 12.1 %collective-permute-start.4 = (f32[512,128]{1,0:T(8,128)S(1)}, f32[512,128]{1,0:T(8,128)S(1)}, u32[]{:S(2)}, u32[]{:S(2)}) collective-permute-start(f32[512,128]{1,0:T(8,128)S(1)} %fusion.41), channel_id=1, source_target_pairs={{0,1},{1,0},{2,3},{3,2},{4,5},{5,4},{6,7},{7,6},{8,9},{9,8},{10,11... | collective-permute-start | bytes 786440 | tf_op jit(solution)/shard_map/ppermute | solution.py:31
  9.6 9.9 %collective-permute-start.2 = (bf16[2,72,640]{2,1,0:T(8,128)(2,1)}, bf16[2,72,640]{2,1,0:T(8,128)(2,1)S(1)}, u32[]{:S(2)}, u32[]{:S(2)}) collective-permute-start(bf16[2,72,640]{2,1,0:T(8,128)(2,1)} %get-tuple-element.82), channel_id=1, source_target_pairs={{32,0},{36,4},{40,8},{44,12},{48,16},{52,20},{56,24},{60,28},{64,3... | collective-permute-start | bytes 552968 | tf_op jit(solution)/shard_map/ppermute | solution.py:27
  15.5 7.3 %collective-permute-start.3 = (bf16[2,72,640]{2,1,0:T(8,128)(2,1)}, bf16[2,72,640]{2,1,0:T(8,128)(2,1)S(1)}, u32[]{:S(2)}, u32[]{:S(2)}) collective-permute-start(bf16[2,72,640]{2,1,0:T(8,128)(2,1)} %get-tuple-element.82), channel_id=1, source_target_pairs={{224,0},{228,4},{232,8},{236,12},{240,16},{244,20},{248,24},{252,2... | collective-permute-start | bytes 552968 | tf_op jit(solution)/shard_map/ppermute | solution.py:27
  22.8 6.6 %collective-permute-start.8 = (bf16[2,72,640]{2,1,0:T(8,128)(2,1)S(1)}, bf16[2,72,640]{2,1,0:T(8,128)(2,1)}, u32[]{:S(2)}, u32[]{:S(2)}) collective-permute-start(bf16[2,72,640]{2,1,0:T(8,128)(2,1)S(1)} %collective-permute-done.2), channel_id=1, source_target_pairs={{32,0},{36,4},{40,8},{44,12},{48,16},{52,20},{56,24},{60,28},{64,3... | collective-permute-start | bytes 552968 | tf_op jit(solution)/shard_map/ppermute | solution.py:27
  23.1 7.8 %collective-permute-start.9 = (bf16[2,72,640]{2,1,0:T(8,128)(2,1)S(1)}, bf16[2,72,640]{2,1,0:T(8,128)(2,1)}, u32[]{:S(2)}, u32[]{:S(2)}) collective-permute-start(bf16[2,72,640]{2,1,0:T(8,128)(2,1)S(1)} %collective-permute-done.3), channel_id=1, source_target_pairs={{224,0},{228,4},{232,8},{236,12},{240,16},{244,20},{248,24},{252,2... | collective-permute-start | bytes 552968 | tf_op jit(solution)/shard_map/ppermute | solution.py:27
  24.8 6.0 %collective-permute-start.5 = (bf16[2,72,384]{2,1,0:T(8,128)(2,1)}, bf16[2,72,384]{2,1,0:T(8,128)(2,1)}, u32[]{:S(2)}, u32[]{:S(2)}) collective-permute-start(bf16[2,72,384]{2,1,0:T(8,128)(2,1)} %get-tuple-element.77), channel_id=1, source_target_pairs={{4,0},{8,4},{12,8},{0,12},{20,16},{24,20},{28,24},{16,28},{36,32},... | collective-permute-start | bytes 331784 | tf_op jit(solution)/shard_map/ppermute | solution.py:27
  27.8 6.7 %collective-permute-start.6 = (bf16[2,72,384]{2,1,0:T(8,128)(2,1)}, bf16[2,72,384]{2,1,0:T(8,128)(2,1)}, u32[]{:S(2)}, u32[]{:S(2)}) collective-permute-start(bf16[2,72,384]{2,1,0:T(8,128)(2,1)} %get-tuple-element.77), channel_id=1, source_target_pairs={{8,0},{12,4},{0,8},{4,12},{24,16},{28,20},{16,24},{20,28},{40,32},... | collective-permute-start | bytes 331784 | tf_op jit(solution)/shard_map/ppermute | solution.py:27
  28.5 7.1 %collective-permute-start.7 = (bf16[2,72,384]{2,1,0:T(8,128)(2,1)}, bf16[2,72,384]{2,1,0:T(8,128)(2,1)}, u32[]{:S(2)}, u32[]{:S(2)}) collective-permute-start(bf16[2,72,384]{2,1,0:T(8,128)(2,1)} %get-tuple-element.77), channel_id=1, source_target_pairs={{12,0},{0,4},{4,8},{8,12},{28,16},{16,20},{20,24},{24,28},{44,32},... | collective-permute-start | bytes 331784 | tf_op jit(solution)/shard_map/ppermute | solution.py:27
  29.4 26.7 %collective-permute-start.17 = (bf16[128,4608]{1,0:T(8,128)(2,1)}, bf16[128,4608]{1,0:T(8,128)(2,1)}, u32[]{:S(2)}, u32[]{:S(2)}) collective-permute-start(bf16[128,4608]{1,0:T(8,128)(2,1)} %param.8), channel_id=1, source_target_pairs={{0,2},{1,3},{2,0},{3,1},{4,6},{5,7},{6,4},{7,5},{8,10},{9,11},{10,... | collective-permute-start | bytes 3538952 | tf_op jit(solution)/shard_map/ppermute | solution.py:31
  35.6 9.0 %collective-permute-start.10 = (bf16[2,72,640]{2,1,0:T(8,128)(2,1)}, bf16[2,72,640]{2,1,0:T(8,128)(2,1)}, u32[]{:S(2)}, u32[]{:S(2)}) collective-permute-start(bf16[2,72,640]{2,1,0:T(8,128)(2,1)} %collective-permute-done.8), channel_id=1, source_target_pairs={{32,0},{36,4},{40,8},{44,12},{48,16},{52,20},{56,24},{60,28},{64,3... | collective-permute-start | bytes 552968 | tf_op jit(solution)/shard_map/ppermute | solution.py:27
  38.2 18.0 %collective-permute-start.14 = (bf16[4,2,72,640]{3,2,1,0:T(8,128)(2,1)S(1)}, bf16[4,2,72,640]{3,2,1,0:T(8,128)(2,1)}, u32[]{:S(2)}, u32[]{:S(2)}) collective-permute-start(bf16[4,2,72,640]{3,2,1,0:T(8,128)(2,1)S(1)} %pad_maximum_fusion), channel_id=1, source_target_pairs={{4,0},{8,4},{12,8},{0,12},{20,16},{24,20},{28,24},{16,28},{36,32},... | collective-permute-start | bytes 2211848 | tf_op jit(solution)/shard_map/ppermute | solution.py:27
  38.9 17.3 %collective-permute-start.15 = (bf16[4,2,72,640]{3,2,1,0:T(8,128)(2,1)S(1)}, bf16[4,2,72,640]{3,2,1,0:T(8,128)(2,1)}, u32[]{:S(2)}, u32[]{:S(2)}) collective-permute-start(bf16[4,2,72,640]{3,2,1,0:T(8,128)(2,1)S(1)} %pad_maximum_fusion), channel_id=1, source_target_pairs={{12,0},{0,4},{4,8},{8,12},{28,16},{16,20},{20,24},{24,28},{44,32},... | collective-permute-start | bytes 2211848 | tf_op jit(solution)/shard_map/ppermute | solution.py:27
  40.3 7.1 %collective-permute-start.11 = (bf16[2,72,640]{2,1,0:T(8,128)(2,1)}, bf16[2,72,640]{2,1,0:T(8,128)(2,1)}, u32[]{:S(2)}, u32[]{:S(2)}) collective-permute-start(bf16[2,72,640]{2,1,0:T(8,128)(2,1)} %collective-permute-done.9), channel_id=1, source_target_pairs={{224,0},{228,4},{232,8},{236,12},{240,16},{244,20},{248,24},{252,2... | collective-permute-start | bytes 552968 | tf_op jit(solution)/shard_map/ppermute | solution.py:27
  47.4 6.7 %collective-permute-start.16 = (bf16[2,72,640]{2,1,0:T(8,128)(2,1)}, bf16[2,72,640]{2,1,0:T(8,128)(2,1)}, u32[]{:S(2)}, u32[]{:S(2)}) collective-permute-start(bf16[2,72,640]{2,1,0:T(8,128)(2,1)} %collective-permute-done.10), channel_id=1, source_target_pairs={{32,0},{36,4},{40,8},{44,12},{48,16},{52,20},{56,24},{60,28},{64,3... | collective-permute-start | bytes 552968 | tf_op jit(solution)/shard_map/ppermute | solution.py:27
  48.1 10.6 %collective-permute-start.12 = (bf16[576,384]{1,0:T(8,128)(2,1)S(1)}, bf16[576,384]{1,0:T(8,128)(2,1)S(1)}, u32[]{:S(2)}, u32[]{:S(2)}) collective-permute-start(bf16[576,384]{1,0:T(8,128)(2,1)S(1)} %bitcast.116), channel_id=1, source_target_pairs={{32,0},{36,4},{40,8},{44,12},{48,16},{52,20},{56,24},{60,28},{64,3... | collective-permute-start | bytes 1327112 | tf_op jit(solution)/shard_map/ppermute | solution.py:27
  54.0 9.5 %collective-permute-start.13 = (bf16[576,384]{1,0:T(8,128)(2,1)S(1)}, bf16[576,384]{1,0:T(8,128)(2,1)S(1)}, u32[]{:S(2)}, u32[]{:S(2)}) collective-permute-start(bf16[576,384]{1,0:T(8,128)(2,1)S(1)} %bitcast.117), channel_id=1, source_target_pairs={{224,0},{228,4},{232,8},{236,12},{240,16},{244,20},{248,24},{252,2... | collective-permute-start | bytes 1327112 | tf_op jit(solution)/shard_map/ppermute | solution.py:27
  56.2 21.6 %collective-permute-start.20 = (bf16[4,2,72,640]{3,2,1,0:T(8,128)(2,1)}, bf16[4,2,72,640]{3,2,1,0:T(8,128)(2,1)S(1)}, u32[]{:S(2)}, u32[]{:S(2)}) collective-permute-start(bf16[4,2,72,640]{3,2,1,0:T(8,128)(2,1)} %collective-permute-done.14), channel_id=1, source_target_pairs={{4,0},{8,4},{12,8},{0,12},{20,16},{24,20},{28,24},{16,28},{36,32},... | collective-permute-start | bytes 2211848 | tf_op jit(solution)/shard_map/ppermute | solution.py:27
  63.6 7.1 %collective-permute-start.22 = (bf16[128,4608]{1,0:T(8,128)(2,1)}, bf16[128,4608]{1,0:T(8,128)(2,1)S(1)}, u32[]{:S(2)}, u32[]{:S(2)}) collective-permute-start(bf16[128,4608]{1,0:T(8,128)(2,1)} %collective-permute-done.17), channel_id=1, source_target_pairs={{0,1},{1,0},{2,3},{3,2},{4,5},{5,4},{6,7},{7,6},{8,9},{9,8},{10,11... | collective-permute-start | bytes 3538952 | tf_op jit(solution)/shard_map/ppermute | solution.py:31
  63.6 20.2 %collective-permute-start.21 = (bf16[4,2,72,640]{3,2,1,0:T(8,128)(2,1)S(1)}, bf16[4,2,72,640]{3,2,1,0:T(8,128)(2,1)}, u32[]{:S(2)}, u32[]{:S(2)}) collective-permute-start(bf16[4,2,72,640]{3,2,1,0:T(8,128)(2,1)S(1)} %pad_maximum_fusion.1), channel_id=1, source_target_pairs={{12,0},{0,4},{4,8},{8,12},{28,16},{16,20},{20,24},{24,28},{44,32},... | collective-permute-start | bytes 2211848 | tf_op jit(solution)/shard_map/ppermute | solution.py:27
  63.8 13.6 %collective-permute-start.18 = (bf16[576,384]{1,0:T(8,128)(2,1)S(1)}, bf16[576,384]{1,0:T(8,128)(2,1)}, u32[]{:S(2)}, u32[]{:S(2)}) collective-permute-start(bf16[576,384]{1,0:T(8,128)(2,1)S(1)} %collective-permute-done.12), channel_id=1, source_target_pairs={{32,0},{36,4},{40,8},{44,12},{48,16},{52,20},{56,24},{60,28},{64,3... | collective-permute-start | bytes 1327112 | tf_op jit(solution)/shard_map/ppermute | solution.py:27
  64.4 13.3 %collective-permute-start.19 = (bf16[576,384]{1,0:T(8,128)(2,1)S(1)}, bf16[576,384]{1,0:T(8,128)(2,1)}, u32[]{:S(2)}, u32[]{:S(2)}) collective-permute-start(bf16[576,384]{1,0:T(8,128)(2,1)S(1)} %collective-permute-done.13), channel_id=1, source_target_pairs={{224,0},{228,4},{232,8},{236,12},{240,16},{244,20},{248,24},{252,2... | collective-permute-start | bytes 1327112 | tf_op jit(solution)/shard_map/ppermute | solution.py:27
  83.8 9.5 %collective-permute-start.27 = (f32[512,128]{1,0:T(8,128)S(1)}, f32[512,128]{1,0:T(8,128)S(1)}, u32[]{:S(2)}, u32[]{:S(2)}) collective-permute-start(f32[512,128]{1,0:T(8,128)S(1)} %add.146), channel_id=1, source_target_pairs={{0,2},{1,3},{2,0},{3,1},{4,6},{5,7},{6,4},{7,5},{8,10},{9,11},{10,... | collective-permute-start | bytes 786440 | tf_op jit(solution)/shard_map/ppermute | solution.py:31
  85.2 15.0 %collective-permute-start.25 = (bf16[576,384]{1,0:T(8,128)(2,1)}, bf16[576,384]{1,0:T(8,128)(2,1)S(1)}, u32[]{:S(2)}, u32[]{:S(2)}) collective-permute-start(bf16[576,384]{1,0:T(8,128)(2,1)} %collective-permute-done.18), channel_id=1, source_target_pairs={{32,0},{36,4},{40,8},{44,12},{48,16},{52,20},{56,24},{60,28},{64,3... | collective-permute-start | bytes 1327112 | tf_op jit(solution)/shard_map/ppermute | solution.py:27
  86.0 14.2 %collective-permute-start.26 = (bf16[576,384]{1,0:T(8,128)(2,1)}, bf16[576,384]{1,0:T(8,128)(2,1)S(1)}, u32[]{:S(2)}, u32[]{:S(2)}) collective-permute-start(bf16[576,384]{1,0:T(8,128)(2,1)} %collective-permute-done.19), channel_id=1, source_target_pairs={{224,0},{228,4},{232,8},{236,12},{240,16},{244,20},{248,24},{252,2... | collective-permute-start | bytes 1327112 | tf_op jit(solution)/shard_map/ppermute | solution.py:27
  87.3 24.4 %collective-permute-start.23 = (bf16[4,2,72,640]{3,2,1,0:T(8,128)(2,1)S(1)}, bf16[4,2,72,640]{3,2,1,0:T(8,128)(2,1)S(1)}, u32[]{:S(2)}, u32[]{:S(2)}) collective-permute-start(bf16[4,2,72,640]{3,2,1,0:T(8,128)(2,1)S(1)} %pad_maximum_fusion.1), channel_id=1, source_target_pairs={{4,0},{8,4},{12,8},{0,12},{20,16},{24,20},{28,24},{16,28},{36,32},... | collective-permute-start | bytes 2211848 | tf_op jit(solution)/shard_map/ppermute | solution.py:27
  88.3 23.4 %collective-permute-start.24 = (bf16[4,2,72,640]{3,2,1,0:T(8,128)(2,1)}, bf16[4,2,72,640]{3,2,1,0:T(8,128)(2,1)S(1)}, u32[]{:S(2)}, u32[]{:S(2)}) collective-permute-start(bf16[4,2,72,640]{3,2,1,0:T(8,128)(2,1)} %collective-permute-done.21), channel_id=1, source_target_pairs={{12,0},{0,4},{4,8},{8,12},{28,16},{16,20},{20,24},{24,28},{44,32},... | collective-permute-start | bytes 2211848 | tf_op jit(solution)/shard_map/ppermute | solution.py:27
  103.2 6.3 %collective-permute-start.28 = (bf16[288,384]{1,0:T(8,128)(2,1)S(1)}, bf16[288,384]{1,0:T(8,128)(2,1)S(1)}, u32[]{:S(2)}, u32[]{:S(2)}) collective-permute-start(bf16[288,384]{1,0:T(8,128)(2,1)S(1)} %slice.71), channel_id=1, source_target_pairs={{32,0},{36,4},{40,8},{44,12},{48,16},{52,20},{56,24},{60,28},{64,3... | collective-permute-start | bytes 663560 | tf_op jit(solution)/shard_map/ppermute | solution.py:27
  103.8 7.1 %collective-permute-start.29 = (bf16[288,384]{1,0:T(8,128)(2,1)S(1)}, bf16[288,384]{1,0:T(8,128)(2,1)S(1)}, u32[]{:S(2)}, u32[]{:S(2)}) collective-permute-start(bf16[288,384]{1,0:T(8,128)(2,1)S(1)} %slice.72), channel_id=1, source_target_pairs={{224,0},{228,4},{232,8},{236,12},{240,16},{244,20},{248,24},{252,2... | collective-permute-start | bytes 663560 | tf_op jit(solution)/shard_map/ppermute | solution.py:27
  (8 other events, 77.3 us)

commit v11 on v9

--- a/solution.py
+++ b/solution.py
@@ -170,6 +170,9 @@
     b_p2, b_m2 = fetch(b_p1, dz=1), fetch(b_m1, dz=-1)
 
     from_both = swap_tensor(from_chip, 1)
+    partial, core_partial, from_both = together(partial, core_partial, from_both)
+    chip_sum = partial + core_partial
+    far_sum = swap_tensor(chip_sum, 2)
     gradients = jnp.zeros((row_count, depth), output_gradient.dtype)
     for block, mask in ((own_rows, 0), (from_core, 1), (from_chip, 2), (from_both, 3)):
         gradients = lax.dynamic_update_slice_in_dim(
@@ -204,37 +207,31 @@
         [(1, b_own), (0, b_m1), (2, b_p1)],
     )
 
+    adapter_input = ((chip_sum + far_sum) * select_rows).astype(jnp.bfloat16)
+    (adapter_input,) = together(adapter_input)
+    up_factor_gradient = ADAPTER_SCALE * contract(adapter_input, gradients, 0, 0)
+
     (
-        b_p2, b_m2, low_o, high_m, high, low_all, by_z, adapter_backward, partial,
-        core_partial, down_factor_gradient, b_total,
+        b_p2, b_m2, low_o, high_m, high, low_all, by_z, adapter_backward,
+        up_factor_gradient, down_factor_gradient, b_total,
     ) = together(
-        b_p2, b_m2, low_o, high_m, high, low_all, by_z, adapter_backward, partial,
-        core_partial, down_factor_gradient, b_total,
+        b_p2, b_m2, low_o, high_m, high, low_all, by_z, adapter_backward,
+        up_factor_gradient, down_factor_gradient, b_total,
     )
     high_p, high_o = fetch(high, dy=1), fetch(high_m, dy=-1)
     b_p3, b_m3 = fetch(b_p2, dz=1), fetch(b_m2, dz=-1)
-    chip_sum = partial + core_partial
-    far_sum = swap_tensor(chip_sum, 2)
-    low_all, low_o, far_sum, chip_sum, b_q2, b_n2 = together(
-        low_all, low_o, far_sum, chip_sum, b_p2, b_m2
-    )
     low_all = placed(low_all, low_o, 2)
     a_total = product(
         ADAPTER_SCALE * contract(adapter_backward, adapter_down_factors[:a_width], 1, 1),
         [(i, low_all[i]) for i in range(4)],
     )
-    b_p3, b_m3, a_total, chip_sum, far_sum = together(b_p3, b_m3, a_total, chip_sum, far_sum)
+    b_p2, b_m2, b_p3, b_m3, a_total = together(b_p2, b_m2, b_p3, b_m3, a_total)
     cut = b_own.shape[0] // 2 // 16 * 16
     b_p4, b_m4 = fetch(b_p3[:cut], dz=1), fetch(b_m3[cut:], dz=-1)
-    adapter_input = ((chip_sum + far_sum) * select_rows).astype(jnp.bfloat16)
-    (adapter_input,) = together(adapter_input)
-    up_factor_gradient = ADAPTER_SCALE * contract(adapter_input, gradients, 0, 0)
     high_all = placed(spread(high), high_m, 3)
-    b_total = product(b_total, [(7, b_n2), (3, b_q2), (6, b_m3), (4, b_p3)])
-
-    b_p4, b_m4, high_all, b_total, up_factor_gradient = together(
-        b_p4, b_m4, high_all, b_total, up_factor_gradient
-    )
+    b_total = product(b_total, [(7, b_m2), (3, b_p2), (6, b_m3), (4, b_p3)])
+
+    b_p4, b_m4, high_all, b_total = together(b_p4, b_m4, high_all, b_total)
     b_total = product(b_total, [(5, jnp.concatenate([b_p4, b_m4], 0))])
     b_out = jnp.where(active_rows[:, None], b_total, 0.0).astype(jnp.bfloat16)
 

time: 113 us -> 117 us (1.035); the launches traced: 113 us -> 116 us
  local copies, waits for them, and re-layouts: 10.6 us -> 6.75 us
  waiting for transfers between devices: 39.7 us -> 43.3 us
  matrix products: 15.1 us -> 17.9 us
    ppermute x5, waiting for transfers between devices: 2.73 us -> 5.72 us  [swap_tensor(): return lax.ppermute(x, 'tensor', [(t, t ^ mask) for t in range(4)])]
    dynamic_update_slice x9, local copies, waits for them, and re-layouts: 5.1 us -> 2.77 us  [placed(): lax.dynamic_update_slice_in_dim(array, jnp.expand_dims(chunk, at), (y + d...]
    dot_general x16, matrix products: 13.4 us -> 15.5 us  [contract(): lax.dot_general(left, right, (((left_dim,), (right_dim,)), ((), ())), pre...]
    dynamic_update_slice x4, local copies, waits for them, and re-layouts: 1.74 us -> 0.46 us  [body(): lax.dynamic_update_slice_in_dim(gradients, block, (tensor ^ mask) * part_...]
    another operation x1, other arithmetic: 1.31 us -> 0.11 us  [body(): high = jnp.stack([a_p3, a_p4, a_m3, a_m2])]
  transfers between devices with their start and end apart: 30 -> 30, of which waited for: 14 -> 15; matrix products, arithmetic and copies ran while one was open for 24% -> 21% of each run, Pallas kernels for 4% -> 4%
where the time goes in v11:
time: 117 us; the launch traced here: 116 us
  waiting for transfers between devices  43.3 us (37%)
  starting transfers between devices  34.9 us (30%)
  matrix products  17.9 us (15%)
  Pallas kernels  8.09 us (7%)
  local copies, waits for them, and re-layouts  6.75 us (6%)
  other arithmetic  2.85 us (2%)
  between operations  1.76 us (2%)
    ppermute x25, waiting for transfers between devices, fetch(): return lax.ppermute(x, 'dp', pairs)  37.6 us
    ppermute x25, starting transfers between devices, fetch(): return lax.ppermute(x, 'dp', pairs)  31.4 us
    dot_general x16, matrix products, contract(): lax.dot_general(left, right, (((left_dim,), (right_dim,)), ((), ())), pre...  15.5 us
    ppermute x5, waiting for transfers between devices, swap_tensor(): return lax.ppermute(x, 'tensor', [(t, t ^ mask) for t in range(4)])  5.72 us
    pallas_call x2, Pallas kernels, in_vmem(): pl.pallas_call(kernel, in_specs=[pl.BlockSpec(memory_space=pltpu.VMEM)] *...  4.76 us
    ppermute x5, starting transfers between devices, swap_tensor(): return lax.ppermute(x, 'tensor', [(t, t ^ mask) for t in range(4)])  3.55 us
    dynamic_update_slice x9, local copies, waits for them, and re-layouts, placed(): lax.dynamic_update_slice_in_dim(array, jnp.expand_dims(chunk, at), (y + d...  2.77 us
    dot_general x1, matrix products, body(): jnp.dot(head_outputs, adapter_down_factors, preferred_element_type=jnp.fl...  2.41 us
  transfers between devices with their start and end apart: 30, of which 15 were waited for; matrix products, arithmetic and copies ran while one was open for 21% of the time, Pallas kernels for 4%

profile of v11, /device:TPU:6, one launch (start us, length us, event | category | flops | bytes accessed | tf_op | source)
XLA Modules:
  0.0 115.6 jit_solution(5578967531358712322)
XLA Ops:
  1.7 2.4 %fusion.41 = f32[512,128]{1,0:T(8,128)} fusion(bf16[512,1024]{1,0:T(8,128)(2,1)} %head_ref.1, bf16[1024,128]{1,0:T(8,128)(2,1)} %param.10), kind=kOutput, calls=%fused_computation.78 | convolution fusion | flops 134217728 | bytes 1572864 | tf_op jit(solution)/shard_map/dot_general | solution.py:126
  4.2 3.0 %collective-permute-done.far_ref = bf16[72,1024]{1,0:T(8,128)(2,1)S(1)} collective-permute-done((bf16[72,1024]{1,0:T(8,128)(2,1)}, bf16[72,1024]{1,0:T(8,128)(2,1)S(1)}, u32[]{:S(2)}, u32[]{:S(2)}) %collective-permute-start) | collective-permute-done | bytes 147488 | tf_op jit(solution)/shard_map/ppermute | solution.py:27
  7.9 1.7 %shard_map.94 = (bf16[2,72,640]{2,1,0:T(8,128)(2,1)}, bf16[2,72,384]{2,1,0:T(8,128)(2,1)}) custom-call(s32[1]{0:T(128)} %bitcast.x_ref, bf16[72,1024]{1,0:T(8,128)(2,1)} %mine_ref.1, bf16[72,1024]{1,0:T(8,128)(2,1)} %copy-done.4), custom_call_target="tpu_custom_call" | custom-call | tf_op jit(solution)/shard_map/pallas_call | solution.py:84
  9.6 5.9 %collective-permute-start.2 = (bf16[2,72,640]{2,1,0:T(8,128)(2,1)}, bf16[2,72,640]{2,1,0:T(8,128)(2,1)}, u32[]{:S(2)}, u32[]{:S(2)}) collective-permute-start(bf16[2,72,640]{2,1,0:T(8,128)(2,1)} %get-tuple-element.67), channel_id=1, source_target_pairs={{32,0},{36,4},{40,8},{44,12},{48,16},{52,20},{56,24},{60,28},{64,3... | collective-permute-start | bytes 552968 | tf_op jit(solution)/shard_map/ppermute | solution.py:27
  15.5 3.0 %collective-permute-start.9 = (bf16[2,72,384]{2,1,0:T(8,128)(2,1)}, bf16[2,72,384]{2,1,0:T(8,128)(2,1)}, u32[]{:S(2)}, u32[]{:S(2)}) collective-permute-start(bf16[2,72,384]{2,1,0:T(8,128)(2,1)} %get-tuple-element.65), channel_id=1, source_target_pairs={{4,0},{8,4},{12,8},{0,12},{20,16},{24,20},{28,24},{16,28},{36,32},... | collective-permute-start | bytes 331784 | tf_op jit(solution)/shard_map/ppermute | solution.py:27
  20.7 2.2 %collective-permute-done.3 = bf16[2,72,640]{2,1,0:T(8,128)(2,1)} collective-permute-done((bf16[2,72,640]{2,1,0:T(8,128)(2,1)}, bf16[2,72,640]{2,1,0:T(8,128)(2,1)}, u32[]{:S(2)}, u32[]{:S(2)}) %collective-permute-start.3) | collective-permute-done | bytes 184352 | tf_op jit(solution)/shard_map/ppermute | solution.py:27
  22.9 3.2 %collective-permute-start.10 = (bf16[2,72,384]{2,1,0:T(8,128)(2,1)}, bf16[2,72,384]{2,1,0:T(8,128)(2,1)S(1)}, u32[]{:S(2)}, u32[]{:S(2)}) collective-permute-start(bf16[2,72,384]{2,1,0:T(8,128)(2,1)} %get-tuple-element.65), channel_id=1, source_target_pairs={{8,0},{12,4},{0,8},{4,12},{24,16},{28,20},{16,24},{20,28},{40,32},... | collective-permute-start | bytes 331784 | tf_op jit(solution)/shard_map/ppermute | solution.py:27
  26.4 1.7 %collective-permute-start.6 = (bf16[2,72,640]{2,1,0:T(8,128)(2,1)}, bf16[2,72,640]{2,1,0:T(8,128)(2,1)S(1)}, u32[]{:S(2)}, u32[]{:S(2)}) collective-permute-start(bf16[2,72,640]{2,1,0:T(8,128)(2,1)} %collective-permute-done.3), channel_id=1, source_target_pairs={{224,0},{228,4},{232,8},{236,12},{240,16},{244,20},{248,24},{252,2... | collective-permute-start | bytes 552968 | tf_op jit(solution)/shard_map/ppermute | solution.py:27
  30.0 1.8 %collective-permute-done.5 = bf16[2,72,640]{2,1,0:T(8,128)(2,1)S(1)} collective-permute-done((bf16[2,72,640]{2,1,0:T(8,128)(2,1)}, bf16[2,72,640]{2,1,0:T(8,128)(2,1)S(1)}, u32[]{:S(2)}, u32[]{:S(2)}) %collective-permute-start.5) | collective-permute-done | bytes 184352 | tf_op jit(solution)/shard_map/ppermute | solution.py:27
  31.8 1.5 %collective-permute-done.6 = bf16[2,72,640]{2,1,0:T(8,128)(2,1)S(1)} collective-permute-done((bf16[2,72,640]{2,1,0:T(8,128)(2,1)}, bf16[2,72,640]{2,1,0:T(8,128)(2,1)S(1)}, u32[]{:S(2)}, u32[]{:S(2)}) %collective-permute-start.6) | collective-permute-done | bytes 184352 | tf_op jit(solution)/shard_map/ppermute | solution.py:27
  36.7 2.0 %collective-permute-start.8 = (bf16[2,72,640]{2,1,0:T(8,128)(2,1)S(1)}, bf16[2,72,640]{2,1,0:T(8,128)(2,1)S(1)}, u32[]{:S(2)}, u32[]{:S(2)}) collective-permute-start(bf16[2,72,640]{2,1,0:T(8,128)(2,1)S(1)} %collective-permute-done.6), channel_id=1, source_target_pairs={{224,0},{228,4},{232,8},{236,12},{240,16},{244,20},{248,24},{252,2... | collective-permute-start | bytes 552968 | tf_op jit(solution)/shard_map/ppermute | solution.py:27
  38.9 4.5 %collective-permute-done.8 = bf16[2,72,640]{2,1,0:T(8,128)(2,1)S(1)} collective-permute-done((bf16[2,72,640]{2,1,0:T(8,128)(2,1)S(1)}, bf16[2,72,640]{2,1,0:T(8,128)(2,1)S(1)}, u32[]{:S(2)}, u32[]{:S(2)}) %collective-permute-start.8) | collective-permute-done | bytes 184352 | tf_op jit(solution)/shard_map/ppermute | solution.py:27
  44.3 6.3 %collective-permute-done.16 = bf16[2,72,640]{2,1,0:T(8,128)(2,1)S(1)} collective-permute-done((bf16[2,72,640]{2,1,0:T(8,128)(2,1)S(1)}, bf16[2,72,640]{2,1,0:T(8,128)(2,1)S(1)}, u32[]{:S(2)}, u32[]{:S(2)}) %collective-permute-start.16) | collective-permute-done | bytes 184352 | tf_op jit(solution)/shard_map/ppermute | solution.py:27
  53.7 1.8 %collective-permute-done.12 = bf16[576,384]{1,0:T(8,128)(2,1)} collective-permute-done((bf16[576,384]{1,0:T(8,128)(2,1)S(1)}, bf16[576,384]{1,0:T(8,128)(2,1)}, u32[]{:S(2)}, u32[]{:S(2)}) %collective-permute-start.12) | collective-permute-done | bytes 442400 | tf_op jit(solution)/shard_map/ppermute | solution.py:27
  55.5 4.8 %collective-permute-done.13 = bf16[576,384]{1,0:T(8,128)(2,1)} collective-permute-done((bf16[576,384]{1,0:T(8,128)(2,1)S(1)}, bf16[576,384]{1,0:T(8,128)(2,1)}, u32[]{:S(2)}, u32[]{:S(2)}) %collective-permute-start.13) | collective-permute-done | bytes 442400 | tf_op jit(solution)/shard_map/ppermute | solution.py:27
  61.6 1.7 %collective-permute-start.19 = (bf16[576,384]{1,0:T(8,128)(2,1)}, bf16[576,384]{1,0:T(8,128)(2,1)}, u32[]{:S(2)}, u32[]{:S(2)}) collective-permute-start(bf16[576,384]{1,0:T(8,128)(2,1)} %collective-permute-done.13), channel_id=1, source_target_pairs={{224,0},{228,4},{232,8},{236,12},{240,16},{244,20},{248,24},{252,2... | collective-permute-start | bytes 1327112 | tf_op jit(solution)/shard_map/ppermute | solution.py:27
  65.5 1.6 %shard_map.95.z_ref = bf16[8,512,576]{2,1,0:T(8,128)(2,1)S(1)} custom-call(s32[1]{0:T(128)} %bitcast.20.start_ref, bf16[512,4608]{1,0:T(8,128)(2,1)S(1)} %constant_dynamic-update-slice_fusion.g_ref), custom_call_target="tpu_custom_call" | custom-call | tf_op jit(solution)/shard_map/pallas_call | solution.py:49
  67.1 1.5 %fusion.5 = f32[512,384]{1,0:T(8,128)S(1)} fusion(bf16[576,384]{1,0:T(8,128)(2,1)} %collective-permute-done.13, bf16[8,512,576]{2,1,0:T(8,128)(2,1)S(1)} %shard_map.95.z_ref), kind=kOutput, calls=%fused_computation.25 | convolution fusion | flops 226492416 | bytes 1884160 | tf_op jit(solution)/shard_map/dot_general | solution.py:15
  68.7 1.5 %fusion.4 = f32[512,384]{1,0:T(8,128)S(1)} fusion(bf16[576,384]{1,0:T(8,128)(2,1)} %collective-permute-done.12, bf16[8,512,576]{2,1,0:T(8,128)(2,1)S(1)} %shard_map.95.z_ref), kind=kOutput, calls=%fused_computation.23 | convolution fusion | flops 226492416 | bytes 1884160 | tf_op jit(solution)/shard_map/dot_general | solution.py:15
  73.0 1.9 %collective-permute-start.23 = (f32[512,128]{1,0:T(8,128)S(1)}, f32[512,128]{1,0:T(8,128)S(1)}, u32[]{:S(2)}, u32[]{:S(2)}) collective-permute-start(f32[512,128]{1,0:T(8,128)S(1)} %add.143), channel_id=1, source_target_pairs={{0,2},{1,3},{2,0},{3,1},{4,6},{5,7},{6,4},{7,5},{8,10},{9,11},{10,... | collective-permute-start | bytes 786440 | tf_op jit(solution)/shard_map/ppermute | solution.py:31
  76.7 5.7 %collective-permute-done.23 = f32[512,128]{1,0:T(8,128)S(1)} collective-permute-done((f32[512,128]{1,0:T(8,128)S(1)}, f32[512,128]{1,0:T(8,128)S(1)}, u32[]{:S(2)}, u32[]{:S(2)}) %collective-permute-start.23) | collective-permute-done | bytes 262176 | tf_op jit(solution)/shard_map/ppermute | solution.py:31
  82.7 2.2 %convolution_multiply_fusion = f32[128,4608]{1,0:T(8,128)} fusion(bf16[512,128]{1,0:T(8,128)(2,1)S(1)} %select_convert_fusion.1, bf16[512,4608]{1,0:T(8,128)(2,1)S(1)} %constant_dynamic-update-slice_fusion.g_ref), kind=kOutput, calls=%fused_computation | convolution fusion | flops 604569600 | bytes 7208960 | tf_op jit(solution)/shard_map/dot_general | solution.py:15
  86.4 1.6 %collective-permute-start.26 = (bf16[576,384]{1,0:T(8,128)(2,1)}, bf16[576,384]{1,0:T(8,128)(2,1)S(1)}, u32[]{:S(2)}, u32[]{:S(2)}) collective-permute-start(bf16[576,384]{1,0:T(8,128)(2,1)} %collective-permute-done.18), channel_id=1, source_target_pairs={{32,0},{36,4},{40,8},{44,12},{48,16},{52,20},{56,24},{60,28},{64,3... | collective-permute-start | bytes 1327112 | tf_op jit(solution)/shard_map/ppermute | solution.py:27
  88.5 2.1 %collective-permute-start.24 = (bf16[4,2,72,640]{3,2,1,0:T(8,128)(2,1)S(1)}, bf16[4,2,72,640]{3,2,1,0:T(8,128)(2,1)S(1)}, u32[]{:S(2)}, u32[]{:S(2)}) collective-permute-start(bf16[4,2,72,640]{3,2,1,0:T(8,128)(2,1)S(1)} %pad_maximum_fusion.1), channel_id=1, source_target_pairs={{4,0},{8,4},{12,8},{0,12},{20,16},{24,20},{28,24},{16,28},{36,32},... | collective-permute-start | bytes 2211848 | tf_op jit(solution)/shard_map/ppermute | solution.py:27
  94.4 3.1 %collective-permute-done.26 = bf16[576,384]{1,0:T(8,128)(2,1)S(1)} collective-permute-done((bf16[576,384]{1,0:T(8,128)(2,1)}, bf16[576,384]{1,0:T(8,128)(2,1)S(1)}, u32[]{:S(2)}, u32[]{:S(2)}) %collective-permute-start.26) | collective-permute-done | bytes 442400 | tf_op jit(solution)/shard_map/ppermute | solution.py:27
  97.6 2.4 %collective-permute-done.27 = bf16[576,384]{1,0:T(8,128)(2,1)S(1)} collective-permute-done((bf16[576,384]{1,0:T(8,128)(2,1)}, bf16[576,384]{1,0:T(8,128)(2,1)S(1)}, u32[]{:S(2)}, u32[]{:S(2)}) %collective-permute-start.27) | collective-permute-done | bytes 442400 | tf_op jit(solution)/shard_map/ppermute | solution.py:27
  100.5 1.5 %fusion.14 = f32[512,384]{1,0:T(8,128)S(1)} fusion(bf16[576,384]{1,0:T(8,128)(2,1)} %collective-permute-done.19, bf16[8,512,576]{2,1,0:T(8,128)(2,1)S(1)} %shard_map.95.z_ref), kind=kOutput, calls=%fused_computation.33 | convolution fusion | flops 226492416 | bytes 1884160 | tf_op jit(solution)/shard_map/dot_general | solution.py:15
  102.0 1.5 %fusion.16 = f32[512,384]{1,0:T(8,128)S(1)} fusion(bf16[576,384]{1,0:T(8,128)(2,1)} %collective-permute-done.18, bf16[8,512,576]{2,1,0:T(8,128)(2,1)S(1)} %shard_map.95.z_ref), kind=kOutput, calls=%fused_computation.35 | convolution fusion | flops 226492416 | bytes 1884160 | tf_op jit(solution)/shard_map/dot_general | solution.py:15
  104.0 1.7 %collective-permute-start.29 = (bf16[288,384]{1,0:T(8,128)(2,1)S(1)}, bf16[288,384]{1,0:T(8,128)(2,1)S(1)}, u32[]{:S(2)}, u32[]{:S(2)}) collective-permute-start(bf16[288,384]{1,0:T(8,128)(2,1)S(1)} %slice.72), channel_id=1, source_target_pairs={{224,0},{228,4},{232,8},{236,12},{240,16},{244,20},{248,24},{252,2... | collective-permute-start | bytes 663560 | tf_op jit(solution)/shard_map/ppermute | solution.py:27
  106.3 3.4 %collective-permute-done.28 = bf16[288,384]{1,0:T(8,128)(2,1)S(1)} collective-permute-done((bf16[288,384]{1,0:T(8,128)(2,1)S(1)}, bf16[288,384]{1,0:T(8,128)(2,1)S(1)}, u32[]{:S(2)}, u32[]{:S(2)}) %collective-permute-start.28) | collective-permute-done | bytes 221216 | tf_op jit(solution)/shard_map/ppermute | solution.py:27
  109.6 1.5 %collective-permute-done.29 = bf16[288,384]{1,0:T(8,128)(2,1)S(1)} collective-permute-done((bf16[288,384]{1,0:T(8,128)(2,1)S(1)}, bf16[288,384]{1,0:T(8,128)(2,1)S(1)}, u32[]{:S(2)}, u32[]{:S(2)}) %collective-permute-start.29) | collective-permute-done | bytes 221216 | tf_op jit(solution)/shard_map/ppermute | solution.py:27
  112.1 3.5 %shard_map.97 = bf16[512,1024]{1,0:T(8,128)(2,1)} custom-call(bf16[8,512,576]{2,1,0:T(8,128)(2,1)S(1)} %shard_map.95.z_ref, bf16[4,576,640]{2,1,0:T(8,128)(2,1)S(1)} %bitcast.111, f32[512,640]{1,0:T(8,128)S(1)} %convolution_add_fusion.total_ref, f32[512,1]{1,0:T(8,128)S(1)} %fusion.35.live_ref, bf16[512,384]{1,0:T(8,128)(2,1)S(1)} %select_convert_fusion.b_ref), custom_call_target="tpu_custom_call" | custom-call | tf_op jit(solution)/shard_map/pallas_call | solution.py:97
  (90 shorter events, 29.3 us)
Async XLA Ops:
  0.6 69.6 %copy-start = (bf16[128,4608]{1,0:T(8,128)(2,1)S(1)}, bf16[128,4608]{1,0:T(8,128)(2,1)}, u32[]{:S(2)}) copy-start(bf16[128,4608]{1,0:T(8,128)(2,1)} %param.11) | copy-start | bytes 3538948
  0.6 50.5 %copy-start.5 = (s32[512]{0:T(512)S(1)}, s32[512]{0:T(512)}, u32[]{:S(2)}) copy-start(s32[512]{0:T(512)} %param.12) | copy-start | bytes 6148
  0.7 6.6 %collective-permute-start.1 = (bf16[128,4608]{1,0:T(8,128)(2,1)}, bf16[128,4608]{1,0:T(8,128)(2,1)S(1)}, u32[]{:S(2)}, u32[]{:S(2)}) collective-permute-start(bf16[128,4608]{1,0:T(8,128)(2,1)} %param.8), channel_id=1, source_target_pairs={{0,1},{1,0},{2,3},{3,2},{4,5},{5,4},{6,7},{7,6},{8,9},{9,8},{10,11... | collective-permute-start | bytes 3538952 | tf_op jit(solution)/shard_map/ppermute | solution.py:31
  0.8 6.5 %collective-permute-start = (bf16[72,1024]{1,0:T(8,128)(2,1)}, bf16[72,1024]{1,0:T(8,128)(2,1)S(1)}, u32[]{:S(2)}, u32[]{:S(2)}) collective-permute-start(bf16[72,1024]{1,0:T(8,128)(2,1)} %mine_ref.1), channel_id=1, source_target_pairs={{16,0},{20,4},{24,8},{28,12},{0,16},{4,20},{8,24},{12,28},{48,32},... | collective-permute-start | bytes 442376 | tf_op jit(solution)/shard_map/ppermute | solution.py:27
  4.1 16.5 %collective-permute-start.4 = (f32[512,128]{1,0:T(8,128)}, f32[512,128]{1,0:T(8,128)}, u32[]{:S(2)}, u32[]{:S(2)}) collective-permute-start(f32[512,128]{1,0:T(8,128)} %fusion.41), channel_id=1, source_target_pairs={{0,1},{1,0},{2,3},{3,2},{4,5},{5,4},{6,7},{7,6},{8,9},{9,8},{10,11... | collective-permute-start | bytes 786440 | tf_op jit(solution)/shard_map/ppermute | solution.py:31
  9.6 11.1 %collective-permute-start.2 = (bf16[2,72,640]{2,1,0:T(8,128)(2,1)}, bf16[2,72,640]{2,1,0:T(8,128)(2,1)}, u32[]{:S(2)}, u32[]{:S(2)}) collective-permute-start(bf16[2,72,640]{2,1,0:T(8,128)(2,1)} %get-tuple-element.67), channel_id=1, source_target_pairs={{32,0},{36,4},{40,8},{44,12},{48,16},{52,20},{56,24},{60,28},{64,3... | collective-permute-start | bytes 552968 | tf_op jit(solution)/shard_map/ppermute | solution.py:27
  15.5 7.4 %collective-permute-start.3 = (bf16[2,72,640]{2,1,0:T(8,128)(2,1)}, bf16[2,72,640]{2,1,0:T(8,128)(2,1)}, u32[]{:S(2)}, u32[]{:S(2)}) collective-permute-start(bf16[2,72,640]{2,1,0:T(8,128)(2,1)} %get-tuple-element.67), channel_id=1, source_target_pairs={{224,0},{228,4},{232,8},{236,12},{240,16},{244,20},{248,24},{252,2... | collective-permute-start | bytes 552968 | tf_op jit(solution)/shard_map/ppermute | solution.py:27
  15.5 10.9 %collective-permute-start.9 = (bf16[2,72,384]{2,1,0:T(8,128)(2,1)}, bf16[2,72,384]{2,1,0:T(8,128)(2,1)}, u32[]{:S(2)}, u32[]{:S(2)}) collective-permute-start(bf16[2,72,384]{2,1,0:T(8,128)(2,1)} %get-tuple-element.65), channel_id=1, source_target_pairs={{4,0},{8,4},{12,8},{0,12},{20,16},{24,20},{28,24},{16,28},{36,32},... | collective-permute-start | bytes 331784 | tf_op jit(solution)/shard_map/ppermute | solution.py:27
  18.5 32.8 %collective-permute-start.17 = (bf16[128,4608]{1,0:T(8,128)(2,1)}, bf16[128,4608]{1,0:T(8,128)(2,1)S(1)}, u32[]{:S(2)}, u32[]{:S(2)}) collective-permute-start(bf16[128,4608]{1,0:T(8,128)(2,1)} %param.8), channel_id=1, source_target_pairs={{0,2},{1,3},{2,0},{3,1},{4,6},{5,7},{6,4},{7,5},{8,10},{9,11},{10,... | collective-permute-start | bytes 3538952 | tf_op jit(solution)/shard_map/ppermute | solution.py:31
  20.6 16.1 %collective-permute-start.11 = (bf16[2,72,384]{2,1,0:T(8,128)(2,1)}, bf16[2,72,384]{2,1,0:T(8,128)(2,1)S(1)}, u32[]{:S(2)}, u32[]{:S(2)}) collective-permute-start(bf16[2,72,384]{2,1,0:T(8,128)(2,1)} %get-tuple-element.65), channel_id=1, source_target_pairs={{12,0},{0,4},{4,8},{8,12},{28,16},{16,20},{20,24},{24,28},{44,32},... | collective-permute-start | bytes 331784 | tf_op jit(solution)/shard_map/ppermute | solution.py:27
  22.9 7.1 %collective-permute-start.10 = (bf16[2,72,384]{2,1,0:T(8,128)(2,1)}, bf16[2,72,384]{2,1,0:T(8,128)(2,1)S(1)}, u32[]{:S(2)}, u32[]{:S(2)}) collective-permute-start(bf16[2,72,384]{2,1,0:T(8,128)(2,1)} %get-tuple-element.65), channel_id=1, source_target_pairs={{8,0},{12,4},{0,8},{4,12},{24,16},{28,20},{16,24},{20,28},{40,32},... | collective-permute-start | bytes 331784 | tf_op jit(solution)/shard_map/ppermute | solution.py:27
  26.1 5.7 %collective-permute-start.5 = (bf16[2,72,640]{2,1,0:T(8,128)(2,1)}, bf16[2,72,640]{2,1,0:T(8,128)(2,1)S(1)}, u32[]{:S(2)}, u32[]{:S(2)}) collective-permute-start(bf16[2,72,640]{2,1,0:T(8,128)(2,1)} %collective-permute-done.2), channel_id=1, source_target_pairs={{32,0},{36,4},{40,8},{44,12},{48,16},{52,20},{56,24},{60,28},{64,3... | collective-permute-start | bytes 552968 | tf_op jit(solution)/shard_map/ppermute | solution.py:27
  26.4 7.0 %collective-permute-start.6 = (bf16[2,72,640]{2,1,0:T(8,128)(2,1)}, bf16[2,72,640]{2,1,0:T(8,128)(2,1)S(1)}, u32[]{:S(2)}, u32[]{:S(2)}) collective-permute-start(bf16[2,72,640]{2,1,0:T(8,128)(2,1)} %collective-permute-done.3), channel_id=1, source_target_pairs={{224,0},{228,4},{232,8},{236,12},{240,16},{244,20},{248,24},{252,2... | collective-permute-start | bytes 552968 | tf_op jit(solution)/shard_map/ppermute | solution.py:27
  33.3 5.5 %collective-permute-start.7 = (bf16[2,72,640]{2,1,0:T(8,128)(2,1)S(1)}, bf16[2,72,640]{2,1,0:T(8,128)(2,1)S(1)}, u32[]{:S(2)}, u32[]{:S(2)}) collective-permute-start(bf16[2,72,640]{2,1,0:T(8,128)(2,1)S(1)} %collective-permute-done.5), channel_id=1, source_target_pairs={{32,0},{36,4},{40,8},{44,12},{48,16},{52,20},{56,24},{60,28},{64,3... | collective-permute-start | bytes 552968 | tf_op jit(solution)/shard_map/ppermute | solution.py:27
  34.6 16.7 %collective-permute-start.14 = (bf16[4,2,72,640]{3,2,1,0:T(8,128)(2,1)S(1)}, bf16[4,2,72,640]{3,2,1,0:T(8,128)(2,1)S(1)}, u32[]{:S(2)}, u32[]{:S(2)}) collective-permute-start(bf16[4,2,72,640]{3,2,1,0:T(8,128)(2,1)S(1)} %pad_maximum_fusion), channel_id=1, source_target_pairs={{4,0},{8,4},{12,8},{0,12},{20,16},{24,20},{28,24},{16,28},{36,32},... | collective-permute-start | bytes 2211848 | tf_op jit(solution)/shard_map/ppermute | solution.py:27
  35.7 16.6 %collective-permute-start.15 = (bf16[4,2,72,640]{3,2,1,0:T(8,128)(2,1)S(1)}, bf16[4,2,72,640]{3,2,1,0:T(8,128)(2,1)S(1)}, u32[]{:S(2)}, u32[]{:S(2)}) collective-permute-start(bf16[4,2,72,640]{3,2,1,0:T(8,128)(2,1)S(1)} %pad_maximum_fusion), channel_id=1, source_target_pairs={{12,0},{0,4},{4,8},{8,12},{28,16},{16,20},{20,24},{24,28},{44,32},... | collective-permute-start | bytes 2211848 | tf_op jit(solution)/shard_map/ppermute | solution.py:27
  36.7 6.7 %collective-permute-start.8 = (bf16[2,72,640]{2,1,0:T(8,128)(2,1)S(1)}, bf16[2,72,640]{2,1,0:T(8,128)(2,1)S(1)}, u32[]{:S(2)}, u32[]{:S(2)}) collective-permute-start(bf16[2,72,640]{2,1,0:T(8,128)(2,1)S(1)} %collective-permute-done.6), channel_id=1, source_target_pairs={{224,0},{228,4},{232,8},{236,12},{240,16},{244,20},{248,24},{252,2... | collective-permute-start | bytes 552968 | tf_op jit(solution)/shard_map/ppermute | solution.py:27
  43.4 7.2 %collective-permute-start.16 = (bf16[2,72,640]{2,1,0:T(8,128)(2,1)S(1)}, bf16[2,72,640]{2,1,0:T(8,128)(2,1)S(1)}, u32[]{:S(2)}, u32[]{:S(2)}) collective-permute-start(bf16[2,72,640]{2,1,0:T(8,128)(2,1)S(1)} %collective-permute-done.7), channel_id=1, source_target_pairs={{32,0},{36,4},{40,8},{44,12},{48,16},{52,20},{56,24},{60,28},{64,3... | collective-permute-start | bytes 552968 | tf_op jit(solution)/shard_map/ppermute | solution.py:27
  43.5 12.0 %collective-permute-start.12 = (bf16[576,384]{1,0:T(8,128)(2,1)S(1)}, bf16[576,384]{1,0:T(8,128)(2,1)}, u32[]{:S(2)}, u32[]{:S(2)}) collective-permute-start(bf16[576,384]{1,0:T(8,128)(2,1)S(1)} %bitcast.116), channel_id=1, source_target_pairs={{32,0},{36,4},{40,8},{44,12},{48,16},{52,20},{56,24},{60,28},{64,3... | collective-permute-start | bytes 1327112 | tf_op jit(solution)/shard_map/ppermute | solution.py:27
  50.6 9.6 %collective-permute-start.13 = (bf16[576,384]{1,0:T(8,128)(2,1)S(1)}, bf16[576,384]{1,0:T(8,128)(2,1)}, u32[]{:S(2)}, u32[]{:S(2)}) collective-permute-start(bf16[576,384]{1,0:T(8,128)(2,1)S(1)} %bitcast.117), channel_id=1, source_target_pairs={{224,0},{228,4},{232,8},{236,12},{240,16},{244,20},{248,24},{252,2... | collective-permute-start | bytes 1327112 | tf_op jit(solution)/shard_map/ppermute | solution.py:27
  52.3 32.5 %collective-permute-start.20 = (bf16[4,2,72,640]{3,2,1,0:T(8,128)(2,1)S(1)}, bf16[4,2,72,640]{3,2,1,0:T(8,128)(2,1)}, u32[]{:S(2)}, u32[]{:S(2)}) collective-permute-start(bf16[4,2,72,640]{3,2,1,0:T(8,128)(2,1)S(1)} %collective-permute-done.14), channel_id=1, source_target_pairs={{4,0},{8,4},{12,8},{0,12},{20,16},{24,20},{28,24},{16,28},{36,32},... | collective-permute-start | bytes 2211848 | tf_op jit(solution)/shard_map/ppermute | solution.py:27
  60.2 5.1 %collective-permute-start.22 = (bf16[128,4608]{1,0:T(8,128)(2,1)S(1)}, bf16[128,4608]{1,0:T(8,128)(2,1)S(1)}, u32[]{:S(2)}, u32[]{:S(2)}) collective-permute-start(bf16[128,4608]{1,0:T(8,128)(2,1)S(1)} %collective-permute-done.17), channel_id=1, source_target_pairs={{0,1},{1,0},{2,3},{3,2},{4,5},{5,4},{6,7},{7,6},{8,9},{9,8},{10,11... | collective-permute-start | bytes 3538952 | tf_op jit(solution)/shard_map/ppermute | solution.py:31
  60.2 24.7 %collective-permute-start.21 = (bf16[4,2,72,640]{3,2,1,0:T(8,128)(2,1)S(1)}, bf16[4,2,72,640]{3,2,1,0:T(8,128)(2,1)S(1)}, u32[]{:S(2)}, u32[]{:S(2)}) collective-permute-start(bf16[4,2,72,640]{3,2,1,0:T(8,128)(2,1)S(1)} %pad_maximum_fusion.1), channel_id=1, source_target_pairs={{12,0},{0,4},{4,8},{8,12},{28,16},{16,20},{20,24},{24,28},{44,32},... | collective-permute-start | bytes 2211848 | tf_op jit(solution)/shard_map/ppermute | solution.py:27
  61.4 23.5 %collective-permute-start.18 = (bf16[576,384]{1,0:T(8,128)(2,1)}, bf16[576,384]{1,0:T(8,128)(2,1)}, u32[]{:S(2)}, u32[]{:S(2)}) collective-permute-start(bf16[576,384]{1,0:T(8,128)(2,1)} %collective-permute-done.12), channel_id=1, source_target_pairs={{32,0},{36,4},{40,8},{44,12},{48,16},{52,20},{56,24},{60,28},{64,3... | collective-permute-start | bytes 1327112 | tf_op jit(solution)/shard_map/ppermute | solution.py:27
  61.6 23.3 %collective-permute-start.19 = (bf16[576,384]{1,0:T(8,128)(2,1)}, bf16[576,384]{1,0:T(8,128)(2,1)}, u32[]{:S(2)}, u32[]{:S(2)}) collective-permute-start(bf16[576,384]{1,0:T(8,128)(2,1)} %collective-permute-done.13), channel_id=1, source_target_pairs={{224,0},{228,4},{232,8},{236,12},{240,16},{244,20},{248,24},{252,2... | collective-permute-start | bytes 1327112 | tf_op jit(solution)/shard_map/ppermute | solution.py:27
  73.0 9.5 %collective-permute-start.23 = (f32[512,128]{1,0:T(8,128)S(1)}, f32[512,128]{1,0:T(8,128)S(1)}, u32[]{:S(2)}, u32[]{:S(2)}) collective-permute-start(f32[512,128]{1,0:T(8,128)S(1)} %add.143), channel_id=1, source_target_pairs={{0,2},{1,3},{2,0},{3,1},{4,6},{5,7},{6,4},{7,5},{8,10},{9,11},{10,... | collective-permute-start | bytes 786440 | tf_op jit(solution)/shard_map/ppermute | solution.py:31
  86.4 11.1 %collective-permute-start.26 = (bf16[576,384]{1,0:T(8,128)(2,1)}, bf16[576,384]{1,0:T(8,128)(2,1)S(1)}, u32[]{:S(2)}, u32[]{:S(2)}) collective-permute-start(bf16[576,384]{1,0:T(8,128)(2,1)} %collective-permute-done.18), channel_id=1, source_target_pairs={{32,0},{36,4},{40,8},{44,12},{48,16},{52,20},{56,24},{60,28},{64,3... | collective-permute-start | bytes 1327112 | tf_op jit(solution)/shard_map/ppermute | solution.py:27
  88.0 12.0 %collective-permute-start.27 = (bf16[576,384]{1,0:T(8,128)(2,1)}, bf16[576,384]{1,0:T(8,128)(2,1)S(1)}, u32[]{:S(2)}, u32[]{:S(2)}) collective-permute-start(bf16[576,384]{1,0:T(8,128)(2,1)} %collective-permute-done.19), channel_id=1, source_target_pairs={{224,0},{228,4},{232,8},{236,12},{240,16},{244,20},{248,24},{252,2... | collective-permute-start | bytes 1327112 | tf_op jit(solution)/shard_map/ppermute | solution.py:27
  88.5 23.3 %collective-permute-start.24 = (bf16[4,2,72,640]{3,2,1,0:T(8,128)(2,1)S(1)}, bf16[4,2,72,640]{3,2,1,0:T(8,128)(2,1)S(1)}, u32[]{:S(2)}, u32[]{:S(2)}) collective-permute-start(bf16[4,2,72,640]{3,2,1,0:T(8,128)(2,1)S(1)} %pad_maximum_fusion.1), channel_id=1, source_target_pairs={{4,0},{8,4},{12,8},{0,12},{20,16},{24,20},{28,24},{16,28},{36,32},... | collective-permute-start | bytes 2211848 | tf_op jit(solution)/shard_map/ppermute | solution.py:27
  90.6 21.2 %collective-permute-start.25 = (bf16[4,2,72,640]{3,2,1,0:T(8,128)(2,1)S(1)}, bf16[4,2,72,640]{3,2,1,0:T(8,128)(2,1)S(1)}, u32[]{:S(2)}, u32[]{:S(2)}) collective-permute-start(bf16[4,2,72,640]{3,2,1,0:T(8,128)(2,1)S(1)} %collective-permute-done.21), channel_id=1, source_target_pairs={{12,0},{0,4},{4,8},{8,12},{28,16},{16,20},{20,24},{24,28},{44,32},... | collective-permute-start | bytes 2211848 | tf_op jit(solution)/shard_map/ppermute | solution.py:27
  103.6 6.0 %collective-permute-start.28 = (bf16[288,384]{1,0:T(8,128)(2,1)S(1)}, bf16[288,384]{1,0:T(8,128)(2,1)S(1)}, u32[]{:S(2)}, u32[]{:S(2)}) collective-permute-start(bf16[288,384]{1,0:T(8,128)(2,1)S(1)} %slice.71), channel_id=1, source_target_pairs={{32,0},{36,4},{40,8},{44,12},{48,16},{52,20},{56,24},{60,28},{64,3... | collective-permute-start | bytes 663560 | tf_op jit(solution)/shard_map/ppermute | solution.py:27
  104.0 7.1 %collective-permute-start.29 = (bf16[288,384]{1,0:T(8,128)(2,1)S(1)}, bf16[288,384]{1,0:T(8,128)(2,1)S(1)}, u32[]{:S(2)}, u32[]{:S(2)}) collective-permute-start(bf16[288,384]{1,0:T(8,128)(2,1)S(1)} %slice.72), channel_id=1, source_target_pairs={{224,0},{228,4},{232,8},{236,12},{240,16},{244,20},{248,24},{252,2... | collective-permute-start | bytes 663560 | tf_op jit(solution)/shard_map/ppermute | solution.py:27
  (4 other events, 7.2 us)
